TPU v7x, 32 devices: a whole 2x2x4 slice. The times are simulated.
32 devices in a mesh: pipe: 4 (over y, core), seq: 8 (over z, x).
Axes of the slice: x: 2, y: 2, z: 4, core: 2. Of those that a mesh axis runs over, the one named last changes fastest.
Arguments:
- act_in: bfloat16 [4, 1024, 2048], P('pipe', 'seq'), may hold values from -20 to 20
- saved_in: bfloat16 [4, 1024, 2048], P('pipe', 'seq'), may hold values from -20 to 20
- grad_in: bfloat16 [4, 1024, 2048], P('pipe', 'seq'), may hold values from -18 to 18
- gain: float32 [4, 2048], P('pipe'), may hold values from 0.5 to 1.5
- weight: bfloat16 [4, 512, 4, 512], P('pipe', 'seq'), may hold values from -0.25 to 0.25
- left_blocks: bfloat16 [4, 16, 64, 64], P('pipe', 'seq'), may hold values from -0.75 to 0.75
- right_blocks: bfloat16 [4, 64, 16, 16], P('pipe', 'seq'), may hold values from -1.5 to 1.5
Outputs:
- handed_on: bfloat16 [4, 1024, 2048], P('pipe', 'seq')
- grad_handed: bfloat16 [4, 1024, 2048], P('pipe', 'seq')
- grad_weight: float32 [4, 512, 4, 512], P('pipe', 'seq')
- grad_gain: float32 [4, 2048], P('pipe')
- grad_left: float32 [4, 16, 64, 64], P('pipe', 'seq')
- grad_right: float32 [4, 64, 16, 16], P('pipe', 'seq')
All inputs are finite; a program needn't handle non-finite values.
Results may differ from a plain program's by a relative error of at most 0.0076.
Values may be sent and summed in bfloat16 or wider, within the bound.
No kernel may reach another device: no remote copies, remote signals or barrier semaphores. Data moves between devices by JAX's collectives and lax.ppermute only.
A program may use at most 64 MiB of HBM per device.

v0:
```python
import jax
import jax.numpy as jnp
from jax import lax
from jax.sharding import PartitionSpec as P


def shifted_2(block, axis, distance):
    devices = range(lax.axis_size(axis))
    route = [((i - distance) % len(devices), i) for i in devices]
    return lax.ppermute(block, axis, route)


def normalize(rows, gain_row):
    widened = rows.astype(jnp.float32)
    inv_rms = lax.rsqrt(jnp.mean(widened * widened, axis=-1, keepdims=True) + 1e-06)
    normed = widened * inv_rms
    return (inv_rms, normed, (normed * gain_row).astype(jnp.bfloat16))


def shards(act_in, saved_in, grad_in, gain, weight, left_blocks, right_blocks):
    current = act_in[0]
    stored = saved_in[0]
    upstream = grad_in[0]
    gain_row = gain[0]
    left_factor = left_blocks[0]
    right_factor = right_blocks[0]
    tokens_dev, model_width = current.shape
    nblocks = weight.shape[2]
    inner_width = weight.shape[3]
    groups = left_factor.shape[0]
    block_len = left_factor.shape[1]
    cur_scale, cur_norm, cur_in = normalize(current, gain_row)
    sto_scale, sto_norm, sto_in = normalize(stored, gain_row)
    cur_split = cur_in.reshape(tokens_dev, nblocks, inner_width)
    sto_split = sto_in.reshape(tokens_dev, nblocks, inner_width)
    full_weight = lax.all_gather(weight, "seq", axis=1, tiled=True)[0]
    cur_proj = jnp.einsum(
        "tki,ikj->tkj", cur_split, full_weight, preferred_element_type=jnp.float32
    )
    sto_proj = jnp.einsum(
        "tki,ikj->tkj", sto_split, full_weight, preferred_element_type=jnp.float32
    )
    cur_u = cur_proj.astype(jnp.bfloat16).reshape(groups, block_len, model_width)
    sto_u = sto_proj.astype(jnp.bfloat16).reshape(groups, block_len, model_width)
    cur_first = jnp.einsum(
        "abc,acd->abd", left_factor, cur_u, preferred_element_type=jnp.float32
    ).astype(jnp.bfloat16)
    sto_first = jnp.einsum(
        "abc,acd->abd", left_factor, sto_u, preferred_element_type=jnp.float32
    ).astype(jnp.bfloat16)
    upstream_g = upstream.reshape(groups, block_len, model_width)
    adjoint_mix = (upstream_g.astype(jnp.float32) * sto_u.astype(jnp.float32)).astype(jnp.bfloat16)

    def monarch(first_mix):
        shifted = lax.all_to_all(first_mix, "seq", split_axis=1, concat_axis=0, tiled=True)
        second = jnp.einsum(
            "bxy,ybd->xbd", right_factor, shifted, preferred_element_type=jnp.float32
        ).astype(jnp.bfloat16)
        return (lax.all_to_all(second, "seq", split_axis=0, concat_axis=1, tiled=True), shifted)

    cur_mix, unused = monarch(cur_first)
    sto_mix, sto_shifted = monarch(sto_first)
    adjoint_shifted = lax.all_to_all(adjoint_mix, "seq", split_axis=1, concat_axis=0, tiled=True)
    adjoint_second = jnp.einsum(
        "bxy,xbd->ybd", right_factor, adjoint_shifted, preferred_element_type=jnp.float32
    ).astype(jnp.bfloat16)
    right_grad = jnp.einsum(
        "xbd,ybd->bxy", adjoint_shifted, sto_shifted, preferred_element_type=jnp.float32
    )
    adjoint_first = lax.all_to_all(adjoint_second, "seq", split_axis=0, concat_axis=1, tiled=True)
    output = (
        current.astype(jnp.float32)
        + cur_u.reshape(tokens_dev, model_width).astype(jnp.float32)
        * cur_mix.reshape(tokens_dev, model_width).astype(jnp.float32)
    ).astype(jnp.bfloat16)
    handed_on = shifted_2(output, "pipe", 1)
    local_grad = upstream_g.astype(jnp.float32) * sto_mix.astype(jnp.float32) + jnp.einsum(
        "abc,abd->acd", left_factor, adjoint_first, preferred_element_type=jnp.float32
    )
    proj_grad = local_grad.astype(jnp.bfloat16).reshape(tokens_dev, nblocks, inner_width)
    left_grad = jnp.einsum("abd,acd->abc", adjoint_first, sto_u, preferred_element_type=jnp.float32)
    normed_grad = jnp.einsum(
        "tkj,ikj->tki", proj_grad, full_weight, preferred_element_type=jnp.float32
    )
    normed_grad = normed_grad.reshape(tokens_dev, model_width)
    weight_grad = lax.psum_scatter(
        jnp.einsum("tki,tkj->ikj", sto_split, proj_grad, preferred_element_type=jnp.float32),
        "seq",
        scatter_dimension=0,
        tiled=True,
    )
    gain_grad = lax.psum(jnp.sum(normed_grad * sto_norm, axis=0), "seq")
    scaled = normed_grad * gain_row
    input_grad = (
        upstream.astype(jnp.float32)
        + sto_scale * (scaled - sto_norm * jnp.mean(scaled * sto_norm, axis=-1, keepdims=True))
    ).astype(jnp.bfloat16)
    grad_handed = shifted_2(input_grad, "pipe", -1)
    return (
        handed_on[None],
        grad_handed[None],
        weight_grad[None],
        gain_grad[None],
        left_grad[None],
        right_grad[None],
    )


def solution(mesh):
    return jax.shard_map(
        shards,
        mesh=mesh,
        in_specs=(
            P("pipe", "seq", None),
            P("pipe", "seq", None),
            P("pipe", "seq", None),
            P("pipe", None),
            P("pipe", "seq", None, None),
            P("pipe", "seq", None, None),
            P("pipe", "seq", None, None),
        ),
        out_specs=(
            P("pipe", "seq", None),
            P("pipe", "seq", None),
            P("pipe", "seq", None, None),
            P("pipe", None),
            P("pipe", "seq", None, None),
            P("pipe", "seq", None, None),
        ),
        check_vma=False,
    )
```

profile of v0, /device:TPU:0, one launch (start us, length us, event | category | flops | bytes accessed | tf_op | source)
XLA Modules:
  0.0 335.9 jit_solution(16606664297137757510)
XLA Ops:
  7.2 1.7 copy.106
  9.5 1.4 reduce.5
  10.8 1.3 copy.115
  12.7 50.1 %all-gather.2.cloned.1.call-done = bf16[1,512,4,512]{3,1,2,0:T(8,128)(2,1)} async-done(((bf16[1,64,4,512]{3,1,2,0:T(8,128)(2,1)}), bf16[1,512,4,512]{3,1,2,0:T(8,128)(2,1)}) %all-gather.2.cloned.1.call-update) | async-done | bytes 2097168 | tf_op jit(solution)/shard_map/all_gather | solution.py:36
  62.8 2.1 fusion.22
  66.0 1.3 copy.119
  67.3 4.2 %all-to-all-start.2 = ((bf16[2,64,2048]{2,0,1:T(2,128)(2,1)}), bf16[2,64,2048]{2,0,1:T(2,128)(2,1)}, u32[]{:S(2)}, u32[]{:S(2)}) async-start(bf16[2,64,2048]{2,0,1:T(2,128)(2,1)} %copy.119), calls=%async_computation.2 | async-start | bytes 1048576 | tf_op jit(solution)/shard_map/all_to_all | solution.py:55
  72.1 1.3 copy.123
  73.5 11.7 %all-to-all-done.2 = bf16[2,64,2048]{2,0,1:T(2,128)(2,1)} async-done(((bf16[2,64,2048]{2,0,1:T(2,128)(2,1)}), bf16[2,64,2048]{2,0,1:T(2,128)(2,1)}, u32[]{:S(2)}, u32[]{:S(2)}) %all-to-all-start.2) | async-done | bytes 524320 | tf_op jit(solution)/shard_map/all_to_all | solution.py:55
  85.2 3.6 %all-to-all-start.4 = ((bf16[2,64,2048]{2,0,1:T(2,128)(2,1)}), bf16[2,64,2048]{2,0,1:T(2,128)(2,1)S(1)}, u32[]{:S(2)}, u32[]{:S(2)}) async-start(bf16[2,64,2048]{2,0,1:T(2,128)(2,1)} %copy.123), calls=%async_computation.4 | async-start | bytes 1048576 | tf_op jit(solution)/shard_map/all_to_all | solution.py:63
  88.8 1.5 copy.151
  91.9 10.8 %all-to-all-done.4 = bf16[2,64,2048]{2,0,1:T(2,128)(2,1)S(1)} async-done(((bf16[2,64,2048]{2,0,1:T(2,128)(2,1)}), bf16[2,64,2048]{2,0,1:T(2,128)(2,1)S(1)}, u32[]{:S(2)}, u32[]{:S(2)}) %all-to-all-start.4) | async-done | bytes 524320 | tf_op jit(solution)/shard_map/all_to_all | solution.py:63
  102.6 4.2 %all-to-all-start.3 = ((bf16[16,8,2048]{2,1,0:T(8,128)(2,1)}), bf16[16,8,2048]{2,1,0:T(8,128)(2,1)}, u32[]{:S(2)}, u32[]{:S(2)}) async-start(bf16[16,8,2048]{2,1,0:T(8,128)(2,1)} %copy.121), calls=%async_computation.3 | async-start | bytes 1048576 | tf_op jit(solution)/shard_map/all_to_all | solution.py:59
  107.1 1.2 copy.105
  109.8 1.5 fusion.2
  112.4 7.8 %all-to-all-done.3 = bf16[16,8,2048]{2,1,0:T(8,128)(2,1)} async-done(((bf16[16,8,2048]{2,1,0:T(8,128)(2,1)}), bf16[16,8,2048]{2,1,0:T(8,128)(2,1)}, u32[]{:S(2)}, u32[]{:S(2)}) %all-to-all-start.3) | async-done | bytes 524320 | tf_op jit(solution)/shard_map/all_to_all | solution.py:59
  120.1 4.2 %all-to-all-start.5 = ((bf16[16,8,2048]{2,1,0:T(8,128)(2,1)}), bf16[16,8,2048]{2,1,0:T(8,128)(2,1)}, u32[]{:S(2)}, u32[]{:S(2)}) async-start(bf16[16,8,2048]{2,1,0:T(8,128)(2,1)} %copy.126), calls=%async_computation.5 | async-start | bytes 1048576 | tf_op jit(solution)/shard_map/all_to_all | solution.py:70
  124.3 1.3 fusion.36
  125.6 1.7 fusion.25
  128.2 1.2 copy.108
  129.4 2.2 reshape.110
  131.6 1.3 fusion.3
  132.9 1.3 copy.109
  134.2 3.4 %all-to-all-done.5 = bf16[16,8,2048]{2,1,0:T(8,128)(2,1)} async-done(((bf16[16,8,2048]{2,1,0:T(8,128)(2,1)}), bf16[16,8,2048]{2,1,0:T(8,128)(2,1)}, u32[]{:S(2)}, u32[]{:S(2)}) %all-to-all-start.5) | async-done | bytes 524320 | tf_op jit(solution)/shard_map/all_to_all | solution.py:70
  137.7 4.1 %all-to-all-start = ((bf16[2,64,2048]{2,0,1:T(2,128)(2,1)}), bf16[2,64,2048]{2,0,1:T(2,128)(2,1)}, u32[]{:S(2)}, u32[]{:S(2)}) async-start(bf16[2,64,2048]{2,0,1:T(2,128)(2,1)} %copy.109), calls=%async_computation | async-start | bytes 1048576 | tf_op jit(solution)/shard_map/all_to_all | solution.py:55
  142.0 2.7 fusion.1
  144.7 2.2 reshape.112
  146.9 2.2 copy.131
  149.2 3.8 %convolution_bitcast_fusion.1 = f32[512,4,512]{0,2,1:T(8,128)} fusion(bf16[128,4,512]{0,2,1:T(8,128)(2,1)} %copy.131, f32[128,4,512]{2,0,1:T(8,128)S(1)} %copy.117, f32[128]{0:T(128)S(1)} %add_rsqrt_fusion, f32[4,512]{1,0:T(4,128)S(1)} %mul.95), kind=kOutput, calls=%fused_computation.13 | convolution fusion | flops 269221888 | bytes 5775872 | tf_op jit(solution)/shard_map/tki,tkj->ikj/dot_general | solution.py:87
  153.0 5.5 %copy.132 = f32[512,4,512]{2,1,0:T(4,128)} copy(f32[512,4,512]{0,2,1:T(8,128)} %convolution_bitcast_fusion.1) | data formatting | bytes 8388608 | tf_op jit(solution)/shard_map/tki,tkj->ikj/transpose | solution.py:87
  158.5 2.3 copy.152
  160.7 2.0 all_to_all.69
  162.7 1.3 fusion.4
  165.1 5.7 %all-to-all-start.1 = ((bf16[16,8,2048]{2,1,0:T(8,128)(2,1)}), bf16[16,8,2048]{2,1,0:T(8,128)(2,1)}, u32[]{:S(2)}, u32[]{:S(2)}) async-start(bf16[16,8,2048]{2,1,0:T(8,128)(2,1)} %copy.111), calls=%async_computation.1 | async-start | bytes 1048576 | tf_op jit(solution)/shard_map/all_to_all | solution.py:59
  170.8 2.3 copy.107
  173.1 26.5 %all-to-all-done.1 = bf16[16,8,2048]{2,1,0:T(8,128)(2,1)} async-done(((bf16[16,8,2048]{2,1,0:T(8,128)(2,1)}), bf16[16,8,2048]{2,1,0:T(8,128)(2,1)}, u32[]{:S(2)}, u32[]{:S(2)}) %all-to-all-start.1) | async-done | bytes 524320 | tf_op jit(solution)/shard_map/all_to_all | solution.py:59
  199.6 1.1 convert_bitcast_fusion
  201.8 2.6 copy.113
  204.4 2.7 fusion.35
  207.1 1.8 multiply_reduce_fusion
  208.9 2.8 copy.130
  211.7 1.7 fusion.31
  213.4 1.8 collective-permute-start.1
  217.5 19.6 %psum.7 = f32[1,2048]{1,0:T(1,128)} all-reduce(f32[1,2048]{1,0:T(1,128)S(1)} %bitcast.168), channel_id=1, replica_groups=mesh['pipe'=4,'seq'=8] {'seq'}, use_global_device_ids=true, to_apply=%region_5.0 | all-reduce | flops 2048 | bytes 16384 | tf_op jit(solution)/shard_map/psum | solution.py:92
  237.1 2.0 convolution_bitcast_fusion.3
  239.1 2.0 copy.133
  242.2 85.1 %all-reduce.3.cloned.1.call-done = f32[512,4,512]{2,1,0:T(4,128)} async-done(((f32[512,4,512]{2,1,0:T(4,128)}), f32[512,4,512]{2,1,0:T(4,128)}) %all-reduce.3.cloned.1.call-update) | async-done | bytes 4194320
  327.2 1.9 dynamic-slice_bitcast_fusion
  (74 shorter events, 12.9 us)
Async XLA Ops:
  7.2 58.5 %copy-start = (bf16[1,2,64,64]{3,2,1,0:T(8,128)(2,1)S(1)}, bf16[1,2,64,64]{3,2,1,0:T(8,128)(2,1)}, u32[]{:S(2)}) copy-start(bf16[1,2,64,64]{3,2,1,0:T(8,128)(2,1)} %param.12) | copy-start | bytes 49156
  7.2 55.6 %all-gather.2.cloned.1.call-start = ((), (), s32[]{:S(2)}) async-start(), calls=%async_computation.6 | async-start | bytes 2359296 | tf_op jit(solution)/shard_map/all_gather | solution.py:36
  12.2 52.7 %copy-start.3 = (bf16[1,128,2048]{1,2,0:T(8,128)(2,1)}, bf16[1,128,2048]{1,2,0:T(8,128)(2,1)S(1)}, u32[]{:S(2)}) copy-start(bf16[1,128,2048]{1,2,0:T(8,128)(2,1)S(1)} %copy.115) | copy-start | bytes 1572868
  65.3 6.2 %copy-start.15 = (bf16[1,128,2048]{2,1,0:T(8,128)(2,1)S(1)}, bf16[1,128,2048]{2,1,0:T(8,128)(2,1)}, u32[]{:S(2)}) copy-start(bf16[1,128,2048]{2,1,0:T(8,128)(2,1)} %param.9) | copy-start | bytes 1572868
  65.7 6.3 %copy-start.12 = (bf16[2,64,2048]{2,1,0:T(8,128)(2,1)}, bf16[2,64,2048]{2,1,0:T(8,128)(2,1)S(1)}, u32[]{:S(2)}) copy-start(bf16[2,64,2048]{2,1,0:T(8,128)(2,1)S(1)} %reshape.111) | copy-start | bytes 1572868
  67.3 17.9 %all-to-all-start.2 = ((bf16[2,64,2048]{2,0,1:T(2,128)(2,1)}), bf16[2,64,2048]{2,0,1:T(2,128)(2,1)}, u32[]{:S(2)}, u32[]{:S(2)}) async-start(bf16[2,64,2048]{2,0,1:T(2,128)(2,1)} %copy.119), calls=%async_computation.2 | async-start | bytes 1048576 | tf_op jit(solution)/shard_map/all_to_all | solution.py:55
  71.8 1.7 copy-start.6
  72.0 13.2 %copy-start.2 = (f32[1,128,2048]{2,1,0:T(8,128)}, f32[1,128,2048]{2,1,0:T(8,128)S(1)}, u32[]{:S(2)}) copy-start(f32[1,128,2048]{2,1,0:T(8,128)S(1)} %copy.116) | copy-start | bytes 3145732
  72.1 18.4 %copy-start.17 = (bf16[1,8,16,16]{3,2,1,0:T(8,128)(2,1)S(1)}, bf16[1,8,16,16]{3,2,1,0:T(8,128)(2,1)}, u32[]{:S(2)}) copy-start(bf16[1,8,16,16]{3,2,1,0:T(8,128)(2,1)} %param.13) | copy-start | bytes 12292
  85.2 17.5 %all-to-all-start.4 = ((bf16[2,64,2048]{2,0,1:T(2,128)(2,1)}), bf16[2,64,2048]{2,0,1:T(2,128)(2,1)S(1)}, u32[]{:S(2)}, u32[]{:S(2)}) async-start(bf16[2,64,2048]{2,0,1:T(2,128)(2,1)} %copy.123), calls=%async_computation.4 | async-start | bytes 1048576 | tf_op jit(solution)/shard_map/all_to_all | solution.py:63
  90.3 16.6 %copy-start.16 = (bf16[1,128,2048]{2,1,0:T(8,128)(2,1)S(1)}, bf16[1,128,2048]{2,1,0:T(8,128)(2,1)}, u32[]{:S(2)}) copy-start(bf16[1,128,2048]{2,1,0:T(8,128)(2,1)} %param.7) | copy-start | bytes 1572868
  90.5 12.2 %copy-start.8 = (bf16[16,8,2048]{2,0,1:T(8,128)(2,1)}, bf16[16,8,2048]{2,0,1:T(8,128)(2,1)S(1)}, u32[]{:S(2)}) copy-start(bf16[16,8,2048]{2,0,1:T(8,128)(2,1)S(1)} %all_to_all.74) | copy-start | bytes 1572868
  102.6 17.5 %all-to-all-start.3 = ((bf16[16,8,2048]{2,1,0:T(8,128)(2,1)}), bf16[16,8,2048]{2,1,0:T(8,128)(2,1)}, u32[]{:S(2)}, u32[]{:S(2)}) async-start(bf16[16,8,2048]{2,1,0:T(8,128)(2,1)} %copy.121), calls=%async_computation.3 | async-start | bytes 1048576 | tf_op jit(solution)/shard_map/all_to_all | solution.py:59
  107.1 1.6 copy-start.5
  109.8 15.9 %copy-start.1 = (bf16[1,512,4,512]{3,1,2,0:T(8,128)(2,1)S(1)}, bf16[1,512,4,512]{3,1,2,0:T(8,128)(2,1)}, u32[]{:S(2)}) copy-start(bf16[1,512,4,512]{3,1,2,0:T(8,128)(2,1)} %all-gather.2.cloned.1.call-done) | copy-start | bytes 6291460
  120.1 17.5 %all-to-all-start.5 = ((bf16[16,8,2048]{2,1,0:T(8,128)(2,1)}), bf16[16,8,2048]{2,1,0:T(8,128)(2,1)}, u32[]{:S(2)}, u32[]{:S(2)}) async-start(bf16[16,8,2048]{2,1,0:T(8,128)(2,1)} %copy.126), calls=%async_computation.5 | async-start | bytes 1048576 | tf_op jit(solution)/shard_map/all_to_all | solution.py:70
  127.4 0.8 copy-start.11
  137.7 20.8 %all-to-all-start = ((bf16[2,64,2048]{2,0,1:T(2,128)(2,1)}), bf16[2,64,2048]{2,0,1:T(2,128)(2,1)}, u32[]{:S(2)}, u32[]{:S(2)}) async-start(bf16[2,64,2048]{2,0,1:T(2,128)(2,1)} %copy.109), calls=%async_computation | async-start | bytes 1048576 | tf_op jit(solution)/shard_map/all_to_all | solution.py:55
  141.8 185.4 %all-reduce.3.cloned.1.call-start = ((), (), s32[]{:S(2)}) async-start(), calls=%async_computation.7 | async-start | bytes 8388608
  165.1 34.5 %all-to-all-start.1 = ((bf16[16,8,2048]{2,1,0:T(8,128)(2,1)}), bf16[16,8,2048]{2,1,0:T(8,128)(2,1)}, u32[]{:S(2)}, u32[]{:S(2)}) async-start(bf16[16,8,2048]{2,1,0:T(8,128)(2,1)} %copy.111), calls=%async_computation.1 | async-start | bytes 1048576 | tf_op jit(solution)/shard_map/all_to_all | solution.py:59
  204.4 2.7 copy-start.14
  207.1 32.0 %collective-permute-start = (bf16[128,2048]{0,1:T(8,128)(2,1)}, bf16[128,2048]{0,1:T(8,128)(2,1)}, u32[]{:S(2)}, u32[]{:S(2)}) collective-permute-start(bf16[128,2048]{0,1:T(8,128)(2,1)} %fusion.35), channel_id=1, source_target_pairs={{24,0},{0,8},{8,16},{16,24},{25,1},{1,9},{9,17},{17,25},{26,2},{2,... | collective-permute-start | bytes 1572872 | tf_op jit(solution)/shard_map/ppermute | solution.py:10
  208.9 2.8 copy-start.4
  208.9 2.8 copy-start.7
  208.9 2.8 copy-start.18
  208.9 6.4 %copy-start.19 = (u32[32]{0:T(128)S(1)}, u32[32]{0:T(128)}, u32[]{:S(2)}) copy-start(u32[32]{0:T(128)} %constant.18) | copy-start | bytes 388
  208.9 7.6 %copy-start.9 = (bf16[16,8,2048]{2,0,1:T(8,128)(2,1)S(1)}, bf16[16,8,2048]{2,0,1:T(8,128)(2,1)}, u32[]{:S(2)}) copy-start(bf16[16,8,2048]{2,0,1:T(8,128)(2,1)} %copy-done.8) | copy-start | bytes 1572868
  208.9 7.6 %copy-start.10 = (bf16[16,8,2048]{2,0,1:T(8,128)(2,1)S(1)}, bf16[16,8,2048]{2,0,1:T(8,128)(2,1)}, u32[]{:S(2)}) copy-start(bf16[16,8,2048]{2,0,1:T(8,128)(2,1)} %all_to_all.79) | copy-start | bytes 1572868
  211.7 25.4 %copy-start.13 = (bf16[2,64,2048]{2,1,0:T(8,128)(2,1)S(1)}, bf16[2,64,2048]{2,1,0:T(8,128)(2,1)}, u32[]{:S(2)}) copy-start(bf16[2,64,2048]{2,1,0:T(8,128)(2,1)} %copy-done.12) | copy-start | bytes 1572868
  213.4 27.7 %collective-permute-start.1 = (bf16[128,2048]{0,1:T(8,128)(2,1)S(1)}, bf16[128,2048]{0,1:T(8,128)(2,1)S(1)}, u32[]{:S(2)}, u32[]{:S(2)}) collective-permute-start(bf16[128,2048]{0,1:T(8,128)(2,1)S(1)} %fusion.31), channel_id=1, source_target_pairs={{8,0},{16,8},{24,16},{0,24},{9,1},{17,9},{25,17},{1,25},{10,2},{18... | collective-permute-start | bytes 1572872 | tf_op jit(solution)/shard_map/ppermute | solution.py:10
Sparse Core Ops, SparseCore 0:
  10.8 51.9 all-gather.1
  158.6 168.6 all-reduce.2
where the time goes:
time: 338 us; the launch traced here: 336 us
  waiting for transfers between devices  195 us (58%)
  local copies, waits for them, and re-layouts  49.6 us (15%)
  starting transfers between devices  28 us (8%)
  matrix products  19.7 us (6%)
  blocking collectives  19.6 us (6%)
  between operations  15.1 us (4%)
  other arithmetic  8.6 us (3%)
    unnamed x3, waiting for transfers between devices  85.1 us
    all_gather x1, waiting for transfers between devices, shards(): full_weight = lax.all_gather(weight, 'seq', axis=1, tiled=True)[0]  50.1 us
    all_to_all x2, waiting for transfers between devices, monarch(): lax.all_to_all(second, 'seq', split_axis=0, concat_axis=1, tiled=True)  34.2 us
    psum x1, blocking collectives, shards(): gain_grad = lax.psum(jnp.sum(normed_grad * sto_norm, axis=0), 'seq')  19.6 us
    all_to_all x2, waiting for transfers between devices, monarch(): lax.all_to_all(first_mix, 'seq', split_axis=1, concat_axis=0, tiled=True)  11.7 us
    all_to_all x1, waiting for transfers between devices, shards(): lax.all_to_all(adjoint_mix, 'seq', split_axis=1, concat_axis=0, tiled=True)  10.8 us
    all_to_all x2, starting transfers between devices, monarch(): lax.all_to_all(second, 'seq', split_axis=0, concat_axis=1, tiled=True)  9.84 us
    unnamed x49, local copies, waits for them, and re-layouts  8.59 us
  transfers between devices with their start and end apart: 10, of which 7 were waited for; matrix products, arithmetic and copies ran while one was open for 20% of the time, Pallas kernels for 0%

commit v1 on v0

v1 whole, which is shorter than its diff:
```python
import functools

import jax
import jax.numpy as jnp
from jax import lax
from jax.experimental import pallas as pl
from jax.experimental.pallas import tpu as pltpu
from jax.sharding import PartitionSpec as P

BF = jnp.bfloat16
F32 = jnp.float32
LANE = 128
SUB = 16
EPS = 1e-06
VMEM = 48 * 1024 * 1024


def position(nb):
    me = lax.axis_index("seq")
    group = me // nb
    place = me % nb
    block = place ^ ((nb // 2) * (group % 2))
    return group, place, block


def split3(x):
    hi = x.astype(BF).astype(F32)
    mid = (x - hi).astype(BF).astype(F32)
    return hi, mid, x - hi - mid


def eye(n):
    return lax.broadcasted_iota(jnp.int32, (n, n), 0) == lax.broadcasted_iota(jnp.int32, (n, n), 1)


def to_row(col):
    return jnp.sum(jnp.where(eye(col.shape[0]), col, 0.0), axis=0, keepdims=True)


def to_col(row):
    return jnp.sum(jnp.where(eye(row.shape[1]), row, 0.0), axis=1, keepdims=True)


def mm(a, b, ca=1, cb=0):
    return lax.dot_general(a, b, (((ca,), (cb,)), ((), ())), preferred_element_type=F32)


def rows(start, size):
    return pl.ds(pl.multiple_of(start, size), size)


def call(body, outs, scratch=(), flops=0, name=None):
    def run(*args):
        nbytes = sum(a.size * a.dtype.itemsize for a in args) + sum(
            o.size * o.dtype.itemsize for o in outs
        )
        return pl.pallas_call(
            body,
            out_shape=list(outs),
            in_specs=[pl.BlockSpec(memory_space=pltpu.VMEM)] * len(args),
            out_specs=[pl.BlockSpec(memory_space=pltpu.VMEM)] * len(outs),
            scratch_shapes=list(scratch),
            compiler_params=pltpu.CompilerParams(vmem_limit_bytes=VMEM),
            cost_estimate=pl.CostEstimate(flops=flops, bytes_accessed=nbytes, transcendentals=0),
            name=name,
        )(*args)

    return run


def sds(shape, dtype=BF):
    return jax.ShapeDtypeStruct(shape, dtype)


def pack_weight_body(nb, w_ref, l_ref, r_ref, *outs):
    _, _, block = position(nb)
    r, bd = w_ref.shape[1], w_ref.shape[2]
    chunks = bd // LANE
    bl, ext = l_ref.shape[1], r_ref.shape[1]
    left = jnp.concatenate([l_ref[j].astype(F32) for j in range(l_ref.shape[0])], axis=1).astype(BF)
    right = jnp.concatenate([r_ref[j].astype(F32) for j in range(r_ref.shape[0])], axis=1).astype(BF)
    for d in range(nb):
        for ch in range(chunks):
            outs[d][ch * r : (ch + 1) * r, :] = w_ref[block ^ d, :, ch * LANE : (ch + 1) * LANE]
        outs[d][chunks * r : chunks * r + bl, :] = left
        outs[d][chunks * r + bl :, :] = right


def pack_tokens_body(nb, with_scale, x_ref, *outs):
    _, _, block = position(nb)
    t, width = x_ref.shape
    bd = width // nb
    chunks = bd // LANE
    if with_scale:
        x = x_ref[...].astype(F32)
        inv = lax.rsqrt(jnp.mean(x * x, axis=-1, keepdims=True) + EPS)
        parts = split3(to_row(inv))
        tile = jnp.concatenate(list(parts) + [jnp.zeros((SUB - 3, t), F32)], axis=0).astype(BF)
    for d in range(nb):
        for ch in range(chunks):
            lanes = pl.ds(pl.multiple_of((block ^ d) * bd + ch * LANE, LANE), LANE)
            outs[d][ch * t : (ch + 1) * t, :] = x_ref[:, lanes]
        if with_scale:
            outs[d][chunks * t :, :] = tile


def relay_body(nb, r4, ext, *refs):
    _, place, _ = position(nb)
    out = refs[nb]
    for d in range(nb):
        to = place ^ d
        out[rows(to * r4, r4), :] = refs[d][:r4, :]
        out[pl.ds(pl.multiple_of(nb * r4 + to * ext, ext), ext), :] = refs[d][refs[d].shape[0] - ext :, :]


def expand_matrix(ext):
    n = SUB * ext
    row = lax.broadcasted_iota(jnp.int32, (n, n), 0)
    col = lax.broadcasted_iota(jnp.int32, (n, n), 1)
    return jnp.where((row // ext == col % SUB) & (row % ext == col // SUB), 1.0, 0.0).astype(BF)


def same_position(n):
    row = lax.broadcasted_iota(jnp.int32, (n, n), 0)
    col = lax.broadcasted_iota(jnp.int32, (n, n), 1)
    return row % SUB == col % SUB


def assemble_body(nb, ngroups, r, ext, bl, *refs):
    group, place, _ = position(nb)
    msgs, relays = refs[:nb], refs[nb : nb + ngroups]
    wk_ref, mq_ref, bd_ref, all_ref = refs[nb + ngroups :]
    chunks = wk_ref.shape[1] // LANE
    r4 = chunks * r
    for e in range(ngroups):
        g = group ^ e
        for c in range(nb):
            for ch in range(chunks):
                wk_ref[rows((g * nb + c) * r, r), ch * LANE : (ch + 1) * LANE] = relays[e][
                    c * r4 + ch * r : c * r4 + (ch + 1) * r, :
                ]
            all_ref[g * nb + c] = relays[e][nb * r4 + c * ext : nb * r4 + (c + 1) * ext, :]
    nq = mq_ref.shape[0]
    per = nb * ngroups // nq
    n = SUB * ext
    turn = expand_matrix(ext)
    spread = jnp.where(
        lax.broadcasted_iota(jnp.int32, (n, ext), 0) // SUB
        == lax.broadcasted_iota(jnp.int32, (n, ext), 1),
        1.0,
        0.0,
    ).astype(BF)
    same = same_position(n)
    for q in range(nq):
        tiles = jnp.concatenate([all_ref[q * per + i] for i in range(per)], axis=1)
        wide = mm(tiles, turn).astype(BF)
        mq_ref[q] = jnp.where(same, mm(spread, wide), 0.0).astype(BF)
    half_row = lax.broadcasted_iota(jnp.int32, (LANE, LANE), 0) // bl
    half_col = lax.broadcasted_iota(jnp.int32, (LANE, LANE), 1) // bl
    for d in range(nb):
        tile = msgs[d][r4 : r4 + bl, :].astype(F32)
        both = jnp.concatenate([tile] * (LANE // bl), axis=0)
        bd_ref[place ^ d] = jnp.where(half_row == half_col, both, 0.0).astype(BF)


def unpack(msg, t, chunks):
    return jnp.concatenate([msg[ch * t : (ch + 1) * t, :] for ch in range(chunks)], axis=1)


def scale_of(msg, t, chunks):
    tile = msg[chunks * t : chunks * t + SUB, :].astype(F32)
    return to_col(tile[0:1] + tile[1:2] + tile[2:3])


def project_body(nb, *refs):
    _, place, block = position(nb)
    msgs = refs[:nb]
    gain_ref, wk_ref, bd_ref, normin_ref, proj_ref, first_ref = refs[nb:]
    t = LANE
    bd = wk_ref.shape[0]
    chunks = bd // LANE
    gain = gain_ref[:, pl.ds(pl.multiple_of(block * bd, LANE), bd)]
    for d in range(nb):
        x = unpack(msgs[d], t, chunks).astype(F32)
        normed = x * scale_of(msgs[d], t, chunks)
        normin_ref[rows((place ^ d) * t, t), :] = (normed * gain).astype(BF)
    proj_ref[...] = mm(normin_ref[...], wk_ref[...]).astype(BF)
    for c in range(nb):
        first_ref[c * t : (c + 1) * t, :] = mm(bd_ref[c], proj_ref[c * t : (c + 1) * t, :]).astype(BF)


def adjoint_body(nb, *refs):
    _, place, _ = position(nb)
    msgs = refs[:nb]
    proj_ref, adj_ref, grad_ref = refs[nb:]
    t = LANE
    chunks = proj_ref.shape[1] // LANE
    for d in range(nb):
        at = rows((place ^ d) * t, t)
        g = unpack(msgs[d], t, chunks)
        grad_ref[at, :] = g
        adj_ref[at, :] = (g.astype(F32) * proj_ref[at, :].astype(F32)).astype(BF)


def gather_positions(group, bl, parts, out_ref):
    blocks = parts[0].shape[0] // bl
    for e, part in enumerate(parts):
        base = (group ^ e) * blocks * SUB
        for q in range(bl // SUB):
            for a in range(blocks):
                out_ref[q, pl.ds(pl.multiple_of(base + a * SUB, SUB), SUB), :] = part[
                    a * bl + q * SUB : a * bl + (q + 1) * SUB, :
                ]


def forward_body(nb, ngroups, bl, *refs):
    group, place, _ = position(nb)
    firsts, rest = refs[:ngroups], refs[ngroups:]
    mq_ref, proj_ref = rest[:2]
    msgs = rest[2 : 2 + nb]
    outs = rest[2 + nb : 2 + 2 * nb]
    f_ref, mixed_ref = rest[2 + 2 * nb :]
    t = LANE
    chunks = proj_ref.shape[1] // LANE
    gather_positions(group, bl, firsts, f_ref)
    blocks = firsts[0].shape[0] // bl
    own = rows(group * blocks * SUB, blocks * SUB)
    for q in range(bl // SUB):
        mixed = mm(mq_ref[q, own, :], f_ref[q]).astype(BF)
        for a in range(blocks):
            mixed_ref[a * bl + q * SUB : a * bl + (q + 1) * SUB, :] = mixed[a * SUB : (a + 1) * SUB, :]
    for d in range(nb):
        at = rows((place ^ d) * t, t)
        x = unpack(msgs[d], t, chunks).astype(F32)
        outs[d][...] = (x + proj_ref[at, :].astype(F32) * mixed_ref[at, :].astype(F32)).astype(BF)


def backward_body(nb, ngroups, bl, ext, *refs):
    group, place, _ = position(nb)
    firsts, adjs, rest = refs[:ngroups], refs[ngroups : 2 * ngroups], refs[2 * ngroups :]
    mq_ref, bd_ref, proj_ref, grad_ref = rest[:4]
    adj_proj_ref = rest[4]
    outs = rest[5 : 5 + nb]
    f_ref, a_ref, mixed_ref, adj_first_ref, left_ref, right_ref = rest[5 + nb :]
    t = LANE
    gather_positions(group, bl, firsts, f_ref)
    gather_positions(group, bl, adjs, a_ref)
    blocks = firsts[0].shape[0] // bl
    own = rows(group * blocks * SUB, blocks * SUB)
    nq = bl // SUB
    n = SUB * ext
    for q in range(nq):
        mixed = mm(mq_ref[q, own, :], f_ref[q]).astype(BF)
        adj_first = mm(mq_ref[q, :, own], a_ref[q], 0, 0).astype(BF)
        for a in range(blocks):
            at = slice(a * bl + q * SUB, a * bl + (q + 1) * SUB)
            mixed_ref[at, :] = mixed[a * SUB : (a + 1) * SUB, :]
            adj_first_ref[at, :] = adj_first[a * SUB : (a + 1) * SUB, :]
    sums = []
    upper = lax.broadcasted_iota(jnp.int32, (bl, LANE), 1) < bl
    for c in range(nb):
        at = slice(c * t, (c + 1) * t)
        grad = grad_ref[at, :].astype(F32)
        proj = proj_ref[at, :]
        adj_first = adj_first_ref[at, :]
        adj_proj = (grad * mixed_ref[at, :].astype(F32) + mm(bd_ref[c], adj_first, 0, 0)).astype(BF)
        adj_proj_ref[at, :] = adj_proj
        sums.append(
            split3(to_row(jnp.sum(adj_proj.astype(F32) * proj.astype(F32), axis=1, keepdims=True)))
        )
        both = mm(adj_first, proj, 1, 1)
        left_ref[c] = jnp.where(upper, both[:bl, :], both[bl:, :]).astype(BF)
    tile = jnp.concatenate(
        [s for three in sums for s in three] + [jnp.zeros((SUB - 3 * nb, t), F32)], axis=0
    ).astype(BF)
    turn = expand_matrix(ext)
    same = same_position(n)
    per = right_ref.shape[0] // nq
    for q in range(nq):
        pairs = jnp.where(same, mm(a_ref[q], f_ref[q], 1, 1), 0.0)
        summed = jnp.sum(pairs.reshape(ext, SUB, n), axis=1).astype(BF)
        turned = mm(summed, turn, 1, 1).astype(BF)
        for i in range(per):
            right_ref[q * per + i] = turned[:, i * LANE : (i + 1) * LANE]
    for d in range(nb):
        to = place ^ d
        outs[d][:bl, :] = left_ref[to]
        outs[d][bl : bl + ext, :] = right_ref[group * nb + to]
        outs[d][bl + ext :, :] = tile


def weight_grad_body(nb, ngroups, normin_ref, adj_proj_ref, wk_ref, gain_ref, *refs):
    group, _, block = position(nb)
    own_ref, gain_part_ref, adj_norm_ref = refs[:3]
    sends = refs[3 : 3 + ngroups - 1]
    gw_ref = refs[3 + ngroups - 1]
    bd = wk_ref.shape[0]
    share = bd // ngroups
    adj_proj = adj_proj_ref[...]
    gw_ref[...] = mm(normin_ref[...], adj_proj, 0, 0)
    adj_norm = mm(adj_proj, wk_ref[...], 1, 1)
    adj_norm_ref[...] = adj_norm
    gain = gain_ref[:, pl.ds(pl.multiple_of(block * bd, LANE), bd)]
    part = jnp.sum(adj_norm * normin_ref[...].astype(F32), axis=0, keepdims=True) / gain
    gain_part_ref[...] = part
    tile = jnp.concatenate(list(split3(part)) + [jnp.zeros((SUB - 3, bd), F32)], axis=0).astype(BF)
    own_ref[...] = gw_ref[rows(group * share, share), :]
    for e in range(1, ngroups):
        sends[e - 1][:share, :] = gw_ref[rows((group ^ e) * share, share), :].astype(BF)
        sends[e - 1][share:, :] = tile


def weight_sum_body(nb, ngroups, own_ref, gain_part_ref, *refs):
    group, place, _ = position(nb)
    recvs = refs[: ngroups - 1]
    outs = refs[ngroups - 1 : ngroups - 1 + nb]
    total_ref, gains_ref = refs[ngroups - 1 + nb :]
    share, bd = own_ref.shape
    r = share // nb
    total = own_ref[...]
    gains_ref[group] = gain_part_ref[...]
    for e in range(1, ngroups):
        total = total + recvs[e - 1][:share, :].astype(F32)
        three = recvs[e - 1][share:, :].astype(F32)
        gains_ref[group ^ e] = three[0:1] + three[1:2] + three[2:3]
    total_ref[...] = total
    gain = gains_ref[0]
    for g in range(1, ngroups):
        gain = gain + gains_ref[g]
    tile = jnp.concatenate(list(split3(gain)) + [jnp.zeros((SUB - 3, bd), F32)], axis=0).astype(BF)
    for d in range(nb):
        outs[d][:r, :] = total_ref[rows((place ^ d) * r, r), :].astype(BF)
        outs[d][r:, :] = tile


def input_grad_body(nb, bl, ext, adj_norm_ref, grad_ref, gain_ref, *refs):
    _, place, block = position(nb)
    msgs, smalls, outs = refs[:nb], refs[nb : 2 * nb], refs[2 * nb :]
    t = LANE
    bd = adj_norm_ref.shape[1]
    chunks = bd // LANE
    width = bd * nb
    gain = gain_ref[:, pl.ds(pl.multiple_of(block * bd, LANE), bd)]
    tile = smalls[0][bl + ext :, :].astype(F32)
    for d in range(1, nb):
        tile = tile + smalls[d][bl + ext :, :].astype(F32)
    means = [
        to_col((tile[3 * c : 3 * c + 1] + tile[3 * c + 1 : 3 * c + 2] + tile[3 * c + 2 : 3 * c + 3]))
        * (1.0 / width)
        for c in range(nb)
    ]
    for d in range(nb):
        to = place ^ d
        at = rows(to * t, t)
        mean = means[0]
        for c in range(1, nb):
            mean = jnp.where(to == c, means[c], mean)
        inv = scale_of(msgs[d], t, chunks)
        normed = unpack(msgs[d], t, chunks).astype(F32) * inv
        scaled = adj_norm_ref[at, :] * gain
        outs[d][...] = (grad_ref[at, :].astype(F32) + inv * (scaled - normed * mean)).astype(BF)


def factors_body(nb, *refs):
    smalls = refs[:nb]
    left_ref, right_ref = refs[nb:]
    na, bl, _ = left_ref.shape
    npos, ext, _ = right_ref.shape
    left = smalls[0][:bl, :].astype(F32)
    right = smalls[0][bl : bl + ext, :].astype(F32)
    for d in range(1, nb):
        left = left + smalls[d][:bl, :].astype(F32)
        right = right + smalls[d][bl : bl + ext, :].astype(F32)
    for j in range(na):
        left_ref[j] = left[:, j * bl : (j + 1) * bl]
    for j in range(npos):
        right_ref[j] = right[:, j * ext : (j + 1) * ext]


def join_body(nb, *refs):
    _, _, block = position(nb)
    out = refs[nb]
    bd = refs[0].shape[1]
    for d in range(nb):
        out[:, pl.ds(pl.multiple_of((block ^ d) * bd, LANE), bd)] = refs[d][...]


def join_weight_body(nb, *refs):
    _, _, block = position(nb)
    gw_ref, gain_ref, by_block = refs[nb:]
    bd = gw_ref.shape[2]
    r = gw_ref.shape[0]
    for d in range(nb):
        by_block[block ^ d] = refs[d][:r, :].astype(F32)
        three = refs[d][r:, :].astype(F32)
        gain_ref[:, pl.ds(pl.multiple_of((block ^ d) * bd, LANE), bd)] = (
            three[0:1] + three[1:2] + three[2:3]
        )
    for k in range(nb):
        gw_ref[:, k, :] = by_block[k]


def shards(act_in, saved_in, grad_in, gain, weight, left_blocks, right_blocks):
    nseq = lax.axis_size("seq")
    npipe = lax.axis_size("pipe")
    _, t, width = act_in.shape
    _, r, nb, bd = weight.shape
    ngroups = nseq // nb
    bl = left_blocks.shape[2]
    ext = right_blocks.shape[2]
    npos = right_blocks.shape[1]
    chunks = bd // LANE
    tg = nb * t
    r4 = chunks * r
    nq = bl // SUB
    n = SUB * ext

    def within(parts):
        return [parts[0]] + [
            lax.ppermute(parts[d], "seq", [(s, s ^ d) for s in range(nseq)]) for d in range(1, nb)
        ]

    def across(block, e):
        mask = nb * e + (nb // 2) * (e % 2)
        return lax.ppermute(block, "seq", [(s, s ^ mask) for s in range(nseq)])

    def handed(parts, step):
        return [
            lax.ppermute(
                parts[d],
                ("pipe", "seq"),
                [
                    (p * nseq + s, ((p + step) % npipe) * nseq + (s ^ d))
                    for p in range(npipe)
                    for s in range(nseq)
                ],
            )
            for d in range(nb)
        ]

    part = functools.partial
    w_msgs = call(
        part(pack_weight_body, nb), [sds((r4 + bl + ext, LANE))] * nb, name="pack_weight"
    )(jnp.transpose(weight[0], (1, 0, 2)), left_blocks[0], right_blocks[0])
    w_msgs = within(w_msgs)
    sto_msgs = within(
        call(part(pack_tokens_body, nb, True), [sds((chunks * t + SUB, LANE))] * nb, name="pack_saved")(
            saved_in[0]
        )
    )
    grad_msgs = within(
        call(part(pack_tokens_body, nb, False), [sds((chunks * t, LANE))] * nb, name="pack_grad")(
            grad_in[0]
        )
    )
    cur_msgs = within(
        call(part(pack_tokens_body, nb, True), [sds((chunks * t + SUB, LANE))] * nb, name="pack_act")(
            act_in[0]
        )
    )
    (relay,) = call(part(relay_body, nb, r4, ext), [sds((nb * (r4 + ext), LANE))], name="relay")(*w_msgs)
    relays = [relay] + [across(relay, e) for e in range(1, ngroups)]
    wk, mq, bd_left = call(
        part(assemble_body, nb, ngroups, r, ext, bl),
        [sds((bd, bd)), sds((nq, n, n)), sds((nb, LANE, LANE))],
        [pltpu.VMEM((nseq, ext, LANE), BF)],
        name="assemble",
    )(*w_msgs, *relays)

    token_arrays = [sds((tg, bd))]
    proj_flops = 2 * tg * bd * bd
    sto_normin, sto_proj, sto_first = call(
        part(project_body, nb), token_arrays * 3, flops=proj_flops, name="project_saved"
    )(*sto_msgs, gain, wk, bd_left)
    sto_firsts = [sto_first] + [across(sto_first, e) for e in range(1, ngroups)]
    adj_mix, grad = call(part(adjoint_body, nb), token_arrays * 2, name="adjoint")(*grad_msgs, sto_proj)
    adj_mixes = [adj_mix] + [across(adj_mix, e) for e in range(1, ngroups)]
    _, cur_proj, cur_first = call(
        part(project_body, nb), token_arrays * 3, flops=proj_flops, name="project_act"
    )(*cur_msgs, gain, wk, bd_left)
    cur_firsts = [cur_first] + [across(cur_first, e) for e in range(1, ngroups)]

    wide = pltpu.VMEM((nq, n, bd), BF)
    tokens = pltpu.VMEM((tg, bd), BF)
    adj_proj, *smalls = call(
        part(backward_body, nb, ngroups, bl, ext),
        token_arrays + [sds((bl + ext + SUB, LANE))] * nb,
        [wide, wide, tokens, tokens, pltpu.VMEM((nb, bl, LANE), BF), pltpu.VMEM((nseq, ext, LANE), BF)],
        flops=nq * n * n * bd * 4,
        name="backward",
    )(*sto_firsts, *adj_mixes, mq, bd_left, sto_proj, grad)
    smalls = within(smalls)
    share = bd // ngroups
    own_gw, gain_part, adj_norm, *sends = call(
        part(weight_grad_body, nb, ngroups),
        [sds((share, bd), F32), sds((1, bd), F32), sds((tg, bd), F32)]
        + [sds((share + SUB, bd))] * (ngroups - 1),
        [pltpu.VMEM((bd, bd), F32)],
        flops=2 * proj_flops,
        name="weight_grad",
    )(sto_normin, adj_proj, wk, gain)
    recvs = [across(sends[e - 1], e) for e in range(1, ngroups)]
    adj_parts = call(
        part(input_grad_body, nb, bl, ext), [sds((t, bd))] * nb, name="input_grad"
    )(adj_norm, grad, gain, *sto_msgs, *smalls)
    adj_parts = handed(adj_parts, -1)
    out_parts = call(
        part(forward_body, nb, ngroups, bl),
        [sds((t, bd))] * nb,
        [wide, tokens],
        flops=nq * n * n * bd * 2,
        name="forward",
    )(*cur_firsts, mq, cur_proj, *cur_msgs)
    out_parts = handed(out_parts, 1)
    gw_parts = within(
        call(
            part(weight_sum_body, nb, ngroups),
            [sds((r + SUB, bd))] * nb,
            [pltpu.VMEM((share, bd), F32), pltpu.VMEM((ngroups, 1, bd), F32)],
            name="weight_sum",
        )(own_gw, gain_part, *recvs)
    )
    left_grad, right_grad = call(
        part(factors_body, nb),
        [sds((left_blocks.shape[1], bl, bl), F32), sds((npos, ext, ext), F32)],
        name="factors",
    )(*smalls)
    (handed_on,) = call(part(join_body, nb), [sds((t, width))], name="join_out")(*out_parts)
    (grad_handed,) = call(part(join_body, nb), [sds((t, width))], name="join_grad")(*adj_parts)
    weight_grad, gain_grad = call(
        part(join_weight_body, nb),
        [sds((r, nb, bd), F32), sds((1, width), F32)],
        [pltpu.VMEM((nb, r, bd), F32)],
        name="join_weight",
    )(*gw_parts)
    return (
        handed_on[None],
        grad_handed[None],
        weight_grad[None],
        gain_grad,
        left_grad[None],
        right_grad[None],
    )


def solution(mesh):
    tokens = P("pipe", "seq", None)
    factor = P("pipe", "seq", None, None)
    return jax.shard_map(
        shards,
        mesh=mesh,
        in_specs=(tokens, tokens, tokens, P("pipe", None), factor, factor, factor),
        out_specs=(tokens, tokens, factor, P("pipe", None), factor, factor),
        check_vma=False,
    )
```

time: 338 us -> 139 us (0.41)
  waiting for transfers between devices: 195 us -> 46 us
  starting transfers between devices: 28 us -> 80.2 us
  local copies, waits for them, and re-layouts: 49.6 us -> 1.04 us
  matrix products: 19.7 us -> 0 us
  blocking collectives: 19.6 us -> 0 us
  between operations: 15.1 us -> 0.82 us
  Pallas kernels: 0 us -> 11.1 us
  other arithmetic: 8.6 us -> 0 us
    unnamed x3 -> x0, waiting for transfers between devices: 85.1 us -> none
    ppermute x2 -> x31, starting transfers between devices: 1.82 us -> 80.2 us  [the longest x8 36.8 us: handed(): lax.ppermute(parts[d], ('pipe', 'seq'), [(p * nseq + s, (p + step) % npip...]
    all_to_all x6 -> x0, waiting for transfers between devices: 60.2 us -> none  [the longest x2 34.2 us: monarch(): lax.all_to_all(second, 'seq', split_axis=0, concat_axis=1, tiled=True)]
    all_gather x1 -> x0, waiting for transfers between devices: 50.1 us -> none  [shards(): full_weight = lax.all_gather(weight, 'seq', axis=1, tiled=True)[0]]
    ppermute x2 -> x31, waiting for transfers between devices: 0.01 us -> 46 us  [the longest x5 28 us: across(): return lax.ppermute(block, 'seq', [(s, s ^ mask) for s in range(nseq)])]
    all_to_all x6 -> x0, starting transfers between devices: 25.9 us -> none  [the longest x2 9.84 us: monarch(): lax.all_to_all(second, 'seq', split_axis=0, concat_axis=1, tiled=True)]
    dot_general x12 -> x0, matrix products: 19.7 us -> none  [the longest x1 3.79 us: shards(): jnp.einsum('tki,tkj->ikj', sto_split, proj_grad, preferred_element_type=j...]
    psum x1 -> x0, blocking collectives: 19.6 us -> none  [shards(): gain_grad = lax.psum(jnp.sum(normed_grad * sto_norm, axis=0), 'seq')]
  transfers between devices with their start and end apart: 10 -> 31, of which waited for: 7 -> 15; matrix products, arithmetic and copies ran while one was open for 20% -> 0% of each run, Pallas kernels for 0% -> 7%
where the time goes in v1:
time: 139 us
  starting transfers between devices  80.2 us (58%)
  waiting for transfers between devices  46 us (33%)
  Pallas kernels  11.1 us (8%)
    ppermute x8, starting transfers between devices, handed(): lax.ppermute(parts[d], ('pipe', 'seq'), [(p * nseq + s, (p + step) % npip...  36.8 us
    ppermute x18, starting transfers between devices, within(): lax.ppermute(parts[d], 'seq', [(s, s ^ d) for s in range(nseq)])  32.6 us
    ppermute x5, waiting for transfers between devices, across(): return lax.ppermute(block, 'seq', [(s, s ^ mask) for s in range(nseq)])  28 us
    ppermute x18, waiting for transfers between devices, within(): lax.ppermute(parts[d], 'seq', [(s, s ^ d) for s in range(nseq)])  16.7 us
    pallas_call x18, Pallas kernels, run(): pl.pallas_call(body, out_shape=list(outs), in_specs=[pl.BlockSpec(memory_...  11.1 us
    ppermute x5, starting transfers between devices, across(): return lax.ppermute(block, 'seq', [(s, s ^ mask) for s in range(nseq)])  10.9 us
  transfers between devices with their start and end apart: 31, of which 15 were waited for; matrix products, arithmetic and copies ran while one was open for 0% of the time, Pallas kernels for 7%

profile of v1, /device:TPU:0, one launch (start us, length us, event | category | flops | bytes accessed | tf_op | source)
XLA Modules:
  0.0 139.2 jit_solution(7613417371510254042)
XLA Ops:
  0.7 1.0 copy.15
  1.8 3.0 %collective-permute-start.3 = (bf16[336,128]{1,0:T(8,128)(2,1)S(1)}, bf16[336,128]{1,0:T(8,128)(2,1)S(1)}, u32[]{:S(2)}, u32[]{:S(2)}) collective-permute-start(bf16[336,128]{1,0:T(8,128)(2,1)S(1)} %get-tuple-element.62), channel_id=1, source_target_pairs={{0,1},{1,0},{2,3},{3,2},{4,5},{5,4},{6,7},{7,6},{8,9},{9,8},{10,11... | collective-permute-start | bytes 258056 | tf_op jit(solution)/shard_map/ppermute | solution.py:420
  4.8 1.6 %collective-permute-start.4 = (bf16[336,128]{1,0:T(8,128)(2,1)S(1)}, bf16[336,128]{1,0:T(8,128)(2,1)S(1)}, u32[]{:S(2)}, u32[]{:S(2)}) collective-permute-start(bf16[336,128]{1,0:T(8,128)(2,1)S(1)} %get-tuple-element.63), channel_id=1, source_target_pairs={{0,2},{1,3},{2,0},{3,1},{4,6},{5,7},{6,4},{7,5},{8,10},{9,11},{10,... | collective-permute-start | bytes 258056 | tf_op jit(solution)/shard_map/ppermute | solution.py:420
  6.4 1.0 collective-permute-done.3.refs_1_
  7.3 2.7 %collective-permute-done.4.refs_2_ = bf16[336,128]{1,0:T(8,128)(2,1)S(1)} collective-permute-done((bf16[336,128]{1,0:T(8,128)(2,1)S(1)}, bf16[336,128]{1,0:T(8,128)(2,1)S(1)}, u32[]{:S(2)}, u32[]{:S(2)}) %collective-permute-start.4) | collective-permute-done | bytes 86048 | tf_op jit(solution)/shard_map/ppermute | solution.py:420
  10.0 1.7 %collective-permute-done.5.refs_3_ = bf16[336,128]{1,0:T(8,128)(2,1)S(1)} collective-permute-done((bf16[336,128]{1,0:T(8,128)(2,1)S(1)}, bf16[336,128]{1,0:T(8,128)(2,1)S(1)}, u32[]{:S(2)}, u32[]{:S(2)}) %collective-permute-start.5) | collective-permute-done | bytes 86048 | tf_op jit(solution)/shard_map/ppermute | solution.py:420
  11.8 2.7 %collective-permute-start.6 = (bf16[1088,128]{1,0:T(8,128)(2,1)S(1)}, bf16[1088,128]{1,0:T(8,128)(2,1)S(1)}, u32[]{:S(2)}, u32[]{:S(2)}) collective-permute-start(bf16[1088,128]{1,0:T(8,128)(2,1)S(1)} %relay.1.refs_4_), channel_id=1, source_target_pairs={{0,6},{1,7},{2,4},{3,5},{4,2},{5,3},{6,0},{7,1},{8,14},{9,15},{10,... | collective-permute-start | bytes 835592 | tf_op jit(solution)/shard_map/ppermute | solution.py:425
  14.6 1.4 collective-permute-start.16
  16.2 0.8 collective-permute-start.12
  17.5 2.2 %collective-permute-start.14 = (bf16[528,128]{1,0:T(8,128)(2,1)S(1)}, bf16[528,128]{1,0:T(8,128)(2,1)S(1)}, u32[]{:S(2)}, u32[]{:S(2)}) collective-permute-start(bf16[528,128]{1,0:T(8,128)(2,1)S(1)} %get-tuple-element.77), channel_id=1, source_target_pairs={{0,3},{1,2},{2,1},{3,0},{4,7},{5,6},{6,5},{7,4},{8,11},{9,10},{10,... | collective-permute-start | bytes 405512 | tf_op jit(solution)/shard_map/ppermute | solution.py:420
  20.2 3.1 %collective-permute-done.6.refs_5_ = bf16[1088,128]{1,0:T(8,128)(2,1)S(1)} collective-permute-done((bf16[1088,128]{1,0:T(8,128)(2,1)S(1)}, bf16[1088,128]{1,0:T(8,128)(2,1)S(1)}, u32[]{:S(2)}, u32[]{:S(2)}) %collective-permute-start.6) | collective-permute-done | bytes 278560 | tf_op jit(solution)/shard_map/ppermute | solution.py:425
  23.3 3.4 %collective-permute-start.18 = (bf16[512,128]{1,0:T(8,128)(2,1)S(1)}, bf16[512,128]{1,0:T(8,128)(2,1)S(1)}, u32[]{:S(2)}, u32[]{:S(2)}) collective-permute-start(bf16[512,128]{1,0:T(8,128)(2,1)S(1)} %get-tuple-element.83), channel_id=1, source_target_pairs={{0,3},{1,2},{2,1},{3,0},{4,7},{5,6},{6,5},{7,4},{8,11},{9,10},{10,... | collective-permute-start | bytes 393224 | tf_op jit(solution)/shard_map/ppermute | solution.py:420
  26.9 0.7 assemble.1
  27.6 0.9 collective-permute-start
  28.5 2.7 %collective-permute-start.2 = (bf16[528,128]{1,0:T(8,128)(2,1)S(1)}, bf16[528,128]{1,0:T(8,128)(2,1)S(1)}, u32[]{:S(2)}, u32[]{:S(2)}) collective-permute-start(bf16[528,128]{1,0:T(8,128)(2,1)S(1)} %get-tuple-element.60), channel_id=1, source_target_pairs={{0,3},{1,2},{2,1},{3,0},{4,7},{5,6},{6,5},{7,4},{8,11},{9,10},{10,... | collective-permute-start | bytes 405512 | tf_op jit(solution)/shard_map/ppermute | solution.py:420
  31.2 0.8 project_saved.1
  32.0 1.9 %collective-permute-done.18.refs_3_ = bf16[512,128]{1,0:T(8,128)(2,1)S(1)} collective-permute-done((bf16[512,128]{1,0:T(8,128)(2,1)S(1)}, bf16[512,128]{1,0:T(8,128)(2,1)S(1)}, u32[]{:S(2)}, u32[]{:S(2)}) %collective-permute-start.18) | collective-permute-done | bytes 131104 | tf_op jit(solution)/shard_map/ppermute | solution.py:420
  34.0 2.0 %collective-permute-start.19 = (bf16[512,512]{1,0:T(8,128)(2,1)S(1)}, bf16[512,512]{1,0:T(8,128)(2,1)S(1)}, u32[]{:S(2)}, u32[]{:S(2)}) collective-permute-start(bf16[512,512]{1,0:T(8,128)(2,1)S(1)} %get-tuple-element.85.refs_2_), channel_id=1, source_target_pairs={{0,6},{1,7},{2,4},{3,5},{4,2},{5,3},{6,0},{7,1},{8,14},{9,15},{10,... | collective-permute-start | bytes 1572872 | tf_op jit(solution)/shard_map/ppermute | solution.py:425
  36.0 1.9 %collective-permute-start.15 = (bf16[512,512]{1,0:T(8,128)(2,1)S(1)}, bf16[512,512]{1,0:T(8,128)(2,1)S(1)}, u32[]{:S(2)}, u32[]{:S(2)}) collective-permute-start(bf16[512,512]{1,0:T(8,128)(2,1)S(1)} %get-tuple-element.79.refs_0_), channel_id=1, source_target_pairs={{0,6},{1,7},{2,4},{3,5},{4,2},{5,3},{6,0},{7,1},{8,14},{9,15},{10,... | collective-permute-start | bytes 1572872 | tf_op jit(solution)/shard_map/ppermute | solution.py:425
  37.9 1.9 %collective-permute-done.2.refs_3_.refs_7_ = bf16[528,128]{1,0:T(8,128)(2,1)S(1)} collective-permute-done((bf16[528,128]{1,0:T(8,128)(2,1)S(1)}, bf16[528,128]{1,0:T(8,128)(2,1)S(1)}, u32[]{:S(2)}, u32[]{:S(2)}) %collective-permute-start.2) | collective-permute-done | bytes 135200 | tf_op jit(solution)/shard_map/ppermute | solution.py:420
  39.8 1.4 %project_act.1 = (bf16[512,512]{1,0:T(8,128)(2,1)}, bf16[512,512]{1,0:T(8,128)(2,1)S(1)}, bf16[512,512]{1,0:T(8,128)(2,1)S(1)}) custom-call(bf16[528,128]{1,0:T(8,128)(2,1)S(1)} %get-tuple-element.57.refs_0_.refs_4_, bf16[528,128]{1,0:T(8,128)(2,1)S(1)} %collective-permute-done.refs_1_.refs_5_, bf16[528,128]{1,0:T(8,128)(2,1)S(1)} %collective-permute-done.1.refs_2_.refs_6_, ...), custom_call_target="tpu_custom_call" | custom-call | flops 268435456 | bytes 2777088 | tf_op jit(solution)/shard_map/project_act/pallas_call | solution.py:57
  41.3 2.3 %collective-permute-start.7 = (bf16[512,512]{1,0:T(8,128)(2,1)S(1)}, bf16[512,512]{1,0:T(8,128)(2,1)S(1)}, u32[]{:S(2)}, u32[]{:S(2)}) collective-permute-start(bf16[512,512]{1,0:T(8,128)(2,1)S(1)} %get-tuple-element.67.refs_0_), channel_id=1, source_target_pairs={{0,6},{1,7},{2,4},{3,5},{4,2},{5,3},{6,0},{7,1},{8,14},{9,15},{10,... | collective-permute-start | bytes 1572872 | tf_op jit(solution)/shard_map/ppermute | solution.py:425
  43.6 7.2 %collective-permute-done.19.refs_3_ = bf16[512,512]{1,0:T(8,128)(2,1)S(1)} collective-permute-done((bf16[512,512]{1,0:T(8,128)(2,1)S(1)}, bf16[512,512]{1,0:T(8,128)(2,1)S(1)}, u32[]{:S(2)}, u32[]{:S(2)}) %collective-permute-start.19) | collective-permute-done | bytes 524320 | tf_op jit(solution)/shard_map/ppermute | solution.py:425
  50.8 11.2 %collective-permute-done.15.refs_1_ = bf16[512,512]{1,0:T(8,128)(2,1)S(1)} collective-permute-done((bf16[512,512]{1,0:T(8,128)(2,1)S(1)}, bf16[512,512]{1,0:T(8,128)(2,1)S(1)}, u32[]{:S(2)}, u32[]{:S(2)}) %collective-permute-start.15) | collective-permute-done | bytes 524320 | tf_op jit(solution)/shard_map/ppermute | solution.py:425
  62.1 2.0 %backward.1 = (bf16[512,512]{1,0:T(8,128)(2,1)S(1)}, bf16[96,128]{1,0:T(8,128)(2,1)S(1)}, bf16[96,128]{1,0:T(8,128)(2,1)S(1)}, bf16[96,128]{1,0:T(8,128)(2,1)S(1)}, bf16[96,128]{1,0:T(8,128)(2,1)S(1)}) custom-call(bf16[512,512]{1,0:T(8,128)(2,1)S(1)} %get-tuple-element.79.refs_0_, bf16[512,512]{1,0:T(8,128)(2,1)S(1)} %collective-permute-done.15.refs_1_, ...), custom_call_target="tpu_custom_call" | custom-call | flops 536870912 | bytes 4423680 | tf_op jit(solution)/shard_map/backward/pallas_call | solution.py:57
  64.1 0.8 weight_grad.1
  64.9 1.9 %collective-permute-start.27 = (bf16[272,512]{1,0:T(8,128)(2,1)S(1)}, bf16[272,512]{1,0:T(8,128)(2,1)S(1)}, u32[]{:S(2)}, u32[]{:S(2)}) collective-permute-start(bf16[272,512]{1,0:T(8,128)(2,1)S(1)} %get-tuple-element.99), channel_id=1, source_target_pairs={{0,6},{1,7},{2,4},{3,5},{4,2},{5,3},{6,0},{7,1},{8,14},{9,15},{10,... | collective-permute-start | bytes 835592 | tf_op jit(solution)/shard_map/ppermute | solution.py:425
  66.8 6.5 %collective-permute-done.7.refs_1_ = bf16[512,512]{1,0:T(8,128)(2,1)S(1)} collective-permute-done((bf16[512,512]{1,0:T(8,128)(2,1)S(1)}, bf16[512,512]{1,0:T(8,128)(2,1)S(1)}, u32[]{:S(2)}, u32[]{:S(2)}) %collective-permute-start.7) | collective-permute-done | bytes 524320 | tf_op jit(solution)/shard_map/ppermute | solution.py:425
  73.3 0.6 forward.1
  73.9 30.4 %collective-permute-start.10 = (bf16[128,512]{1,0:T(8,128)(2,1)S(1)}, bf16[128,512]{1,0:T(8,128)(2,1)S(1)}, u32[]{:S(2)}, u32[]{:S(2)}) collective-permute-start(bf16[128,512]{1,0:T(8,128)(2,1)S(1)} %get-tuple-element.72), channel_id=1, source_target_pairs={{0,10},{1,11},{2,8},{3,9},{4,14},{5,15},{6,12},{7,13},{8,18},{9,19... | collective-permute-start | bytes 393224 | tf_op jit(solution)/shard_map/ppermute | solution.py:429
  104.3 1.1 collective-permute-start.11
  105.9 9.8 %collective-permute-start.21 = (bf16[96,128]{1,0:T(8,128)(2,1)S(1)}, bf16[96,128]{1,0:T(8,128)(2,1)S(1)}, u32[]{:S(2)}, u32[]{:S(2)}) collective-permute-start(bf16[96,128]{1,0:T(8,128)(2,1)S(1)} %get-tuple-element.91), channel_id=1, source_target_pairs={{0,2},{1,3},{2,0},{3,1},{4,6},{5,7},{6,4},{7,5},{8,10},{9,11},{10,... | collective-permute-start | bytes 73736 | tf_op jit(solution)/shard_map/ppermute | solution.py:420
  116.0 2.4 %collective-permute-done.21.refs_6_.refs_2_ = bf16[96,128]{1,0:T(8,128)(2,1)S(1)} collective-permute-done((bf16[96,128]{1,0:T(8,128)(2,1)S(1)}, bf16[96,128]{1,0:T(8,128)(2,1)S(1)}, u32[]{:S(2)}, u32[]{:S(2)}) %collective-permute-start.21) | collective-permute-done | bytes 24608 | tf_op jit(solution)/shard_map/ppermute | solution.py:420
  118.4 1.8 %collective-permute-start.22 = (bf16[96,128]{1,0:T(8,128)(2,1)S(1)}, bf16[96,128]{1,0:T(8,128)(2,1)S(1)}, u32[]{:S(2)}, u32[]{:S(2)}) collective-permute-start(bf16[96,128]{1,0:T(8,128)(2,1)S(1)} %get-tuple-element.92), channel_id=1, source_target_pairs={{0,3},{1,2},{2,1},{3,0},{4,7},{5,6},{6,5},{7,4},{8,11},{9,10},{10,... | collective-permute-start | bytes 73736 | tf_op jit(solution)/shard_map/ppermute | solution.py:420
  120.2 2.9 %collective-permute-done.22.refs_7_.refs_3_ = bf16[96,128]{1,0:T(8,128)(2,1)S(1)} collective-permute-done((bf16[96,128]{1,0:T(8,128)(2,1)S(1)}, bf16[96,128]{1,0:T(8,128)(2,1)S(1)}, u32[]{:S(2)}, u32[]{:S(2)}) %collective-permute-start.22) | collective-permute-done | bytes 24608 | tf_op jit(solution)/shard_map/ppermute | solution.py:420
  123.6 2.0 %collective-permute-start.23 = (bf16[128,512]{1,0:T(8,128)(2,1)S(1)}, bf16[128,512]{1,0:T(8,128)(2,1)S(1)}, u32[]{:S(2)}, u32[]{:S(2)}) collective-permute-start(bf16[128,512]{1,0:T(8,128)(2,1)S(1)} %get-tuple-element.93), channel_id=1, source_target_pairs={{0,24},{1,25},{2,26},{3,27},{4,28},{5,29},{6,30},{7,31},{8,0},{9,1... | collective-permute-start | bytes 393224 | tf_op jit(solution)/shard_map/ppermute | solution.py:429
  125.6 0.7 collective-permute-start.24
  126.3 1.3 collective-permute-start.25
  127.6 0.9 collective-permute-start.26
  128.7 1.0 collective-permute-start.28
  129.7 1.3 collective-permute-done.23.refs_0_
  131.0 1.5 %collective-permute-start.29 = (bf16[80,512]{1,0:T(8,128)(2,1)S(1)}, bf16[80,512]{1,0:T(8,128)(2,1)S(1)}, u32[]{:S(2)}, u32[]{:S(2)}) collective-permute-start(bf16[80,512]{1,0:T(8,128)(2,1)S(1)} %get-tuple-element.102), channel_id=1, source_target_pairs={{0,2},{1,3},{2,0},{3,1},{4,6},{5,7},{6,4},{7,5},{8,10},{9,11},{10,... | collective-permute-start | bytes 245768 | tf_op jit(solution)/shard_map/ppermute | solution.py:420
  132.5 1.1 collective-permute-start.30
  133.7 0.7 factors.1
  134.4 0.8 join_out.1
  135.2 0.8 join_grad.1
  136.5 1.7 %collective-permute-done.30.refs_3_ = bf16[80,512]{1,0:T(8,128)(2,1)S(1)} collective-permute-done((bf16[80,512]{1,0:T(8,128)(2,1)S(1)}, bf16[80,512]{1,0:T(8,128)(2,1)S(1)}, u32[]{:S(2)}, u32[]{:S(2)}) %collective-permute-start.30) | collective-permute-done | bytes 81952 | tf_op jit(solution)/shard_map/ppermute | solution.py:420
  138.2 0.9 join_weight.1
  (45 shorter events, 3.7 us)
Async XLA Ops:
  0.6 1.0 copy-start.4
  0.6 1.0 copy-start.5
  1.7 12.8 %copy-start = (bf16[1,128,2048]{2,1,0:T(8,128)(2,1)S(1)}, bf16[1,128,2048]{2,1,0:T(8,128)(2,1)}, u32[]{:S(2)}) copy-start(bf16[1,128,2048]{2,1,0:T(8,128)(2,1)} %param.9) | copy-start | bytes 1572868
  1.8 5.5 %collective-permute-start.3 = (bf16[336,128]{1,0:T(8,128)(2,1)S(1)}, bf16[336,128]{1,0:T(8,128)(2,1)S(1)}, u32[]{:S(2)}, u32[]{:S(2)}) collective-permute-start(bf16[336,128]{1,0:T(8,128)(2,1)S(1)} %get-tuple-element.62), channel_id=1, source_target_pairs={{0,1},{1,0},{2,3},{3,2},{4,5},{5,4},{6,7},{7,6},{8,9},{9,8},{10,11... | collective-permute-start | bytes 258056 | tf_op jit(solution)/shard_map/ppermute | solution.py:420
  4.8 5.3 %collective-permute-start.4 = (bf16[336,128]{1,0:T(8,128)(2,1)S(1)}, bf16[336,128]{1,0:T(8,128)(2,1)S(1)}, u32[]{:S(2)}, u32[]{:S(2)}) collective-permute-start(bf16[336,128]{1,0:T(8,128)(2,1)S(1)} %get-tuple-element.63), channel_id=1, source_target_pairs={{0,2},{1,3},{2,0},{3,1},{4,6},{5,7},{6,4},{7,5},{8,10},{9,11},{10,... | collective-permute-start | bytes 258056 | tf_op jit(solution)/shard_map/ppermute | solution.py:420
  6.4 5.4 %collective-permute-start.5 = (bf16[336,128]{1,0:T(8,128)(2,1)S(1)}, bf16[336,128]{1,0:T(8,128)(2,1)S(1)}, u32[]{:S(2)}, u32[]{:S(2)}) collective-permute-start(bf16[336,128]{1,0:T(8,128)(2,1)S(1)} %get-tuple-element.64), channel_id=1, source_target_pairs={{0,3},{1,2},{2,1},{3,0},{4,7},{5,6},{6,5},{7,4},{8,11},{9,10},{10,... | collective-permute-start | bytes 258056 | tf_op jit(solution)/shard_map/ppermute | solution.py:420
  11.8 4.3 %copy-start.1 = (bf16[1,128,2048]{2,1,0:T(8,128)(2,1)S(1)}, bf16[1,128,2048]{2,1,0:T(8,128)(2,1)}, u32[]{:S(2)}) copy-start(bf16[1,128,2048]{2,1,0:T(8,128)(2,1)} %param.8) | copy-start | bytes 1572868
  11.8 11.5 %collective-permute-start.6 = (bf16[1088,128]{1,0:T(8,128)(2,1)S(1)}, bf16[1088,128]{1,0:T(8,128)(2,1)S(1)}, u32[]{:S(2)}, u32[]{:S(2)}) collective-permute-start(bf16[1088,128]{1,0:T(8,128)(2,1)S(1)} %relay.1.refs_4_), channel_id=1, source_target_pairs={{0,6},{1,7},{2,4},{3,5},{4,2},{5,3},{6,0},{7,1},{8,14},{9,15},{10,... | collective-permute-start | bytes 835592 | tf_op jit(solution)/shard_map/ppermute | solution.py:425
  14.5 12.2 %copy-start.2 = (bf16[1,128,2048]{2,1,0:T(8,128)(2,1)S(1)}, bf16[1,128,2048]{2,1,0:T(8,128)(2,1)}, u32[]{:S(2)}) copy-start(bf16[1,128,2048]{2,1,0:T(8,128)(2,1)} %param.7) | copy-start | bytes 1572868
  14.6 5.2 %collective-permute-start.16 = (bf16[512,128]{1,0:T(8,128)(2,1)S(1)}, bf16[512,128]{1,0:T(8,128)(2,1)S(1)}, u32[]{:S(2)}, u32[]{:S(2)}) collective-permute-start(bf16[512,128]{1,0:T(8,128)(2,1)S(1)} %get-tuple-element.81), channel_id=1, source_target_pairs={{0,1},{1,0},{2,3},{3,2},{4,5},{5,4},{6,7},{7,6},{8,9},{9,8},{10,11... | collective-permute-start | bytes 393224 | tf_op jit(solution)/shard_map/ppermute | solution.py:420
  16.2 11.3 %collective-permute-start.12 = (bf16[528,128]{1,0:T(8,128)(2,1)S(1)}, bf16[528,128]{1,0:T(8,128)(2,1)S(1)}, u32[]{:S(2)}, u32[]{:S(2)}) collective-permute-start(bf16[528,128]{1,0:T(8,128)(2,1)S(1)} %get-tuple-element.75), channel_id=1, source_target_pairs={{0,1},{1,0},{2,3},{3,2},{4,5},{5,4},{6,7},{7,6},{8,9},{9,8},{10,11... | collective-permute-start | bytes 405512 | tf_op jit(solution)/shard_map/ppermute | solution.py:420
  17.0 11.5 %collective-permute-start.13 = (bf16[528,128]{1,0:T(8,128)(2,1)S(1)}, bf16[528,128]{1,0:T(8,128)(2,1)S(1)}, u32[]{:S(2)}, u32[]{:S(2)}) collective-permute-start(bf16[528,128]{1,0:T(8,128)(2,1)S(1)} %get-tuple-element.76), channel_id=1, source_target_pairs={{0,2},{1,3},{2,0},{3,1},{4,6},{5,7},{6,4},{7,5},{8,10},{9,11},{10,... | collective-permute-start | bytes 405512 | tf_op jit(solution)/shard_map/ppermute | solution.py:420
  17.5 11.0 %collective-permute-start.14 = (bf16[528,128]{1,0:T(8,128)(2,1)S(1)}, bf16[528,128]{1,0:T(8,128)(2,1)S(1)}, u32[]{:S(2)}, u32[]{:S(2)}) collective-permute-start(bf16[528,128]{1,0:T(8,128)(2,1)S(1)} %get-tuple-element.77), channel_id=1, source_target_pairs={{0,3},{1,2},{2,1},{3,0},{4,7},{5,6},{6,5},{7,4},{8,11},{9,10},{10,... | collective-permute-start | bytes 405512 | tf_op jit(solution)/shard_map/ppermute | solution.py:420
  19.8 12.1 %collective-permute-start.17 = (bf16[512,128]{1,0:T(8,128)(2,1)S(1)}, bf16[512,128]{1,0:T(8,128)(2,1)S(1)}, u32[]{:S(2)}, u32[]{:S(2)}) collective-permute-start(bf16[512,128]{1,0:T(8,128)(2,1)S(1)} %get-tuple-element.82), channel_id=1, source_target_pairs={{0,2},{1,3},{2,0},{3,1},{4,6},{5,7},{6,4},{7,5},{8,10},{9,11},{10,... | collective-permute-start | bytes 393224 | tf_op jit(solution)/shard_map/ppermute | solution.py:420
  23.3 10.6 %collective-permute-start.18 = (bf16[512,128]{1,0:T(8,128)(2,1)S(1)}, bf16[512,128]{1,0:T(8,128)(2,1)S(1)}, u32[]{:S(2)}, u32[]{:S(2)}) collective-permute-start(bf16[512,128]{1,0:T(8,128)(2,1)S(1)} %get-tuple-element.83), channel_id=1, source_target_pairs={{0,3},{1,2},{2,1},{3,0},{4,7},{5,6},{6,5},{7,4},{8,11},{9,10},{10,... | collective-permute-start | bytes 393224 | tf_op jit(solution)/shard_map/ppermute | solution.py:420
  27.6 3.6 %copy-start.3 = (f32[1,2048]{1,0:T(1,128)S(1)}, f32[1,2048]{1,0:T(1,128)}, u32[]{:S(2)}) copy-start(f32[1,2048]{1,0:T(1,128)} %gain_ref.3) | copy-start | bytes 24580
  27.6 10.3 %collective-permute-start = (bf16[528,128]{1,0:T(8,128)(2,1)S(1)}, bf16[528,128]{1,0:T(8,128)(2,1)S(1)}, u32[]{:S(2)}, u32[]{:S(2)}) collective-permute-start(bf16[528,128]{1,0:T(8,128)(2,1)S(1)} %get-tuple-element.58), channel_id=1, source_target_pairs={{0,1},{1,0},{2,3},{3,2},{4,5},{5,4},{6,7},{7,6},{8,9},{9,8},{10,11... | collective-permute-start | bytes 405512 | tf_op jit(solution)/shard_map/ppermute | solution.py:420
  28.5 9.4 %collective-permute-start.1 = (bf16[528,128]{1,0:T(8,128)(2,1)S(1)}, bf16[528,128]{1,0:T(8,128)(2,1)S(1)}, u32[]{:S(2)}, u32[]{:S(2)}) collective-permute-start(bf16[528,128]{1,0:T(8,128)(2,1)S(1)} %get-tuple-element.59), channel_id=1, source_target_pairs={{0,2},{1,3},{2,0},{3,1},{4,6},{5,7},{6,4},{7,5},{8,10},{9,11},{10,... | collective-permute-start | bytes 405512 | tf_op jit(solution)/shard_map/ppermute | solution.py:420
  28.5 11.3 %collective-permute-start.2 = (bf16[528,128]{1,0:T(8,128)(2,1)S(1)}, bf16[528,128]{1,0:T(8,128)(2,1)S(1)}, u32[]{:S(2)}, u32[]{:S(2)}) collective-permute-start(bf16[528,128]{1,0:T(8,128)(2,1)S(1)} %get-tuple-element.60), channel_id=1, source_target_pairs={{0,3},{1,2},{2,1},{3,0},{4,7},{5,6},{6,5},{7,4},{8,11},{9,10},{10,... | collective-permute-start | bytes 405512 | tf_op jit(solution)/shard_map/ppermute | solution.py:420
  34.0 16.8 %collective-permute-start.19 = (bf16[512,512]{1,0:T(8,128)(2,1)S(1)}, bf16[512,512]{1,0:T(8,128)(2,1)S(1)}, u32[]{:S(2)}, u32[]{:S(2)}) collective-permute-start(bf16[512,512]{1,0:T(8,128)(2,1)S(1)} %get-tuple-element.85.refs_2_), channel_id=1, source_target_pairs={{0,6},{1,7},{2,4},{3,5},{4,2},{5,3},{6,0},{7,1},{8,14},{9,15},{10,... | collective-permute-start | bytes 1572872 | tf_op jit(solution)/shard_map/ppermute | solution.py:425
  36.0 26.1 %collective-permute-start.15 = (bf16[512,512]{1,0:T(8,128)(2,1)S(1)}, bf16[512,512]{1,0:T(8,128)(2,1)S(1)}, u32[]{:S(2)}, u32[]{:S(2)}) collective-permute-start(bf16[512,512]{1,0:T(8,128)(2,1)S(1)} %get-tuple-element.79.refs_0_), channel_id=1, source_target_pairs={{0,6},{1,7},{2,4},{3,5},{4,2},{5,3},{6,0},{7,1},{8,14},{9,15},{10,... | collective-permute-start | bytes 1572872 | tf_op jit(solution)/shard_map/ppermute | solution.py:425
  41.3 32.0 %collective-permute-start.7 = (bf16[512,512]{1,0:T(8,128)(2,1)S(1)}, bf16[512,512]{1,0:T(8,128)(2,1)S(1)}, u32[]{:S(2)}, u32[]{:S(2)}) collective-permute-start(bf16[512,512]{1,0:T(8,128)(2,1)S(1)} %get-tuple-element.67.refs_0_), channel_id=1, source_target_pairs={{0,6},{1,7},{2,4},{3,5},{4,2},{5,3},{6,0},{7,1},{8,14},{9,15},{10,... | collective-permute-start | bytes 1572872 | tf_op jit(solution)/shard_map/ppermute | solution.py:425
  64.9 62.8 %collective-permute-start.27 = (bf16[272,512]{1,0:T(8,128)(2,1)S(1)}, bf16[272,512]{1,0:T(8,128)(2,1)S(1)}, u32[]{:S(2)}, u32[]{:S(2)}) collective-permute-start(bf16[272,512]{1,0:T(8,128)(2,1)S(1)} %get-tuple-element.99), channel_id=1, source_target_pairs={{0,6},{1,7},{2,4},{3,5},{4,2},{5,3},{6,0},{7,1},{8,14},{9,15},{10,... | collective-permute-start | bytes 835592 | tf_op jit(solution)/shard_map/ppermute | solution.py:425
  73.9 49.6 %collective-permute-start.10 = (bf16[128,512]{1,0:T(8,128)(2,1)S(1)}, bf16[128,512]{1,0:T(8,128)(2,1)S(1)}, u32[]{:S(2)}, u32[]{:S(2)}) collective-permute-start(bf16[128,512]{1,0:T(8,128)(2,1)S(1)} %get-tuple-element.72), channel_id=1, source_target_pairs={{0,10},{1,11},{2,8},{3,9},{4,14},{5,15},{6,12},{7,13},{8,18},{9,19... | collective-permute-start | bytes 393224 | tf_op jit(solution)/shard_map/ppermute | solution.py:429
  104.3 21.2 %collective-permute-start.11 = (bf16[128,512]{1,0:T(8,128)(2,1)S(1)}, bf16[128,512]{1,0:T(8,128)(2,1)S(1)}, u32[]{:S(2)}, u32[]{:S(2)}) collective-permute-start(bf16[128,512]{1,0:T(8,128)(2,1)S(1)} %get-tuple-element.73), channel_id=1, source_target_pairs={{0,11},{1,10},{2,9},{3,8},{4,15},{5,14},{6,13},{7,12},{8,19},{9,18... | collective-permute-start | bytes 393224 | tf_op jit(solution)/shard_map/ppermute | solution.py:429
  105.4 10.3 %collective-permute-start.20 = (bf16[96,128]{1,0:T(8,128)(2,1)S(1)}, bf16[96,128]{1,0:T(8,128)(2,1)S(1)}, u32[]{:S(2)}, u32[]{:S(2)}) collective-permute-start(bf16[96,128]{1,0:T(8,128)(2,1)S(1)} %get-tuple-element.90), channel_id=1, source_target_pairs={{0,1},{1,0},{2,3},{3,2},{4,5},{5,4},{6,7},{7,6},{8,9},{9,8},{10,11... | collective-permute-start | bytes 73736 | tf_op jit(solution)/shard_map/ppermute | solution.py:420
  105.9 12.5 %collective-permute-start.21 = (bf16[96,128]{1,0:T(8,128)(2,1)S(1)}, bf16[96,128]{1,0:T(8,128)(2,1)S(1)}, u32[]{:S(2)}, u32[]{:S(2)}) collective-permute-start(bf16[96,128]{1,0:T(8,128)(2,1)S(1)} %get-tuple-element.91), channel_id=1, source_target_pairs={{0,2},{1,3},{2,0},{3,1},{4,6},{5,7},{6,4},{7,5},{8,10},{9,11},{10,... | collective-permute-start | bytes 73736 | tf_op jit(solution)/shard_map/ppermute | solution.py:420
  115.7 10.6 %collective-permute-start.8 = (bf16[128,512]{1,0:T(8,128)(2,1)S(1)}, bf16[128,512]{1,0:T(8,128)(2,1)S(1)}, u32[]{:S(2)}, u32[]{:S(2)}) collective-permute-start(bf16[128,512]{1,0:T(8,128)(2,1)S(1)} %get-tuple-element.70), channel_id=1, source_target_pairs={{0,8},{1,9},{2,10},{3,11},{4,12},{5,13},{6,14},{7,15},{8,16},{9,17... | collective-permute-start | bytes 393224 | tf_op jit(solution)/shard_map/ppermute | solution.py:429
  118.4 4.7 %collective-permute-start.22 = (bf16[96,128]{1,0:T(8,128)(2,1)S(1)}, bf16[96,128]{1,0:T(8,128)(2,1)S(1)}, u32[]{:S(2)}, u32[]{:S(2)}) collective-permute-start(bf16[96,128]{1,0:T(8,128)(2,1)S(1)} %get-tuple-element.92), channel_id=1, source_target_pairs={{0,3},{1,2},{2,1},{3,0},{4,7},{5,6},{6,5},{7,4},{8,11},{9,10},{10,... | collective-permute-start | bytes 73736 | tf_op jit(solution)/shard_map/ppermute | solution.py:420
  123.1 5.6 %collective-permute-start.9 = (bf16[128,512]{1,0:T(8,128)(2,1)S(1)}, bf16[128,512]{1,0:T(8,128)(2,1)S(1)}, u32[]{:S(2)}, u32[]{:S(2)}) collective-permute-start(bf16[128,512]{1,0:T(8,128)(2,1)S(1)} %get-tuple-element.71), channel_id=1, source_target_pairs={{0,9},{1,8},{2,11},{3,10},{4,13},{5,12},{6,15},{7,14},{8,17},{9,16... | collective-permute-start | bytes 393224 | tf_op jit(solution)/shard_map/ppermute | solution.py:429
  123.6 7.4 %collective-permute-start.23 = (bf16[128,512]{1,0:T(8,128)(2,1)S(1)}, bf16[128,512]{1,0:T(8,128)(2,1)S(1)}, u32[]{:S(2)}, u32[]{:S(2)}) collective-permute-start(bf16[128,512]{1,0:T(8,128)(2,1)S(1)} %get-tuple-element.93), channel_id=1, source_target_pairs={{0,24},{1,25},{2,26},{3,27},{4,28},{5,29},{6,30},{7,31},{8,0},{9,1... | collective-permute-start | bytes 393224 | tf_op jit(solution)/shard_map/ppermute | solution.py:429
  125.6 7.0 %collective-permute-start.24 = (bf16[128,512]{1,0:T(8,128)(2,1)S(1)}, bf16[128,512]{1,0:T(8,128)(2,1)S(1)}, u32[]{:S(2)}, u32[]{:S(2)}) collective-permute-start(bf16[128,512]{1,0:T(8,128)(2,1)S(1)} %get-tuple-element.94), channel_id=1, source_target_pairs={{0,25},{1,24},{2,27},{3,26},{4,29},{5,28},{6,31},{7,30},{8,1},{9,0... | collective-permute-start | bytes 393224 | tf_op jit(solution)/shard_map/ppermute | solution.py:429
  126.3 8.9 %collective-permute-start.25 = (bf16[128,512]{1,0:T(8,128)(2,1)S(1)}, bf16[128,512]{1,0:T(8,128)(2,1)S(1)}, u32[]{:S(2)}, u32[]{:S(2)}) collective-permute-start(bf16[128,512]{1,0:T(8,128)(2,1)S(1)} %get-tuple-element.95), channel_id=1, source_target_pairs={{0,26},{1,27},{2,24},{3,25},{4,30},{5,31},{6,28},{7,29},{8,2},{9,3... | collective-permute-start | bytes 393224 | tf_op jit(solution)/shard_map/ppermute | solution.py:429
  127.6 7.6 %collective-permute-start.26 = (bf16[128,512]{1,0:T(8,128)(2,1)S(1)}, bf16[128,512]{1,0:T(8,128)(2,1)S(1)}, u32[]{:S(2)}, u32[]{:S(2)}) collective-permute-start(bf16[128,512]{1,0:T(8,128)(2,1)S(1)} %get-tuple-element.96), channel_id=1, source_target_pairs={{0,27},{1,26},{2,25},{3,24},{4,31},{5,30},{6,29},{7,28},{8,3},{9,2... | collective-permute-start | bytes 393224 | tf_op jit(solution)/shard_map/ppermute | solution.py:429
  128.7 7.5 %collective-permute-start.28 = (bf16[80,512]{1,0:T(8,128)(2,1)S(1)}, bf16[80,512]{1,0:T(8,128)(2,1)S(1)}, u32[]{:S(2)}, u32[]{:S(2)}) collective-permute-start(bf16[80,512]{1,0:T(8,128)(2,1)S(1)} %get-tuple-element.101), channel_id=1, source_target_pairs={{0,1},{1,0},{2,3},{3,2},{4,5},{5,4},{6,7},{7,6},{8,9},{9,8},{10,11... | collective-permute-start | bytes 245768 | tf_op jit(solution)/shard_map/ppermute | solution.py:420
  131.0 5.5 %collective-permute-start.29 = (bf16[80,512]{1,0:T(8,128)(2,1)S(1)}, bf16[80,512]{1,0:T(8,128)(2,1)S(1)}, u32[]{:S(2)}, u32[]{:S(2)}) collective-permute-start(bf16[80,512]{1,0:T(8,128)(2,1)S(1)} %get-tuple-element.102), channel_id=1, source_target_pairs={{0,2},{1,3},{2,0},{3,1},{4,6},{5,7},{6,4},{7,5},{8,10},{9,11},{10,... | collective-permute-start | bytes 245768 | tf_op jit(solution)/shard_map/ppermute | solution.py:420
  132.5 5.7 %collective-permute-start.30 = (bf16[80,512]{1,0:T(8,128)(2,1)S(1)}, bf16[80,512]{1,0:T(8,128)(2,1)S(1)}, u32[]{:S(2)}, u32[]{:S(2)}) collective-permute-start(bf16[80,512]{1,0:T(8,128)(2,1)S(1)} %get-tuple-element.103), channel_id=1, source_target_pairs={{0,3},{1,2},{2,1},{3,0},{4,7},{5,6},{6,5},{7,4},{8,11},{9,10},{10,... | collective-permute-start | bytes 245768 | tf_op jit(solution)/shard_map/ppermute | solution.py:420

commit v2 on v1

v2 whole, which is shorter than its diff:
```python
import functools

import jax
import jax.numpy as jnp
from jax import lax
from jax.experimental import pallas as pl
from jax.experimental.pallas import tpu as pltpu
from jax.sharding import PartitionSpec as P

BF = jnp.bfloat16
F32 = jnp.float32
LANE = 128
SUB = 16
EPS = 1e-06
COST = {"norm_saved": 2.0, "adjoint": 6.0, "mix_saved": 1, "norm_act": 3.0, "backward": 1, "mix_act": 2, "input_grad": 2}
VMEM = 48 * 1024 * 1024


def position(ngroups):
    me = lax.axis_index("seq")
    return me % ngroups, me // ngroups


def natural(pos, nb, ngroups, na):
    return ((pos // na % nb) * ngroups + pos // (nb * na)) * na + pos % na


def split3(x):
    hi = x.astype(BF).astype(F32)
    mid = (x - hi).astype(BF).astype(F32)
    return hi, mid, x - hi - mid


def eye(n):
    return lax.broadcasted_iota(jnp.int32, (n, n), 0) == lax.broadcasted_iota(jnp.int32, (n, n), 1)


def to_row(col):
    return jnp.sum(jnp.where(eye(col.shape[0]), col, 0.0), axis=0, keepdims=True)


def to_col(row):
    return jnp.sum(jnp.where(eye(row.shape[1]), row, 0.0), axis=1, keepdims=True)


def mm(a, b, ca=1, cb=0):
    return lax.dot_general(a, b, (((ca,), (cb,)), ((), ())), preferred_element_type=F32)


def rows(start, size):
    return pl.ds(pl.multiple_of(start, size), size)


def call(body, outs, scratch=(), flops=0, name=None):
    def run(*args, after=()):
        nin, nwait = len(args), len(after)

        def without_waits(*refs):
            return body(*refs[:nin], *refs[nin + nwait :])

        return pl.pallas_call(
            without_waits,
            out_shape=list(outs),
            in_specs=[pl.BlockSpec(memory_space=pltpu.VMEM)] * nin
            + [pl.BlockSpec(memory_space=pl.ANY)] * nwait,
            out_specs=[pl.BlockSpec(memory_space=pltpu.VMEM)] * len(outs),
            scratch_shapes=list(scratch),
            compiler_params=pltpu.CompilerParams(vmem_limit_bytes=VMEM),
            cost_estimate=pl.CostEstimate(flops=int(COST.get(name, 0.0) * 1e9), bytes_accessed=0, transcendentals=0),
            name=name,
        )(*args, *after)

    return run


def sds(shape, dtype=BF):
    return jax.ShapeDtypeStruct(shape, dtype)


def pack_weight_body(nb, ngroups, w_ref, l_ref, r_ref, *outs):
    _, block = position(ngroups)
    r, bd = w_ref.shape[1], w_ref.shape[2]
    chunks = bd // LANE
    bl, ext = l_ref.shape[1], r_ref.shape[1]
    left = jnp.concatenate([l_ref[j].astype(F32) for j in range(l_ref.shape[0])], axis=1).astype(BF)
    right = jnp.concatenate([r_ref[j].astype(F32) for j in range(r_ref.shape[0])], axis=1).astype(BF)
    for d in range(nb):
        for ch in range(chunks):
            outs[d][ch * r : (ch + 1) * r, :] = w_ref[block ^ d, :, ch * LANE : (ch + 1) * LANE]
        outs[d][chunks * r : chunks * r + bl, :] = left
        outs[d][chunks * r + bl :, :] = right


def pack_tokens_body(nb, ngroups, with_scale, x_ref, *outs):
    _, block = position(ngroups)
    t, width = x_ref.shape
    bd = width // nb
    chunks = bd // LANE
    if with_scale:
        x = x_ref[...].astype(F32)
        inv = lax.rsqrt(jnp.mean(x * x, axis=-1, keepdims=True) + EPS)
        parts = split3(to_row(inv))
        tile = jnp.concatenate(list(parts) + [jnp.zeros((SUB - 3, t), F32)], axis=0).astype(BF)
    for d in range(nb):
        for ch in range(chunks):
            lanes = pl.ds(pl.multiple_of((block ^ d) * bd + ch * LANE, LANE), LANE)
            outs[d][ch * t : (ch + 1) * t, :] = x_ref[:, lanes]
        if with_scale:
            outs[d][chunks * t :, :] = tile


def relay_body(nb, ngroups, r4, ext, *refs):
    _, place = position(ngroups)
    out = refs[nb]
    for d in range(nb):
        to = place ^ d
        out[rows(to * r4, r4), :] = refs[d][:r4, :]
        out[pl.ds(pl.multiple_of(nb * r4 + to * ext, ext), ext), :] = refs[d][refs[d].shape[0] - ext :, :]


def expand_matrix(ext, nb, ngroups, na):
    n = SUB * ext
    row = lax.broadcasted_iota(jnp.int32, (n, n), 0)
    col = lax.broadcasted_iota(jnp.int32, (n, n), 1)
    return jnp.where((row // ext == col % SUB) & (row % ext == natural(col // SUB, nb, ngroups, na)), 1.0, 0.0).astype(BF)


def same_position(n):
    row = lax.broadcasted_iota(jnp.int32, (n, n), 0)
    col = lax.broadcasted_iota(jnp.int32, (n, n), 1)
    return row % SUB == col % SUB


def assemble_body(nb, ngroups, r, ext, bl, *refs):
    group, place = position(ngroups)
    na = LANE // bl
    msgs, relays = refs[:nb], refs[nb : nb + ngroups]
    wk_ref, mq_ref, bd_ref, all_ref = refs[nb + ngroups :]
    chunks = wk_ref.shape[1] // LANE
    r4 = chunks * r
    for e in range(ngroups):
        g = group ^ e
        for c in range(nb):
            for ch in range(chunks):
                wk_ref[rows((c * ngroups + g) * r, r), ch * LANE : (ch + 1) * LANE] = relays[e][
                    c * r4 + ch * r : c * r4 + (ch + 1) * r, :
                ]
            all_ref[c * ngroups + g] = relays[e][nb * r4 + c * ext : nb * r4 + (c + 1) * ext, :]
    nq = mq_ref.shape[0]
    per = nb * ngroups // nq
    n = SUB * ext
    turn = expand_matrix(ext, nb, ngroups, na)
    spread = jnp.where(
        natural(lax.broadcasted_iota(jnp.int32, (n, ext), 0) // SUB, nb, ngroups, na)
        == lax.broadcasted_iota(jnp.int32, (n, ext), 1),
        1.0,
        0.0,
    ).astype(BF)
    same = same_position(n)
    for q in range(nq):
        tiles = jnp.concatenate([all_ref[q * per + i] for i in range(per)], axis=1)
        wide = mm(tiles, turn).astype(BF)
        mq_ref[q] = jnp.where(same, mm(spread, wide), 0.0).astype(BF)
    half_row = lax.broadcasted_iota(jnp.int32, (LANE, LANE), 0) // bl
    half_col = lax.broadcasted_iota(jnp.int32, (LANE, LANE), 1) // bl
    for d in range(nb):
        tile = msgs[d][r4 : r4 + bl, :].astype(F32)
        both = jnp.concatenate([tile] * (LANE // bl), axis=0)
        bd_ref[place ^ d] = jnp.where(half_row == half_col, both, 0.0).astype(BF)


def unpack(msg, t, chunks):
    return jnp.concatenate([msg[ch * t : (ch + 1) * t, :] for ch in range(chunks)], axis=1)


def scale_of(msg, t, chunks):
    tile = msg[chunks * t : chunks * t + SUB, :].astype(F32)
    return to_col(tile[0:1] + tile[1:2] + tile[2:3])


def norm_body(nb, ngroups, *refs):
    _, place = position(ngroups)
    msgs = refs[:nb]
    gain_ref, normin_ref = refs[nb:]
    t = LANE
    bd = normin_ref.shape[1]
    chunks = bd // LANE
    gain = gain_ref[:, pl.ds(pl.multiple_of(place * bd, LANE), bd)]
    for d in range(nb):
        x = unpack(msgs[d], t, chunks).astype(F32)
        normed = x * scale_of(msgs[d], t, chunks)
        normin_ref[rows((place ^ d) * t, t), :] = (normed * gain).astype(BF)


def project_body(normin_ref, wk_ref, bd_ref, proj_ref, first_ref):
    t = LANE
    proj_ref[...] = mm(normin_ref[...], wk_ref[...]).astype(BF)
    for c in range(bd_ref.shape[0]):
        at = slice(c * t, (c + 1) * t)
        first_ref[at, :] = mm(bd_ref[c], proj_ref[at, :]).astype(BF)


def adjoint_body(nb, ngroups, *refs):
    _, place = position(ngroups)
    msgs = refs[:nb]
    proj_ref, adj_ref, grad_ref = refs[nb:]
    t = LANE
    chunks = proj_ref.shape[1] // LANE
    for d in range(nb):
        at = rows((place ^ d) * t, t)
        g = unpack(msgs[d], t, chunks)
        grad_ref[at, :] = g
        adj_ref[at, :] = (g.astype(F32) * proj_ref[at, :].astype(F32)).astype(BF)


def gather_positions(group, bl, parts, out_ref):
    blocks = parts[0].shape[0] // bl
    for e, part in enumerate(parts):
        base = (group ^ e) * blocks * SUB
        for q in range(bl // SUB):
            for a in range(blocks):
                out_ref[q, pl.ds(pl.multiple_of(base + a * SUB, SUB), SUB), :] = part[
                    a * bl + q * SUB : a * bl + (q + 1) * SUB, :
                ]


def mix_body(ngroups, bl, *refs):
    group, _ = position(ngroups)
    firsts = refs[:ngroups]
    mq_ref, f_ref, mixed_ref = refs[ngroups:]
    gather_positions(group, bl, firsts, f_ref)
    blocks = firsts[0].shape[0] // bl
    own = rows(group * blocks * SUB, blocks * SUB)
    for q in range(bl // SUB):
        mixed = mm(mq_ref[q, own, :], f_ref[q]).astype(BF)
        for a in range(blocks):
            mixed_ref[a * bl + q * SUB : a * bl + (q + 1) * SUB, :] = mixed[a * SUB : (a + 1) * SUB, :]


def output_body(nb, ngroups, mixed_ref, proj_ref, *refs):
    _, place = position(ngroups)
    msgs, outs = refs[:nb], refs[nb:]
    t = LANE
    chunks = proj_ref.shape[1] // LANE
    for d in range(nb):
        at = rows((place ^ d) * t, t)
        x = unpack(msgs[d], t, chunks).astype(F32)
        outs[d][...] = (x + proj_ref[at, :].astype(F32) * mixed_ref[at, :].astype(F32)).astype(BF)


def backward_body(nb, ngroups, bl, *refs):
    group, _ = position(ngroups)
    adjs, rest = refs[:ngroups], refs[ngroups:]
    mixed_ref, mq_ref, bd_ref, grad_ref, adj_proj_ref, a_ref, adj_first_ref = rest
    t = LANE
    gather_positions(group, bl, adjs, a_ref)
    blocks = adjs[0].shape[0] // bl
    own = rows(group * blocks * SUB, blocks * SUB)
    for q in range(bl // SUB):
        adj_first = mm(mq_ref[q, :, own], a_ref[q], 0, 0).astype(BF)
        for a in range(blocks):
            at = slice(a * bl + q * SUB, a * bl + (q + 1) * SUB)
            adj_first_ref[at, :] = adj_first[a * SUB : (a + 1) * SUB, :]
    for c in range(nb):
        at = slice(c * t, (c + 1) * t)
        grad = grad_ref[at, :].astype(F32)
        adj_first = adj_first_ref[at, :]
        mixed = mixed_ref[at, :].astype(F32)
        adj_proj_ref[at, :] = (grad * mixed + mm(bd_ref[c], adj_first, 0, 0)).astype(BF)


def factor_grads_body(nb, ngroups, bl, ext, f_ref, a_ref, adj_first_ref, proj_ref, left_ref, right_ref):
    group, _ = position(ngroups)
    na = LANE // bl
    t = LANE
    nq = f_ref.shape[0]
    n = SUB * ext
    upper = lax.broadcasted_iota(jnp.int32, (bl, LANE), 1) < bl
    for c in range(nb):
        at = slice(c * t, (c + 1) * t)
        both = mm(adj_first_ref[at, :], proj_ref[at, :], 1, 1)
        left_ref[c] = jnp.where(upper, both[:bl, :], both[bl:, :]).astype(BF)
    turn = expand_matrix(ext, nb, ngroups, na)
    same = same_position(n)
    order = jnp.where(
        natural(lax.broadcasted_iota(jnp.int32, (ext, ext), 0), nb, ngroups, na)
        == lax.broadcasted_iota(jnp.int32, (ext, ext), 1),
        1.0,
        0.0,
    ).astype(BF)
    per = right_ref.shape[0] // nq
    for q in range(nq):
        pairs = jnp.where(same, mm(a_ref[q], f_ref[q], 1, 1), 0.0)
        summed = jnp.sum(pairs.reshape(ext, SUB, n), axis=1).astype(BF)
        turned = mm(order, mm(summed, turn, 1, 1).astype(BF), 0, 0).astype(BF)
        for i in range(per):
            right_ref[q * per + i] = turned[:, i * LANE : (i + 1) * LANE]


def adj_norm_body(nb, ngroups, normin_ref, adj_proj_ref, wk_ref, gain_ref, *refs):
    _, place = position(ngroups)
    gain_part_ref, outs, adj_norm_ref = refs[0], refs[1 : 1 + nb], refs[1 + nb]
    bd = wk_ref.shape[0]
    t = LANE
    adj_norm = mm(adj_proj_ref[...], wk_ref[...], 1, 1)
    adj_norm_ref[...] = adj_norm
    gain = gain_ref[:, pl.ds(pl.multiple_of(place * bd, LANE), bd)]
    gain_part_ref[...] = jnp.sum(adj_norm * normin_ref[...].astype(F32), axis=0, keepdims=True) / gain
    for d in range(nb):
        outs[d][...] = adj_norm_ref[rows((place ^ d) * t, t), :].astype(BF)


def weight_grad_body(nb, ngroups, normin_ref, adj_proj_ref, gain_part_ref, own_ref, *refs):
    group, _ = position(ngroups)
    sends, gw_ref = refs[: ngroups - 1], refs[ngroups - 1]
    share, bd = own_ref.shape
    r = share // nb
    gw_ref[...] = mm(normin_ref[...], adj_proj_ref[...], 0, 0)
    tile = jnp.concatenate(
        list(split3(gain_part_ref[...])) + [jnp.zeros((SUB - 3, bd), F32)], axis=0
    ).astype(BF)
    for c in range(nb):
        at = slice(c * r, (c + 1) * r)
        own_ref[at, :] = gw_ref[rows((c * ngroups + group) * r, r), :]
        for e in range(1, ngroups):
            sends[e - 1][at, :] = gw_ref[rows((c * ngroups + (group ^ e)) * r, r), :].astype(BF)
    for e in range(1, ngroups):
        sends[e - 1][share:, :] = tile


def weight_sum_body(nb, ngroups, own_ref, gain_part_ref, left_ref, right_ref, *refs):
    group, place = position(ngroups)
    recvs = refs[: ngroups - 1]
    outs = refs[ngroups - 1 : ngroups - 1 + nb]
    total_ref, gains_ref = refs[ngroups - 1 + nb :]
    share, bd = own_ref.shape
    chunks = bd // LANE
    bl, ext = left_ref.shape[1], right_ref.shape[1]
    r = share // nb
    total = own_ref[...]
    gains_ref[group] = gain_part_ref[...]
    for e in range(1, ngroups):
        total = total + recvs[e - 1][:share, :].astype(F32)
        three = recvs[e - 1][share:, :].astype(F32)
        gains_ref[group ^ e] = three[0:1] + three[1:2] + three[2:3]
    total_ref[...] = total.astype(BF)
    gain = gains_ref[0]
    for g in range(1, ngroups):
        gain = gain + gains_ref[g]
    three = split3(gain)
    parts = [p[:, ch * LANE : (ch + 1) * LANE] for p in three for ch in range(chunks)]
    tile = jnp.concatenate(parts + [jnp.zeros((SUB - len(parts), LANE), F32)], axis=0).astype(BF)
    for d in range(nb):
        to = place ^ d
        for ch in range(chunks):
            outs[d][ch * r : (ch + 1) * r, :] = total_ref[rows(to * r, r), ch * LANE : (ch + 1) * LANE]
        at = chunks * r
        outs[d][at : at + bl, :] = left_ref[to]
        outs[d][at + bl : at + bl + ext, :] = right_ref[to * ngroups + group]
        outs[d][at + bl + ext :, :] = tile


def input_grad_body(nb, ngroups, x_ref, grad_ref, gain_ref, *refs):
    _, place = position(ngroups)
    parts, out, adj_ref = refs[:nb], refs[nb], refs[nb + 1]
    bd = parts[0].shape[1]
    for d in range(nb):
        adj_ref[:, pl.ds(pl.multiple_of((place ^ d) * bd, LANE), bd)] = parts[d][...].astype(F32)
    x = x_ref[...].astype(F32)
    inv = lax.rsqrt(jnp.mean(x * x, axis=-1, keepdims=True) + EPS)
    normed = x * inv
    scaled = adj_ref[...] * gain_ref[...]
    mean = jnp.mean(scaled * normed, axis=-1, keepdims=True)
    out[...] = (grad_ref[...].astype(F32) + inv * (scaled - normed * mean)).astype(BF)


def join_body(nb, ngroups, *refs):
    _, block = position(ngroups)
    out = refs[nb]
    bd = refs[0].shape[1]
    for d in range(nb):
        out[:, pl.ds(pl.multiple_of((block ^ d) * bd, LANE), bd)] = refs[d][...]


def join_weight_body(nb, ngroups, *refs):
    _, block = position(ngroups)
    gw_ref, gain_ref, left_out, right_out, by_block = refs[nb:]
    r, _, bd = gw_ref.shape
    chunks = bd // LANE
    na, bl, _ = left_out.shape
    npos, ext, _ = right_out.shape
    at = chunks * r
    left = refs[0][at : at + bl, :].astype(F32)
    right = refs[0][at + bl : at + bl + ext, :].astype(F32)
    for d in range(1, nb):
        left = left + refs[d][at : at + bl, :].astype(F32)
        right = right + refs[d][at + bl : at + bl + ext, :].astype(F32)
    for j in range(na):
        left_out[j] = left[:, j * bl : (j + 1) * bl]
    for j in range(npos):
        right_out[j] = right[:, j * ext : (j + 1) * ext]
    for d in range(nb):
        k = block ^ d
        by_block[k] = unpack(refs[d], r, chunks).astype(F32)
        tile = refs[d][at + bl + ext :, :].astype(F32)
        for ch in range(chunks):
            gain_ref[:, pl.ds(pl.multiple_of(k * bd + ch * LANE, LANE), LANE)] = (
                tile[ch : ch + 1] + tile[chunks + ch : chunks + ch + 1] + tile[2 * chunks + ch : 2 * chunks + ch + 1]
            )
    for k in range(nb):
        gw_ref[:, k, :] = by_block[k]


def shards(act_in, saved_in, grad_in, gain, weight, left_blocks, right_blocks):
    nseq = lax.axis_size("seq")
    npipe = lax.axis_size("pipe")
    _, t, width = act_in.shape
    _, r, nb, bd = weight.shape
    ngroups = nseq // nb
    bl = left_blocks.shape[2]
    ext = right_blocks.shape[2]
    npos = right_blocks.shape[1]
    chunks = bd // LANE
    tg = nb * t
    r4 = chunks * r
    nq = bl // SUB
    n = SUB * ext

    def within(parts):
        return [parts[0]] + [
            lax.ppermute(parts[d], "seq", [(s, s ^ (d * ngroups)) for s in range(nseq)]) for d in range(1, nb)
        ]

    def across(block, e):
        return lax.ppermute(block, "seq", [(s, s ^ e) for s in range(nseq)])

    def gathered(block):
        return [block] + [across(block, e) for e in range(1, ngroups)]

    def handed(parts, step):
        return [
            lax.ppermute(
                parts[d],
                ("pipe", "seq"),
                [
                    (p * nseq + s, ((p + step) % npipe) * nseq + (s ^ (d * ngroups)))
                    for p in range(npipe)
                    for s in range(nseq)
                ],
            )
            for d in range(nb)
        ]

    part = functools.partial
    def run(name, body, outs, scratch=()):
        return call(body, outs, scratch, name=name)

    pack = part(pack_tokens_body, nb, ngroups)
    norm = part(norm_body, nb, ngroups)
    mix = part(mix_body, ngroups, bl)
    join = part(join_body, nb, ngroups)
    scaled_msgs, plain_msgs = [sds((chunks * t + SUB, LANE))] * nb, [sds((chunks * t, LANE))] * nb
    tokens = [sds((tg, bd))]
    pieces = [sds((t, bd))] * nb
    wide = [sds((nq, n, bd))]
    share = bd // ngroups

    w_msgs = run("pack_weight", part(pack_weight_body, nb, ngroups), [sds((r4 + bl + ext, LANE))] * nb)(
        jnp.transpose(weight[0], (1, 0, 2)), left_blocks[0], right_blocks[0]
    )
    sto_msgs = run("pack_saved", part(pack, True), scaled_msgs)(saved_in[0], after=w_msgs[:1])
    grad_msgs = run("pack_grad", part(pack, False), plain_msgs)(grad_in[0], after=sto_msgs[:1])
    w_msgs, sto_msgs, grad_msgs = within(w_msgs), within(sto_msgs), within(grad_msgs)
    (relay,) = run("relay", part(relay_body, nb, ngroups, r4, ext), [sds((nb * (r4 + ext), LANE))])(
        *w_msgs, after=grad_msgs[:1]
    )
    relays = gathered(relay)
    (sto_normin,) = run("norm_saved", norm, tokens)(*sto_msgs, gain)
    wk, mq, bd_left = run(
        "assemble",
        part(assemble_body, nb, ngroups, r, ext, bl),
        [sds((bd, bd)), sds((nq, n, n)), sds((nb, LANE, LANE))],
        [pltpu.VMEM((nseq, ext, LANE), BF)],
    )(*w_msgs, *relays, after=[sto_normin])
    sto_proj, sto_first = run("project_saved", project_body, tokens * 2)(sto_normin, wk, bd_left)
    sto_firsts = gathered(sto_first)
    cur_msgs = run("pack_act", part(pack, True), scaled_msgs)(act_in[0], after=[sto_first])
    adj_mix, grad = run("adjoint", part(adjoint_body, nb, ngroups), tokens * 2)(
        *grad_msgs, sto_proj, after=cur_msgs[:1]
    )
    cur_msgs = within(cur_msgs)
    adj_mixes = gathered(adj_mix)
    sto_f, sto_mixed = run("mix_saved", mix, wide + tokens)(*sto_firsts, mq, after=[adj_mix])
    (cur_normin,) = run("norm_act", norm, tokens)(*cur_msgs, gain, after=[sto_mixed])
    cur_proj, cur_first = run("project_act", project_body, tokens * 2)(cur_normin, wk, bd_left)
    cur_firsts = gathered(cur_first)
    adj_proj, adj_f, adj_first = run(
        "backward", part(backward_body, nb, ngroups, bl), tokens + wide + tokens
    )(*adj_mixes, sto_mixed, mq, bd_left, grad, after=[cur_first])
    gain_part, *adj_parts = run(
        "adj_norm",
        part(adj_norm_body, nb, ngroups),
        [sds((1, bd), F32)] + pieces,
        [pltpu.VMEM((tg, bd), F32)],
    )(sto_normin, adj_proj, wk, gain)
    adj_parts = within(adj_parts)
    own_gw, *sends = run(
        "weight_grad",
        part(weight_grad_body, nb, ngroups),
        [sds((share, bd), F32)] + [sds((share + SUB, bd))] * (ngroups - 1),
        [pltpu.VMEM((bd, bd), F32)],
    )(sto_normin, adj_proj, gain_part)
    recvs = [across(sends[e - 1], e) for e in range(1, ngroups)]
    left_tiles, right_tiles = run(
        "factor_grads",
        part(factor_grads_body, nb, ngroups, bl, ext),
        [sds((nb, bl, LANE)), sds((nseq, ext, LANE))],
    )(sto_f, adj_f, adj_first, sto_proj, after=[own_gw])
    _, cur_mixed = run("mix_act", mix, wide + tokens)(*cur_firsts, mq, after=[left_tiles])
    out_parts = run("output", part(output_body, nb, ngroups), pieces)(cur_mixed, cur_proj, *cur_msgs)
    gw_parts = run(
        "weight_sum",
        part(weight_sum_body, nb, ngroups),
        [sds((r4 + bl + ext + SUB, LANE))] * nb,
        [pltpu.VMEM((share, bd), BF), pltpu.VMEM((ngroups, 1, bd), F32)],
    )(own_gw, gain_part, left_tiles, right_tiles, *recvs, after=out_parts[:1])
    (adj_x,) = run(
        "input_grad", part(input_grad_body, nb, ngroups), [sds((t, width))], [pltpu.VMEM((t, width), F32)]
    )(saved_in[0], grad_in[0], gain, *adj_parts, after=gw_parts[:1])
    out_parts, gw_parts = handed(out_parts, 1), within(gw_parts)
    grad_handed = lax.ppermute(adj_x, "pipe", [(p, (p - 1) % npipe) for p in range(npipe)])
    (handed_on,) = run("join_out", join, [sds((t, width))])(*out_parts, after=[adj_x])
    weight_grad, gain_grad, left_grad, right_grad = run(
        "join_weight",
        part(join_weight_body, nb, ngroups),
        [
            sds((r, nb, bd), F32),
            sds((1, width), F32),
            sds((left_blocks.shape[1], bl, bl), F32),
            sds((npos, ext, ext), F32),
        ],
        [pltpu.VMEM((nb, r, bd), F32)],
    )(*gw_parts, after=[handed_on])
    return (
        handed_on[None],
        grad_handed[None],
        weight_grad[None],
        gain_grad,
        left_grad[None],
        right_grad[None],
    )


def solution(mesh):
    tokens = P("pipe", "seq", None)
    factor = P("pipe", "seq", None, None)
    return jax.shard_map(
        shards,
        mesh=mesh,
        in_specs=(tokens, tokens, tokens, P("pipe", None), factor, factor, factor),
        out_specs=(tokens, tokens, factor, P("pipe", None), factor, factor),
        check_vma=False,
    )
```

time: 139 us -> 99.9 us (0.72)
  starting transfers between devices: 80.2 us -> 58.2 us
  waiting for transfers between devices: 46 us -> 26.3 us
  local copies, waits for them, and re-layouts: 1.04 us -> 2.92 us
    ppermute x8 -> x4, starting transfers between devices: 36.8 us -> 6.38 us  [handed(): lax.ppermute(parts[d], ('pipe', 'seq'), [(p * nseq + s, (p + step) % npip...]
    ppermute x23 -> x24, waiting for transfers between devices: 44.7 us -> 20 us  [the longest x5 10.1 us: across(): return lax.ppermute(block, 'seq', [(s, s ^ e) for s in range(nseq)])]
    ppermute x23 -> x24, starting transfers between devices: 43.5 us -> 51.8 us  [the longest x18 43.6 us: within(): lax.ppermute(parts[d], 'seq', [(s, s ^ d * ngroups) for s in range(nseq)])]
    ppermute x8 -> x4, waiting for transfers between devices: 1.33 us -> 6.3 us  [handed(): lax.ppermute(parts[d], ('pipe', 'seq'), [(p * nseq + s, (p + step) % npip...]
    unnamed x13 -> x16, local copies, waits for them, and re-layouts: 1.04 us -> 2.92 us
    pallas_call x18 -> x22, Pallas kernels: 11.1 us -> 11.4 us  [run(): pl.pallas_call(without_waits, out_shape=list(outs), in_specs=[pl.BlockSpe...]
  transfers between devices with their start and end apart: 31 -> 28, of which waited for: 15 -> 12; matrix products, arithmetic and copies ran while one was open for 0% -> 0% of each run, Pallas kernels for 7% -> 11%
where the time goes in v2:
time: 99.9 us; the launch traced here: 99.7 us
  starting transfers between devices  58.2 us (58%)
  waiting for transfers between devices  26.3 us (26%)
  Pallas kernels  11.4 us (11%)
  local copies, waits for them, and re-layouts  2.92 us (3%)
    ppermute x18, starting transfers between devices, within(): lax.ppermute(parts[d], 'seq', [(s, s ^ d * ngroups) for s in range(nseq)])  43.6 us
    pallas_call x22, Pallas kernels, run(): pl.pallas_call(without_waits, out_shape=list(outs), in_specs=[pl.BlockSpe...  11.4 us
    ppermute x5, waiting for transfers between devices, across(): return lax.ppermute(block, 'seq', [(s, s ^ e) for s in range(nseq)])  10.1 us
    ppermute x18, waiting for transfers between devices, within(): lax.ppermute(parts[d], 'seq', [(s, s ^ d * ngroups) for s in range(nseq)])  9.83 us
    ppermute x5, starting transfers between devices, across(): return lax.ppermute(block, 'seq', [(s, s ^ e) for s in range(nseq)])  8.17 us
    ppermute x4, starting transfers between devices, handed(): lax.ppermute(parts[d], ('pipe', 'seq'), [(p * nseq + s, (p + step) % npip...  6.38 us
    ppermute x4, waiting for transfers between devices, handed(): lax.ppermute(parts[d], ('pipe', 'seq'), [(p * nseq + s, (p + step) % npip...  6.3 us
    unnamed x16, local copies, waits for them, and re-layouts  2.92 us
  transfers between devices with their start and end apart: 28, of which 12 were waited for; matrix products, arithmetic and copies ran while one was open for 0% of the time, Pallas kernels for 11%

profile of v2, /device:TPU:0, one launch (start us, length us, event | category | flops | bytes accessed | tf_op | source)
XLA Modules:
  0.0 99.7 jit_solution(16475190129011276459)
XLA Ops:
  0.7 1.1 %copy.15 = bf16[1,64,4,512]{3,1,2,0:T(8,128)(2,1)S(1)} copy(bf16[1,64,4,512]{3,2,1,0:T(4,128)(2,1)} %param.11) | data formatting | bytes 524288 | tf_op args[4]
  1.8 3.1 %collective-permute-start.3 = (bf16[336,128]{1,0:T(8,128)(2,1)S(1)}, bf16[336,128]{1,0:T(8,128)(2,1)S(1)}, u32[]{:S(2)}, u32[]{:S(2)}) collective-permute-start(bf16[336,128]{1,0:T(8,128)(2,1)S(1)} %get-tuple-element.63), channel_id=1, source_target_pairs={{0,2},{1,3},{2,0},{3,1},{4,6},{5,7},{6,4},{7,5},{8,10},{9,11},{10,... | collective-permute-start | bytes 258056 | tf_op jit(solution)/shard_map/ppermute | solution.py:431
  4.9 2.6 %collective-permute-start.4 = (bf16[336,128]{1,0:T(8,128)(2,1)S(1)}, bf16[336,128]{1,0:T(8,128)(2,1)S(1)}, u32[]{:S(2)}, u32[]{:S(2)}) collective-permute-start(bf16[336,128]{1,0:T(8,128)(2,1)S(1)} %get-tuple-element.64), channel_id=1, source_target_pairs={{0,4},{1,5},{2,6},{3,7},{4,0},{5,1},{6,2},{7,3},{8,12},{9,13},{10,... | collective-permute-start | bytes 258056 | tf_op jit(solution)/shard_map/ppermute | solution.py:431
  7.8 1.0 collective-permute-start
  8.7 3.5 %collective-permute-start.1 = (bf16[528,128]{1,0:T(8,128)(2,1)S(1)}, bf16[528,128]{1,0:T(8,128)(2,1)S(1)}, u32[]{:S(2)}, u32[]{:S(2)}) collective-permute-start(bf16[528,128]{1,0:T(8,128)(2,1)S(1)} %get-tuple-element.61), channel_id=1, source_target_pairs={{0,4},{1,5},{2,6},{3,7},{4,0},{5,1},{6,2},{7,3},{8,12},{9,13},{10,... | collective-permute-start | bytes 405512 | tf_op jit(solution)/shard_map/ppermute | solution.py:431
  12.4 1.9 %collective-permute-done.4.refs_2_ = bf16[336,128]{1,0:T(8,128)(2,1)S(1)} collective-permute-done((bf16[336,128]{1,0:T(8,128)(2,1)S(1)}, bf16[336,128]{1,0:T(8,128)(2,1)S(1)}, u32[]{:S(2)}, u32[]{:S(2)}) %collective-permute-start.4) | collective-permute-done | bytes 86048 | tf_op jit(solution)/shard_map/ppermute | solution.py:431
  14.3 0.5 collective-permute-done.5.refs_3_
  14.8 1.6 %collective-permute-start.6 = (bf16[1088,128]{1,0:T(8,128)(2,1)S(1)}, bf16[1088,128]{1,0:T(8,128)(2,1)S(1)}, u32[]{:S(2)}, u32[]{:S(2)}) collective-permute-start(bf16[1088,128]{1,0:T(8,128)(2,1)S(1)} %relay.1.refs_4_), channel_id=1, source_target_pairs={{0,1},{1,0},{2,3},{3,2},{4,5},{5,4},{6,7},{7,6},{8,9},{9,8},{10,11... | collective-permute-start | bytes 835592 | tf_op jit(solution)/shard_map/ppermute | solution.py:435
  16.4 6.6 %collective-permute-start.11 = (bf16[512,128]{1,0:T(8,128)(2,1)S(1)}, bf16[512,128]{1,0:T(8,128)(2,1)S(1)}, u32[]{:S(2)}, u32[]{:S(2)}) collective-permute-start(bf16[512,128]{1,0:T(8,128)(2,1)S(1)} %get-tuple-element.75), channel_id=1, source_target_pairs={{0,2},{1,3},{2,0},{3,1},{4,6},{5,7},{6,4},{7,5},{8,10},{9,11},{10,... | collective-permute-start | bytes 393224 | tf_op jit(solution)/shard_map/ppermute | solution.py:431
  23.0 1.9 %collective-permute-start.12 = (bf16[512,128]{1,0:T(8,128)(2,1)S(1)}, bf16[512,128]{1,0:T(8,128)(2,1)S(1)}, u32[]{:S(2)}, u32[]{:S(2)}) collective-permute-start(bf16[512,128]{1,0:T(8,128)(2,1)S(1)} %get-tuple-element.76), channel_id=1, source_target_pairs={{0,4},{1,5},{2,6},{3,7},{4,0},{5,1},{6,2},{7,3},{8,12},{9,13},{10,... | collective-permute-start | bytes 393224 | tf_op jit(solution)/shard_map/ppermute | solution.py:431
  25.0 1.5 %collective-permute-done.1.refs_2_ = bf16[528,128]{1,0:T(8,128)(2,1)S(1)} collective-permute-done((bf16[528,128]{1,0:T(8,128)(2,1)S(1)}, bf16[528,128]{1,0:T(8,128)(2,1)S(1)}, u32[]{:S(2)}, u32[]{:S(2)}) %collective-permute-start.1) | collective-permute-done | bytes 135200 | tf_op jit(solution)/shard_map/ppermute | solution.py:431
  26.5 2.6 %collective-permute-start.13 = (bf16[512,128]{1,0:T(8,128)(2,1)S(1)}, bf16[512,128]{1,0:T(8,128)(2,1)S(1)}, u32[]{:S(2)}, u32[]{:S(2)}) collective-permute-start(bf16[512,128]{1,0:T(8,128)(2,1)S(1)} %get-tuple-element.77), channel_id=1, source_target_pairs={{0,6},{1,7},{2,4},{3,5},{4,2},{5,3},{6,0},{7,1},{8,14},{9,15},{10,... | collective-permute-start | bytes 393224 | tf_op jit(solution)/shard_map/ppermute | solution.py:431
  29.3 0.7 assemble.1
  30.0 0.6 project_saved.1
  30.6 1.6 %collective-permute-start.10 = (bf16[512,512]{1,0:T(8,128)(2,1)S(1)}, bf16[512,512]{1,0:T(8,128)(2,1)S(1)}, u32[]{:S(2)}, u32[]{:S(2)}) collective-permute-start(bf16[512,512]{1,0:T(8,128)(2,1)S(1)} %get-tuple-element.69.refs_1_.refs_0_), channel_id=1, source_target_pairs={{0,1},{1,0},{2,3},{3,2},{4,5},{5,4},{6,7},{7,6},{8,9},{9,8},{10,11... | collective-permute-start | bytes 1572872 | tf_op jit(solution)/shard_map/ppermute | solution.py:435
  32.4 5.1 %collective-permute-start.7 = (bf16[528,128]{1,0:T(8,128)(2,1)S(1)}, bf16[528,128]{1,0:T(8,128)(2,1)S(1)}, u32[]{:S(2)}, u32[]{:S(2)}) collective-permute-start(bf16[528,128]{1,0:T(8,128)(2,1)S(1)} %get-tuple-element.71), channel_id=1, source_target_pairs={{0,2},{1,3},{2,0},{3,1},{4,6},{5,7},{6,4},{7,5},{8,10},{9,11},{10,... | collective-permute-start | bytes 405512 | tf_op jit(solution)/shard_map/ppermute | solution.py:431
  37.9 2.6 %collective-permute-start.9 = (bf16[528,128]{1,0:T(8,128)(2,1)S(1)}, bf16[528,128]{1,0:T(8,128)(2,1)S(1)}, u32[]{:S(2)}, u32[]{:S(2)}) collective-permute-start(bf16[528,128]{1,0:T(8,128)(2,1)S(1)} %get-tuple-element.73), channel_id=1, source_target_pairs={{0,6},{1,7},{2,4},{3,5},{4,2},{5,3},{6,0},{7,1},{8,14},{9,15},{10,... | collective-permute-start | bytes 405512 | tf_op jit(solution)/shard_map/ppermute | solution.py:431
  40.6 1.6 %collective-permute-start.15 = (bf16[512,512]{1,0:T(8,128)(2,1)S(1)}, bf16[512,512]{1,0:T(8,128)(2,1)S(1)}, u32[]{:S(2)}, u32[]{:S(2)}) collective-permute-start(bf16[512,512]{1,0:T(8,128)(2,1)S(1)} %get-tuple-element.79.refs_3_.refs_0_), channel_id=1, source_target_pairs={{0,1},{1,0},{2,3},{3,2},{4,5},{5,4},{6,7},{7,6},{8,9},{9,8},{10,11... | collective-permute-start | bytes 1572872 | tf_op jit(solution)/shard_map/ppermute | solution.py:435
  42.2 2.4 %collective-permute-done.10.refs_1_ = bf16[512,512]{1,0:T(8,128)(2,1)S(1)} collective-permute-done((bf16[512,512]{1,0:T(8,128)(2,1)S(1)}, bf16[512,512]{1,0:T(8,128)(2,1)S(1)}, u32[]{:S(2)}, u32[]{:S(2)}) %collective-permute-start.10) | collective-permute-done | bytes 524320 | tf_op jit(solution)/shard_map/ppermute | solution.py:435
  45.0 2.9 %collective-permute-done.8.refs_2_.refs_4_ = bf16[528,128]{1,0:T(8,128)(2,1)S(1)} collective-permute-done((bf16[528,128]{1,0:T(8,128)(2,1)S(1)}, bf16[528,128]{1,0:T(8,128)(2,1)S(1)}, u32[]{:S(2)}, u32[]{:S(2)}) %collective-permute-start.8) | collective-permute-done | bytes 135200 | tf_op jit(solution)/shard_map/ppermute | solution.py:431
  48.1 0.6 project_act.1
  48.7 1.6 %collective-permute-start.14 = (bf16[512,512]{1,0:T(8,128)(2,1)S(1)}, bf16[512,512]{1,0:T(8,128)(2,1)S(1)}, u32[]{:S(2)}, u32[]{:S(2)}) collective-permute-start(bf16[512,512]{1,0:T(8,128)(2,1)S(1)} %get-tuple-element.81.refs_6_.refs_0_), channel_id=1, source_target_pairs={{0,1},{1,0},{2,3},{3,2},{4,5},{5,4},{6,7},{7,6},{8,9},{9,8},{10,11... | collective-permute-start | bytes 1572872 | tf_op jit(solution)/shard_map/ppermute | solution.py:435
  50.3 5.6 %collective-permute-done.15.refs_1_ = bf16[512,512]{1,0:T(8,128)(2,1)S(1)} collective-permute-done((bf16[512,512]{1,0:T(8,128)(2,1)S(1)}, bf16[512,512]{1,0:T(8,128)(2,1)S(1)}, u32[]{:S(2)}, u32[]{:S(2)}) %collective-permute-start.15) | collective-permute-done | bytes 524320 | tf_op jit(solution)/shard_map/ppermute | solution.py:435
  55.8 0.6 backward.1
  56.5 0.5 adj_norm.1
  57.0 0.5 weight_grad.1
  57.6 2.0 %collective-permute-start.23 = (bf16[272,512]{1,0:T(8,128)(2,1)S(1)}, bf16[272,512]{1,0:T(8,128)(2,1)S(1)}, u32[]{:S(2)}, u32[]{:S(2)}) collective-permute-start(bf16[272,512]{1,0:T(8,128)(2,1)S(1)} %get-tuple-element.101), channel_id=1, source_target_pairs={{0,1},{1,0},{2,3},{3,2},{4,5},{5,4},{6,7},{7,6},{8,9},{9,8},{10,11... | collective-permute-start | bytes 835592 | tf_op jit(solution)/shard_map/ppermute | solution.py:435
  59.5 2.6 %collective-permute-start.20 = (bf16[128,512]{1,0:T(8,128)(2,1)S(1)}, bf16[128,512]{1,0:T(8,128)(2,1)S(1)}, u32[]{:S(2)}, u32[]{:S(2)}) collective-permute-start(bf16[128,512]{1,0:T(8,128)(2,1)S(1)} %get-tuple-element.97), channel_id=1, source_target_pairs={{0,2},{1,3},{2,0},{3,1},{4,6},{5,7},{6,4},{7,5},{8,10},{9,11},{10,... | collective-permute-start | bytes 393224 | tf_op jit(solution)/shard_map/ppermute | solution.py:431
  62.1 1.2 %collective-permute-start.21 = (bf16[128,512]{1,0:T(8,128)(2,1)S(1)}, bf16[128,512]{1,0:T(8,128)(2,1)S(1)}, u32[]{:S(2)}, u32[]{:S(2)}) collective-permute-start(bf16[128,512]{1,0:T(8,128)(2,1)S(1)} %get-tuple-element.98), channel_id=1, source_target_pairs={{0,4},{1,5},{2,6},{3,7},{4,0},{5,1},{6,2},{7,3},{8,12},{9,13},{10,... | collective-permute-start | bytes 393224 | tf_op jit(solution)/shard_map/ppermute | solution.py:431
  63.3 1.5 %collective-permute-start.22 = (bf16[128,512]{1,0:T(8,128)(2,1)S(1)}, bf16[128,512]{1,0:T(8,128)(2,1)S(1)}, u32[]{:S(2)}, u32[]{:S(2)}) collective-permute-start(bf16[128,512]{1,0:T(8,128)(2,1)S(1)} %get-tuple-element.99), channel_id=1, source_target_pairs={{0,6},{1,7},{2,4},{3,5},{4,2},{5,3},{6,0},{7,1},{8,14},{9,15},{10,... | collective-permute-start | bytes 393224 | tf_op jit(solution)/shard_map/ppermute | solution.py:431
  64.8 2.1 %factor_grads.1 = (bf16[4,64,128]{2,1,0:T(8,128)(2,1)S(1)}, bf16[8,16,128]{2,1,0:T(8,128)(2,1)S(1)}) custom-call(bf16[4,256,512]{2,1,0:T(8,128)(2,1)S(1)} %get-tuple-element.82.refs_0_, bf16[4,256,512]{2,1,0:T(8,128)(2,1)S(1)} %get-tuple-element.84.refs_1_, bf16[512,512]{1,0:T(8,128)(2,1)S(1)} %get-tuple-element.85.refs_2_, ...), custom_call_target="tpu_custom_call" | custom-call | tf_op jit(solution)/shard_map/factor_grads/pallas_call | solution.py:61
  67.1 1.2 %mix_act.1 = (bf16[4,256,512]{2,1,0:T(8,128)(2,1)}, bf16[512,512]{1,0:T(8,128)(2,1)S(1)}) custom-call(bf16[512,512]{1,0:T(8,128)(2,1)S(1)} %get-tuple-element.81.refs_6_.refs_0_, bf16[512,512]{1,0:T(8,128)(2,1)S(1)} %collective-permute-done.14.refs_1_, bf16[4,256,256]{2,1,0:T(8,128)(2,1)S(1)} %get-tuple-element.74.refs_2_.refs_3_, ...), custom_call_target="tpu_custom_call" | custom-call | flops 2000000000 | tf_op jit(solution)/shard_map/mix_act/pallas_call | solution.py:61
  68.5 2.0 %collective-permute-done.23.refs_4_ = bf16[272,512]{1,0:T(8,128)(2,1)S(1)} collective-permute-done((bf16[272,512]{1,0:T(8,128)(2,1)S(1)}, bf16[272,512]{1,0:T(8,128)(2,1)S(1)}, u32[]{:S(2)}, u32[]{:S(2)}) %collective-permute-start.23) | collective-permute-done | bytes 278560 | tf_op jit(solution)/shard_map/ppermute | solution.py:435
  70.8 0.7 input_grad.1.refs_4_
  71.6 0.5 collective-permute-start.16
  72.1 3.5 %collective-permute-start.17 = (bf16[128,512]{1,0:T(8,128)(2,1)S(1)}, bf16[128,512]{1,0:T(8,128)(2,1)S(1)}, u32[]{:S(2)}, u32[]{:S(2)}) collective-permute-start(bf16[128,512]{1,0:T(8,128)(2,1)S(1)} %get-tuple-element.93), channel_id=1, source_target_pairs={{0,10},{1,11},{2,8},{3,9},{4,14},{5,15},{6,12},{7,13},{8,18},{9,19... | collective-permute-start | bytes 393224 | tf_op jit(solution)/shard_map/ppermute | solution.py:442
  75.6 1.0 %collective-permute-start.18 = (bf16[128,512]{1,0:T(8,128)(2,1)S(1)}, bf16[128,512]{1,0:T(8,128)(2,1)S(1)}, u32[]{:S(2)}, u32[]{:S(2)}) collective-permute-start(bf16[128,512]{1,0:T(8,128)(2,1)S(1)} %get-tuple-element.94), channel_id=1, source_target_pairs={{0,12},{1,13},{2,14},{3,15},{4,8},{5,9},{6,10},{7,11},{8,20},{9,21... | collective-permute-start | bytes 393224 | tf_op jit(solution)/shard_map/ppermute | solution.py:442
  76.7 1.3 %collective-permute-start.19 = (bf16[128,512]{1,0:T(8,128)(2,1)S(1)}, bf16[128,512]{1,0:T(8,128)(2,1)S(1)}, u32[]{:S(2)}, u32[]{:S(2)}) collective-permute-start(bf16[128,512]{1,0:T(8,128)(2,1)S(1)} %get-tuple-element.95), channel_id=1, source_target_pairs={{0,14},{1,15},{2,12},{3,13},{4,10},{5,11},{6,8},{7,9},{8,22},{9,23... | collective-permute-start | bytes 393224 | tf_op jit(solution)/shard_map/ppermute | solution.py:442
  78.0 0.5 collective-permute-done.16.refs_0_
  78.5 3.0 %collective-permute-start.25 = (bf16[352,128]{1,0:T(8,128)(2,1)S(1)}, bf16[352,128]{1,0:T(8,128)(2,1)S(1)}, u32[]{:S(2)}, u32[]{:S(2)}) collective-permute-start(bf16[352,128]{1,0:T(8,128)(2,1)S(1)} %get-tuple-element.103), channel_id=1, source_target_pairs={{0,2},{1,3},{2,0},{3,1},{4,6},{5,7},{6,4},{7,5},{8,10},{9,11},{10,... | collective-permute-start | bytes 270344 | tf_op jit(solution)/shard_map/ppermute | solution.py:431
  81.6 1.5 %collective-permute-start.26 = (bf16[352,128]{1,0:T(8,128)(2,1)S(1)}, bf16[352,128]{1,0:T(8,128)(2,1)S(1)}, u32[]{:S(2)}, u32[]{:S(2)}) collective-permute-start(bf16[352,128]{1,0:T(8,128)(2,1)S(1)} %get-tuple-element.104), channel_id=1, source_target_pairs={{0,4},{1,5},{2,6},{3,7},{4,0},{5,1},{6,2},{7,3},{8,12},{9,13},{10,... | collective-permute-start | bytes 270344 | tf_op jit(solution)/shard_map/ppermute | solution.py:431
  83.0 5.8 %collective-permute-done.18.refs_2_ = bf16[128,512]{1,0:T(8,128)(2,1)S(1)} collective-permute-done((bf16[128,512]{1,0:T(8,128)(2,1)S(1)}, bf16[128,512]{1,0:T(8,128)(2,1)S(1)}, u32[]{:S(2)}, u32[]{:S(2)}) %collective-permute-start.18) | collective-permute-done | bytes 131104 | tf_op jit(solution)/shard_map/ppermute | solution.py:442
  88.8 4.4 %collective-permute-start.27 = (bf16[352,128]{1,0:T(8,128)(2,1)S(1)}, bf16[352,128]{1,0:T(8,128)(2,1)S(1)}, u32[]{:S(2)}, u32[]{:S(2)}) collective-permute-start(bf16[352,128]{1,0:T(8,128)(2,1)S(1)} %get-tuple-element.105), channel_id=1, source_target_pairs={{0,6},{1,7},{2,4},{3,5},{4,2},{5,3},{6,0},{7,1},{8,14},{9,15},{10,... | collective-permute-start | bytes 270344 | tf_op jit(solution)/shard_map/ppermute | solution.py:431
  93.2 0.8 join_out.1.refs_4_
  94.1 2.8 %collective-permute-done.26.refs_2_ = bf16[352,128]{1,0:T(8,128)(2,1)S(1)} collective-permute-done((bf16[352,128]{1,0:T(8,128)(2,1)S(1)}, bf16[352,128]{1,0:T(8,128)(2,1)S(1)}, u32[]{:S(2)}, u32[]{:S(2)}) %collective-permute-start.26) | collective-permute-done | bytes 90144 | tf_op jit(solution)/shard_map/ppermute | solution.py:431
  96.9 1.0 %copy-done = bf16[128,2048]{1,0:T(8,128)(2,1)S(1)} copy-done((bf16[128,2048]{1,0:T(8,128)(2,1)S(1)}, bf16[128,2048]{1,0:T(8,128)(2,1)}, u32[]{:S(2)}) %copy-start) | copy-done | bytes 524312
  98.0 1.0 join_weight.1
  98.9 0.8 copy.17
  (46 shorter events, 3.0 us)
Async XLA Ops:
  0.6 1.1 %copy-start.4 = (bf16[1,2,64,64]{3,2,1,0:T(8,128)(2,1)S(1)}, bf16[1,2,64,64]{3,2,1,0:T(8,128)(2,1)}, u32[]{:S(2)}) copy-start(bf16[1,2,64,64]{3,2,1,0:T(8,128)(2,1)} %param.12) | copy-start | bytes 49156
  0.6 1.1 %copy-start.5 = (bf16[1,8,16,16]{3,2,1,0:T(8,128)(2,1)S(1)}, bf16[1,8,16,16]{3,2,1,0:T(8,128)(2,1)}, u32[]{:S(2)}) copy-start(bf16[1,8,16,16]{3,2,1,0:T(8,128)(2,1)} %param.13) | copy-start | bytes 12292
  0.7 6.9 %copy-start.2 = (bf16[1,128,2048]{2,1,0:T(8,128)(2,1)S(1)}, bf16[1,128,2048]{2,1,0:T(8,128)(2,1)}, u32[]{:S(2)}) copy-start(bf16[1,128,2048]{2,1,0:T(8,128)(2,1)} %param.8) | copy-start | bytes 1572868
  1.7 10.6 %copy-start.1 = (bf16[1,128,2048]{2,1,0:T(8,128)(2,1)S(1)}, bf16[1,128,2048]{2,1,0:T(8,128)(2,1)}, u32[]{:S(2)}) copy-start(bf16[1,128,2048]{2,1,0:T(8,128)(2,1)} %param.9) | copy-start | bytes 1572868
  1.8 10.4 %collective-permute-start.3 = (bf16[336,128]{1,0:T(8,128)(2,1)S(1)}, bf16[336,128]{1,0:T(8,128)(2,1)S(1)}, u32[]{:S(2)}, u32[]{:S(2)}) collective-permute-start(bf16[336,128]{1,0:T(8,128)(2,1)S(1)} %get-tuple-element.63), channel_id=1, source_target_pairs={{0,2},{1,3},{2,0},{3,1},{4,6},{5,7},{6,4},{7,5},{8,10},{9,11},{10,... | collective-permute-start | bytes 258056 | tf_op jit(solution)/shard_map/ppermute | solution.py:431
  4.9 9.4 %collective-permute-start.4 = (bf16[336,128]{1,0:T(8,128)(2,1)S(1)}, bf16[336,128]{1,0:T(8,128)(2,1)S(1)}, u32[]{:S(2)}, u32[]{:S(2)}) collective-permute-start(bf16[336,128]{1,0:T(8,128)(2,1)S(1)} %get-tuple-element.64), channel_id=1, source_target_pairs={{0,4},{1,5},{2,6},{3,7},{4,0},{5,1},{6,2},{7,3},{8,12},{9,13},{10,... | collective-permute-start | bytes 258056 | tf_op jit(solution)/shard_map/ppermute | solution.py:431
  7.5 7.3 %collective-permute-start.5 = (bf16[336,128]{1,0:T(8,128)(2,1)S(1)}, bf16[336,128]{1,0:T(8,128)(2,1)S(1)}, u32[]{:S(2)}, u32[]{:S(2)}) collective-permute-start(bf16[336,128]{1,0:T(8,128)(2,1)S(1)} %get-tuple-element.65), channel_id=1, source_target_pairs={{0,6},{1,7},{2,4},{3,5},{4,2},{5,3},{6,0},{7,1},{8,14},{9,15},{10,... | collective-permute-start | bytes 258056 | tf_op jit(solution)/shard_map/ppermute | solution.py:431
  7.8 15.3 %collective-permute-start = (bf16[528,128]{1,0:T(8,128)(2,1)S(1)}, bf16[528,128]{1,0:T(8,128)(2,1)S(1)}, u32[]{:S(2)}, u32[]{:S(2)}) collective-permute-start(bf16[528,128]{1,0:T(8,128)(2,1)S(1)} %get-tuple-element.60), channel_id=1, source_target_pairs={{0,2},{1,3},{2,0},{3,1},{4,6},{5,7},{6,4},{7,5},{8,10},{9,11},{10,... | collective-permute-start | bytes 405512 | tf_op jit(solution)/shard_map/ppermute | solution.py:431
  8.7 17.7 %collective-permute-start.1 = (bf16[528,128]{1,0:T(8,128)(2,1)S(1)}, bf16[528,128]{1,0:T(8,128)(2,1)S(1)}, u32[]{:S(2)}, u32[]{:S(2)}) collective-permute-start(bf16[528,128]{1,0:T(8,128)(2,1)S(1)} %get-tuple-element.61), channel_id=1, source_target_pairs={{0,4},{1,5},{2,6},{3,7},{4,0},{5,1},{6,2},{7,3},{8,12},{9,13},{10,... | collective-permute-start | bytes 405512 | tf_op jit(solution)/shard_map/ppermute | solution.py:431
  12.2 16.9 %collective-permute-start.2 = (bf16[528,128]{1,0:T(8,128)(2,1)S(1)}, bf16[528,128]{1,0:T(8,128)(2,1)S(1)}, u32[]{:S(2)}, u32[]{:S(2)}) collective-permute-start(bf16[528,128]{1,0:T(8,128)(2,1)S(1)} %get-tuple-element.62), channel_id=1, source_target_pairs={{0,6},{1,7},{2,4},{3,5},{4,2},{5,3},{6,0},{7,1},{8,14},{9,15},{10,... | collective-permute-start | bytes 405512 | tf_op jit(solution)/shard_map/ppermute | solution.py:431
  14.8 14.3 %copy-start.6 = (f32[1,2048]{1,0:T(1,128)S(1)}, f32[1,2048]{1,0:T(1,128)}, u32[]{:S(2)}) copy-start(f32[1,2048]{1,0:T(1,128)} %refs_2_.1) | copy-start | bytes 24580
  14.8 14.5 %collective-permute-start.6 = (bf16[1088,128]{1,0:T(8,128)(2,1)S(1)}, bf16[1088,128]{1,0:T(8,128)(2,1)S(1)}, u32[]{:S(2)}, u32[]{:S(2)}) collective-permute-start(bf16[1088,128]{1,0:T(8,128)(2,1)S(1)} %relay.1.refs_4_), channel_id=1, source_target_pairs={{0,1},{1,0},{2,3},{3,2},{4,5},{5,4},{6,7},{7,6},{8,9},{9,8},{10,11... | collective-permute-start | bytes 835592 | tf_op jit(solution)/shard_map/ppermute | solution.py:435
  16.4 21.1 %collective-permute-start.11 = (bf16[512,128]{1,0:T(8,128)(2,1)S(1)}, bf16[512,128]{1,0:T(8,128)(2,1)S(1)}, u32[]{:S(2)}, u32[]{:S(2)}) collective-permute-start(bf16[512,128]{1,0:T(8,128)(2,1)S(1)} %get-tuple-element.75), channel_id=1, source_target_pairs={{0,2},{1,3},{2,0},{3,1},{4,6},{5,7},{6,4},{7,5},{8,10},{9,11},{10,... | collective-permute-start | bytes 393224 | tf_op jit(solution)/shard_map/ppermute | solution.py:431
  23.0 14.9 %collective-permute-start.12 = (bf16[512,128]{1,0:T(8,128)(2,1)S(1)}, bf16[512,128]{1,0:T(8,128)(2,1)S(1)}, u32[]{:S(2)}, u32[]{:S(2)}) collective-permute-start(bf16[512,128]{1,0:T(8,128)(2,1)S(1)} %get-tuple-element.76), channel_id=1, source_target_pairs={{0,4},{1,5},{2,6},{3,7},{4,0},{5,1},{6,2},{7,3},{8,12},{9,13},{10,... | collective-permute-start | bytes 393224 | tf_op jit(solution)/shard_map/ppermute | solution.py:431
  26.5 14.0 %collective-permute-start.13 = (bf16[512,128]{1,0:T(8,128)(2,1)S(1)}, bf16[512,128]{1,0:T(8,128)(2,1)S(1)}, u32[]{:S(2)}, u32[]{:S(2)}) collective-permute-start(bf16[512,128]{1,0:T(8,128)(2,1)S(1)} %get-tuple-element.77), channel_id=1, source_target_pairs={{0,6},{1,7},{2,4},{3,5},{4,2},{5,3},{6,0},{7,1},{8,14},{9,15},{10,... | collective-permute-start | bytes 393224 | tf_op jit(solution)/shard_map/ppermute | solution.py:431
  30.0 2.2 %copy-start.3 = (bf16[1,128,2048]{2,1,0:T(8,128)(2,1)S(1)}, bf16[1,128,2048]{2,1,0:T(8,128)(2,1)}, u32[]{:S(2)}) copy-start(bf16[1,128,2048]{2,1,0:T(8,128)(2,1)} %param.7) | copy-start | bytes 1572868
  30.6 14.0 %collective-permute-start.10 = (bf16[512,512]{1,0:T(8,128)(2,1)S(1)}, bf16[512,512]{1,0:T(8,128)(2,1)S(1)}, u32[]{:S(2)}, u32[]{:S(2)}) collective-permute-start(bf16[512,512]{1,0:T(8,128)(2,1)S(1)} %get-tuple-element.69.refs_1_.refs_0_), channel_id=1, source_target_pairs={{0,1},{1,0},{2,3},{3,2},{4,5},{5,4},{6,7},{7,6},{8,9},{9,8},{10,11... | collective-permute-start | bytes 1572872 | tf_op jit(solution)/shard_map/ppermute | solution.py:435
  32.4 12.6 %collective-permute-start.7 = (bf16[528,128]{1,0:T(8,128)(2,1)S(1)}, bf16[528,128]{1,0:T(8,128)(2,1)S(1)}, u32[]{:S(2)}, u32[]{:S(2)}) collective-permute-start(bf16[528,128]{1,0:T(8,128)(2,1)S(1)} %get-tuple-element.71), channel_id=1, source_target_pairs={{0,2},{1,3},{2,0},{3,1},{4,6},{5,7},{6,4},{7,5},{8,10},{9,11},{10,... | collective-permute-start | bytes 405512 | tf_op jit(solution)/shard_map/ppermute | solution.py:431
  37.5 10.4 %collective-permute-start.8 = (bf16[528,128]{1,0:T(8,128)(2,1)S(1)}, bf16[528,128]{1,0:T(8,128)(2,1)S(1)}, u32[]{:S(2)}, u32[]{:S(2)}) collective-permute-start(bf16[528,128]{1,0:T(8,128)(2,1)S(1)} %get-tuple-element.72), channel_id=1, source_target_pairs={{0,4},{1,5},{2,6},{3,7},{4,0},{5,1},{6,2},{7,3},{8,12},{9,13},{10,... | collective-permute-start | bytes 405512 | tf_op jit(solution)/shard_map/ppermute | solution.py:431
  37.9 10.0 %collective-permute-start.9 = (bf16[528,128]{1,0:T(8,128)(2,1)S(1)}, bf16[528,128]{1,0:T(8,128)(2,1)S(1)}, u32[]{:S(2)}, u32[]{:S(2)}) collective-permute-start(bf16[528,128]{1,0:T(8,128)(2,1)S(1)} %get-tuple-element.73), channel_id=1, source_target_pairs={{0,6},{1,7},{2,4},{3,5},{4,2},{5,3},{6,0},{7,1},{8,14},{9,15},{10,... | collective-permute-start | bytes 405512 | tf_op jit(solution)/shard_map/ppermute | solution.py:431
  40.6 15.2 %collective-permute-start.15 = (bf16[512,512]{1,0:T(8,128)(2,1)S(1)}, bf16[512,512]{1,0:T(8,128)(2,1)S(1)}, u32[]{:S(2)}, u32[]{:S(2)}) collective-permute-start(bf16[512,512]{1,0:T(8,128)(2,1)S(1)} %get-tuple-element.79.refs_3_.refs_0_), channel_id=1, source_target_pairs={{0,1},{1,0},{2,3},{3,2},{4,5},{5,4},{6,7},{7,6},{8,9},{9,8},{10,11... | collective-permute-start | bytes 1572872 | tf_op jit(solution)/shard_map/ppermute | solution.py:435
  48.7 18.4 %collective-permute-start.14 = (bf16[512,512]{1,0:T(8,128)(2,1)S(1)}, bf16[512,512]{1,0:T(8,128)(2,1)S(1)}, u32[]{:S(2)}, u32[]{:S(2)}) collective-permute-start(bf16[512,512]{1,0:T(8,128)(2,1)S(1)} %get-tuple-element.81.refs_6_.refs_0_), channel_id=1, source_target_pairs={{0,1},{1,0},{2,3},{3,2},{4,5},{5,4},{6,7},{7,6},{8,9},{9,8},{10,11... | collective-permute-start | bytes 1572872 | tf_op jit(solution)/shard_map/ppermute | solution.py:435
  57.6 12.9 %collective-permute-start.23 = (bf16[272,512]{1,0:T(8,128)(2,1)S(1)}, bf16[272,512]{1,0:T(8,128)(2,1)S(1)}, u32[]{:S(2)}, u32[]{:S(2)}) collective-permute-start(bf16[272,512]{1,0:T(8,128)(2,1)S(1)} %get-tuple-element.101), channel_id=1, source_target_pairs={{0,1},{1,0},{2,3},{3,2},{4,5},{5,4},{6,7},{7,6},{8,9},{9,8},{10,11... | collective-permute-start | bytes 835592 | tf_op jit(solution)/shard_map/ppermute | solution.py:435
  59.5 11.1 %collective-permute-start.20 = (bf16[128,512]{1,0:T(8,128)(2,1)S(1)}, bf16[128,512]{1,0:T(8,128)(2,1)S(1)}, u32[]{:S(2)}, u32[]{:S(2)}) collective-permute-start(bf16[128,512]{1,0:T(8,128)(2,1)S(1)} %get-tuple-element.97), channel_id=1, source_target_pairs={{0,2},{1,3},{2,0},{3,1},{4,6},{5,7},{6,4},{7,5},{8,10},{9,11},{10,... | collective-permute-start | bytes 393224 | tf_op jit(solution)/shard_map/ppermute | solution.py:431
  62.1 8.7 %collective-permute-start.21 = (bf16[128,512]{1,0:T(8,128)(2,1)S(1)}, bf16[128,512]{1,0:T(8,128)(2,1)S(1)}, u32[]{:S(2)}, u32[]{:S(2)}) collective-permute-start(bf16[128,512]{1,0:T(8,128)(2,1)S(1)} %get-tuple-element.98), channel_id=1, source_target_pairs={{0,4},{1,5},{2,6},{3,7},{4,0},{5,1},{6,2},{7,3},{8,12},{9,13},{10,... | collective-permute-start | bytes 393224 | tf_op jit(solution)/shard_map/ppermute | solution.py:431
  63.3 7.5 %collective-permute-start.22 = (bf16[128,512]{1,0:T(8,128)(2,1)S(1)}, bf16[128,512]{1,0:T(8,128)(2,1)S(1)}, u32[]{:S(2)}, u32[]{:S(2)}) collective-permute-start(bf16[128,512]{1,0:T(8,128)(2,1)S(1)} %get-tuple-element.99), channel_id=1, source_target_pairs={{0,6},{1,7},{2,4},{3,5},{4,2},{5,3},{6,0},{7,1},{8,14},{9,15},{10,... | collective-permute-start | bytes 393224 | tf_op jit(solution)/shard_map/ppermute | solution.py:431
  71.5 27.4 %collective-permute-start.24 = (bf16[128,2048]{1,0:T(8,128)(2,1)S(1)}, bf16[128,2048]{1,0:T(8,128)(2,1)S(1)}, u32[]{:S(2)}, u32[]{:S(2)}) collective-permute-start(bf16[128,2048]{1,0:T(8,128)(2,1)S(1)} %input_grad.1.refs_4_), channel_id=1, source_target_pairs={{0,24},{8,0},{16,8},{24,16},{1,25},{9,1},{17,9},{25,17},{2,26},{10... | collective-permute-start | bytes 1572872 | tf_op jit(solution)/shard_map/ppermute | solution.py:531
  71.6 6.9 %collective-permute-start.16 = (bf16[128,512]{1,0:T(8,128)(2,1)S(1)}, bf16[128,512]{1,0:T(8,128)(2,1)S(1)}, u32[]{:S(2)}, u32[]{:S(2)}) collective-permute-start(bf16[128,512]{1,0:T(8,128)(2,1)S(1)} %get-tuple-element.92.refs_5_), channel_id=1, source_target_pairs={{0,8},{1,9},{2,10},{3,11},{4,12},{5,13},{6,14},{7,15},{8,16},{9,17... | collective-permute-start | bytes 393224 | tf_op jit(solution)/shard_map/ppermute | solution.py:442
  72.1 9.5 %collective-permute-start.17 = (bf16[128,512]{1,0:T(8,128)(2,1)S(1)}, bf16[128,512]{1,0:T(8,128)(2,1)S(1)}, u32[]{:S(2)}, u32[]{:S(2)}) collective-permute-start(bf16[128,512]{1,0:T(8,128)(2,1)S(1)} %get-tuple-element.93), channel_id=1, source_target_pairs={{0,10},{1,11},{2,8},{3,9},{4,14},{5,15},{6,12},{7,13},{8,18},{9,19... | collective-permute-start | bytes 393224 | tf_op jit(solution)/shard_map/ppermute | solution.py:442
  75.6 13.2 %collective-permute-start.18 = (bf16[128,512]{1,0:T(8,128)(2,1)S(1)}, bf16[128,512]{1,0:T(8,128)(2,1)S(1)}, u32[]{:S(2)}, u32[]{:S(2)}) collective-permute-start(bf16[128,512]{1,0:T(8,128)(2,1)S(1)} %get-tuple-element.94), channel_id=1, source_target_pairs={{0,12},{1,13},{2,14},{3,15},{4,8},{5,9},{6,10},{7,11},{8,20},{9,21... | collective-permute-start | bytes 393224 | tf_op jit(solution)/shard_map/ppermute | solution.py:442
  76.7 16.6 %collective-permute-start.19 = (bf16[128,512]{1,0:T(8,128)(2,1)S(1)}, bf16[128,512]{1,0:T(8,128)(2,1)S(1)}, u32[]{:S(2)}, u32[]{:S(2)}) collective-permute-start(bf16[128,512]{1,0:T(8,128)(2,1)S(1)} %get-tuple-element.95), channel_id=1, source_target_pairs={{0,14},{1,15},{2,12},{3,13},{4,10},{5,11},{6,8},{7,9},{8,22},{9,23... | collective-permute-start | bytes 393224 | tf_op jit(solution)/shard_map/ppermute | solution.py:442
  78.5 15.6 %collective-permute-start.25 = (bf16[352,128]{1,0:T(8,128)(2,1)S(1)}, bf16[352,128]{1,0:T(8,128)(2,1)S(1)}, u32[]{:S(2)}, u32[]{:S(2)}) collective-permute-start(bf16[352,128]{1,0:T(8,128)(2,1)S(1)} %get-tuple-element.103), channel_id=1, source_target_pairs={{0,2},{1,3},{2,0},{3,1},{4,6},{5,7},{6,4},{7,5},{8,10},{9,11},{10,... | collective-permute-start | bytes 270344 | tf_op jit(solution)/shard_map/ppermute | solution.py:431
  81.6 15.3 %collective-permute-start.26 = (bf16[352,128]{1,0:T(8,128)(2,1)S(1)}, bf16[352,128]{1,0:T(8,128)(2,1)S(1)}, u32[]{:S(2)}, u32[]{:S(2)}) collective-permute-start(bf16[352,128]{1,0:T(8,128)(2,1)S(1)} %get-tuple-element.104), channel_id=1, source_target_pairs={{0,4},{1,5},{2,6},{3,7},{4,0},{5,1},{6,2},{7,3},{8,12},{9,13},{10,... | collective-permute-start | bytes 270344 | tf_op jit(solution)/shard_map/ppermute | solution.py:431
  88.8 8.1 %collective-permute-start.27 = (bf16[352,128]{1,0:T(8,128)(2,1)S(1)}, bf16[352,128]{1,0:T(8,128)(2,1)S(1)}, u32[]{:S(2)}, u32[]{:S(2)}) collective-permute-start(bf16[352,128]{1,0:T(8,128)(2,1)S(1)} %get-tuple-element.105), channel_id=1, source_target_pairs={{0,6},{1,7},{2,4},{3,5},{4,2},{5,3},{6,0},{7,1},{8,14},{9,15},{10,... | collective-permute-start | bytes 270344 | tf_op jit(solution)/shard_map/ppermute | solution.py:431
  96.9 1.0 %copy-start = (bf16[128,2048]{1,0:T(8,128)(2,1)S(1)}, bf16[128,2048]{1,0:T(8,128)(2,1)}, u32[]{:S(2)}) copy-start(bf16[128,2048]{1,0:T(8,128)(2,1)} %join_out.1.refs_4_) | copy-start | bytes 1572868

commit v3 on v2

v3 whole, which is shorter than its diff:
```python
import functools

import jax
import jax.numpy as jnp
from jax import lax
from jax.experimental import pallas as pl
from jax.experimental.pallas import tpu as pltpu
from jax.sharding import PartitionSpec as P

BF = jnp.bfloat16
F32 = jnp.float32
LANE = 128
SUB = 16
EPS = 1e-06
COST = {"norm_act": 3.0, "norm_saved": 6.0, "mix_act": 1.0, "take_grad": 8.0, "join_out": 2.0}
VMEM = 48 * 1024 * 1024


def position(ngroups):
    me = lax.axis_index("seq")
    return me % ngroups, me // ngroups


def far(d, nb):
    return (nb - d) % nb


def natural(pos, nb, ngroups, na):
    return ((pos // na % nb) * ngroups + pos // (nb * na)) * na + pos % na


def split3(x):
    hi = x.astype(BF).astype(F32)
    mid = (x - hi).astype(BF).astype(F32)
    return hi, mid, x - hi - mid


def eye(n):
    return lax.broadcasted_iota(jnp.int32, (n, n), 0) == lax.broadcasted_iota(jnp.int32, (n, n), 1)


def to_row(col):
    return jnp.sum(jnp.where(eye(col.shape[0]), col, 0.0), axis=0, keepdims=True)


def to_col(row):
    return jnp.sum(jnp.where(eye(row.shape[1]), row, 0.0), axis=1, keepdims=True)


def mm(a, b, ca=1, cb=0):
    return lax.dot_general(a, b, (((ca,), (cb,)), ((), ())), preferred_element_type=F32)


def rows(start, size):
    return pl.ds(pl.multiple_of(start, size), size)


def call(body, outs, scratch, direct, name):
    def run(*args, after=()):
        nin, nwait = len(args), len(after)
        vmem, anywhere = pl.BlockSpec(memory_space=pltpu.VMEM), pl.BlockSpec(memory_space=pl.ANY)

        def without_waits(*refs):
            return body(*refs[:nin], *refs[nin + nwait :])

        return pl.pallas_call(
            without_waits,
            out_shape=list(outs),
            in_specs=[anywhere] * direct + [vmem] * (nin - direct) + [anywhere] * nwait,
            out_specs=[anywhere] * direct + [vmem] * (len(outs) - direct),
            scratch_shapes=list(scratch),
            compiler_params=pltpu.CompilerParams(vmem_limit_bytes=VMEM),
            cost_estimate=pl.CostEstimate(
                flops=int(COST.get(name, 0.0) * 1e9), bytes_accessed=0, transcendentals=0
            ),
            name=name,
        )(*args, *after)

    return run


def sds(shape, dtype=BF):
    return jax.ShapeDtypeStruct(shape, dtype)


def pack_weight_body(nb, ngroups, w_ref, l_ref, r_ref, *outs):
    _, block = position(ngroups)
    r, bd = w_ref.shape[1], w_ref.shape[2]
    chunks = bd // LANE
    bl, ext = l_ref.shape[1], r_ref.shape[1]
    left = jnp.concatenate([l_ref[j].astype(F32) for j in range(l_ref.shape[0])], axis=1).astype(BF)
    right = jnp.concatenate([r_ref[j].astype(F32) for j in range(r_ref.shape[0])], axis=1).astype(BF)
    for d in range(nb):
        for ch in range(chunks):
            outs[d][ch * r : (ch + 1) * r, :] = w_ref[block ^ far(d, nb), :, ch * LANE : (ch + 1) * LANE]
        outs[d][chunks * r : chunks * r + bl, :] = left
        outs[d][chunks * r + bl :, :] = right


def pack_tokens_body(nb, ngroups, with_scale, x_ref, *outs):
    _, block = position(ngroups)
    t, width = x_ref.shape
    bd = width // nb
    chunks = bd // LANE
    if with_scale:
        x = x_ref[...].astype(F32)
        inv = lax.rsqrt(jnp.mean(x * x, axis=-1, keepdims=True) + EPS)
        parts = split3(to_row(inv))
        tile = jnp.concatenate(list(parts) + [jnp.zeros((SUB - 3, t), F32)], axis=0).astype(BF)
    for d in range(nb):
        for ch in range(chunks):
            lanes = pl.ds(pl.multiple_of((block ^ far(d, nb)) * bd + ch * LANE, LANE), LANE)
            outs[d][ch * t : (ch + 1) * t, :] = x_ref[:, lanes]
        if with_scale:
            outs[d][chunks * t :, :] = tile


def pick(n, part_of, part):
    row = lax.broadcasted_iota(jnp.int32, (n, part_of), 0)
    col = lax.broadcasted_iota(jnp.int32, (n, part_of), 1)
    return jnp.where(row == part * part_of + col, 1.0, 0.0).astype(BF)


def split_features_body(nb, ngroups, x_ref, *outs):
    group, _ = position(ngroups)
    part_of = outs[0].shape[2]
    bd = x_ref.shape[1] // nb
    for e in range(ngroups):
        take = pick(bd, part_of, group ^ e)
        for k in range(nb):
            outs[e][k] = mm(x_ref[:, k * bd : (k + 1) * bd], take).astype(BF)


def pack_shares_body(nb, ngroups, *refs):
    group, place = position(ngroups)
    shares, outs = refs[:ngroups], refs[ngroups:]
    t = shares[0].shape[1]
    for d in range(nb):
        for e in range(ngroups):
            outs[d][rows((group ^ e) * t, t), :] = shares[e][place ^ far(d, nb)]


def relay_body(nb, ngroups, r4, ext, *refs):
    _, place = position(ngroups)
    out = refs[nb]
    bl = refs[0].shape[0] - r4 - ext
    for d in range(nb):
        to = place ^ far(d, nb)
        out[rows(to * r4, r4), :] = refs[d][:r4, :]
        out[pl.ds(pl.multiple_of(nb * r4 + to * ext, ext), ext), :] = refs[d][r4 + bl :, :]
        out[pl.ds(pl.multiple_of(nb * (r4 + ext) + to * bl, bl), bl), :] = refs[d][r4 : r4 + bl, :]


def expand_matrix(ext, nb, ngroups, na):
    n = SUB * ext
    row = lax.broadcasted_iota(jnp.int32, (n, n), 0)
    col = lax.broadcasted_iota(jnp.int32, (n, n), 1)
    return jnp.where((row // ext == col % SUB) & (row % ext == natural(col // SUB, nb, ngroups, na)), 1.0, 0.0).astype(BF)


def same_position(n):
    row = lax.broadcasted_iota(jnp.int32, (n, n), 0)
    col = lax.broadcasted_iota(jnp.int32, (n, n), 1)
    return row % SUB == col % SUB


def assemble_body(nb, ngroups, r, ext, bl, *refs):
    group, _ = position(ngroups)
    na = LANE // bl
    relays = refs[:ngroups]
    wk_ref, mq_ref, bd_ref, all_ref = refs[ngroups:]
    chunks = wk_ref.shape[1] // LANE
    r4 = chunks * r
    for e in range(ngroups):
        g = group ^ e
        for c in range(nb):
            for ch in range(chunks):
                wk_ref[rows((c * ngroups + g) * r, r), ch * LANE : (ch + 1) * LANE] = relays[e][
                    c * r4 + ch * r : c * r4 + (ch + 1) * r, :
                ]
            all_ref[c * ngroups + g] = relays[e][nb * r4 + c * ext : nb * r4 + (c + 1) * ext, :]
    nq = mq_ref.shape[0]
    per = nb * ngroups // nq
    n = SUB * ext
    turn = expand_matrix(ext, nb, ngroups, na)
    spread = jnp.where(
        natural(lax.broadcasted_iota(jnp.int32, (n, ext), 0) // SUB, nb, ngroups, na)
        == lax.broadcasted_iota(jnp.int32, (n, ext), 1),
        1.0,
        0.0,
    ).astype(BF)
    same = same_position(n)
    for q in range(nq):
        tiles = jnp.concatenate([all_ref[q * per + i] for i in range(per)], axis=1)
        wide = mm(tiles, turn).astype(BF)
        mq_ref[q] = jnp.where(same, mm(spread, wide), 0.0).astype(BF)
    half_row = lax.broadcasted_iota(jnp.int32, (LANE, LANE), 0) // bl
    half_col = lax.broadcasted_iota(jnp.int32, (LANE, LANE), 1) // bl
    for e in range(ngroups):
        for c in range(nb):
            at = nb * (r4 + ext) + c * bl
            both = jnp.concatenate([relays[e][at : at + bl, :].astype(F32)] * na, axis=0)
            bd_ref[(group ^ e) * nb + c] = jnp.where(half_row == half_col, both, 0.0).astype(BF)


def unpack(msg, t, chunks):
    return jnp.concatenate([msg[ch * t : (ch + 1) * t, :] for ch in range(chunks)], axis=1)


def scale_of(msg, t, chunks):
    tile = msg[chunks * t : chunks * t + SUB, :].astype(F32)
    return to_col(tile[0:1] + tile[1:2] + tile[2:3])


def norm_body(nb, ngroups, *refs):
    _, place = position(ngroups)
    msgs = refs[:nb]
    gain_ref, normin_ref = refs[nb:]
    t = LANE
    bd = normin_ref.shape[1]
    chunks = bd // LANE
    gain = gain_ref[:, pl.ds(pl.multiple_of(place * bd, LANE), bd)]
    for d in range(nb):
        x = unpack(msgs[d], t, chunks).astype(F32)
        normed = x * scale_of(msgs[d], t, chunks)
        normin_ref[rows((place ^ far(d, nb)) * t, t), :] = (normed * gain).astype(BF)


def project_body(nb, ngroups, normin_ref, wk_ref, bd_ref, proj_ref, first_ref):
    group, _ = position(ngroups)
    t = LANE
    proj_ref[...] = mm(normin_ref[...], wk_ref[...]).astype(BF)
    for c in range(nb):
        at = slice(c * t, (c + 1) * t)
        first_ref[at, :] = mm(bd_ref[group * nb + c], proj_ref[at, :]).astype(BF)


def project_shares_body(ngroups, normin_ref, wk_ref, *outs):
    group, _ = position(ngroups)
    bd = wk_ref.shape[0]
    proj = mm(normin_ref[...], wk_ref[...]).astype(BF)
    for e in range(ngroups):
        outs[e][...] = mm(proj, pick(bd, bd // ngroups, group ^ e)).astype(BF)


def gather_positions(group, bl, parts, out_ref):
    blocks = parts[0].shape[0] // bl
    for e, part in enumerate(parts):
        base = (group ^ e) * blocks * SUB
        for q in range(bl // SUB):
            for a in range(blocks):
                out_ref[q, pl.ds(pl.multiple_of(base + a * SUB, SUB), SUB), :] = part[
                    a * bl + q * SUB : a * bl + (q + 1) * SUB, :
                ]


def mix_body(ngroups, bl, *refs):
    group, _ = position(ngroups)
    firsts = refs[:ngroups]
    mq_ref, mixed_ref, f_ref = refs[ngroups:]
    gather_positions(group, bl, firsts, f_ref)
    blocks = firsts[0].shape[0] // bl
    own = rows(group * blocks * SUB, blocks * SUB)
    for q in range(bl // SUB):
        mixed = mm(mq_ref[q, own, :], f_ref[q]).astype(BF)
        for a in range(blocks):
            mixed_ref[a * bl + q * SUB : a * bl + (q + 1) * SUB, :] = mixed[a * SUB : (a + 1) * SUB, :]


def output_body(nb, ngroups, mixed_ref, proj_ref, *refs):
    _, place = position(ngroups)
    msgs, outs = refs[:nb], refs[nb:]
    t = LANE
    chunks = proj_ref.shape[1] // LANE
    for d in range(nb):
        at = rows((place ^ far(d, nb)) * t, t)
        x = unpack(msgs[d], t, chunks).astype(F32)
        outs[d][...] = (x + proj_ref[at, :].astype(F32) * mixed_ref[at, :].astype(F32)).astype(BF)


def to_positions(x_ref, out_ref, bl):
    for q in range(bl // SUB):
        for a in range(x_ref.shape[0] // bl):
            out_ref[q, a * SUB : (a + 1) * SUB, :] = x_ref[a * bl + q * SUB : a * bl + (q + 1) * SUB, :]


def from_positions(x, q, out_ref, bl):
    for a in range(out_ref.shape[0] // bl):
        out_ref[a * bl + q * SUB : a * bl + (q + 1) * SUB, :] = x[a * SUB : (a + 1) * SUB, :]


def mix_shares_body(ngroups, bl, *refs):
    group, _ = position(ngroups)
    parts = refs[:ngroups]
    mq_ref, bd_ref, proj_ref, f_ref, mixed_ref, first_ref = refs[ngroups:]
    t = LANE
    tg = parts[0].shape[0]
    for e in range(ngroups):
        proj_ref[rows((group ^ e) * tg, tg), :] = parts[e][...]
    for c in range(bd_ref.shape[0]):
        at = slice(c * t, (c + 1) * t)
        first_ref[at, :] = mm(bd_ref[c], proj_ref[at, :]).astype(BF)
    to_positions(first_ref, f_ref, bl)
    for q in range(bl // SUB):
        from_positions(mm(mq_ref[q], f_ref[q]).astype(BF), q, mixed_ref, bl)


def take_grad_body(nb, ngroups, *refs):
    _, place = position(ngroups)
    grad_ref = refs[nb]
    t = LANE
    for d in range(nb):
        for g in range(ngroups):
            grad_ref[rows((g * nb + (place ^ far(d, nb))) * t, t), :] = refs[d][g * t : (g + 1) * t, :]


def backward_body(nb, ngroups, bl, *refs):
    group, _ = position(ngroups)
    grad_ref, proj_ref, mixed_ref, mq_ref, bd_ref = refs[:5]
    outs = refs[5 : 5 + ngroups]
    a_ref, adj_first_ref, adj_ref = refs[5 + ngroups :]
    t = LANE
    adj_ref[...] = (grad_ref[...].astype(F32) * proj_ref[...].astype(F32)).astype(BF)
    to_positions(adj_ref, a_ref, bl)
    for q in range(bl // SUB):
        from_positions(mm(mq_ref[q], a_ref[q], 0, 0).astype(BF), q, adj_first_ref, bl)
    for c in range(bd_ref.shape[0]):
        at = slice(c * t, (c + 1) * t)
        grad = grad_ref[at, :].astype(F32)
        mixed = mixed_ref[at, :].astype(F32)
        adj_ref[at, :] = (grad * mixed + mm(bd_ref[c], adj_first_ref[at, :], 0, 0)).astype(BF)
    tg = nb * t
    for e in range(ngroups):
        outs[e][...] = adj_ref[rows((group ^ e) * tg, tg), :]


def factor_grads_body(nb, ngroups, bl, ext, f_ref, a_ref, adj_first_ref, proj_ref, *refs):
    group, _ = position(ngroups)
    outs, right_ref, left_ref = refs[:ngroups], refs[ngroups], refs[ngroups + 1]
    na = LANE // bl
    t = LANE
    nq = f_ref.shape[0]
    n = SUB * ext
    upper = lax.broadcasted_iota(jnp.int32, (bl, LANE), 1) < bl
    for g in range(ngroups):
        for c in range(nb):
            at = slice((g * nb + c) * t, (g * nb + c + 1) * t)
            both = mm(adj_first_ref[at, :], proj_ref[at, :], 1, 1)
            left_ref[g, c * bl : (c + 1) * bl, :] = jnp.where(upper, both[:bl, :], both[bl:, :]).astype(BF)
    turn = expand_matrix(ext, nb, ngroups, na)
    same = same_position(n)
    order = jnp.where(
        natural(lax.broadcasted_iota(jnp.int32, (ext, ext), 0), nb, ngroups, na)
        == lax.broadcasted_iota(jnp.int32, (ext, ext), 1),
        1.0,
        0.0,
    ).astype(BF)
    per = nb * ngroups // nq
    for q in range(nq):
        pairs = jnp.where(same, mm(a_ref[q], f_ref[q], 1, 1), 0.0)
        summed = jnp.sum(pairs.reshape(ext, SUB, n), axis=1).astype(BF)
        turned = mm(order, mm(summed, turn, 1, 1).astype(BF), 0, 0).astype(BF)
        for i in range(per):
            s = q * per + i
            right_ref[s % ngroups, (s // ngroups) * ext : (s // ngroups + 1) * ext, :] = turned[
                :, i * LANE : (i + 1) * LANE
            ]
    for e in range(ngroups):
        outs[e][: nb * bl, :] = left_ref[group ^ e]
        outs[e][nb * bl :, :] = right_ref[group ^ e]


def adj_norm_body(nb, ngroups, normin_ref, wk_ref, gain_ref, *refs):
    group, place = position(ngroups)
    shares, rest = refs[:ngroups], refs[ngroups:]
    adj_proj_ref, gain_part_ref, outs, adj_norm_ref = rest[0], rest[1], rest[2 : 2 + nb], rest[2 + nb]
    bd = wk_ref.shape[0]
    t = LANE
    adj_proj = jnp.zeros(adj_proj_ref.shape, F32)
    for e in range(ngroups):
        adj_proj = adj_proj + mm(shares[e][...], pick(bd, bd // ngroups, group ^ e), 1, 1)
    adj_proj_ref[...] = adj_proj.astype(BF)
    adj_norm = mm(adj_proj_ref[...], wk_ref[...], 1, 1)
    adj_norm_ref[...] = adj_norm
    gain = gain_ref[:, pl.ds(pl.multiple_of(place * bd, LANE), bd)]
    gain_part_ref[...] = jnp.sum(adj_norm * normin_ref[...].astype(F32), axis=0, keepdims=True) / gain
    for d in range(nb):
        outs[d][...] = adj_norm_ref[rows((place ^ far(d, nb)) * t, t), :].astype(BF)


def weight_grad_body(nb, ngroups, normin_ref, adj_proj_ref, gain_part_ref, own_ref, *refs):
    group, _ = position(ngroups)
    sends, gw_ref = refs[: ngroups - 1], refs[ngroups - 1]
    share, bd = own_ref.shape
    r = share // nb
    gw_ref[...] = mm(normin_ref[...], adj_proj_ref[...], 0, 0)
    tile = jnp.concatenate(
        list(split3(gain_part_ref[...])) + [jnp.zeros((SUB - 3, bd), F32)], axis=0
    ).astype(BF)
    for c in range(nb):
        at = slice(c * r, (c + 1) * r)
        own_ref[at, :] = gw_ref[rows((c * ngroups + group) * r, r), :]
        for e in range(1, ngroups):
            sends[e - 1][at, :] = gw_ref[rows((c * ngroups + (group ^ e)) * r, r), :].astype(BF)
    for e in range(1, ngroups):
        sends[e - 1][share:, :] = tile


def sum_tiles_body(*refs):
    total = refs[0][...].astype(F32)
    for ref in refs[1:-1]:
        total = total + ref[...].astype(F32)
    refs[-1][...] = total.astype(BF)


def weight_sum_body(nb, ngroups, bl, ext, own_ref, gain_part_ref, *refs):
    group, place = position(ngroups)
    recvs, tiles_ref = refs[: ngroups - 1], refs[ngroups - 1]
    outs = refs[ngroups : ngroups + nb]
    total_ref, gains_ref = refs[ngroups + nb :]
    share, bd = own_ref.shape
    chunks = bd // LANE
    r = share // nb
    total = own_ref[...]
    gains_ref[group] = gain_part_ref[...]
    for e in range(1, ngroups):
        total = total + recvs[e - 1][:share, :].astype(F32)
        three = recvs[e - 1][share:, :].astype(F32)
        gains_ref[group ^ e] = three[0:1] + three[1:2] + three[2:3]
    total_ref[...] = total.astype(BF)
    gain = gains_ref[0]
    for g in range(1, ngroups):
        gain = gain + gains_ref[g]
    three = split3(gain)
    parts = [p[:, ch * LANE : (ch + 1) * LANE] for p in three for ch in range(chunks)]
    tile = jnp.concatenate(parts + [jnp.zeros((SUB - len(parts), LANE), F32)], axis=0).astype(BF)
    for d in range(nb):
        to = place ^ far(d, nb)
        for ch in range(chunks):
            outs[d][ch * r : (ch + 1) * r, :] = total_ref[rows(to * r, r), ch * LANE : (ch + 1) * LANE]
        at = chunks * r
        outs[d][at : at + bl, :] = tiles_ref[rows(to * bl, bl), :]
        outs[d][at + bl : at + bl + ext, :] = tiles_ref[
            pl.ds(pl.multiple_of(nb * bl + to * ext, ext), ext), :
        ]
        outs[d][at + bl + ext :, :] = tile


def input_grad_body(nb, ngroups, x_ref, grad_ref, gain_ref, *refs):
    _, place = position(ngroups)
    parts, out, adj_ref = refs[:nb], refs[nb], refs[nb + 1]
    bd = parts[0].shape[1]
    for d in range(nb):
        adj_ref[:, pl.ds(pl.multiple_of((place ^ far(d, nb)) * bd, LANE), bd)] = parts[d][...].astype(F32)
    x = x_ref[...].astype(F32)
    inv = lax.rsqrt(jnp.mean(x * x, axis=-1, keepdims=True) + EPS)
    normed = x * inv
    scaled = adj_ref[...] * gain_ref[...]
    mean = jnp.mean(scaled * normed, axis=-1, keepdims=True)
    out[...] = (grad_ref[...].astype(F32) + inv * (scaled - normed * mean)).astype(BF)


def join_body(nb, ngroups, *refs):
    _, block = position(ngroups)
    out = refs[nb]
    bd = refs[0].shape[1]
    for d in range(nb):
        out[:, pl.ds(pl.multiple_of((block ^ far(d, nb)) * bd, LANE), bd)] = refs[d][...]


def join_weight_body(nb, ngroups, *refs):
    _, block = position(ngroups)
    gw_ref, gain_ref, left_out, right_out, by_block = refs[nb:]
    r, _, bd = gw_ref.shape
    chunks = bd // LANE
    na, bl, _ = left_out.shape
    npos, ext, _ = right_out.shape
    at = chunks * r
    left = refs[0][at : at + bl, :].astype(F32)
    right = refs[0][at + bl : at + bl + ext, :].astype(F32)
    for d in range(1, nb):
        left = left + refs[d][at : at + bl, :].astype(F32)
        right = right + refs[d][at + bl : at + bl + ext, :].astype(F32)
    for j in range(na):
        left_out[j] = left[:, j * bl : (j + 1) * bl]
    for j in range(npos):
        right_out[j] = right[:, j * ext : (j + 1) * ext]
    for d in range(nb):
        k = block ^ far(d, nb)
        by_block[k] = unpack(refs[d], r, chunks).astype(F32)
        tile = refs[d][at + bl + ext :, :].astype(F32)
        for ch in range(chunks):
            gain_ref[:, pl.ds(pl.multiple_of(k * bd + ch * LANE, LANE), LANE)] = (
                tile[ch : ch + 1] + tile[chunks + ch : chunks + ch + 1] + tile[2 * chunks + ch : 2 * chunks + ch + 1]
            )
    for k in range(nb):
        gw_ref[:, k, :] = by_block[k]


def shards(act_in, saved_in, grad_in, gain, weight, left_blocks, right_blocks):
    nseq = lax.axis_size("seq")
    npipe = lax.axis_size("pipe")
    _, t, width = act_in.shape
    _, r, nb, bd = weight.shape
    ngroups = nseq // nb
    bl = left_blocks.shape[2]
    ext = right_blocks.shape[2]
    npos = right_blocks.shape[1]
    chunks = bd // LANE
    tg = nb * t
    r4 = chunks * r
    nq = bl // SUB
    n = SUB * ext

    def within(parts):
        return [parts[0]] + [
            lax.ppermute(parts[d], "seq", [(s, s ^ (far(d, nb) * ngroups)) for s in range(nseq)])
            for d in range(1, nb)
        ]

    def across(block, e):
        return lax.ppermute(block, "seq", [(s, s ^ e) for s in range(nseq)])

    def gathered(block):
        return [block] + [across(block, e) for e in range(1, ngroups)]

    def exchanged(parts):
        return list(parts[:1]) + [across(parts[e], e) for e in range(1, ngroups)]

    part = functools.partial
    def run(name, body, outs, scratch=(), direct=0):
        return call(body, outs, scratch, direct, name)

    pack = part(pack_tokens_body, nb, ngroups)
    norm = part(norm_body, nb, ngroups)
    join = part(join_body, nb, ngroups)
    scaled_msgs = [sds((chunks * t + SUB, LANE))] * nb
    tokens = [sds((tg, bd))]
    pieces = [sds((t, bd))] * nb
    rows_of = bd // ngroups
    part_of = bd // ngroups
    shares = [sds((tg, part_of))] * ngroups
    every = [sds((ngroups * tg, part_of))]
    by_position = [sds((nq, n, part_of))]

    def scratch(structs):
        return [pltpu.VMEM(s.shape, s.dtype) for s in structs]

    w_msgs = run("pack_weight", part(pack_weight_body, nb, ngroups), [sds((r4 + bl + ext, LANE))] * nb)(
        jnp.transpose(weight[0], (1, 0, 2)), left_blocks[0], right_blocks[0]
    )
    cur_msgs = run("pack_act", part(pack, True), scaled_msgs)(act_in[0], after=w_msgs[:1])
    grad_shares = run(
        "split_grad", part(split_features_body, nb, ngroups), [sds((nb, t, part_of))] * ngroups
    )(grad_in[0], after=cur_msgs[:1])
    sto_msgs = run("pack_saved", part(pack, True), scaled_msgs)(saved_in[0], after=grad_shares[:1])
    early = sto_msgs[:1]
    w_msgs, cur_msgs = within(w_msgs), within(cur_msgs)
    grad_shares = exchanged(grad_shares)
    sto_msgs = within(sto_msgs)
    (relay,) = run("relay", part(relay_body, nb, ngroups, r4, ext), [sds((nb * (r4 + ext + bl), LANE))])(
        *w_msgs, after=early
    )
    relays = gathered(relay)
    (cur_normin,) = run("norm_act", norm, tokens)(*cur_msgs, gain, after=[relay])
    wk, mq, bd_left = run(
        "assemble",
        part(assemble_body, nb, ngroups, r, ext, bl),
        [sds((bd, bd)), sds((nq, n, n)), sds((nseq, LANE, LANE))],
        [pltpu.VMEM((nseq, ext, LANE), BF)],
    )(*relays, after=[cur_normin])
    cur_proj, cur_first = run("project_act", part(project_body, nb, ngroups), tokens * 2)(
        cur_normin, wk, bd_left
    )
    cur_firsts = gathered(cur_first)
    grad_msgs = run("pack_grad", part(pack_shares_body, nb, ngroups), [sds((ngroups * t, part_of))] * nb)(
        *grad_shares, after=[cur_first]
    )
    grad_msgs = within(grad_msgs)
    (sto_normin,) = run("norm_saved", norm, tokens)(*sto_msgs, gain, after=grad_msgs[:1])
    sto_shares = run("project_saved", part(project_shares_body, ngroups), shares)(sto_normin, wk)
    sto_wait = sto_shares[:1]
    sto_shares = exchanged(sto_shares)
    (cur_mixed,) = run(
        "mix_act", part(mix_body, ngroups, bl), tokens, scratch([sds((nq, n, bd))])
    )(*cur_firsts, mq, after=sto_wait)
    out_parts = run("output", part(output_body, nb, ngroups), pieces)(cur_mixed, cur_proj, *cur_msgs)
    (grad,) = run("take_grad", part(take_grad_body, nb, ngroups), every)(*grad_msgs, after=out_parts[:1])
    sto_proj, sto_f, sto_mixed = run(
        "mix_saved", part(mix_shares_body, ngroups, bl), every + by_position + every, scratch(every)
    )(*sto_shares, mq, bd_left, after=[grad])
    out_parts = within(out_parts)
    *adj_shares, adj_f, adj_first = run(
        "backward", part(backward_body, nb, ngroups, bl), shares + by_position + every, scratch(every)
    )(grad, sto_proj, sto_mixed, mq, bd_left)
    adj_wait = adj_shares[:1]
    adj_shares = exchanged(adj_shares)
    tiles = run(
        "factor_grads",
        part(factor_grads_body, nb, ngroups, bl, ext),
        [sds((nb * (bl + ext), LANE))] * ngroups,
        scratch([sds((ngroups, nb * ext, LANE)), sds((ngroups, nb * bl, LANE))]),
    )(sto_f, adj_f, adj_first, sto_proj, after=adj_wait)
    tiles_wait = tiles[:1]
    tiles = exchanged(tiles)
    (out,) = run("join_out", join, [sds((t, width))])(*out_parts, after=tiles_wait)
    adj_proj, gain_part, *adj_parts = run(
        "adj_norm",
        part(adj_norm_body, nb, ngroups),
        tokens + [sds((1, bd), F32)] + pieces,
        scratch([sds((tg, bd), F32)]),
    )(sto_normin, wk, gain, *adj_shares, after=[out])
    adj_wait = adj_parts[:1]
    adj_parts = within(adj_parts)
    (tile_sum,) = run("sum_tiles", sum_tiles_body, [sds((nb * (bl + ext), LANE))])(*tiles, after=adj_wait)
    own_gw, *sends = run(
        "weight_grad",
        part(weight_grad_body, nb, ngroups),
        [sds((rows_of, bd), F32)] + [sds((rows_of + SUB, bd))] * (ngroups - 1),
        scratch([sds((bd, bd), F32)]),
    )(sto_normin, adj_proj, gain_part, after=[tile_sum])
    recvs = [across(sends[e - 1], e) for e in range(1, ngroups)]
    gw_parts = run(
        "weight_sum",
        part(weight_sum_body, nb, ngroups, bl, ext),
        [sds((r4 + bl + ext + SUB, LANE))] * nb,
        scratch([sds((rows_of, bd)), sds((ngroups, 1, bd), F32)]),
    )(own_gw, gain_part, *recvs, tile_sum)
    handed_on = lax.ppermute(out, "pipe", [(p, (p + 1) % npipe) for p in range(npipe)])
    (adj_x,) = run(
        "input_grad", part(input_grad_body, nb, ngroups), [sds((t, width))], scratch([sds((t, width), F32)])
    )(saved_in[0], grad_in[0], gain, *adj_parts, after=gw_parts[:1])
    gw_parts = within(gw_parts)
    grad_handed = lax.ppermute(adj_x, "pipe", [(p, (p - 1) % npipe) for p in range(npipe)])
    weight_grad, gain_grad, left_grad, right_grad = run(
        "join_weight",
        part(join_weight_body, nb, ngroups),
        [
            sds((r, nb, bd), F32),
            sds((1, width), F32),
            sds((left_blocks.shape[1], bl, bl), F32),
            sds((npos, ext, ext), F32),
        ],
        scratch([sds((nb, r, bd), F32)]),
    )(*gw_parts, after=[adj_x])
    return (
        handed_on[None],
        grad_handed[None],
        weight_grad[None],
        gain_grad,
        left_grad[None],
        right_grad[None],
    )


def solution(mesh):
    tokens = P("pipe", "seq", None)
    factor = P("pipe", "seq", None, None)
    return jax.shard_map(
        shards,
        mesh=mesh,
        in_specs=(tokens, tokens, tokens, P("pipe", None), factor, factor, factor),
        out_specs=(tokens, tokens, factor, P("pipe", None), factor, factor),
        check_vma=False,
    )
```

time: 99.9 us -> 92.1 us (0.922)
  starting transfers between devices: 58.2 us -> 50.5 us
  waiting for transfers between devices: 26.3 us -> 28.3 us
  Pallas kernels: 11.4 us -> 9.59 us
    ppermute x22, starting transfers between devices: 50 us -> 39.7 us  [the longest x21 39.7 us: within(): lax.ppermute(parts[d], 'seq', [(s, s ^ far(d, nb) * ngroups) for s in ran...]
    ppermute x22, waiting for transfers between devices: 16.1 us -> 25.1 us  [the longest x21 25.1 us: within(): lax.ppermute(parts[d], 'seq', [(s, s ^ far(d, nb) * ngroups) for s in ran...]
    ppermute x5 -> x7, waiting for transfers between devices: 10.1 us -> 3.22 us  [across(): return lax.ppermute(block, 'seq', [(s, s ^ e) for s in range(nseq)])]
    ppermute x5 -> x7, starting transfers between devices: 8.17 us -> 10.7 us  [across(): return lax.ppermute(block, 'seq', [(s, s ^ e) for s in range(nseq)])]
    pallas_call x22 -> x24, Pallas kernels: 11.4 us -> 9.59 us  [run(): pl.pallas_call(without_waits, out_shape=list(outs), in_specs=[anywhere] *...]
    unnamed x16 -> x15, local copies, waits for them, and re-layouts: 2.92 us -> 2.67 us
  transfers between devices with their start and end apart: 28 -> 30, of which waited for: 12 -> 12; matrix products, arithmetic and copies ran while one was open for 0% -> 0% of each run, Pallas kernels for 11% -> 10%
where the time goes in v3:
time: 92.1 us; the launch traced here: 91.9 us
  starting transfers between devices  50.5 us (55%)
  waiting for transfers between devices  28.3 us (31%)
  Pallas kernels  9.59 us (10%)
  local copies, waits for them, and re-layouts  2.67 us (3%)
    ppermute x21, starting transfers between devices, within(): lax.ppermute(parts[d], 'seq', [(s, s ^ far(d, nb) * ngroups) for s in ran...  39.7 us
    ppermute x21, waiting for transfers between devices, within(): lax.ppermute(parts[d], 'seq', [(s, s ^ far(d, nb) * ngroups) for s in ran...  25.1 us
    ppermute x7, starting transfers between devices, across(): return lax.ppermute(block, 'seq', [(s, s ^ e) for s in range(nseq)])  10.7 us
    pallas_call x24, Pallas kernels, run(): pl.pallas_call(without_waits, out_shape=list(outs), in_specs=[anywhere] *...  9.59 us
    ppermute x7, waiting for transfers between devices, across(): return lax.ppermute(block, 'seq', [(s, s ^ e) for s in range(nseq)])  3.22 us
    unnamed x15, local copies, waits for them, and re-layouts  2.67 us
  transfers between devices with their start and end apart: 30, of which 12 were waited for; matrix products, arithmetic and copies ran while one was open for 0% of the time, Pallas kernels for 10%

profile of v3, /device:TPU:0, one launch (start us, length us, event | category | flops | bytes accessed | tf_op | source)
XLA Modules:
  0.0 91.9 jit_solution(15932308079057484443)
XLA Ops:
  0.7 1.1 %copy.15 = bf16[1,64,4,512]{3,1,2,0:T(8,128)(2,1)S(1)} copy(bf16[1,64,4,512]{3,2,1,0:T(4,128)(2,1)} %param.11) | data formatting | bytes 524288 | tf_op args[4]
  1.8 5.1 %collective-permute-start.3 = (bf16[336,128]{1,0:T(8,128)(2,1)S(1)}, bf16[336,128]{1,0:T(8,128)(2,1)S(1)}, u32[]{:S(2)}, u32[]{:S(2)}) collective-permute-start(bf16[336,128]{1,0:T(8,128)(2,1)S(1)} %get-tuple-element.65), channel_id=1, source_target_pairs={{0,6},{1,7},{2,4},{3,5},{4,2},{5,3},{6,0},{7,1},{8,14},{9,15},{10,... | collective-permute-start | bytes 258056 | tf_op jit(solution)/shard_map/ppermute | solution.py:517
  7.0 0.6 collective-permute-start.5
  7.8 3.8 %collective-permute-start = (bf16[528,128]{1,0:T(8,128)(2,1)S(1)}, bf16[528,128]{1,0:T(8,128)(2,1)S(1)}, u32[]{:S(2)}, u32[]{:S(2)}) collective-permute-start(bf16[528,128]{1,0:T(8,128)(2,1)S(1)} %get-tuple-element.62), channel_id=1, source_target_pairs={{0,6},{1,7},{2,4},{3,5},{4,2},{5,3},{6,0},{7,1},{8,14},{9,15},{10,... | collective-permute-start | bytes 405512 | tf_op jit(solution)/shard_map/ppermute | solution.py:517
  11.7 3.7 %collective-permute-start.2 = (bf16[528,128]{1,0:T(8,128)(2,1)S(1)}, bf16[528,128]{1,0:T(8,128)(2,1)S(1)}, u32[]{:S(2)}, u32[]{:S(2)}) collective-permute-start(bf16[528,128]{1,0:T(8,128)(2,1)S(1)} %get-tuple-element.64), channel_id=1, source_target_pairs={{0,2},{1,3},{2,0},{3,1},{4,6},{5,7},{6,4},{7,5},{8,10},{9,11},{10,... | collective-permute-start | bytes 405512 | tf_op jit(solution)/shard_map/ppermute | solution.py:517
  15.4 0.5 split_grad.1
  16.1 4.8 %collective-permute-done.4.refs_2_ = bf16[336,128]{1,0:T(8,128)(2,1)S(1)} collective-permute-done((bf16[336,128]{1,0:T(8,128)(2,1)S(1)}, bf16[336,128]{1,0:T(8,128)(2,1)S(1)}, u32[]{:S(2)}, u32[]{:S(2)}) %collective-permute-start.4) | collective-permute-done | bytes 86048 | tf_op jit(solution)/shard_map/ppermute | solution.py:517
  20.9 1.5 %collective-permute-start.6 = (bf16[1344,128]{1,0:T(8,128)(2,1)S(1)}, bf16[1344,128]{1,0:T(8,128)(2,1)S(1)}, u32[]{:S(2)}, u32[]{:S(2)}) collective-permute-start(bf16[1344,128]{1,0:T(8,128)(2,1)S(1)} %relay.1.refs_5_.refs_0_), channel_id=1, source_target_pairs={{0,1},{1,0},{2,3},{3,2},{4,5},{5,4},{6,7},{7,6},{8,9},{9,8},{10,11... | collective-permute-start | bytes 1032200 | tf_op jit(solution)/shard_map/ppermute | solution.py:522
  22.4 0.6 collective-permute-start.11
  23.0 2.6 %collective-permute-start.8 = (bf16[528,128]{1,0:T(8,128)(2,1)S(1)}, bf16[528,128]{1,0:T(8,128)(2,1)S(1)}, u32[]{:S(2)}, u32[]{:S(2)}) collective-permute-start(bf16[528,128]{1,0:T(8,128)(2,1)S(1)} %get-tuple-element.74), channel_id=1, source_target_pairs={{0,6},{1,7},{2,4},{3,5},{4,2},{5,3},{6,0},{7,1},{8,14},{9,15},{10,... | collective-permute-start | bytes 405512 | tf_op jit(solution)/shard_map/ppermute | solution.py:517
  25.6 2.5 %collective-permute-done.1.refs_2_.refs_4_ = bf16[528,128]{1,0:T(8,128)(2,1)S(1)} collective-permute-done((bf16[528,128]{1,0:T(8,128)(2,1)S(1)}, bf16[528,128]{1,0:T(8,128)(2,1)S(1)}, u32[]{:S(2)}, u32[]{:S(2)}) %collective-permute-start.1) | collective-permute-done | bytes 135200 | tf_op jit(solution)/shard_map/ppermute | solution.py:517
  28.1 3.3 %collective-permute-start.10 = (bf16[528,128]{1,0:T(8,128)(2,1)S(1)}, bf16[528,128]{1,0:T(8,128)(2,1)S(1)}, u32[]{:S(2)}, u32[]{:S(2)}) collective-permute-start(bf16[528,128]{1,0:T(8,128)(2,1)S(1)} %get-tuple-element.76), channel_id=1, source_target_pairs={{0,2},{1,3},{2,0},{3,1},{4,6},{5,7},{6,4},{7,5},{8,10},{9,11},{10,... | collective-permute-start | bytes 405512 | tf_op jit(solution)/shard_map/ppermute | solution.py:517
  31.6 0.7 assemble.1
  32.3 0.6 project_act.1
  32.9 1.6 %collective-permute-start.7 = (bf16[512,512]{1,0:T(8,128)(2,1)S(1)}, bf16[512,512]{1,0:T(8,128)(2,1)S(1)}, u32[]{:S(2)}, u32[]{:S(2)}) collective-permute-start(bf16[512,512]{1,0:T(8,128)(2,1)S(1)} %get-tuple-element.72.refs_2_.refs_0_), channel_id=1, source_target_pairs={{0,1},{1,0},{2,3},{3,2},{4,5},{5,4},{6,7},{7,6},{8,9},{9,8},{10,11... | collective-permute-start | bytes 1572872 | tf_op jit(solution)/shard_map/ppermute | solution.py:522
  34.5 1.1 %collective-permute-start.16 = (bf16[256,256]{1,0:T(8,128)(2,1)S(1)}, bf16[256,256]{1,0:T(8,128)(2,1)S(1)}, u32[]{:S(2)}, u32[]{:S(2)}) collective-permute-start(bf16[256,256]{1,0:T(8,128)(2,1)S(1)} %get-tuple-element.86), channel_id=1, source_target_pairs={{0,6},{1,7},{2,4},{3,5},{4,2},{5,3},{6,0},{7,1},{8,14},{9,15},{10,... | collective-permute-start | bytes 393224 | tf_op jit(solution)/shard_map/ppermute | solution.py:517
  35.6 6.1 %collective-permute-start.17 = (bf16[256,256]{1,0:T(8,128)(2,1)S(1)}, bf16[256,256]{1,0:T(8,128)(2,1)S(1)}, u32[]{:S(2)}, u32[]{:S(2)}) collective-permute-start(bf16[256,256]{1,0:T(8,128)(2,1)S(1)} %get-tuple-element.87), channel_id=1, source_target_pairs={{0,4},{1,5},{2,6},{3,7},{4,0},{5,1},{6,2},{7,3},{8,12},{9,13},{10,... | collective-permute-start | bytes 393224 | tf_op jit(solution)/shard_map/ppermute | solution.py:517
  41.7 2.6 %collective-permute-done.9.refs_2_ = bf16[528,128]{1,0:T(8,128)(2,1)S(1)} collective-permute-done((bf16[528,128]{1,0:T(8,128)(2,1)S(1)}, bf16[528,128]{1,0:T(8,128)(2,1)S(1)}, u32[]{:S(2)}, u32[]{:S(2)}) %collective-permute-start.9) | collective-permute-done | bytes 135200 | tf_op jit(solution)/shard_map/ppermute | solution.py:517
  44.5 0.7 project_saved.1
  45.2 1.5 %collective-permute-start.15 = (bf16[512,256]{1,0:T(8,128)(2,1)S(1)}, bf16[512,256]{1,0:T(8,128)(2,1)S(1)}, u32[]{:S(2)}, u32[]{:S(2)}) collective-permute-start(bf16[512,256]{1,0:T(8,128)(2,1)S(1)} %get-tuple-element.85), channel_id=1, source_target_pairs={{0,1},{1,0},{2,3},{3,2},{4,5},{5,4},{6,7},{7,6},{8,9},{9,8},{10,11... | collective-permute-start | bytes 786440 | tf_op jit(solution)/shard_map/ppermute | solution.py:522
  46.7 0.4 mix_act.1.refs_0_
  47.3 1.4 %collective-permute-start.12 = (bf16[128,512]{1,0:T(8,128)(2,1)S(1)}, bf16[128,512]{1,0:T(8,128)(2,1)S(1)}, u32[]{:S(2)}, u32[]{:S(2)}) collective-permute-start(bf16[128,512]{1,0:T(8,128)(2,1)S(1)} %get-tuple-element.82), channel_id=1, source_target_pairs={{0,6},{1,7},{2,4},{3,5},{4,2},{5,3},{6,0},{7,1},{8,14},{9,15},{10,... | collective-permute-start | bytes 393224 | tf_op jit(solution)/shard_map/ppermute | solution.py:517
  48.7 2.2 %collective-permute-start.13 = (bf16[128,512]{1,0:T(8,128)(2,1)S(1)}, bf16[128,512]{1,0:T(8,128)(2,1)S(1)}, u32[]{:S(2)}, u32[]{:S(2)}) collective-permute-start(bf16[128,512]{1,0:T(8,128)(2,1)S(1)} %get-tuple-element.83), channel_id=1, source_target_pairs={{0,4},{1,5},{2,6},{3,7},{4,0},{5,1},{6,2},{7,3},{8,12},{9,13},{10,... | collective-permute-start | bytes 393224 | tf_op jit(solution)/shard_map/ppermute | solution.py:517
  50.8 1.9 %collective-permute-done.17.refs_2_ = bf16[256,256]{1,0:T(8,128)(2,1)S(1)} collective-permute-done((bf16[256,256]{1,0:T(8,128)(2,1)S(1)}, bf16[256,256]{1,0:T(8,128)(2,1)S(1)}, u32[]{:S(2)}, u32[]{:S(2)}) %collective-permute-start.17) | collective-permute-done | bytes 131104 | tf_op jit(solution)/shard_map/ppermute | solution.py:517
  52.7 0.5 collective-permute-start.14
  53.3 0.6 mix_saved.1
  53.9 0.6 backward.1
  54.6 3.5 %collective-permute-start.20 = (bf16[512,256]{1,0:T(8,128)(2,1)S(1)}, bf16[512,256]{1,0:T(8,128)(2,1)S(1)}, u32[]{:S(2)}, u32[]{:S(2)}) collective-permute-start(bf16[512,256]{1,0:T(8,128)(2,1)S(1)} %get-tuple-element.96), channel_id=1, source_target_pairs={{0,1},{1,0},{2,3},{3,2},{4,5},{5,4},{6,7},{7,6},{8,9},{9,8},{10,11... | collective-permute-start | bytes 786440 | tf_op jit(solution)/shard_map/ppermute | solution.py:522
  58.1 0.9 %factor_grads.1 = (bf16[320,128]{1,0:T(8,128)(2,1)S(1)}, bf16[320,128]{1,0:T(8,128)(2,1)S(1)}) custom-call(bf16[4,256,256]{2,1,0:T(8,128)(2,1)S(1)} %get-tuple-element.89.refs_0_, bf16[4,256,256]{2,1,0:T(8,128)(2,1)S(1)} %get-tuple-element.92.refs_1_, bf16[1024,256]{1,0:T(8,128)(2,1)S(1)} %get-tuple-element.93.refs_2_, ...), custom_call_target="tpu_custom_call" | custom-call | tf_op jit(solution)/shard_map/factor_grads/pallas_call | solution.py:66
  59.1 0.8 collective-permute-done.13.refs_2_
  60.2 2.2 %collective-permute-done.20.refs_4_ = bf16[512,256]{1,0:T(8,128)(2,1)S(1)} collective-permute-done((bf16[512,256]{1,0:T(8,128)(2,1)S(1)}, bf16[512,256]{1,0:T(8,128)(2,1)S(1)}, u32[]{:S(2)}, u32[]{:S(2)}) %collective-permute-start.20) | collective-permute-done | bytes 262176 | tf_op jit(solution)/shard_map/ppermute | solution.py:522
  62.4 0.8 adj_norm.1
  63.2 1.0 %collective-permute-done.24.refs_1_ = bf16[320,128]{1,0:T(8,128)(2,1)S(1)} collective-permute-done((bf16[320,128]{1,0:T(8,128)(2,1)S(1)}, bf16[320,128]{1,0:T(8,128)(2,1)S(1)}, u32[]{:S(2)}, u32[]{:S(2)}) %collective-permute-start.24) | collective-permute-done | bytes 81952 | tf_op jit(solution)/shard_map/ppermute | solution.py:522
  64.3 0.5 weight_grad.1
  64.8 2.0 %collective-permute-start.25 = (bf16[272,512]{1,0:T(8,128)(2,1)S(1)}, bf16[272,512]{1,0:T(8,128)(2,1)S(1)}, u32[]{:S(2)}, u32[]{:S(2)}) collective-permute-start(bf16[272,512]{1,0:T(8,128)(2,1)S(1)} %get-tuple-element.105), channel_id=1, source_target_pairs={{0,1},{1,0},{2,3},{3,2},{4,5},{5,4},{6,7},{7,6},{8,9},{9,8},{10,11... | collective-permute-start | bytes 835592 | tf_op jit(solution)/shard_map/ppermute | solution.py:522
  66.9 3.4 %collective-permute-start.21 = (bf16[128,512]{1,0:T(8,128)(2,1)S(1)}, bf16[128,512]{1,0:T(8,128)(2,1)S(1)}, u32[]{:S(2)}, u32[]{:S(2)}) collective-permute-start(bf16[128,512]{1,0:T(8,128)(2,1)S(1)} %get-tuple-element.98), channel_id=1, source_target_pairs={{0,6},{1,7},{2,4},{3,5},{4,2},{5,3},{6,0},{7,1},{8,14},{9,15},{10,... | collective-permute-start | bytes 393224 | tf_op jit(solution)/shard_map/ppermute | solution.py:517
  70.2 1.0 %collective-permute-start.22 = (bf16[128,512]{1,0:T(8,128)(2,1)S(1)}, bf16[128,512]{1,0:T(8,128)(2,1)S(1)}, u32[]{:S(2)}, u32[]{:S(2)}) collective-permute-start(bf16[128,512]{1,0:T(8,128)(2,1)S(1)} %get-tuple-element.99), channel_id=1, source_target_pairs={{0,4},{1,5},{2,6},{3,7},{4,0},{5,1},{6,2},{7,3},{8,12},{9,13},{10,... | collective-permute-start | bytes 393224 | tf_op jit(solution)/shard_map/ppermute | solution.py:517
  71.2 0.6 collective-permute-start.23
  71.9 1.8 %collective-permute-done.21.refs_4_ = bf16[128,512]{1,0:T(8,128)(2,1)S(1)} collective-permute-done((bf16[128,512]{1,0:T(8,128)(2,1)S(1)}, bf16[128,512]{1,0:T(8,128)(2,1)S(1)}, u32[]{:S(2)}, u32[]{:S(2)}) %collective-permute-start.21) | collective-permute-done | bytes 131104 | tf_op jit(solution)/shard_map/ppermute | solution.py:517
  73.7 4.1 %collective-permute-done.22.refs_5_ = bf16[128,512]{1,0:T(8,128)(2,1)S(1)} collective-permute-done((bf16[128,512]{1,0:T(8,128)(2,1)S(1)}, bf16[128,512]{1,0:T(8,128)(2,1)S(1)}, u32[]{:S(2)}, u32[]{:S(2)}) %collective-permute-start.22) | collective-permute-done | bytes 131104 | tf_op jit(solution)/shard_map/ppermute | solution.py:517
  77.9 0.7 input_grad.1.refs_4_
  78.6 3.4 %collective-permute-start.27 = (bf16[352,128]{1,0:T(8,128)(2,1)S(1)}, bf16[352,128]{1,0:T(8,128)(2,1)S(1)}, u32[]{:S(2)}, u32[]{:S(2)}) collective-permute-start(bf16[352,128]{1,0:T(8,128)(2,1)S(1)} %get-tuple-element.107), channel_id=1, source_target_pairs={{0,6},{1,7},{2,4},{3,5},{4,2},{5,3},{6,0},{7,1},{8,14},{9,15},{10,... | collective-permute-start | bytes 270344 | tf_op jit(solution)/shard_map/ppermute | solution.py:517
  82.1 1.0 %collective-permute-start.29 = (bf16[352,128]{1,0:T(8,128)(2,1)S(1)}, bf16[352,128]{1,0:T(8,128)(2,1)S(1)}, u32[]{:S(2)}, u32[]{:S(2)}) collective-permute-start(bf16[352,128]{1,0:T(8,128)(2,1)S(1)} %get-tuple-element.109), channel_id=1, source_target_pairs={{0,2},{1,3},{2,0},{3,1},{4,6},{5,7},{6,4},{7,5},{8,10},{9,11},{10,... | collective-permute-start | bytes 270344 | tf_op jit(solution)/shard_map/ppermute | solution.py:517
  83.1 2.9 %collective-permute-done.27.refs_1_ = bf16[352,128]{1,0:T(8,128)(2,1)S(1)} collective-permute-done((bf16[352,128]{1,0:T(8,128)(2,1)S(1)}, bf16[352,128]{1,0:T(8,128)(2,1)S(1)}, u32[]{:S(2)}, u32[]{:S(2)}) %collective-permute-start.27) | collective-permute-done | bytes 90144 | tf_op jit(solution)/shard_map/ppermute | solution.py:517
  86.0 3.4 %collective-permute-done.28.refs_2_ = bf16[352,128]{1,0:T(8,128)(2,1)S(1)} collective-permute-done((bf16[352,128]{1,0:T(8,128)(2,1)S(1)}, bf16[352,128]{1,0:T(8,128)(2,1)S(1)}, u32[]{:S(2)}, u32[]{:S(2)}) %collective-permute-start.28) | collective-permute-done | bytes 90144 | tf_op jit(solution)/shard_map/ppermute | solution.py:517
  89.4 1.0 %join_weight.1 = (f32[64,4,512]{2,1,0:T(4,128)}, f32[1,2048]{1,0:T(1,128)}, f32[2,64,64]{2,1,0:T(8,128)}, f32[8,16,16]{2,1,0:T(8,128)}) custom-call(bf16[352,128]{1,0:T(8,128)(2,1)S(1)} %get-tuple-element.106.refs_7_.refs_0_, bf16[352,128]{1,0:T(8,128)(2,1)S(1)} %collective-permute-done.27.refs_1_, bf16[352,128]{1,0:T(8,128)(2,1)S(1)} %collective-permute-done.28.refs_2_, ...), custom_call_target="tpu_custom_call" | custom-call | tf_op jit(solution)/shard_map/join_weight/pallas_call | solution.py:66
  90.3 0.8 copy.18
  91.1 0.8 copy.19
  (51 shorter events, 2.0 us)
Async XLA Ops:
  0.6 1.1 %copy-start.5 = (bf16[1,8,16,16]{3,2,1,0:T(8,128)(2,1)S(1)}, bf16[1,8,16,16]{3,2,1,0:T(8,128)(2,1)}, u32[]{:S(2)}) copy-start(bf16[1,8,16,16]{3,2,1,0:T(8,128)(2,1)} %param.13) | copy-start | bytes 12292
  0.6 1.1 %copy-start.4 = (bf16[1,2,64,64]{3,2,1,0:T(8,128)(2,1)S(1)}, bf16[1,2,64,64]{3,2,1,0:T(8,128)(2,1)}, u32[]{:S(2)}) copy-start(bf16[1,2,64,64]{3,2,1,0:T(8,128)(2,1)} %param.12) | copy-start | bytes 49156
  0.7 7.0 %copy-start.2 = (bf16[1,128,2048]{2,1,0:T(8,128)(2,1)S(1)}, bf16[1,128,2048]{2,1,0:T(8,128)(2,1)}, u32[]{:S(2)}) copy-start(bf16[1,128,2048]{2,1,0:T(8,128)(2,1)} %param.7) | copy-start | bytes 1572868
  1.7 13.6 %copy-start = (bf16[1,128,2048]{2,1,0:T(8,128)(2,1)S(1)}, bf16[1,128,2048]{2,1,0:T(8,128)(2,1)}, u32[]{:S(2)}) copy-start(bf16[1,128,2048]{2,1,0:T(8,128)(2,1)} %param.9) | copy-start | bytes 1572868
  1.8 9.8 %collective-permute-start.3 = (bf16[336,128]{1,0:T(8,128)(2,1)S(1)}, bf16[336,128]{1,0:T(8,128)(2,1)S(1)}, u32[]{:S(2)}, u32[]{:S(2)}) collective-permute-start(bf16[336,128]{1,0:T(8,128)(2,1)S(1)} %get-tuple-element.65), channel_id=1, source_target_pairs={{0,6},{1,7},{2,4},{3,5},{4,2},{5,3},{6,0},{7,1},{8,14},{9,15},{10,... | collective-permute-start | bytes 258056 | tf_op jit(solution)/shard_map/ppermute | solution.py:517
  7.0 13.9 %collective-permute-start.4 = (bf16[336,128]{1,0:T(8,128)(2,1)S(1)}, bf16[336,128]{1,0:T(8,128)(2,1)S(1)}, u32[]{:S(2)}, u32[]{:S(2)}) collective-permute-start(bf16[336,128]{1,0:T(8,128)(2,1)S(1)} %get-tuple-element.66), channel_id=1, source_target_pairs={{0,4},{1,5},{2,6},{3,7},{4,0},{5,1},{6,2},{7,3},{8,12},{9,13},{10,... | collective-permute-start | bytes 258056 | tf_op jit(solution)/shard_map/ppermute | solution.py:517
  7.0 13.9 %collective-permute-start.5 = (bf16[336,128]{1,0:T(8,128)(2,1)S(1)}, bf16[336,128]{1,0:T(8,128)(2,1)S(1)}, u32[]{:S(2)}, u32[]{:S(2)}) collective-permute-start(bf16[336,128]{1,0:T(8,128)(2,1)S(1)} %get-tuple-element.67), channel_id=1, source_target_pairs={{0,2},{1,3},{2,0},{3,1},{4,6},{5,7},{6,4},{7,5},{8,10},{9,11},{10,... | collective-permute-start | bytes 258056 | tf_op jit(solution)/shard_map/ppermute | solution.py:517
  7.6 8.2 %copy-start.1 = (bf16[1,128,2048]{2,1,0:T(8,128)(2,1)S(1)}, bf16[1,128,2048]{2,1,0:T(8,128)(2,1)}, u32[]{:S(2)}) copy-start(bf16[1,128,2048]{2,1,0:T(8,128)(2,1)} %param.8) | copy-start | bytes 1572868
  7.8 15.2 %collective-permute-start = (bf16[528,128]{1,0:T(8,128)(2,1)S(1)}, bf16[528,128]{1,0:T(8,128)(2,1)S(1)}, u32[]{:S(2)}, u32[]{:S(2)}) collective-permute-start(bf16[528,128]{1,0:T(8,128)(2,1)S(1)} %get-tuple-element.62), channel_id=1, source_target_pairs={{0,6},{1,7},{2,4},{3,5},{4,2},{5,3},{6,0},{7,1},{8,14},{9,15},{10,... | collective-permute-start | bytes 405512 | tf_op jit(solution)/shard_map/ppermute | solution.py:517
  11.6 16.4 %collective-permute-start.1 = (bf16[528,128]{1,0:T(8,128)(2,1)S(1)}, bf16[528,128]{1,0:T(8,128)(2,1)S(1)}, u32[]{:S(2)}, u32[]{:S(2)}) collective-permute-start(bf16[528,128]{1,0:T(8,128)(2,1)S(1)} %get-tuple-element.63), channel_id=1, source_target_pairs={{0,4},{1,5},{2,6},{3,7},{4,0},{5,1},{6,2},{7,3},{8,12},{9,13},{10,... | collective-permute-start | bytes 405512 | tf_op jit(solution)/shard_map/ppermute | solution.py:517
  11.7 16.4 %collective-permute-start.2 = (bf16[528,128]{1,0:T(8,128)(2,1)S(1)}, bf16[528,128]{1,0:T(8,128)(2,1)S(1)}, u32[]{:S(2)}, u32[]{:S(2)}) collective-permute-start(bf16[528,128]{1,0:T(8,128)(2,1)S(1)} %get-tuple-element.64), channel_id=1, source_target_pairs={{0,2},{1,3},{2,0},{3,1},{4,6},{5,7},{6,4},{7,5},{8,10},{9,11},{10,... | collective-permute-start | bytes 405512 | tf_op jit(solution)/shard_map/ppermute | solution.py:517
  20.9 10.5 %copy-start.3 = (f32[1,2048]{1,0:T(1,128)S(1)}, f32[1,2048]{1,0:T(1,128)}, u32[]{:S(2)}) copy-start(f32[1,2048]{1,0:T(1,128)} %refs_2_.3) | copy-start | bytes 24580
  20.9 10.7 %collective-permute-start.6 = (bf16[1344,128]{1,0:T(8,128)(2,1)S(1)}, bf16[1344,128]{1,0:T(8,128)(2,1)S(1)}, u32[]{:S(2)}, u32[]{:S(2)}) collective-permute-start(bf16[1344,128]{1,0:T(8,128)(2,1)S(1)} %relay.1.refs_5_.refs_0_), channel_id=1, source_target_pairs={{0,1},{1,0},{2,3},{3,2},{4,5},{5,4},{6,7},{7,6},{8,9},{9,8},{10,11... | collective-permute-start | bytes 1032200 | tf_op jit(solution)/shard_map/ppermute | solution.py:522
  22.4 12.1 %collective-permute-start.11 = (bf16[4,128,256]{2,1,0:T(8,128)(2,1)S(1)}, bf16[4,128,256]{2,1,0:T(8,128)(2,1)S(1)}, u32[]{:S(2)}, u32[]{:S(2)}) collective-permute-start(bf16[4,128,256]{2,1,0:T(8,128)(2,1)S(1)} %get-tuple-element.77), channel_id=1, source_target_pairs={{0,1},{1,0},{2,3},{3,2},{4,5},{5,4},{6,7},{7,6},{8,9},{9,8},{10,11... | collective-permute-start | bytes 786440 | tf_op jit(solution)/shard_map/ppermute | solution.py:522
  23.0 12.6 %collective-permute-start.8 = (bf16[528,128]{1,0:T(8,128)(2,1)S(1)}, bf16[528,128]{1,0:T(8,128)(2,1)S(1)}, u32[]{:S(2)}, u32[]{:S(2)}) collective-permute-start(bf16[528,128]{1,0:T(8,128)(2,1)S(1)} %get-tuple-element.74), channel_id=1, source_target_pairs={{0,6},{1,7},{2,4},{3,5},{4,2},{5,3},{6,0},{7,1},{8,14},{9,15},{10,... | collective-permute-start | bytes 405512 | tf_op jit(solution)/shard_map/ppermute | solution.py:517
  28.1 16.2 %collective-permute-start.9 = (bf16[528,128]{1,0:T(8,128)(2,1)S(1)}, bf16[528,128]{1,0:T(8,128)(2,1)S(1)}, u32[]{:S(2)}, u32[]{:S(2)}) collective-permute-start(bf16[528,128]{1,0:T(8,128)(2,1)S(1)} %get-tuple-element.75), channel_id=1, source_target_pairs={{0,4},{1,5},{2,6},{3,7},{4,0},{5,1},{6,2},{7,3},{8,12},{9,13},{10,... | collective-permute-start | bytes 405512 | tf_op jit(solution)/shard_map/ppermute | solution.py:517
  28.1 16.2 %collective-permute-start.10 = (bf16[528,128]{1,0:T(8,128)(2,1)S(1)}, bf16[528,128]{1,0:T(8,128)(2,1)S(1)}, u32[]{:S(2)}, u32[]{:S(2)}) collective-permute-start(bf16[528,128]{1,0:T(8,128)(2,1)S(1)} %get-tuple-element.76), channel_id=1, source_target_pairs={{0,2},{1,3},{2,0},{3,1},{4,6},{5,7},{6,4},{7,5},{8,10},{9,11},{10,... | collective-permute-start | bytes 405512 | tf_op jit(solution)/shard_map/ppermute | solution.py:517
  32.9 13.7 %collective-permute-start.7 = (bf16[512,512]{1,0:T(8,128)(2,1)S(1)}, bf16[512,512]{1,0:T(8,128)(2,1)S(1)}, u32[]{:S(2)}, u32[]{:S(2)}) collective-permute-start(bf16[512,512]{1,0:T(8,128)(2,1)S(1)} %get-tuple-element.72.refs_2_.refs_0_), channel_id=1, source_target_pairs={{0,1},{1,0},{2,3},{3,2},{4,5},{5,4},{6,7},{7,6},{8,9},{9,8},{10,11... | collective-permute-start | bytes 1572872 | tf_op jit(solution)/shard_map/ppermute | solution.py:522
  34.5 14.1 %collective-permute-start.16 = (bf16[256,256]{1,0:T(8,128)(2,1)S(1)}, bf16[256,256]{1,0:T(8,128)(2,1)S(1)}, u32[]{:S(2)}, u32[]{:S(2)}) collective-permute-start(bf16[256,256]{1,0:T(8,128)(2,1)S(1)} %get-tuple-element.86), channel_id=1, source_target_pairs={{0,6},{1,7},{2,4},{3,5},{4,2},{5,3},{6,0},{7,1},{8,14},{9,15},{10,... | collective-permute-start | bytes 393224 | tf_op jit(solution)/shard_map/ppermute | solution.py:517
  35.6 17.1 %collective-permute-start.17 = (bf16[256,256]{1,0:T(8,128)(2,1)S(1)}, bf16[256,256]{1,0:T(8,128)(2,1)S(1)}, u32[]{:S(2)}, u32[]{:S(2)}) collective-permute-start(bf16[256,256]{1,0:T(8,128)(2,1)S(1)} %get-tuple-element.87), channel_id=1, source_target_pairs={{0,4},{1,5},{2,6},{3,7},{4,0},{5,1},{6,2},{7,3},{8,12},{9,13},{10,... | collective-permute-start | bytes 393224 | tf_op jit(solution)/shard_map/ppermute | solution.py:517
  44.3 9.0 %collective-permute-start.18 = (bf16[256,256]{1,0:T(8,128)(2,1)S(1)}, bf16[256,256]{1,0:T(8,128)(2,1)S(1)}, u32[]{:S(2)}, u32[]{:S(2)}) collective-permute-start(bf16[256,256]{1,0:T(8,128)(2,1)S(1)} %get-tuple-element.88), channel_id=1, source_target_pairs={{0,2},{1,3},{2,0},{3,1},{4,6},{5,7},{6,4},{7,5},{8,10},{9,11},{10,... | collective-permute-start | bytes 393224 | tf_op jit(solution)/shard_map/ppermute | solution.py:517
  45.2 8.1 %collective-permute-start.15 = (bf16[512,256]{1,0:T(8,128)(2,1)S(1)}, bf16[512,256]{1,0:T(8,128)(2,1)S(1)}, u32[]{:S(2)}, u32[]{:S(2)}) collective-permute-start(bf16[512,256]{1,0:T(8,128)(2,1)S(1)} %get-tuple-element.85), channel_id=1, source_target_pairs={{0,1},{1,0},{2,3},{3,2},{4,5},{5,4},{6,7},{7,6},{8,9},{9,8},{10,11... | collective-permute-start | bytes 786440 | tf_op jit(solution)/shard_map/ppermute | solution.py:522
  47.3 11.8 %collective-permute-start.12 = (bf16[128,512]{1,0:T(8,128)(2,1)S(1)}, bf16[128,512]{1,0:T(8,128)(2,1)S(1)}, u32[]{:S(2)}, u32[]{:S(2)}) collective-permute-start(bf16[128,512]{1,0:T(8,128)(2,1)S(1)} %get-tuple-element.82), channel_id=1, source_target_pairs={{0,6},{1,7},{2,4},{3,5},{4,2},{5,3},{6,0},{7,1},{8,14},{9,15},{10,... | collective-permute-start | bytes 393224 | tf_op jit(solution)/shard_map/ppermute | solution.py:517
  48.7 11.2 %collective-permute-start.13 = (bf16[128,512]{1,0:T(8,128)(2,1)S(1)}, bf16[128,512]{1,0:T(8,128)(2,1)S(1)}, u32[]{:S(2)}, u32[]{:S(2)}) collective-permute-start(bf16[128,512]{1,0:T(8,128)(2,1)S(1)} %get-tuple-element.83), channel_id=1, source_target_pairs={{0,4},{1,5},{2,6},{3,7},{4,0},{5,1},{6,2},{7,3},{8,12},{9,13},{10,... | collective-permute-start | bytes 393224 | tf_op jit(solution)/shard_map/ppermute | solution.py:517
  52.7 7.5 %collective-permute-start.14 = (bf16[128,512]{1,0:T(8,128)(2,1)S(1)}, bf16[128,512]{1,0:T(8,128)(2,1)S(1)}, u32[]{:S(2)}, u32[]{:S(2)}) collective-permute-start(bf16[128,512]{1,0:T(8,128)(2,1)S(1)} %get-tuple-element.84), channel_id=1, source_target_pairs={{0,2},{1,3},{2,0},{3,1},{4,6},{5,7},{6,4},{7,5},{8,10},{9,11},{10,... | collective-permute-start | bytes 393224 | tf_op jit(solution)/shard_map/ppermute | solution.py:517
  54.6 7.9 %collective-permute-start.20 = (bf16[512,256]{1,0:T(8,128)(2,1)S(1)}, bf16[512,256]{1,0:T(8,128)(2,1)S(1)}, u32[]{:S(2)}, u32[]{:S(2)}) collective-permute-start(bf16[512,256]{1,0:T(8,128)(2,1)S(1)} %get-tuple-element.96), channel_id=1, source_target_pairs={{0,1},{1,0},{2,3},{3,2},{4,5},{5,4},{6,7},{7,6},{8,9},{9,8},{10,11... | collective-permute-start | bytes 786440 | tf_op jit(solution)/shard_map/ppermute | solution.py:522
  59.0 5.3 %collective-permute-start.24 = (bf16[320,128]{1,0:T(8,128)(2,1)S(1)}, bf16[320,128]{1,0:T(8,128)(2,1)S(1)}, u32[]{:S(2)}, u32[]{:S(2)}) collective-permute-start(bf16[320,128]{1,0:T(8,128)(2,1)S(1)} %get-tuple-element.103), channel_id=1, source_target_pairs={{0,1},{1,0},{2,3},{3,2},{4,5},{5,4},{6,7},{7,6},{8,9},{9,8},{10,11... | collective-permute-start | bytes 245768 | tf_op jit(solution)/shard_map/ppermute | solution.py:522
  64.8 6.9 %collective-permute-start.25 = (bf16[272,512]{1,0:T(8,128)(2,1)S(1)}, bf16[272,512]{1,0:T(8,128)(2,1)S(1)}, u32[]{:S(2)}, u32[]{:S(2)}) collective-permute-start(bf16[272,512]{1,0:T(8,128)(2,1)S(1)} %get-tuple-element.105), channel_id=1, source_target_pairs={{0,1},{1,0},{2,3},{3,2},{4,5},{5,4},{6,7},{7,6},{8,9},{9,8},{10,11... | collective-permute-start | bytes 835592 | tf_op jit(solution)/shard_map/ppermute | solution.py:522
  66.9 6.9 %collective-permute-start.21 = (bf16[128,512]{1,0:T(8,128)(2,1)S(1)}, bf16[128,512]{1,0:T(8,128)(2,1)S(1)}, u32[]{:S(2)}, u32[]{:S(2)}) collective-permute-start(bf16[128,512]{1,0:T(8,128)(2,1)S(1)} %get-tuple-element.98), channel_id=1, source_target_pairs={{0,6},{1,7},{2,4},{3,5},{4,2},{5,3},{6,0},{7,1},{8,14},{9,15},{10,... | collective-permute-start | bytes 393224 | tf_op jit(solution)/shard_map/ppermute | solution.py:517
  70.2 7.6 %collective-permute-start.22 = (bf16[128,512]{1,0:T(8,128)(2,1)S(1)}, bf16[128,512]{1,0:T(8,128)(2,1)S(1)}, u32[]{:S(2)}, u32[]{:S(2)}) collective-permute-start(bf16[128,512]{1,0:T(8,128)(2,1)S(1)} %get-tuple-element.99), channel_id=1, source_target_pairs={{0,4},{1,5},{2,6},{3,7},{4,0},{5,1},{6,2},{7,3},{8,12},{9,13},{10,... | collective-permute-start | bytes 393224 | tf_op jit(solution)/shard_map/ppermute | solution.py:517
  71.2 6.7 %collective-permute-start.23 = (bf16[128,512]{1,0:T(8,128)(2,1)S(1)}, bf16[128,512]{1,0:T(8,128)(2,1)S(1)}, u32[]{:S(2)}, u32[]{:S(2)}) collective-permute-start(bf16[128,512]{1,0:T(8,128)(2,1)S(1)} %get-tuple-element.100), channel_id=1, source_target_pairs={{0,2},{1,3},{2,0},{3,1},{4,6},{5,7},{6,4},{7,5},{8,10},{9,11},{10,... | collective-permute-start | bytes 393224 | tf_op jit(solution)/shard_map/ppermute | solution.py:517
  71.7 18.6 %collective-permute-start.19 = (bf16[128,2048]{1,0:T(8,128)(2,1)S(1)}, bf16[128,2048]{1,0:T(8,128)(2,1)S(1)}, u32[]{:S(2)}, u32[]{:S(2)}) collective-permute-start(bf16[128,2048]{1,0:T(8,128)(2,1)S(1)} %join_out.1.refs_5_), channel_id=1, source_target_pairs={{0,8},{8,16},{16,24},{24,0},{1,9},{9,17},{17,25},{25,1},{2,10},{10... | collective-permute-start | bytes 1572872 | tf_op jit(solution)/shard_map/ppermute | solution.py:629
  78.6 11.8 %collective-permute-start.26 = (bf16[128,2048]{1,0:T(8,128)(2,1)S(1)}, bf16[128,2048]{1,0:T(8,128)(2,1)S(1)}, u32[]{:S(2)}, u32[]{:S(2)}) collective-permute-start(bf16[128,2048]{1,0:T(8,128)(2,1)S(1)} %input_grad.1.refs_4_), channel_id=1, source_target_pairs={{0,24},{8,0},{16,8},{24,16},{1,25},{9,1},{17,9},{25,17},{2,26},{10... | collective-permute-start | bytes 1572872 | tf_op jit(solution)/shard_map/ppermute | solution.py:634
  78.6 7.4 %collective-permute-start.27 = (bf16[352,128]{1,0:T(8,128)(2,1)S(1)}, bf16[352,128]{1,0:T(8,128)(2,1)S(1)}, u32[]{:S(2)}, u32[]{:S(2)}) collective-permute-start(bf16[352,128]{1,0:T(8,128)(2,1)S(1)} %get-tuple-element.107), channel_id=1, source_target_pairs={{0,6},{1,7},{2,4},{3,5},{4,2},{5,3},{6,0},{7,1},{8,14},{9,15},{10,... | collective-permute-start | bytes 270344 | tf_op jit(solution)/shard_map/ppermute | solution.py:517
  82.1 7.3 %collective-permute-start.28 = (bf16[352,128]{1,0:T(8,128)(2,1)S(1)}, bf16[352,128]{1,0:T(8,128)(2,1)S(1)}, u32[]{:S(2)}, u32[]{:S(2)}) collective-permute-start(bf16[352,128]{1,0:T(8,128)(2,1)S(1)} %get-tuple-element.108), channel_id=1, source_target_pairs={{0,4},{1,5},{2,6},{3,7},{4,0},{5,1},{6,2},{7,3},{8,12},{9,13},{10,... | collective-permute-start | bytes 270344 | tf_op jit(solution)/shard_map/ppermute | solution.py:517
  82.1 7.3 %collective-permute-start.29 = (bf16[352,128]{1,0:T(8,128)(2,1)S(1)}, bf16[352,128]{1,0:T(8,128)(2,1)S(1)}, u32[]{:S(2)}, u32[]{:S(2)}) collective-permute-start(bf16[352,128]{1,0:T(8,128)(2,1)S(1)} %get-tuple-element.109), channel_id=1, source_target_pairs={{0,2},{1,3},{2,0},{3,1},{4,6},{5,7},{6,4},{7,5},{8,10},{9,11},{10,... | collective-permute-start | bytes 270344 | tf_op jit(solution)/shard_map/ppermute | solution.py:517

commit v4 on v3

--- a/solution.py
+++ b/solution.py
@@ -12,7 +12,7 @@
 LANE = 128
 SUB = 16
 EPS = 1e-06
-COST = {"norm_act": 3.0, "norm_saved": 6.0, "mix_act": 1.0, "take_grad": 8.0, "join_out": 2.0}
+COST = {"relay": 3, "norm_saved": 3.0, "take_grad": 6.0, "far_act": 3, "norm_act": 2, "weight_sum": 2, "join_weight": 5.9}
 VMEM = 48 * 1024 * 1024
 
 
@@ -67,7 +67,7 @@
             without_waits,
             out_shape=list(outs),
             in_specs=[anywhere] * direct + [vmem] * (nin - direct) + [anywhere] * nwait,
-            out_specs=[anywhere] * direct + [vmem] * (len(outs) - direct),
+            out_specs=[pl.BlockSpec(memory_space=pltpu.HBM)] * direct + [vmem] * (len(outs) - direct),
             scratch_shapes=list(scratch),
             compiler_params=pltpu.CompilerParams(vmem_limit_bytes=VMEM),
             cost_estimate=pl.CostEstimate(
@@ -388,9 +388,10 @@
         outs[d][...] = adj_norm_ref[rows((place ^ far(d, nb)) * t, t), :].astype(BF)
 
 
-def weight_grad_body(nb, ngroups, normin_ref, adj_proj_ref, gain_part_ref, own_ref, *refs):
-    group, _ = position(ngroups)
-    sends, gw_ref = refs[: ngroups - 1], refs[ngroups - 1]
+def weight_grad_body(nb, ngroups, normin_ref, adj_proj_ref, gain_part_ref, *refs):
+    group, _ = position(ngroups)
+    tiles, own_ref = refs[: ngroups - 1], refs[ngroups - 1]
+    sends, gw_ref = refs[ngroups : 2 * ngroups - 1], refs[2 * ngroups - 1]
     share, bd = own_ref.shape
     r = share // nb
     gw_ref[...] = mm(normin_ref[...], adj_proj_ref[...], 0, 0)
@@ -403,21 +404,20 @@
         for e in range(1, ngroups):
             sends[e - 1][at, :] = gw_ref[rows((c * ngroups + (group ^ e)) * r, r), :].astype(BF)
     for e in range(1, ngroups):
-        sends[e - 1][share:, :] = tile
-
-
-def sum_tiles_body(*refs):
-    total = refs[0][...].astype(F32)
-    for ref in refs[1:-1]:
-        total = total + ref[...].astype(F32)
-    refs[-1][...] = total.astype(BF)
+        sends[e - 1][share : share + SUB, :] = tile
+        high = tiles[e - 1].shape[0] * LANE // bd
+        for ch in range(bd // LANE):
+            sends[e - 1][share + SUB :, ch * LANE : (ch + 1) * LANE] = tiles[e - 1][
+                ch * high : (ch + 1) * high, :
+            ]
 
 
 def weight_sum_body(nb, ngroups, bl, ext, own_ref, gain_part_ref, *refs):
     group, place = position(ngroups)
     recvs, tiles_ref = refs[: ngroups - 1], refs[ngroups - 1]
+    high = tiles_ref.shape[0] * LANE // own_ref.shape[1]
     outs = refs[ngroups : ngroups + nb]
-    total_ref, gains_ref = refs[ngroups + nb :]
+    total_ref, gains_ref, sums_ref = refs[ngroups + nb :]
     share, bd = own_ref.shape
     chunks = bd // LANE
     r = share // nb
@@ -425,9 +425,15 @@
     gains_ref[group] = gain_part_ref[...]
     for e in range(1, ngroups):
         total = total + recvs[e - 1][:share, :].astype(F32)
-        three = recvs[e - 1][share:, :].astype(F32)
+        three = recvs[e - 1][share : share + SUB, :].astype(F32)
         gains_ref[group ^ e] = three[0:1] + three[1:2] + three[2:3]
     total_ref[...] = total.astype(BF)
+    for ch in range(chunks):
+        at = slice(ch * high, (ch + 1) * high)
+        tile_sum = tiles_ref[at, :].astype(F32)
+        for recv in recvs:
+            tile_sum = tile_sum + recv[share + SUB :, ch * LANE : (ch + 1) * LANE].astype(F32)
+        sums_ref[at, :] = tile_sum.astype(BF)
     gain = gains_ref[0]
     for g in range(1, ngroups):
         gain = gain + gains_ref[g]
@@ -439,8 +445,8 @@
         for ch in range(chunks):
             outs[d][ch * r : (ch + 1) * r, :] = total_ref[rows(to * r, r), ch * LANE : (ch + 1) * LANE]
         at = chunks * r
-        outs[d][at : at + bl, :] = tiles_ref[rows(to * bl, bl), :]
-        outs[d][at + bl : at + bl + ext, :] = tiles_ref[
+        outs[d][at : at + bl, :] = sums_ref[rows(to * bl, bl), :]
+        outs[d][at + bl : at + bl + ext, :] = sums_ref[
             pl.ds(pl.multiple_of(nb * bl + to * ext, ext), ext), :
         ]
         outs[d][at + bl + ext :, :] = tile
@@ -470,7 +476,8 @@
 
 def join_weight_body(nb, ngroups, *refs):
     _, block = position(ngroups)
-    gw_ref, gain_ref, left_out, right_out, by_block = refs[nb:]
+    gw_ref, gain_ref, left_out, right_out, done_ref, by_block = refs[nb:]
+    done_ref[...] = jnp.zeros(done_ref.shape, done_ref.dtype)
     r, _, bd = gw_ref.shape
     chunks = bd // LANE
     na, bl, _ = left_out.shape
@@ -497,6 +504,15 @@
         gw_ref[:, k, :] = by_block[k]
 
 
+def arrived_body(out_ref):
+    out_ref[...] = jnp.zeros(out_ref.shape, out_ref.dtype)
+
+
+def store_body(x_ref, out_ref, done_ref):
+    out_ref[...] = x_ref[...]
+    done_ref[...] = jnp.zeros(done_ref.shape, done_ref.dtype)
+
+
 def shards(act_in, saved_in, grad_in, gain, weight, left_blocks, right_blocks):
     nseq = lax.axis_size("seq")
     npipe = lax.axis_size("pipe")
@@ -524,6 +540,20 @@
     def gathered(block):
         return [block] + [across(block, e) for e in range(1, ngroups)]
 
+    def handed(parts, step):
+        return [
+            lax.ppermute(
+                parts[d],
+                ("pipe", "seq"),
+                [
+                    (p * nseq + s, (p + step) % npipe * nseq + (s ^ (far(d, nb) * ngroups)))
+                    for p in range(npipe)
+                    for s in range(nseq)
+                ],
+            )
+            for d in range(nb)
+        ]
+
     def exchanged(parts):
         return list(parts[:1]) + [across(parts[e], e) for e in range(1, ngroups)]
 
@@ -549,47 +579,34 @@
     w_msgs = run("pack_weight", part(pack_weight_body, nb, ngroups), [sds((r4 + bl + ext, LANE))] * nb)(
         jnp.transpose(weight[0], (1, 0, 2)), left_blocks[0], right_blocks[0]
     )
-    cur_msgs = run("pack_act", part(pack, True), scaled_msgs)(act_in[0], after=w_msgs[:1])
     grad_shares = run(
         "split_grad", part(split_features_body, nb, ngroups), [sds((nb, t, part_of))] * ngroups
-    )(grad_in[0], after=cur_msgs[:1])
+    )(grad_in[0], after=w_msgs[:1])
     sto_msgs = run("pack_saved", part(pack, True), scaled_msgs)(saved_in[0], after=grad_shares[:1])
     early = sto_msgs[:1]
-    w_msgs, cur_msgs = within(w_msgs), within(cur_msgs)
-    grad_shares = exchanged(grad_shares)
-    sto_msgs = within(sto_msgs)
+    w_msgs, grad_shares, sto_msgs = within(w_msgs), exchanged(grad_shares), within(sto_msgs)
     (relay,) = run("relay", part(relay_body, nb, ngroups, r4, ext), [sds((nb * (r4 + ext + bl), LANE))])(
         *w_msgs, after=early
     )
     relays = gathered(relay)
-    (cur_normin,) = run("norm_act", norm, tokens)(*cur_msgs, gain, after=[relay])
+    grad_msgs = run("pack_grad", part(pack_shares_body, nb, ngroups), [sds((ngroups * t, part_of))] * nb)(
+        *grad_shares, after=[relay]
+    )
+    (sto_normin,) = run("norm_saved", norm, tokens)(*sto_msgs, gain, after=grad_msgs[:1])
     wk, mq, bd_left = run(
         "assemble",
         part(assemble_body, nb, ngroups, r, ext, bl),
         [sds((bd, bd)), sds((nq, n, n)), sds((nseq, LANE, LANE))],
         [pltpu.VMEM((nseq, ext, LANE), BF)],
-    )(*relays, after=[cur_normin])
-    cur_proj, cur_first = run("project_act", part(project_body, nb, ngroups), tokens * 2)(
-        cur_normin, wk, bd_left
-    )
-    cur_firsts = gathered(cur_first)
-    grad_msgs = run("pack_grad", part(pack_shares_body, nb, ngroups), [sds((ngroups * t, part_of))] * nb)(
-        *grad_shares, after=[cur_first]
-    )
+    )(*relays, after=[sto_normin])
+    sto_shares = run("project_saved", part(project_shares_body, ngroups), shares)(sto_normin, wk)
+    cur_msgs = run("pack_act", part(pack, True), scaled_msgs)(act_in[0], after=sto_shares[:1])
     grad_msgs = within(grad_msgs)
-    (sto_normin,) = run("norm_saved", norm, tokens)(*sto_msgs, gain, after=grad_msgs[:1])
-    sto_shares = run("project_saved", part(project_shares_body, ngroups), shares)(sto_normin, wk)
-    sto_wait = sto_shares[:1]
-    sto_shares = exchanged(sto_shares)
-    (cur_mixed,) = run(
-        "mix_act", part(mix_body, ngroups, bl), tokens, scratch([sds((nq, n, bd))])
-    )(*cur_firsts, mq, after=sto_wait)
-    out_parts = run("output", part(output_body, nb, ngroups), pieces)(cur_mixed, cur_proj, *cur_msgs)
-    (grad,) = run("take_grad", part(take_grad_body, nb, ngroups), every)(*grad_msgs, after=out_parts[:1])
+    (grad,) = run("take_grad", part(take_grad_body, nb, ngroups), every)(*grad_msgs, after=cur_msgs[:1])
+    sto_shares, cur_msgs = exchanged(sto_shares), within(cur_msgs)
     sto_proj, sto_f, sto_mixed = run(
         "mix_saved", part(mix_shares_body, ngroups, bl), every + by_position + every, scratch(every)
     )(*sto_shares, mq, bd_left, after=[grad])
-    out_parts = within(out_parts)
     *adj_shares, adj_f, adj_first = run(
         "backward", part(backward_body, nb, ngroups, bl), shares + by_position + every, scratch(every)
     )(grad, sto_proj, sto_mixed, mq, bd_left)
@@ -602,37 +619,46 @@
         scratch([sds((ngroups, nb * ext, LANE)), sds((ngroups, nb * bl, LANE))]),
     )(sto_f, adj_f, adj_first, sto_proj, after=adj_wait)
     tiles_wait = tiles[:1]
-    tiles = exchanged(tiles)
-    (out,) = run("join_out", join, [sds((t, width))])(*out_parts, after=tiles_wait)
+    (act_arrived,) = run("far_act", arrived_body, [sds((8, LANE), F32)])(after=[*tiles_wait, *cur_msgs[1:3]])
     adj_proj, gain_part, *adj_parts = run(
         "adj_norm",
         part(adj_norm_body, nb, ngroups),
         tokens + [sds((1, bd), F32)] + pieces,
         scratch([sds((tg, bd), F32)]),
-    )(sto_normin, wk, gain, *adj_shares, after=[out])
+    )(sto_normin, wk, gain, *adj_shares, after=[act_arrived])
     adj_wait = adj_parts[:1]
     adj_parts = within(adj_parts)
-    (tile_sum,) = run("sum_tiles", sum_tiles_body, [sds((nb * (bl + ext), LANE))])(*tiles, after=adj_wait)
     own_gw, *sends = run(
         "weight_grad",
         part(weight_grad_body, nb, ngroups),
-        [sds((rows_of, bd), F32)] + [sds((rows_of + SUB, bd))] * (ngroups - 1),
+        [sds((rows_of, bd), F32)] + [sds((rows_of + SUB + nb * (bl + ext) // chunks, bd))] * (ngroups - 1),
         scratch([sds((bd, bd), F32)]),
-    )(sto_normin, adj_proj, gain_part, after=[tile_sum])
+    )(sto_normin, adj_proj, gain_part, *tiles[1:], after=adj_wait)
     recvs = [across(sends[e - 1], e) for e in range(1, ngroups)]
+    (cur_normin,) = run("norm_act", norm, tokens)(*cur_msgs, gain, after=[own_gw])
+    cur_proj, cur_first = run("project_act", part(project_body, nb, ngroups), tokens * 2)(
+        cur_normin, wk, bd_left
+    )
+    cur_firsts = gathered(cur_first)
+    (adj_arrived,) = run("far_adj", arrived_body, [sds((8, LANE), F32)])(after=[cur_first, *adj_parts[1:3]])
     gw_parts = run(
         "weight_sum",
         part(weight_sum_body, nb, ngroups, bl, ext),
         [sds((r4 + bl + ext + SUB, LANE))] * nb,
-        scratch([sds((rows_of, bd)), sds((ngroups, 1, bd), F32)]),
-    )(own_gw, gain_part, *recvs, tile_sum)
-    handed_on = lax.ppermute(out, "pipe", [(p, (p + 1) % npipe) for p in range(npipe)])
+        scratch([sds((rows_of, bd)), sds((ngroups, 1, bd), F32), sds((nb * (bl + ext), LANE))]),
+    )(own_gw, gain_part, *recvs, tiles[0], after=[adj_arrived])
     (adj_x,) = run(
         "input_grad", part(input_grad_body, nb, ngroups), [sds((t, width))], scratch([sds((t, width), F32)])
     )(saved_in[0], grad_in[0], gain, *adj_parts, after=gw_parts[:1])
+    (cur_mixed,) = run(
+        "mix_act", part(mix_body, ngroups, bl), tokens, scratch([sds((nq, n, bd))])
+    )(*cur_firsts, mq, after=[adj_x])
     gw_parts = within(gw_parts)
+    out_parts = run("output", part(output_body, nb, ngroups), pieces)(cur_mixed, cur_proj, *cur_msgs)
+    out_wait = out_parts[:1]
+    out_parts = handed(out_parts, 1)
     grad_handed = lax.ppermute(adj_x, "pipe", [(p, (p - 1) % npipe) for p in range(npipe)])
-    weight_grad, gain_grad, left_grad, right_grad = run(
+    weight_grad, gain_grad, left_grad, right_grad, done = run(
         "join_weight",
         part(join_weight_body, nb, ngroups),
         [
@@ -640,9 +666,14 @@
             sds((1, width), F32),
             sds((left_blocks.shape[1], bl, bl), F32),
             sds((npos, ext, ext), F32),
+            sds((8, LANE), F32),
         ],
         scratch([sds((nb, r, bd), F32)]),
-    )(*gw_parts, after=[adj_x])
+    )(*gw_parts, after=out_wait)
+    grad_handed, done = run("store", store_body, [sds((t, width)), sds((8, LANE), F32)])(
+        grad_handed, after=[done]
+    )
+    (handed_on,) = run("join_out", join, [sds((t, width))])(*out_parts, after=[done])
     return (
         handed_on[None],
         grad_handed[None],

time: 92.1 us -> 89.9 us (0.976)
  starting transfers between devices: 50.5 us -> 44.7 us
  waiting for transfers between devices: 28.3 us -> 31.7 us
  Pallas kernels: 9.59 us -> 11.2 us
  local copies, waits for them, and re-layouts: 2.67 us -> 1.09 us
    ppermute x21 -> x18, starting transfers between devices: 39.7 us -> 28.5 us  [within(): lax.ppermute(parts[d], 'seq', [(s, s ^ far(d, nb) * ngroups) for s in ran...]
    ppermute x1 -> x4, starting transfers between devices: 0.01 us -> 5.29 us  [handed(): lax.ppermute(parts[d], ('pipe', 'seq'), [(p * nseq + s, (p + step) % npip...]
    ppermute x1 -> x4, waiting for transfers between devices: 0.01 us -> 5.14 us  [handed(): lax.ppermute(parts[d], ('pipe', 'seq'), [(p * nseq + s, (p + step) % npip...]
    ppermute x7 -> x6, waiting for transfers between devices: 3.22 us -> 0.78 us  [across(): return lax.ppermute(block, 'seq', [(s, s ^ e) for s in range(nseq)])]
    ppermute x1, waiting for transfers between devices: 0.01 us -> 1.7 us  [shards(): lax.ppermute(adj_x, 'pipe', [(p, (p - 1) % npipe) for p in range(npipe)])]
    pallas_call x24 -> x26, Pallas kernels: 9.59 us -> 11.2 us  [run(): pl.pallas_call(without_waits, out_shape=list(outs), in_specs=[anywhere] *...]
    unnamed x15 -> x13, local copies, waits for them, and re-layouts: 2.67 us -> 1.09 us
    ppermute x21 -> x18, waiting for transfers between devices: 25.1 us -> 24.1 us  [within(): lax.ppermute(parts[d], 'seq', [(s, s ^ far(d, nb) * ngroups) for s in ran...]
  transfers between devices with their start and end apart: 30 -> 29, of which waited for: 12 -> 9; matrix products, arithmetic and copies ran while one was open for 0% -> 0% of each run, Pallas kernels for 10% -> 11%
where the time goes in v4:
time: 89.9 us; the launch traced here: 89.6 us
  starting transfers between devices  44.7 us (50%)
  waiting for transfers between devices  31.7 us (35%)
  Pallas kernels  11.2 us (12%)
  local copies, waits for them, and re-layouts  1.09 us (1%)
    ppermute x18, starting transfers between devices, within(): lax.ppermute(parts[d], 'seq', [(s, s ^ far(d, nb) * ngroups) for s in ran...  28.5 us
    ppermute x18, waiting for transfers between devices, within(): lax.ppermute(parts[d], 'seq', [(s, s ^ far(d, nb) * ngroups) for s in ran...  24.1 us
    pallas_call x26, Pallas kernels, run(): pl.pallas_call(without_waits, out_shape=list(outs), in_specs=[anywhere] *...  11.2 us
    ppermute x6, starting transfers between devices, across(): return lax.ppermute(block, 'seq', [(s, s ^ e) for s in range(nseq)])  10.9 us
    ppermute x4, starting transfers between devices, handed(): lax.ppermute(parts[d], ('pipe', 'seq'), [(p * nseq + s, (p + step) % npip...  5.29 us
    ppermute x4, waiting for transfers between devices, handed(): lax.ppermute(parts[d], ('pipe', 'seq'), [(p * nseq + s, (p + step) % npip...  5.14 us
  transfers between devices with their start and end apart: 29, of which 9 were waited for; matrix products, arithmetic and copies ran while one was open for 0% of the time, Pallas kernels for 11%

profile of v4, /device:TPU:0, one launch (start us, length us, event | category | flops | bytes accessed | tf_op | source)
XLA Modules:
  0.0 89.6 jit_solution(6164814127900198792)
XLA Ops:
  0.7 1.1 %copy.15 = bf16[1,64,4,512]{3,1,2,0:T(8,128)(2,1)S(1)} copy(bf16[1,64,4,512]{3,2,1,0:T(4,128)(2,1)} %param.11) | data formatting | bytes 524288 | tf_op args[4]
  1.8 5.1 %collective-permute-start.4 = (bf16[336,128]{1,0:T(8,128)(2,1)S(1)}, bf16[336,128]{1,0:T(8,128)(2,1)S(1)}, u32[]{:S(2)}, u32[]{:S(2)}) collective-permute-start(bf16[336,128]{1,0:T(8,128)(2,1)S(1)} %get-tuple-element.70), channel_id=1, source_target_pairs={{0,6},{1,7},{2,4},{3,5},{4,2},{5,3},{6,0},{7,1},{8,14},{9,15},{10,... | collective-permute-start | bytes 258056 | tf_op jit(solution)/shard_map/ppermute | solution.py:533
  7.0 0.6 collective-permute-start.6
  7.6 0.4 split_grad.1
  8.1 1.7 %collective-permute-start.3 = (bf16[4,128,256]{2,1,0:T(8,128)(2,1)S(1)}, bf16[4,128,256]{2,1,0:T(8,128)(2,1)S(1)}, u32[]{:S(2)}, u32[]{:S(2)}) collective-permute-start(bf16[4,128,256]{2,1,0:T(8,128)(2,1)S(1)} %get-tuple-element.69), channel_id=1, source_target_pairs={{0,1},{1,0},{2,3},{3,2},{4,5},{5,4},{6,7},{7,6},{8,9},{9,8},{10,11... | collective-permute-start | bytes 786440 | tf_op jit(solution)/shard_map/ppermute | solution.py:538
  9.8 0.2 pack_saved.1
  10.0 3.7 %collective-permute-start = (bf16[528,128]{1,0:T(8,128)(2,1)S(1)}, bf16[528,128]{1,0:T(8,128)(2,1)S(1)}, u32[]{:S(2)}, u32[]{:S(2)}) collective-permute-start(bf16[528,128]{1,0:T(8,128)(2,1)S(1)} %get-tuple-element.66), channel_id=1, source_target_pairs={{0,6},{1,7},{2,4},{3,5},{4,2},{5,3},{6,0},{7,1},{8,14},{9,15},{10,... | collective-permute-start | bytes 405512 | tf_op jit(solution)/shard_map/ppermute | solution.py:533
  13.7 1.4 %collective-permute-start.1 = (bf16[528,128]{1,0:T(8,128)(2,1)S(1)}, bf16[528,128]{1,0:T(8,128)(2,1)S(1)}, u32[]{:S(2)}, u32[]{:S(2)}) collective-permute-start(bf16[528,128]{1,0:T(8,128)(2,1)S(1)} %get-tuple-element.67), channel_id=1, source_target_pairs={{0,4},{1,5},{2,6},{3,7},{4,0},{5,1},{6,2},{7,3},{8,12},{9,13},{10,... | collective-permute-start | bytes 405512 | tf_op jit(solution)/shard_map/ppermute | solution.py:533
  15.0 5.4 %collective-permute-done.5.refs_2_ = bf16[336,128]{1,0:T(8,128)(2,1)S(1)} collective-permute-done((bf16[336,128]{1,0:T(8,128)(2,1)S(1)}, bf16[336,128]{1,0:T(8,128)(2,1)S(1)}, u32[]{:S(2)}, u32[]{:S(2)}) %collective-permute-start.5) | collective-permute-done | bytes 86048 | tf_op jit(solution)/shard_map/ppermute | solution.py:533
  20.5 1.9 %collective-permute-start.7 = (bf16[1344,128]{1,0:T(8,128)(2,1)S(1)}, bf16[1344,128]{1,0:T(8,128)(2,1)S(1)}, u32[]{:S(2)}, u32[]{:S(2)}) collective-permute-start(bf16[1344,128]{1,0:T(8,128)(2,1)S(1)} %relay.1.refs_2_.refs_0_), channel_id=1, source_target_pairs={{0,1},{1,0},{2,3},{3,2},{4,5},{5,4},{6,7},{7,6},{8,9},{9,8},{10,11... | collective-permute-start | bytes 1032200 | tf_op jit(solution)/shard_map/ppermute | solution.py:538
  22.4 2.9 %collective-permute-start.11 = (bf16[256,256]{1,0:T(8,128)(2,1)S(1)}, bf16[256,256]{1,0:T(8,128)(2,1)S(1)}, u32[]{:S(2)}, u32[]{:S(2)}) collective-permute-start(bf16[256,256]{1,0:T(8,128)(2,1)S(1)} %get-tuple-element.80), channel_id=1, source_target_pairs={{0,6},{1,7},{2,4},{3,5},{4,2},{5,3},{6,0},{7,1},{8,14},{9,15},{10,... | collective-permute-start | bytes 393224 | tf_op jit(solution)/shard_map/ppermute | solution.py:533
  25.3 1.7 %collective-permute-start.12 = (bf16[256,256]{1,0:T(8,128)(2,1)S(1)}, bf16[256,256]{1,0:T(8,128)(2,1)S(1)}, u32[]{:S(2)}, u32[]{:S(2)}) collective-permute-start(bf16[256,256]{1,0:T(8,128)(2,1)S(1)} %get-tuple-element.81), channel_id=1, source_target_pairs={{0,4},{1,5},{2,6},{3,7},{4,0},{5,1},{6,2},{7,3},{8,12},{9,13},{10,... | collective-permute-start | bytes 393224 | tf_op jit(solution)/shard_map/ppermute | solution.py:533
  27.0 4.6 %collective-permute-done.1.refs_2_ = bf16[528,128]{1,0:T(8,128)(2,1)S(1)} collective-permute-done((bf16[528,128]{1,0:T(8,128)(2,1)S(1)}, bf16[528,128]{1,0:T(8,128)(2,1)S(1)}, u32[]{:S(2)}, u32[]{:S(2)}) %collective-permute-start.1) | collective-permute-done | bytes 135200 | tf_op jit(solution)/shard_map/ppermute | solution.py:533
  31.8 0.7 assemble.1
  32.5 0.7 project_saved.1
  33.3 2.2 %collective-permute-start.14 = (bf16[512,256]{1,0:T(8,128)(2,1)S(1)}, bf16[512,256]{1,0:T(8,128)(2,1)S(1)}, u32[]{:S(2)}, u32[]{:S(2)}) collective-permute-start(bf16[512,256]{1,0:T(8,128)(2,1)S(1)} %get-tuple-element.83), channel_id=1, source_target_pairs={{0,1},{1,0},{2,3},{3,2},{4,5},{5,4},{6,7},{7,6},{8,9},{9,8},{10,11... | collective-permute-start | bytes 786440 | tf_op jit(solution)/shard_map/ppermute | solution.py:538
  35.4 0.2 pack_act.1
  35.7 2.9 %collective-permute-start.8 = (bf16[528,128]{1,0:T(8,128)(2,1)S(1)}, bf16[528,128]{1,0:T(8,128)(2,1)S(1)}, u32[]{:S(2)}, u32[]{:S(2)}) collective-permute-start(bf16[528,128]{1,0:T(8,128)(2,1)S(1)} %get-tuple-element.77), channel_id=1, source_target_pairs={{0,6},{1,7},{2,4},{3,5},{4,2},{5,3},{6,0},{7,1},{8,14},{9,15},{10,... | collective-permute-start | bytes 405512 | tf_op jit(solution)/shard_map/ppermute | solution.py:533
  38.6 0.6 collective-permute-start.9
  39.2 1.6 %collective-permute-done.12.refs_2_ = bf16[256,256]{1,0:T(8,128)(2,1)S(1)} collective-permute-done((bf16[256,256]{1,0:T(8,128)(2,1)S(1)}, bf16[256,256]{1,0:T(8,128)(2,1)S(1)}, u32[]{:S(2)}, u32[]{:S(2)}) %collective-permute-start.12) | collective-permute-done | bytes 131104 | tf_op jit(solution)/shard_map/ppermute | solution.py:533
  40.9 0.6 mix_saved.1
  41.5 0.6 backward.1
  42.2 2.9 %collective-permute-start.15 = (bf16[512,256]{1,0:T(8,128)(2,1)S(1)}, bf16[512,256]{1,0:T(8,128)(2,1)S(1)}, u32[]{:S(2)}, u32[]{:S(2)}) collective-permute-start(bf16[512,256]{1,0:T(8,128)(2,1)S(1)} %get-tuple-element.89), channel_id=1, source_target_pairs={{0,1},{1,0},{2,3},{3,2},{4,5},{5,4},{6,7},{7,6},{8,9},{9,8},{10,11... | collective-permute-start | bytes 786440 | tf_op jit(solution)/shard_map/ppermute | solution.py:538
  45.0 0.9 %factor_grads.1 = (bf16[320,128]{1,0:T(8,128)(2,1)S(1)}, bf16[320,128]{1,0:T(8,128)(2,1)S(1)}) custom-call(bf16[4,256,256]{2,1,0:T(8,128)(2,1)S(1)} %get-tuple-element.90.refs_0_, bf16[4,256,256]{2,1,0:T(8,128)(2,1)S(1)} %get-tuple-element.91.refs_1_, bf16[1024,256]{1,0:T(8,128)(2,1)S(1)} %get-tuple-element.92.refs_2_, ...), custom_call_target="tpu_custom_call" | custom-call | tf_op jit(solution)/shard_map/factor_grads/pallas_call | solution.py:66
  46.0 2.6 %collective-permute-done.9.refs_2_.refs_4_ = bf16[528,128]{1,0:T(8,128)(2,1)S(1)} collective-permute-done((bf16[528,128]{1,0:T(8,128)(2,1)S(1)}, bf16[528,128]{1,0:T(8,128)(2,1)S(1)}, u32[]{:S(2)}, u32[]{:S(2)}) %collective-permute-start.9) | collective-permute-done | bytes 135200 | tf_op jit(solution)/shard_map/ppermute | solution.py:533
  48.6 0.8 collective-permute-done.15.refs_4_
  49.4 0.8 adj_norm.1
  50.2 0.5 weight_grad.1
  50.8 2.1 %collective-permute-start.20 = (bf16[352,512]{1,0:T(8,128)(2,1)S(1)}, bf16[352,512]{1,0:T(8,128)(2,1)S(1)}, u32[]{:S(2)}, u32[]{:S(2)}) collective-permute-start(bf16[352,512]{1,0:T(8,128)(2,1)S(1)} %get-tuple-element.103), channel_id=1, source_target_pairs={{0,1},{1,0},{2,3},{3,2},{4,5},{5,4},{6,7},{7,6},{8,9},{9,8},{10,11... | collective-permute-start | bytes 1081352 | tf_op jit(solution)/shard_map/ppermute | solution.py:538
  53.1 0.6 project_act.1
  53.8 2.7 %collective-permute-start.17 = (bf16[128,512]{1,0:T(8,128)(2,1)S(1)}, bf16[128,512]{1,0:T(8,128)(2,1)S(1)}, u32[]{:S(2)}, u32[]{:S(2)}) collective-permute-start(bf16[128,512]{1,0:T(8,128)(2,1)S(1)} %get-tuple-element.100), channel_id=1, source_target_pairs={{0,6},{1,7},{2,4},{3,5},{4,2},{5,3},{6,0},{7,1},{8,14},{9,15},{10,... | collective-permute-start | bytes 393224 | tf_op jit(solution)/shard_map/ppermute | solution.py:533
  56.5 2.0 %collective-permute-start.18 = (bf16[128,512]{1,0:T(8,128)(2,1)S(1)}, bf16[128,512]{1,0:T(8,128)(2,1)S(1)}, u32[]{:S(2)}, u32[]{:S(2)}) collective-permute-start(bf16[128,512]{1,0:T(8,128)(2,1)S(1)} %get-tuple-element.101), channel_id=1, source_target_pairs={{0,4},{1,5},{2,6},{3,7},{4,0},{5,1},{6,2},{7,3},{8,12},{9,13},{10,... | collective-permute-start | bytes 393224 | tf_op jit(solution)/shard_map/ppermute | solution.py:533
  58.4 0.5 collective-permute-start.19
  58.9 2.8 %collective-permute-done.17.refs_1_.refs_4_ = bf16[128,512]{1,0:T(8,128)(2,1)S(1)} collective-permute-done((bf16[128,512]{1,0:T(8,128)(2,1)S(1)}, bf16[128,512]{1,0:T(8,128)(2,1)S(1)}, u32[]{:S(2)}, u32[]{:S(2)}) %collective-permute-start.17) | collective-permute-done | bytes 131104 | tf_op jit(solution)/shard_map/ppermute | solution.py:533
  61.6 7.1 %collective-permute-done.18.refs_2_.refs_5_ = bf16[128,512]{1,0:T(8,128)(2,1)S(1)} collective-permute-done((bf16[128,512]{1,0:T(8,128)(2,1)S(1)}, bf16[128,512]{1,0:T(8,128)(2,1)S(1)}, u32[]{:S(2)}, u32[]{:S(2)}) %collective-permute-start.18) | collective-permute-done | bytes 131104 | tf_op jit(solution)/shard_map/ppermute | solution.py:533
  68.9 0.6 collective-permute-start.26
  69.5 3.9 %collective-permute-start.28 = (bf16[352,128]{1,0:T(8,128)(2,1)S(1)}, bf16[352,128]{1,0:T(8,128)(2,1)S(1)}, u32[]{:S(2)}, u32[]{:S(2)}) collective-permute-start(bf16[352,128]{1,0:T(8,128)(2,1)S(1)} %get-tuple-element.112), channel_id=1, source_target_pairs={{0,2},{1,3},{2,0},{3,1},{4,6},{5,7},{6,4},{7,5},{8,10},{9,11},{10,... | collective-permute-start | bytes 270344 | tf_op jit(solution)/shard_map/ppermute | solution.py:533
  73.4 0.7 input_grad.1.refs_3_
  74.2 0.4 mix_act.1.refs_0_
  74.6 0.2 output.1
  74.8 0.7 collective-permute-start.22
  75.5 1.6 %collective-permute-start.23 = (bf16[128,512]{1,0:T(8,128)(2,1)S(1)}, bf16[128,512]{1,0:T(8,128)(2,1)S(1)}, u32[]{:S(2)}, u32[]{:S(2)}) collective-permute-start(bf16[128,512]{1,0:T(8,128)(2,1)S(1)} %get-tuple-element.108), channel_id=1, source_target_pairs={{0,12},{1,13},{2,14},{3,15},{4,8},{5,9},{6,10},{7,11},{8,20},{9,21... | collective-permute-start | bytes 393224 | tf_op jit(solution)/shard_map/ppermute | solution.py:545
  77.1 3.0 %collective-permute-start.24 = (bf16[128,512]{1,0:T(8,128)(2,1)S(1)}, bf16[128,512]{1,0:T(8,128)(2,1)S(1)}, u32[]{:S(2)}, u32[]{:S(2)}) collective-permute-start(bf16[128,512]{1,0:T(8,128)(2,1)S(1)} %get-tuple-element.109), channel_id=1, source_target_pairs={{0,10},{1,11},{2,8},{3,9},{4,14},{5,15},{6,12},{7,13},{8,18},{9,19... | collective-permute-start | bytes 393224 | tf_op jit(solution)/shard_map/ppermute | solution.py:545
  80.1 1.0 %join_weight.1 = (f32[64,4,512]{2,1,0:T(4,128)}, f32[1,2048]{1,0:T(1,128)}, f32[2,64,64]{2,1,0:T(8,128)}, f32[8,16,16]{2,1,0:T(8,128)}, f32[8,128]{1,0:T(8,128)S(1)}) custom-call(bf16[352,128]{1,0:T(8,128)(2,1)S(1)} %get-tuple-element.104.refs_7_.refs_0_, bf16[352,128]{1,0:T(8,128)(2,1)S(1)} %collective-permute-done.26.refs_1_, ...), custom_call_target="tpu_custom_call" | custom-call | flops 5900000256 | tf_op jit(solution)/shard_map/join_weight/pallas_call | solution.py:66
  81.0 1.7 %collective-permute-done.25.refs_0_ = bf16[128,2048]{1,0:T(8,128)(2,1)S(1)} collective-permute-done((bf16[128,2048]{1,0:T(8,128)(2,1)S(1)}, bf16[128,2048]{1,0:T(8,128)(2,1)S(1)}, u32[]{:S(2)}, u32[]{:S(2)}) %collective-permute-start.25) | collective-permute-done | bytes 524320 | tf_op jit(solution)/shard_map/ppermute | solution.py:660
  82.7 0.8 store.1
  83.6 5.1 %collective-permute-done.23.refs_2_ = bf16[128,512]{1,0:T(8,128)(2,1)S(1)} collective-permute-done((bf16[128,512]{1,0:T(8,128)(2,1)S(1)}, bf16[128,512]{1,0:T(8,128)(2,1)S(1)}, u32[]{:S(2)}, u32[]{:S(2)}) %collective-permute-start.23) | collective-permute-done | bytes 131104 | tf_op jit(solution)/shard_map/ppermute | solution.py:545
  88.7 0.8 join_out.1
  (49 shorter events, 1.0 us)
Async XLA Ops:
  0.6 1.1 %copy-start.5 = (bf16[1,8,16,16]{3,2,1,0:T(8,128)(2,1)S(1)}, bf16[1,8,16,16]{3,2,1,0:T(8,128)(2,1)}, u32[]{:S(2)}) copy-start(bf16[1,8,16,16]{3,2,1,0:T(8,128)(2,1)} %param.13) | copy-start | bytes 12292
  0.6 1.1 %copy-start.4 = (bf16[1,2,64,64]{3,2,1,0:T(8,128)(2,1)S(1)}, bf16[1,2,64,64]{3,2,1,0:T(8,128)(2,1)}, u32[]{:S(2)}) copy-start(bf16[1,2,64,64]{3,2,1,0:T(8,128)(2,1)} %param.12) | copy-start | bytes 49156
  0.7 7.0 %copy-start.1 = (bf16[1,128,2048]{2,1,0:T(8,128)(2,1)S(1)}, bf16[1,128,2048]{2,1,0:T(8,128)(2,1)}, u32[]{:S(2)}) copy-start(bf16[1,128,2048]{2,1,0:T(8,128)(2,1)} %param.9) | copy-start | bytes 1572868
  1.7 8.1 %copy-start = (bf16[1,128,2048]{2,1,0:T(8,128)(2,1)S(1)}, bf16[1,128,2048]{2,1,0:T(8,128)(2,1)}, u32[]{:S(2)}) copy-start(bf16[1,128,2048]{2,1,0:T(8,128)(2,1)} %param.8) | copy-start | bytes 1572868
  1.8 11.8 %collective-permute-start.4 = (bf16[336,128]{1,0:T(8,128)(2,1)S(1)}, bf16[336,128]{1,0:T(8,128)(2,1)S(1)}, u32[]{:S(2)}, u32[]{:S(2)}) collective-permute-start(bf16[336,128]{1,0:T(8,128)(2,1)S(1)} %get-tuple-element.70), channel_id=1, source_target_pairs={{0,6},{1,7},{2,4},{3,5},{4,2},{5,3},{6,0},{7,1},{8,14},{9,15},{10,... | collective-permute-start | bytes 258056 | tf_op jit(solution)/shard_map/ppermute | solution.py:533
  7.0 13.5 %collective-permute-start.5 = (bf16[336,128]{1,0:T(8,128)(2,1)S(1)}, bf16[336,128]{1,0:T(8,128)(2,1)S(1)}, u32[]{:S(2)}, u32[]{:S(2)}) collective-permute-start(bf16[336,128]{1,0:T(8,128)(2,1)S(1)} %get-tuple-element.71), channel_id=1, source_target_pairs={{0,4},{1,5},{2,6},{3,7},{4,0},{5,1},{6,2},{7,3},{8,12},{9,13},{10,... | collective-permute-start | bytes 258056 | tf_op jit(solution)/shard_map/ppermute | solution.py:533
  7.0 13.5 %collective-permute-start.6 = (bf16[336,128]{1,0:T(8,128)(2,1)S(1)}, bf16[336,128]{1,0:T(8,128)(2,1)S(1)}, u32[]{:S(2)}, u32[]{:S(2)}) collective-permute-start(bf16[336,128]{1,0:T(8,128)(2,1)S(1)} %get-tuple-element.72), channel_id=1, source_target_pairs={{0,2},{1,3},{2,0},{3,1},{4,6},{5,7},{6,4},{7,5},{8,10},{9,11},{10,... | collective-permute-start | bytes 258056 | tf_op jit(solution)/shard_map/ppermute | solution.py:533
  8.1 14.3 %collective-permute-start.3 = (bf16[4,128,256]{2,1,0:T(8,128)(2,1)S(1)}, bf16[4,128,256]{2,1,0:T(8,128)(2,1)S(1)}, u32[]{:S(2)}, u32[]{:S(2)}) collective-permute-start(bf16[4,128,256]{2,1,0:T(8,128)(2,1)S(1)} %get-tuple-element.69), channel_id=1, source_target_pairs={{0,1},{1,0},{2,3},{3,2},{4,5},{5,4},{6,7},{7,6},{8,9},{9,8},{10,11... | collective-permute-start | bytes 786440 | tf_op jit(solution)/shard_map/ppermute | solution.py:538
  10.0 15.3 %collective-permute-start = (bf16[528,128]{1,0:T(8,128)(2,1)S(1)}, bf16[528,128]{1,0:T(8,128)(2,1)S(1)}, u32[]{:S(2)}, u32[]{:S(2)}) collective-permute-start(bf16[528,128]{1,0:T(8,128)(2,1)S(1)} %get-tuple-element.66), channel_id=1, source_target_pairs={{0,6},{1,7},{2,4},{3,5},{4,2},{5,3},{6,0},{7,1},{8,14},{9,15},{10,... | collective-permute-start | bytes 405512 | tf_op jit(solution)/shard_map/ppermute | solution.py:533
  13.7 17.9 %collective-permute-start.1 = (bf16[528,128]{1,0:T(8,128)(2,1)S(1)}, bf16[528,128]{1,0:T(8,128)(2,1)S(1)}, u32[]{:S(2)}, u32[]{:S(2)}) collective-permute-start(bf16[528,128]{1,0:T(8,128)(2,1)S(1)} %get-tuple-element.67), channel_id=1, source_target_pairs={{0,4},{1,5},{2,6},{3,7},{4,0},{5,1},{6,2},{7,3},{8,12},{9,13},{10,... | collective-permute-start | bytes 405512 | tf_op jit(solution)/shard_map/ppermute | solution.py:533
  20.4 11.2 %collective-permute-start.2 = (bf16[528,128]{1,0:T(8,128)(2,1)S(1)}, bf16[528,128]{1,0:T(8,128)(2,1)S(1)}, u32[]{:S(2)}, u32[]{:S(2)}) collective-permute-start(bf16[528,128]{1,0:T(8,128)(2,1)S(1)} %get-tuple-element.68), channel_id=1, source_target_pairs={{0,2},{1,3},{2,0},{3,1},{4,6},{5,7},{6,4},{7,5},{8,10},{9,11},{10,... | collective-permute-start | bytes 405512 | tf_op jit(solution)/shard_map/ppermute | solution.py:533
  20.5 11.1 %copy-start.3 = (f32[1,2048]{1,0:T(1,128)S(1)}, f32[1,2048]{1,0:T(1,128)}, u32[]{:S(2)}) copy-start(f32[1,2048]{1,0:T(1,128)} %refs_2_.3) | copy-start | bytes 24580
  20.5 11.3 %collective-permute-start.7 = (bf16[1344,128]{1,0:T(8,128)(2,1)S(1)}, bf16[1344,128]{1,0:T(8,128)(2,1)S(1)}, u32[]{:S(2)}, u32[]{:S(2)}) collective-permute-start(bf16[1344,128]{1,0:T(8,128)(2,1)S(1)} %relay.1.refs_2_.refs_0_), channel_id=1, source_target_pairs={{0,1},{1,0},{2,3},{3,2},{4,5},{5,4},{6,7},{7,6},{8,9},{9,8},{10,11... | collective-permute-start | bytes 1032200 | tf_op jit(solution)/shard_map/ppermute | solution.py:538
  22.4 16.2 %collective-permute-start.11 = (bf16[256,256]{1,0:T(8,128)(2,1)S(1)}, bf16[256,256]{1,0:T(8,128)(2,1)S(1)}, u32[]{:S(2)}, u32[]{:S(2)}) collective-permute-start(bf16[256,256]{1,0:T(8,128)(2,1)S(1)} %get-tuple-element.80), channel_id=1, source_target_pairs={{0,6},{1,7},{2,4},{3,5},{4,2},{5,3},{6,0},{7,1},{8,14},{9,15},{10,... | collective-permute-start | bytes 393224 | tf_op jit(solution)/shard_map/ppermute | solution.py:533
  25.3 15.5 %collective-permute-start.12 = (bf16[256,256]{1,0:T(8,128)(2,1)S(1)}, bf16[256,256]{1,0:T(8,128)(2,1)S(1)}, u32[]{:S(2)}, u32[]{:S(2)}) collective-permute-start(bf16[256,256]{1,0:T(8,128)(2,1)S(1)} %get-tuple-element.81), channel_id=1, source_target_pairs={{0,4},{1,5},{2,6},{3,7},{4,0},{5,1},{6,2},{7,3},{8,12},{9,13},{10,... | collective-permute-start | bytes 393224 | tf_op jit(solution)/shard_map/ppermute | solution.py:533
  31.6 9.3 %collective-permute-start.13 = (bf16[256,256]{1,0:T(8,128)(2,1)S(1)}, bf16[256,256]{1,0:T(8,128)(2,1)S(1)}, u32[]{:S(2)}, u32[]{:S(2)}) collective-permute-start(bf16[256,256]{1,0:T(8,128)(2,1)S(1)} %get-tuple-element.82), channel_id=1, source_target_pairs={{0,2},{1,3},{2,0},{3,1},{4,6},{5,7},{6,4},{7,5},{8,10},{9,11},{10,... | collective-permute-start | bytes 393224 | tf_op jit(solution)/shard_map/ppermute | solution.py:533
  32.5 2.9 %copy-start.2 = (bf16[1,128,2048]{2,1,0:T(8,128)(2,1)S(1)}, bf16[1,128,2048]{2,1,0:T(8,128)(2,1)}, u32[]{:S(2)}) copy-start(bf16[1,128,2048]{2,1,0:T(8,128)(2,1)} %param.7) | copy-start | bytes 1572868
  33.3 7.6 %collective-permute-start.14 = (bf16[512,256]{1,0:T(8,128)(2,1)S(1)}, bf16[512,256]{1,0:T(8,128)(2,1)S(1)}, u32[]{:S(2)}, u32[]{:S(2)}) collective-permute-start(bf16[512,256]{1,0:T(8,128)(2,1)S(1)} %get-tuple-element.83), channel_id=1, source_target_pairs={{0,1},{1,0},{2,3},{3,2},{4,5},{5,4},{6,7},{7,6},{8,9},{9,8},{10,11... | collective-permute-start | bytes 786440 | tf_op jit(solution)/shard_map/ppermute | solution.py:538
  35.7 10.3 %collective-permute-start.8 = (bf16[528,128]{1,0:T(8,128)(2,1)S(1)}, bf16[528,128]{1,0:T(8,128)(2,1)S(1)}, u32[]{:S(2)}, u32[]{:S(2)}) collective-permute-start(bf16[528,128]{1,0:T(8,128)(2,1)S(1)} %get-tuple-element.77), channel_id=1, source_target_pairs={{0,6},{1,7},{2,4},{3,5},{4,2},{5,3},{6,0},{7,1},{8,14},{9,15},{10,... | collective-permute-start | bytes 405512 | tf_op jit(solution)/shard_map/ppermute | solution.py:533
  38.6 10.0 %collective-permute-start.9 = (bf16[528,128]{1,0:T(8,128)(2,1)S(1)}, bf16[528,128]{1,0:T(8,128)(2,1)S(1)}, u32[]{:S(2)}, u32[]{:S(2)}) collective-permute-start(bf16[528,128]{1,0:T(8,128)(2,1)S(1)} %get-tuple-element.78), channel_id=1, source_target_pairs={{0,4},{1,5},{2,6},{3,7},{4,0},{5,1},{6,2},{7,3},{8,12},{9,13},{10,... | collective-permute-start | bytes 405512 | tf_op jit(solution)/shard_map/ppermute | solution.py:533
  40.8 12.0 %collective-permute-start.10 = (bf16[528,128]{1,0:T(8,128)(2,1)S(1)}, bf16[528,128]{1,0:T(8,128)(2,1)S(1)}, u32[]{:S(2)}, u32[]{:S(2)}) collective-permute-start(bf16[528,128]{1,0:T(8,128)(2,1)S(1)} %get-tuple-element.79), channel_id=1, source_target_pairs={{0,2},{1,3},{2,0},{3,1},{4,6},{5,7},{6,4},{7,5},{8,10},{9,11},{10,... | collective-permute-start | bytes 405512 | tf_op jit(solution)/shard_map/ppermute | solution.py:533
  42.2 7.2 %collective-permute-start.15 = (bf16[512,256]{1,0:T(8,128)(2,1)S(1)}, bf16[512,256]{1,0:T(8,128)(2,1)S(1)}, u32[]{:S(2)}, u32[]{:S(2)}) collective-permute-start(bf16[512,256]{1,0:T(8,128)(2,1)S(1)} %get-tuple-element.89), channel_id=1, source_target_pairs={{0,1},{1,0},{2,3},{3,2},{4,5},{5,4},{6,7},{7,6},{8,9},{9,8},{10,11... | collective-permute-start | bytes 786440 | tf_op jit(solution)/shard_map/ppermute | solution.py:538
  50.8 18.0 %collective-permute-start.20 = (bf16[352,512]{1,0:T(8,128)(2,1)S(1)}, bf16[352,512]{1,0:T(8,128)(2,1)S(1)}, u32[]{:S(2)}, u32[]{:S(2)}) collective-permute-start(bf16[352,512]{1,0:T(8,128)(2,1)S(1)} %get-tuple-element.103), channel_id=1, source_target_pairs={{0,1},{1,0},{2,3},{3,2},{4,5},{5,4},{6,7},{7,6},{8,9},{9,8},{10,11... | collective-permute-start | bytes 1081352 | tf_op jit(solution)/shard_map/ppermute | solution.py:538
  53.7 20.5 %collective-permute-start.16 = (bf16[512,512]{1,0:T(8,128)(2,1)S(1)}, bf16[512,512]{1,0:T(8,128)(2,1)S(1)}, u32[]{:S(2)}, u32[]{:S(2)}) collective-permute-start(bf16[512,512]{1,0:T(8,128)(2,1)S(1)} %get-tuple-element.99.refs_0_), channel_id=1, source_target_pairs={{0,1},{1,0},{2,3},{3,2},{4,5},{5,4},{6,7},{7,6},{8,9},{9,8},{10,11... | collective-permute-start | bytes 1572872 | tf_op jit(solution)/shard_map/ppermute | solution.py:538
  53.8 7.9 %collective-permute-start.17 = (bf16[128,512]{1,0:T(8,128)(2,1)S(1)}, bf16[128,512]{1,0:T(8,128)(2,1)S(1)}, u32[]{:S(2)}, u32[]{:S(2)}) collective-permute-start(bf16[128,512]{1,0:T(8,128)(2,1)S(1)} %get-tuple-element.100), channel_id=1, source_target_pairs={{0,6},{1,7},{2,4},{3,5},{4,2},{5,3},{6,0},{7,1},{8,14},{9,15},{10,... | collective-permute-start | bytes 393224 | tf_op jit(solution)/shard_map/ppermute | solution.py:533
  56.5 12.3 %collective-permute-start.18 = (bf16[128,512]{1,0:T(8,128)(2,1)S(1)}, bf16[128,512]{1,0:T(8,128)(2,1)S(1)}, u32[]{:S(2)}, u32[]{:S(2)}) collective-permute-start(bf16[128,512]{1,0:T(8,128)(2,1)S(1)} %get-tuple-element.101), channel_id=1, source_target_pairs={{0,4},{1,5},{2,6},{3,7},{4,0},{5,1},{6,2},{7,3},{8,12},{9,13},{10,... | collective-permute-start | bytes 393224 | tf_op jit(solution)/shard_map/ppermute | solution.py:533
  58.4 15.0 %collective-permute-start.19 = (bf16[128,512]{1,0:T(8,128)(2,1)S(1)}, bf16[128,512]{1,0:T(8,128)(2,1)S(1)}, u32[]{:S(2)}, u32[]{:S(2)}) collective-permute-start(bf16[128,512]{1,0:T(8,128)(2,1)S(1)} %get-tuple-element.102), channel_id=1, source_target_pairs={{0,2},{1,3},{2,0},{3,1},{4,6},{5,7},{6,4},{7,5},{8,10},{9,11},{10,... | collective-permute-start | bytes 393224 | tf_op jit(solution)/shard_map/ppermute | solution.py:533
  68.9 6.5 %collective-permute-start.26 = (bf16[352,128]{1,0:T(8,128)(2,1)S(1)}, bf16[352,128]{1,0:T(8,128)(2,1)S(1)}, u32[]{:S(2)}, u32[]{:S(2)}) collective-permute-start(bf16[352,128]{1,0:T(8,128)(2,1)S(1)} %get-tuple-element.110), channel_id=1, source_target_pairs={{0,6},{1,7},{2,4},{3,5},{4,2},{5,3},{6,0},{7,1},{8,14},{9,15},{10,... | collective-permute-start | bytes 270344 | tf_op jit(solution)/shard_map/ppermute | solution.py:533
  69.5 7.6 %collective-permute-start.27 = (bf16[352,128]{1,0:T(8,128)(2,1)S(1)}, bf16[352,128]{1,0:T(8,128)(2,1)S(1)}, u32[]{:S(2)}, u32[]{:S(2)}) collective-permute-start(bf16[352,128]{1,0:T(8,128)(2,1)S(1)} %get-tuple-element.111), channel_id=1, source_target_pairs={{0,4},{1,5},{2,6},{3,7},{4,0},{5,1},{6,2},{7,3},{8,12},{9,13},{10,... | collective-permute-start | bytes 270344 | tf_op jit(solution)/shard_map/ppermute | solution.py:533
  69.5 10.6 %collective-permute-start.28 = (bf16[352,128]{1,0:T(8,128)(2,1)S(1)}, bf16[352,128]{1,0:T(8,128)(2,1)S(1)}, u32[]{:S(2)}, u32[]{:S(2)}) collective-permute-start(bf16[352,128]{1,0:T(8,128)(2,1)S(1)} %get-tuple-element.112), channel_id=1, source_target_pairs={{0,2},{1,3},{2,0},{3,1},{4,6},{5,7},{6,4},{7,5},{8,10},{9,11},{10,... | collective-permute-start | bytes 270344 | tf_op jit(solution)/shard_map/ppermute | solution.py:533
  74.1 8.7 %collective-permute-start.25 = (bf16[128,2048]{1,0:T(8,128)(2,1)S(1)}, bf16[128,2048]{1,0:T(8,128)(2,1)S(1)}, u32[]{:S(2)}, u32[]{:S(2)}) collective-permute-start(bf16[128,2048]{1,0:T(8,128)(2,1)S(1)} %input_grad.1.refs_3_), channel_id=1, source_target_pairs={{0,24},{8,0},{16,8},{24,16},{1,25},{9,1},{17,9},{25,17},{2,26},{10... | collective-permute-start | bytes 1572872 | tf_op jit(solution)/shard_map/ppermute | solution.py:660
  74.8 8.8 %collective-permute-start.22 = (bf16[128,512]{1,0:T(8,128)(2,1)S(1)}, bf16[128,512]{1,0:T(8,128)(2,1)S(1)}, u32[]{:S(2)}, u32[]{:S(2)}) collective-permute-start(bf16[128,512]{1,0:T(8,128)(2,1)S(1)} %get-tuple-element.107), channel_id=1, source_target_pairs={{0,14},{1,15},{2,12},{3,13},{4,10},{5,11},{6,8},{7,9},{8,22},{9,23... | collective-permute-start | bytes 393224 | tf_op jit(solution)/shard_map/ppermute | solution.py:545
  75.5 13.2 %collective-permute-start.23 = (bf16[128,512]{1,0:T(8,128)(2,1)S(1)}, bf16[128,512]{1,0:T(8,128)(2,1)S(1)}, u32[]{:S(2)}, u32[]{:S(2)}) collective-permute-start(bf16[128,512]{1,0:T(8,128)(2,1)S(1)} %get-tuple-element.108), channel_id=1, source_target_pairs={{0,12},{1,13},{2,14},{3,15},{4,8},{5,9},{6,10},{7,11},{8,20},{9,21... | collective-permute-start | bytes 393224 | tf_op jit(solution)/shard_map/ppermute | solution.py:545
  77.1 11.6 %collective-permute-start.24 = (bf16[128,512]{1,0:T(8,128)(2,1)S(1)}, bf16[128,512]{1,0:T(8,128)(2,1)S(1)}, u32[]{:S(2)}, u32[]{:S(2)}) collective-permute-start(bf16[128,512]{1,0:T(8,128)(2,1)S(1)} %get-tuple-element.109), channel_id=1, source_target_pairs={{0,10},{1,11},{2,8},{3,9},{4,14},{5,15},{6,12},{7,13},{8,18},{9,19... | collective-permute-start | bytes 393224 | tf_op jit(solution)/shard_map/ppermute | solution.py:545
  80.1 8.6 %collective-permute-start.21 = (bf16[128,512]{1,0:T(8,128)(2,1)S(1)}, bf16[128,512]{1,0:T(8,128)(2,1)S(1)}, u32[]{:S(2)}, u32[]{:S(2)}) collective-permute-start(bf16[128,512]{1,0:T(8,128)(2,1)S(1)} %get-tuple-element.106.refs_4_), channel_id=1, source_target_pairs={{0,8},{1,9},{2,10},{3,11},{4,12},{5,13},{6,14},{7,15},{8,16},{9,17... | collective-permute-start | bytes 393224 | tf_op jit(solution)/shard_map/ppermute | solution.py:545

commit v5 on v4

--- a/solution.py
+++ b/solution.py
@@ -12,7 +12,7 @@
 LANE = 128
 SUB = 16
 EPS = 1e-06
-COST = {"relay": 3, "norm_saved": 3.0, "take_grad": 6.0, "far_act": 3, "norm_act": 2, "weight_sum": 2, "join_weight": 5.9}
+COST = {"relay": 3, "norm_saved": 3.0, "take_grad": 6.0, "norm_act": 3, "join_weight": 3, "join_out": 5, "far_adj": 2}
 VMEM = 48 * 1024 * 1024
 
 
@@ -468,7 +468,8 @@
 
 def join_body(nb, ngroups, *refs):
     _, block = position(ngroups)
-    out = refs[nb]
+    out, done_ref = refs[nb:]
+    done_ref[...] = jnp.zeros(done_ref.shape, done_ref.dtype)
     bd = refs[0].shape[1]
     for d in range(nb):
         out[:, pl.ds(pl.multiple_of((block ^ far(d, nb)) * bd, LANE), bd)] = refs[d][...]
@@ -476,8 +477,7 @@
 
 def join_weight_body(nb, ngroups, *refs):
     _, block = position(ngroups)
-    gw_ref, gain_ref, left_out, right_out, done_ref, by_block = refs[nb:]
-    done_ref[...] = jnp.zeros(done_ref.shape, done_ref.dtype)
+    gw_ref, gain_ref, left_out, right_out, by_block = refs[nb:]
     r, _, bd = gw_ref.shape
     chunks = bd // LANE
     na, bl, _ = left_out.shape
@@ -619,13 +619,17 @@
         scratch([sds((ngroups, nb * ext, LANE)), sds((ngroups, nb * bl, LANE))]),
     )(sto_f, adj_f, adj_first, sto_proj, after=adj_wait)
     tiles_wait = tiles[:1]
-    (act_arrived,) = run("far_act", arrived_body, [sds((8, LANE), F32)])(after=[*tiles_wait, *cur_msgs[1:3]])
+    (cur_normin,) = run("norm_act", norm, tokens)(*cur_msgs, gain, after=tiles_wait)
+    cur_proj, cur_first = run("project_act", part(project_body, nb, ngroups), tokens * 2)(
+        cur_normin, wk, bd_left
+    )
+    cur_firsts = gathered(cur_first)
     adj_proj, gain_part, *adj_parts = run(
         "adj_norm",
         part(adj_norm_body, nb, ngroups),
         tokens + [sds((1, bd), F32)] + pieces,
         scratch([sds((tg, bd), F32)]),
-    )(sto_normin, wk, gain, *adj_shares, after=[act_arrived])
+    )(sto_normin, wk, gain, *adj_shares, after=[cur_first])
     adj_wait = adj_parts[:1]
     adj_parts = within(adj_parts)
     own_gw, *sends = run(
@@ -635,30 +639,31 @@
         scratch([sds((bd, bd), F32)]),
     )(sto_normin, adj_proj, gain_part, *tiles[1:], after=adj_wait)
     recvs = [across(sends[e - 1], e) for e in range(1, ngroups)]
-    (cur_normin,) = run("norm_act", norm, tokens)(*cur_msgs, gain, after=[own_gw])
-    cur_proj, cur_first = run("project_act", part(project_body, nb, ngroups), tokens * 2)(
-        cur_normin, wk, bd_left
-    )
-    cur_firsts = gathered(cur_first)
-    (adj_arrived,) = run("far_adj", arrived_body, [sds((8, LANE), F32)])(after=[cur_first, *adj_parts[1:3]])
+    (adj_arrived,) = run("far_adj", arrived_body, [sds((8, LANE), F32)])(after=[own_gw, *adj_parts[1:3]])
+    (cur_mixed,) = run(
+        "mix_act", part(mix_body, ngroups, bl), tokens, scratch([sds((nq, n, bd))])
+    )(*cur_firsts, mq, after=[adj_arrived])
+    out_parts = run("output", part(output_body, nb, ngroups), pieces)(cur_mixed, cur_proj, *cur_msgs)
+    (adj_x,) = run(
+        "input_grad", part(input_grad_body, nb, ngroups), [sds((t, width))], scratch([sds((t, width), F32)])
+    )(saved_in[0], grad_in[0], gain, *adj_parts, after=out_parts[:1])
     gw_parts = run(
         "weight_sum",
         part(weight_sum_body, nb, ngroups, bl, ext),
         [sds((r4 + bl + ext + SUB, LANE))] * nb,
         scratch([sds((rows_of, bd)), sds((ngroups, 1, bd), F32), sds((nb * (bl + ext), LANE))]),
-    )(own_gw, gain_part, *recvs, tiles[0], after=[adj_arrived])
-    (adj_x,) = run(
-        "input_grad", part(input_grad_body, nb, ngroups), [sds((t, width))], scratch([sds((t, width), F32)])
-    )(saved_in[0], grad_in[0], gain, *adj_parts, after=gw_parts[:1])
-    (cur_mixed,) = run(
-        "mix_act", part(mix_body, ngroups, bl), tokens, scratch([sds((nq, n, bd))])
-    )(*cur_firsts, mq, after=[adj_x])
+    )(own_gw, gain_part, *recvs, tiles[0], after=[adj_x])
+    gw_wait = gw_parts[:1]
     gw_parts = within(gw_parts)
-    out_parts = run("output", part(output_body, nb, ngroups), pieces)(cur_mixed, cur_proj, *cur_msgs)
-    out_wait = out_parts[:1]
     out_parts = handed(out_parts, 1)
     grad_handed = lax.ppermute(adj_x, "pipe", [(p, (p - 1) % npipe) for p in range(npipe)])
-    weight_grad, gain_grad, left_grad, right_grad, done = run(
+    handed_on, done = run("join_out", join, [sds((t, width)), sds((8, LANE), F32)])(
+        *out_parts, after=gw_wait
+    )
+    grad_handed, done = run("store", store_body, [sds((t, width)), sds((8, LANE), F32)])(
+        grad_handed, after=[done]
+    )
+    weight_grad, gain_grad, left_grad, right_grad = run(
         "join_weight",
         part(join_weight_body, nb, ngroups),
         [
@@ -666,14 +671,9 @@
             sds((1, width), F32),
             sds((left_blocks.shape[1], bl, bl), F32),
             sds((npos, ext, ext), F32),
-            sds((8, LANE), F32),
         ],
         scratch([sds((nb, r, bd), F32)]),
-    )(*gw_parts, after=out_wait)
-    grad_handed, done = run("store", store_body, [sds((t, width)), sds((8, LANE), F32)])(
-        grad_handed, after=[done]
-    )
-    (handed_on,) = run("join_out", join, [sds((t, width))])(*out_parts, after=[done])
+    )(*gw_parts, after=[done])
     return (
         handed_on[None],
         grad_handed[None],

time: 89.9 us -> 88.8 us (0.988)
  waiting for transfers between devices: 31.7 us -> 29.8 us
  starting transfers between devices: 44.7 us -> 45.7 us
    ppermute x18, starting transfers between devices: 28.5 us -> 25.7 us  [within(): lax.ppermute(parts[d], 'seq', [(s, s ^ far(d, nb) * ngroups) for s in ran...]
    ppermute x6, starting transfers between devices: 10.9 us -> 13.6 us  [across(): return lax.ppermute(block, 'seq', [(s, s ^ e) for s in range(nseq)])]
    ppermute x1, waiting for transfers between devices: 1.7 us -> 0.01 us  [shards(): lax.ppermute(adj_x, 'pipe', [(p, (p - 1) % npipe) for p in range(npipe)])]
    ppermute x4, waiting for transfers between devices: 5.14 us -> 6.44 us  [handed(): lax.ppermute(parts[d], ('pipe', 'seq'), [(p * nseq + s, (p + step) % npip...]
    ppermute x1, starting transfers between devices: 0.06 us -> 1.17 us  [shards(): lax.ppermute(adj_x, 'pipe', [(p, (p - 1) % npipe) for p in range(npipe)])]
    pallas_call x26 -> x25, Pallas kernels: 11.2 us -> 11.2 us  [run(): pl.pallas_call(without_waits, out_shape=list(outs), in_specs=[anywhere] *...]
  transfers between devices with their start and end apart: 29 -> 29, of which waited for: 9 -> 10; matrix products, arithmetic and copies ran while one was open for 0% -> 0% of each run, Pallas kernels for 11% -> 11%
where the time goes in v5:
time: 88.8 us; the launch traced here: 88.6 us
  starting transfers between devices  45.7 us (51%)
  waiting for transfers between devices  29.8 us (34%)
  Pallas kernels  11.2 us (13%)
  local copies, waits for them, and re-layouts  1.09 us (1%)
    ppermute x18, starting transfers between devices, within(): lax.ppermute(parts[d], 'seq', [(s, s ^ far(d, nb) * ngroups) for s in ran...  25.7 us
    ppermute x18, waiting for transfers between devices, within(): lax.ppermute(parts[d], 'seq', [(s, s ^ far(d, nb) * ngroups) for s in ran...  23.3 us
    ppermute x6, starting transfers between devices, across(): return lax.ppermute(block, 'seq', [(s, s ^ e) for s in range(nseq)])  13.6 us
    pallas_call x25, Pallas kernels, run(): pl.pallas_call(without_waits, out_shape=list(outs), in_specs=[anywhere] *...  11.2 us
    ppermute x4, waiting for transfers between devices, handed(): lax.ppermute(parts[d], ('pipe', 'seq'), [(p * nseq + s, (p + step) % npip...  6.44 us
    ppermute x4, starting transfers between devices, handed(): lax.ppermute(parts[d], ('pipe', 'seq'), [(p * nseq + s, (p + step) % npip...  5.17 us
  transfers between devices with their start and end apart: 29, of which 10 were waited for; matrix products, arithmetic and copies ran while one was open for 0% of the time, Pallas kernels for 11%

profile of v5, /device:TPU:0, one launch (start us, length us, event | category | flops | bytes accessed | tf_op | source)
XLA Modules:
  0.0 88.6 jit_solution(13622911627694647746)
XLA Ops:
  0.7 1.1 %copy.15 = bf16[1,64,4,512]{3,1,2,0:T(8,128)(2,1)S(1)} copy(bf16[1,64,4,512]{3,2,1,0:T(4,128)(2,1)} %param.11) | data formatting | bytes 524288 | tf_op args[4]
  1.8 5.1 %collective-permute-start.4 = (bf16[336,128]{1,0:T(8,128)(2,1)S(1)}, bf16[336,128]{1,0:T(8,128)(2,1)S(1)}, u32[]{:S(2)}, u32[]{:S(2)}) collective-permute-start(bf16[336,128]{1,0:T(8,128)(2,1)S(1)} %get-tuple-element.71), channel_id=1, source_target_pairs={{0,6},{1,7},{2,4},{3,5},{4,2},{5,3},{6,0},{7,1},{8,14},{9,15},{10,... | collective-permute-start | bytes 258056 | tf_op jit(solution)/shard_map/ppermute | solution.py:533
  7.0 0.6 collective-permute-start.6
  7.6 0.4 split_grad.1
  8.1 1.7 %collective-permute-start.3 = (bf16[4,128,256]{2,1,0:T(8,128)(2,1)S(1)}, bf16[4,128,256]{2,1,0:T(8,128)(2,1)S(1)}, u32[]{:S(2)}, u32[]{:S(2)}) collective-permute-start(bf16[4,128,256]{2,1,0:T(8,128)(2,1)S(1)} %get-tuple-element.70), channel_id=1, source_target_pairs={{0,1},{1,0},{2,3},{3,2},{4,5},{5,4},{6,7},{7,6},{8,9},{9,8},{10,11... | collective-permute-start | bytes 786440 | tf_op jit(solution)/shard_map/ppermute | solution.py:538
  9.8 0.2 pack_saved.1
  10.0 3.7 %collective-permute-start = (bf16[528,128]{1,0:T(8,128)(2,1)S(1)}, bf16[528,128]{1,0:T(8,128)(2,1)S(1)}, u32[]{:S(2)}, u32[]{:S(2)}) collective-permute-start(bf16[528,128]{1,0:T(8,128)(2,1)S(1)} %get-tuple-element.67), channel_id=1, source_target_pairs={{0,6},{1,7},{2,4},{3,5},{4,2},{5,3},{6,0},{7,1},{8,14},{9,15},{10,... | collective-permute-start | bytes 405512 | tf_op jit(solution)/shard_map/ppermute | solution.py:533
  13.7 1.4 %collective-permute-start.1 = (bf16[528,128]{1,0:T(8,128)(2,1)S(1)}, bf16[528,128]{1,0:T(8,128)(2,1)S(1)}, u32[]{:S(2)}, u32[]{:S(2)}) collective-permute-start(bf16[528,128]{1,0:T(8,128)(2,1)S(1)} %get-tuple-element.68), channel_id=1, source_target_pairs={{0,4},{1,5},{2,6},{3,7},{4,0},{5,1},{6,2},{7,3},{8,12},{9,13},{10,... | collective-permute-start | bytes 405512 | tf_op jit(solution)/shard_map/ppermute | solution.py:533
  15.0 5.4 %collective-permute-done.5.refs_2_ = bf16[336,128]{1,0:T(8,128)(2,1)S(1)} collective-permute-done((bf16[336,128]{1,0:T(8,128)(2,1)S(1)}, bf16[336,128]{1,0:T(8,128)(2,1)S(1)}, u32[]{:S(2)}, u32[]{:S(2)}) %collective-permute-start.5) | collective-permute-done | bytes 86048 | tf_op jit(solution)/shard_map/ppermute | solution.py:533
  20.5 1.9 %collective-permute-start.7 = (bf16[1344,128]{1,0:T(8,128)(2,1)S(1)}, bf16[1344,128]{1,0:T(8,128)(2,1)S(1)}, u32[]{:S(2)}, u32[]{:S(2)}) collective-permute-start(bf16[1344,128]{1,0:T(8,128)(2,1)S(1)} %relay.1.refs_2_.refs_0_), channel_id=1, source_target_pairs={{0,1},{1,0},{2,3},{3,2},{4,5},{5,4},{6,7},{7,6},{8,9},{9,8},{10,11... | collective-permute-start | bytes 1032200 | tf_op jit(solution)/shard_map/ppermute | solution.py:538
  22.4 2.9 %collective-permute-start.12 = (bf16[256,256]{1,0:T(8,128)(2,1)S(1)}, bf16[256,256]{1,0:T(8,128)(2,1)S(1)}, u32[]{:S(2)}, u32[]{:S(2)}) collective-permute-start(bf16[256,256]{1,0:T(8,128)(2,1)S(1)} %get-tuple-element.84), channel_id=1, source_target_pairs={{0,6},{1,7},{2,4},{3,5},{4,2},{5,3},{6,0},{7,1},{8,14},{9,15},{10,... | collective-permute-start | bytes 393224 | tf_op jit(solution)/shard_map/ppermute | solution.py:533
  25.3 1.7 %collective-permute-start.13 = (bf16[256,256]{1,0:T(8,128)(2,1)S(1)}, bf16[256,256]{1,0:T(8,128)(2,1)S(1)}, u32[]{:S(2)}, u32[]{:S(2)}) collective-permute-start(bf16[256,256]{1,0:T(8,128)(2,1)S(1)} %get-tuple-element.85), channel_id=1, source_target_pairs={{0,4},{1,5},{2,6},{3,7},{4,0},{5,1},{6,2},{7,3},{8,12},{9,13},{10,... | collective-permute-start | bytes 393224 | tf_op jit(solution)/shard_map/ppermute | solution.py:533
  27.0 4.6 %collective-permute-done.1.refs_2_ = bf16[528,128]{1,0:T(8,128)(2,1)S(1)} collective-permute-done((bf16[528,128]{1,0:T(8,128)(2,1)S(1)}, bf16[528,128]{1,0:T(8,128)(2,1)S(1)}, u32[]{:S(2)}, u32[]{:S(2)}) %collective-permute-start.1) | collective-permute-done | bytes 135200 | tf_op jit(solution)/shard_map/ppermute | solution.py:533
  31.8 0.7 assemble.1
  32.5 0.7 project_saved.1
  33.3 2.2 %collective-permute-start.11 = (bf16[512,256]{1,0:T(8,128)(2,1)S(1)}, bf16[512,256]{1,0:T(8,128)(2,1)S(1)}, u32[]{:S(2)}, u32[]{:S(2)}) collective-permute-start(bf16[512,256]{1,0:T(8,128)(2,1)S(1)} %get-tuple-element.81), channel_id=1, source_target_pairs={{0,1},{1,0},{2,3},{3,2},{4,5},{5,4},{6,7},{7,6},{8,9},{9,8},{10,11... | collective-permute-start | bytes 786440 | tf_op jit(solution)/shard_map/ppermute | solution.py:538
  35.7 2.9 %collective-permute-start.8 = (bf16[528,128]{1,0:T(8,128)(2,1)S(1)}, bf16[528,128]{1,0:T(8,128)(2,1)S(1)}, u32[]{:S(2)}, u32[]{:S(2)}) collective-permute-start(bf16[528,128]{1,0:T(8,128)(2,1)S(1)} %get-tuple-element.78), channel_id=1, source_target_pairs={{0,6},{1,7},{2,4},{3,5},{4,2},{5,3},{6,0},{7,1},{8,14},{9,15},{10,... | collective-permute-start | bytes 405512 | tf_op jit(solution)/shard_map/ppermute | solution.py:533
  38.6 0.6 collective-permute-start.9
  39.2 1.6 %collective-permute-done.13.refs_2_ = bf16[256,256]{1,0:T(8,128)(2,1)S(1)} collective-permute-done((bf16[256,256]{1,0:T(8,128)(2,1)S(1)}, bf16[256,256]{1,0:T(8,128)(2,1)S(1)}, u32[]{:S(2)}, u32[]{:S(2)}) %collective-permute-start.13) | collective-permute-done | bytes 131104 | tf_op jit(solution)/shard_map/ppermute | solution.py:533
  40.9 0.6 mix_saved.1
  41.5 0.6 backward.1
  42.2 2.9 %collective-permute-start.16 = (bf16[512,256]{1,0:T(8,128)(2,1)S(1)}, bf16[512,256]{1,0:T(8,128)(2,1)S(1)}, u32[]{:S(2)}, u32[]{:S(2)}) collective-permute-start(bf16[512,256]{1,0:T(8,128)(2,1)S(1)} %get-tuple-element.95), channel_id=1, source_target_pairs={{0,1},{1,0},{2,3},{3,2},{4,5},{5,4},{6,7},{7,6},{8,9},{9,8},{10,11... | collective-permute-start | bytes 786440 | tf_op jit(solution)/shard_map/ppermute | solution.py:538
  45.0 0.9 %factor_grads.1 = (bf16[320,128]{1,0:T(8,128)(2,1)S(1)}, bf16[320,128]{1,0:T(8,128)(2,1)S(1)}) custom-call(bf16[4,256,256]{2,1,0:T(8,128)(2,1)S(1)} %get-tuple-element.87.refs_0_, bf16[4,256,256]{2,1,0:T(8,128)(2,1)S(1)} %get-tuple-element.90.refs_1_, bf16[1024,256]{1,0:T(8,128)(2,1)S(1)} %get-tuple-element.91.refs_2_, ...), custom_call_target="tpu_custom_call" | custom-call | tf_op jit(solution)/shard_map/factor_grads/pallas_call | solution.py:66
  46.0 2.6 %collective-permute-done.9.refs_2_.refs_4_ = bf16[528,128]{1,0:T(8,128)(2,1)S(1)} collective-permute-done((bf16[528,128]{1,0:T(8,128)(2,1)S(1)}, bf16[528,128]{1,0:T(8,128)(2,1)S(1)}, u32[]{:S(2)}, u32[]{:S(2)}) %collective-permute-start.9) | collective-permute-done | bytes 135200 | tf_op jit(solution)/shard_map/ppermute | solution.py:533
  48.8 0.6 project_act.1
  49.4 2.6 %collective-permute-start.15 = (bf16[512,512]{1,0:T(8,128)(2,1)S(1)}, bf16[512,512]{1,0:T(8,128)(2,1)S(1)}, u32[]{:S(2)}, u32[]{:S(2)}) collective-permute-start(bf16[512,512]{1,0:T(8,128)(2,1)S(1)} %get-tuple-element.94.refs_5_.refs_0_), channel_id=1, source_target_pairs={{0,1},{1,0},{2,3},{3,2},{4,5},{5,4},{6,7},{7,6},{8,9},{9,8},{10,11... | collective-permute-start | bytes 1572872 | tf_op jit(solution)/shard_map/ppermute | solution.py:538
  52.0 0.8 adj_norm.1
  52.9 2.6 %collective-permute-start.17 = (bf16[128,512]{1,0:T(8,128)(2,1)S(1)}, bf16[128,512]{1,0:T(8,128)(2,1)S(1)}, u32[]{:S(2)}, u32[]{:S(2)}) collective-permute-start(bf16[128,512]{1,0:T(8,128)(2,1)S(1)} %get-tuple-element.101), channel_id=1, source_target_pairs={{0,6},{1,7},{2,4},{3,5},{4,2},{5,3},{6,0},{7,1},{8,14},{9,15},{10,... | collective-permute-start | bytes 393224 | tf_op jit(solution)/shard_map/ppermute | solution.py:533
  55.5 0.5 weight_grad.1
  56.0 2.3 %collective-permute-start.23 = (bf16[352,512]{1,0:T(8,128)(2,1)S(1)}, bf16[352,512]{1,0:T(8,128)(2,1)S(1)}, u32[]{:S(2)}, u32[]{:S(2)}) collective-permute-start(bf16[352,512]{1,0:T(8,128)(2,1)S(1)} %get-tuple-element.108), channel_id=1, source_target_pairs={{0,1},{1,0},{2,3},{3,2},{4,5},{5,4},{6,7},{7,6},{8,9},{9,8},{10,11... | collective-permute-start | bytes 1081352 | tf_op jit(solution)/shard_map/ppermute | solution.py:538
  58.4 0.5 collective-permute-start.24
  58.8 2.0 %collective-permute-done.17.refs_1_.refs_4_ = bf16[128,512]{1,0:T(8,128)(2,1)S(1)} collective-permute-done((bf16[128,512]{1,0:T(8,128)(2,1)S(1)}, bf16[128,512]{1,0:T(8,128)(2,1)S(1)}, u32[]{:S(2)}, u32[]{:S(2)}) %collective-permute-start.17) | collective-permute-done | bytes 131104 | tf_op jit(solution)/shard_map/ppermute | solution.py:533
  60.8 4.5 %collective-permute-done.18.refs_2_.refs_5_ = bf16[128,512]{1,0:T(8,128)(2,1)S(1)} collective-permute-done((bf16[128,512]{1,0:T(8,128)(2,1)S(1)}, bf16[128,512]{1,0:T(8,128)(2,1)S(1)}, u32[]{:S(2)}, u32[]{:S(2)}) %collective-permute-start.18) | collective-permute-done | bytes 131104 | tf_op jit(solution)/shard_map/ppermute | solution.py:533
  65.3 0.4 mix_act.1.refs_0_
  65.9 0.4 collective-permute-start.20
  66.3 1.4 %collective-permute-start.21 = (bf16[128,512]{1,0:T(8,128)(2,1)S(1)}, bf16[128,512]{1,0:T(8,128)(2,1)S(1)}, u32[]{:S(2)}, u32[]{:S(2)}) collective-permute-start(bf16[128,512]{1,0:T(8,128)(2,1)S(1)} %get-tuple-element.106), channel_id=1, source_target_pairs={{0,12},{1,13},{2,14},{3,15},{4,8},{5,9},{6,10},{7,11},{8,20},{9,21... | collective-permute-start | bytes 393224 | tf_op jit(solution)/shard_map/ppermute | solution.py:545
  67.7 2.0 %collective-permute-start.22 = (bf16[128,512]{1,0:T(8,128)(2,1)S(1)}, bf16[128,512]{1,0:T(8,128)(2,1)S(1)}, u32[]{:S(2)}, u32[]{:S(2)}) collective-permute-start(bf16[128,512]{1,0:T(8,128)(2,1)S(1)} %get-tuple-element.107), channel_id=1, source_target_pairs={{0,10},{1,11},{2,8},{3,9},{4,14},{5,15},{6,12},{7,13},{8,18},{9,19... | collective-permute-start | bytes 393224 | tf_op jit(solution)/shard_map/ppermute | solution.py:545
  69.8 1.3 %collective-permute-start.19 = (bf16[128,512]{1,0:T(8,128)(2,1)S(1)}, bf16[128,512]{1,0:T(8,128)(2,1)S(1)}, u32[]{:S(2)}, u32[]{:S(2)}) collective-permute-start(bf16[128,512]{1,0:T(8,128)(2,1)S(1)} %get-tuple-element.104.refs_7_), channel_id=1, source_target_pairs={{0,8},{1,9},{2,10},{3,11},{4,12},{5,13},{6,14},{7,15},{8,16},{9,17... | collective-permute-start | bytes 393224 | tf_op jit(solution)/shard_map/ppermute | solution.py:545
  71.1 0.7 input_grad.1.refs_4_
  71.8 1.2 %collective-permute-start.25 = (bf16[128,2048]{1,0:T(8,128)(2,1)S(1)}, bf16[128,2048]{1,0:T(8,128)(2,1)S(1)}, u32[]{:S(2)}, u32[]{:S(2)}) collective-permute-start(bf16[128,2048]{1,0:T(8,128)(2,1)S(1)} %input_grad.1.refs_4_), channel_id=1, source_target_pairs={{0,24},{8,0},{16,8},{24,16},{1,25},{9,1},{17,9},{25,17},{2,26},{10... | collective-permute-start | bytes 1572872 | tf_op jit(solution)/shard_map/ppermute | solution.py:659
  73.1 1.4 %collective-permute-done.20.refs_1_ = bf16[128,512]{1,0:T(8,128)(2,1)S(1)} collective-permute-done((bf16[128,512]{1,0:T(8,128)(2,1)S(1)}, bf16[128,512]{1,0:T(8,128)(2,1)S(1)}, u32[]{:S(2)}, u32[]{:S(2)}) %collective-permute-start.20) | collective-permute-done | bytes 131104 | tf_op jit(solution)/shard_map/ppermute | solution.py:545
  74.5 2.5 %collective-permute-start.26 = (bf16[352,128]{1,0:T(8,128)(2,1)S(1)}, bf16[352,128]{1,0:T(8,128)(2,1)S(1)}, u32[]{:S(2)}, u32[]{:S(2)}) collective-permute-start(bf16[352,128]{1,0:T(8,128)(2,1)S(1)} %get-tuple-element.114), channel_id=1, source_target_pairs={{0,6},{1,7},{2,4},{3,5},{4,2},{5,3},{6,0},{7,1},{8,14},{9,15},{10,... | collective-permute-start | bytes 270344 | tf_op jit(solution)/shard_map/ppermute | solution.py:533
  77.0 5.1 %collective-permute-done.21.refs_2_ = bf16[128,512]{1,0:T(8,128)(2,1)S(1)} collective-permute-done((bf16[128,512]{1,0:T(8,128)(2,1)S(1)}, bf16[128,512]{1,0:T(8,128)(2,1)S(1)}, u32[]{:S(2)}, u32[]{:S(2)}) %collective-permute-start.21) | collective-permute-done | bytes 131104 | tf_op jit(solution)/shard_map/ppermute | solution.py:545
  82.1 1.2 %collective-permute-start.28 = (bf16[352,128]{1,0:T(8,128)(2,1)S(1)}, bf16[352,128]{1,0:T(8,128)(2,1)S(1)}, u32[]{:S(2)}, u32[]{:S(2)}) collective-permute-start(bf16[352,128]{1,0:T(8,128)(2,1)S(1)} %get-tuple-element.116), channel_id=1, source_target_pairs={{0,2},{1,3},{2,0},{3,1},{4,6},{5,7},{6,4},{7,5},{8,10},{9,11},{10,... | collective-permute-start | bytes 270344 | tf_op jit(solution)/shard_map/ppermute | solution.py:533
  83.3 0.8 join_out.1
  84.1 0.8 store.1
  85.0 2.6 %collective-permute-done.27.refs_2_ = bf16[352,128]{1,0:T(8,128)(2,1)S(1)} collective-permute-done((bf16[352,128]{1,0:T(8,128)(2,1)S(1)}, bf16[352,128]{1,0:T(8,128)(2,1)S(1)}, u32[]{:S(2)}, u32[]{:S(2)}) %collective-permute-start.27) | collective-permute-done | bytes 90144 | tf_op jit(solution)/shard_map/ppermute | solution.py:533
  87.7 1.0 %join_weight.1 = (f32[64,4,512]{2,1,0:T(4,128)}, f32[1,2048]{1,0:T(1,128)}, f32[2,64,64]{2,1,0:T(8,128)}, f32[8,16,16]{2,1,0:T(8,128)}) custom-call(bf16[352,128]{1,0:T(8,128)(2,1)S(1)} %get-tuple-element.110.refs_4_.refs_0_, bf16[352,128]{1,0:T(8,128)(2,1)S(1)} %collective-permute-done.26.refs_1_, bf16[352,128]{1,0:T(8,128)(2,1)S(1)} %collective-permute-done.27.refs_2_, ...), custom_call_target="tpu_custom_call" | custom-call | flops 3000000000 | tf_op jit(solution)/shard_map/join_weight/pallas_call | solution.py:66
  (48 shorter events, 1.4 us)
Async XLA Ops:
  0.6 1.1 %copy-start.5 = (bf16[1,8,16,16]{3,2,1,0:T(8,128)(2,1)S(1)}, bf16[1,8,16,16]{3,2,1,0:T(8,128)(2,1)}, u32[]{:S(2)}) copy-start(bf16[1,8,16,16]{3,2,1,0:T(8,128)(2,1)} %param.13) | copy-start | bytes 12292
  0.6 1.1 %copy-start.4 = (bf16[1,2,64,64]{3,2,1,0:T(8,128)(2,1)S(1)}, bf16[1,2,64,64]{3,2,1,0:T(8,128)(2,1)}, u32[]{:S(2)}) copy-start(bf16[1,2,64,64]{3,2,1,0:T(8,128)(2,1)} %param.12) | copy-start | bytes 49156
  0.7 7.0 %copy-start.1 = (bf16[1,128,2048]{2,1,0:T(8,128)(2,1)S(1)}, bf16[1,128,2048]{2,1,0:T(8,128)(2,1)}, u32[]{:S(2)}) copy-start(bf16[1,128,2048]{2,1,0:T(8,128)(2,1)} %param.9) | copy-start | bytes 1572868
  1.7 8.1 %copy-start = (bf16[1,128,2048]{2,1,0:T(8,128)(2,1)S(1)}, bf16[1,128,2048]{2,1,0:T(8,128)(2,1)}, u32[]{:S(2)}) copy-start(bf16[1,128,2048]{2,1,0:T(8,128)(2,1)} %param.8) | copy-start | bytes 1572868
  1.8 11.8 %collective-permute-start.4 = (bf16[336,128]{1,0:T(8,128)(2,1)S(1)}, bf16[336,128]{1,0:T(8,128)(2,1)S(1)}, u32[]{:S(2)}, u32[]{:S(2)}) collective-permute-start(bf16[336,128]{1,0:T(8,128)(2,1)S(1)} %get-tuple-element.71), channel_id=1, source_target_pairs={{0,6},{1,7},{2,4},{3,5},{4,2},{5,3},{6,0},{7,1},{8,14},{9,15},{10,... | collective-permute-start | bytes 258056 | tf_op jit(solution)/shard_map/ppermute | solution.py:533
  7.0 13.5 %collective-permute-start.5 = (bf16[336,128]{1,0:T(8,128)(2,1)S(1)}, bf16[336,128]{1,0:T(8,128)(2,1)S(1)}, u32[]{:S(2)}, u32[]{:S(2)}) collective-permute-start(bf16[336,128]{1,0:T(8,128)(2,1)S(1)} %get-tuple-element.72), channel_id=1, source_target_pairs={{0,4},{1,5},{2,6},{3,7},{4,0},{5,1},{6,2},{7,3},{8,12},{9,13},{10,... | collective-permute-start | bytes 258056 | tf_op jit(solution)/shard_map/ppermute | solution.py:533
  7.0 13.5 %collective-permute-start.6 = (bf16[336,128]{1,0:T(8,128)(2,1)S(1)}, bf16[336,128]{1,0:T(8,128)(2,1)S(1)}, u32[]{:S(2)}, u32[]{:S(2)}) collective-permute-start(bf16[336,128]{1,0:T(8,128)(2,1)S(1)} %get-tuple-element.73), channel_id=1, source_target_pairs={{0,2},{1,3},{2,0},{3,1},{4,6},{5,7},{6,4},{7,5},{8,10},{9,11},{10,... | collective-permute-start | bytes 258056 | tf_op jit(solution)/shard_map/ppermute | solution.py:533
  8.1 14.3 %collective-permute-start.3 = (bf16[4,128,256]{2,1,0:T(8,128)(2,1)S(1)}, bf16[4,128,256]{2,1,0:T(8,128)(2,1)S(1)}, u32[]{:S(2)}, u32[]{:S(2)}) collective-permute-start(bf16[4,128,256]{2,1,0:T(8,128)(2,1)S(1)} %get-tuple-element.70), channel_id=1, source_target_pairs={{0,1},{1,0},{2,3},{3,2},{4,5},{5,4},{6,7},{7,6},{8,9},{9,8},{10,11... | collective-permute-start | bytes 786440 | tf_op jit(solution)/shard_map/ppermute | solution.py:538
  10.0 15.3 %collective-permute-start = (bf16[528,128]{1,0:T(8,128)(2,1)S(1)}, bf16[528,128]{1,0:T(8,128)(2,1)S(1)}, u32[]{:S(2)}, u32[]{:S(2)}) collective-permute-start(bf16[528,128]{1,0:T(8,128)(2,1)S(1)} %get-tuple-element.67), channel_id=1, source_target_pairs={{0,6},{1,7},{2,4},{3,5},{4,2},{5,3},{6,0},{7,1},{8,14},{9,15},{10,... | collective-permute-start | bytes 405512 | tf_op jit(solution)/shard_map/ppermute | solution.py:533
  13.7 17.9 %collective-permute-start.1 = (bf16[528,128]{1,0:T(8,128)(2,1)S(1)}, bf16[528,128]{1,0:T(8,128)(2,1)S(1)}, u32[]{:S(2)}, u32[]{:S(2)}) collective-permute-start(bf16[528,128]{1,0:T(8,128)(2,1)S(1)} %get-tuple-element.68), channel_id=1, source_target_pairs={{0,4},{1,5},{2,6},{3,7},{4,0},{5,1},{6,2},{7,3},{8,12},{9,13},{10,... | collective-permute-start | bytes 405512 | tf_op jit(solution)/shard_map/ppermute | solution.py:533
  20.4 11.2 %collective-permute-start.2 = (bf16[528,128]{1,0:T(8,128)(2,1)S(1)}, bf16[528,128]{1,0:T(8,128)(2,1)S(1)}, u32[]{:S(2)}, u32[]{:S(2)}) collective-permute-start(bf16[528,128]{1,0:T(8,128)(2,1)S(1)} %get-tuple-element.69), channel_id=1, source_target_pairs={{0,2},{1,3},{2,0},{3,1},{4,6},{5,7},{6,4},{7,5},{8,10},{9,11},{10,... | collective-permute-start | bytes 405512 | tf_op jit(solution)/shard_map/ppermute | solution.py:533
  20.5 11.1 %copy-start.3 = (f32[1,2048]{1,0:T(1,128)S(1)}, f32[1,2048]{1,0:T(1,128)}, u32[]{:S(2)}) copy-start(f32[1,2048]{1,0:T(1,128)} %refs_2_.3) | copy-start | bytes 24580
  20.5 11.3 %collective-permute-start.7 = (bf16[1344,128]{1,0:T(8,128)(2,1)S(1)}, bf16[1344,128]{1,0:T(8,128)(2,1)S(1)}, u32[]{:S(2)}, u32[]{:S(2)}) collective-permute-start(bf16[1344,128]{1,0:T(8,128)(2,1)S(1)} %relay.1.refs_2_.refs_0_), channel_id=1, source_target_pairs={{0,1},{1,0},{2,3},{3,2},{4,5},{5,4},{6,7},{7,6},{8,9},{9,8},{10,11... | collective-permute-start | bytes 1032200 | tf_op jit(solution)/shard_map/ppermute | solution.py:538
  22.4 16.2 %collective-permute-start.12 = (bf16[256,256]{1,0:T(8,128)(2,1)S(1)}, bf16[256,256]{1,0:T(8,128)(2,1)S(1)}, u32[]{:S(2)}, u32[]{:S(2)}) collective-permute-start(bf16[256,256]{1,0:T(8,128)(2,1)S(1)} %get-tuple-element.84), channel_id=1, source_target_pairs={{0,6},{1,7},{2,4},{3,5},{4,2},{5,3},{6,0},{7,1},{8,14},{9,15},{10,... | collective-permute-start | bytes 393224 | tf_op jit(solution)/shard_map/ppermute | solution.py:533
  25.3 15.5 %collective-permute-start.13 = (bf16[256,256]{1,0:T(8,128)(2,1)S(1)}, bf16[256,256]{1,0:T(8,128)(2,1)S(1)}, u32[]{:S(2)}, u32[]{:S(2)}) collective-permute-start(bf16[256,256]{1,0:T(8,128)(2,1)S(1)} %get-tuple-element.85), channel_id=1, source_target_pairs={{0,4},{1,5},{2,6},{3,7},{4,0},{5,1},{6,2},{7,3},{8,12},{9,13},{10,... | collective-permute-start | bytes 393224 | tf_op jit(solution)/shard_map/ppermute | solution.py:533
  31.6 9.3 %collective-permute-start.14 = (bf16[256,256]{1,0:T(8,128)(2,1)S(1)}, bf16[256,256]{1,0:T(8,128)(2,1)S(1)}, u32[]{:S(2)}, u32[]{:S(2)}) collective-permute-start(bf16[256,256]{1,0:T(8,128)(2,1)S(1)} %get-tuple-element.86), channel_id=1, source_target_pairs={{0,2},{1,3},{2,0},{3,1},{4,6},{5,7},{6,4},{7,5},{8,10},{9,11},{10,... | collective-permute-start | bytes 393224 | tf_op jit(solution)/shard_map/ppermute | solution.py:533
  32.5 2.9 %copy-start.2 = (bf16[1,128,2048]{2,1,0:T(8,128)(2,1)S(1)}, bf16[1,128,2048]{2,1,0:T(8,128)(2,1)}, u32[]{:S(2)}) copy-start(bf16[1,128,2048]{2,1,0:T(8,128)(2,1)} %param.7) | copy-start | bytes 1572868
  33.3 7.6 %collective-permute-start.11 = (bf16[512,256]{1,0:T(8,128)(2,1)S(1)}, bf16[512,256]{1,0:T(8,128)(2,1)S(1)}, u32[]{:S(2)}, u32[]{:S(2)}) collective-permute-start(bf16[512,256]{1,0:T(8,128)(2,1)S(1)} %get-tuple-element.81), channel_id=1, source_target_pairs={{0,1},{1,0},{2,3},{3,2},{4,5},{5,4},{6,7},{7,6},{8,9},{9,8},{10,11... | collective-permute-start | bytes 786440 | tf_op jit(solution)/shard_map/ppermute | solution.py:538
  35.7 10.3 %collective-permute-start.8 = (bf16[528,128]{1,0:T(8,128)(2,1)S(1)}, bf16[528,128]{1,0:T(8,128)(2,1)S(1)}, u32[]{:S(2)}, u32[]{:S(2)}) collective-permute-start(bf16[528,128]{1,0:T(8,128)(2,1)S(1)} %get-tuple-element.78), channel_id=1, source_target_pairs={{0,6},{1,7},{2,4},{3,5},{4,2},{5,3},{6,0},{7,1},{8,14},{9,15},{10,... | collective-permute-start | bytes 405512 | tf_op jit(solution)/shard_map/ppermute | solution.py:533
  38.6 10.0 %collective-permute-start.9 = (bf16[528,128]{1,0:T(8,128)(2,1)S(1)}, bf16[528,128]{1,0:T(8,128)(2,1)S(1)}, u32[]{:S(2)}, u32[]{:S(2)}) collective-permute-start(bf16[528,128]{1,0:T(8,128)(2,1)S(1)} %get-tuple-element.79), channel_id=1, source_target_pairs={{0,4},{1,5},{2,6},{3,7},{4,0},{5,1},{6,2},{7,3},{8,12},{9,13},{10,... | collective-permute-start | bytes 405512 | tf_op jit(solution)/shard_map/ppermute | solution.py:533
  40.8 7.8 %collective-permute-start.10 = (bf16[528,128]{1,0:T(8,128)(2,1)S(1)}, bf16[528,128]{1,0:T(8,128)(2,1)S(1)}, u32[]{:S(2)}, u32[]{:S(2)}) collective-permute-start(bf16[528,128]{1,0:T(8,128)(2,1)S(1)} %get-tuple-element.80), channel_id=1, source_target_pairs={{0,2},{1,3},{2,0},{3,1},{4,6},{5,7},{6,4},{7,5},{8,10},{9,11},{10,... | collective-permute-start | bytes 405512 | tf_op jit(solution)/shard_map/ppermute | solution.py:533
  42.2 9.9 %collective-permute-start.16 = (bf16[512,256]{1,0:T(8,128)(2,1)S(1)}, bf16[512,256]{1,0:T(8,128)(2,1)S(1)}, u32[]{:S(2)}, u32[]{:S(2)}) collective-permute-start(bf16[512,256]{1,0:T(8,128)(2,1)S(1)} %get-tuple-element.95), channel_id=1, source_target_pairs={{0,1},{1,0},{2,3},{3,2},{4,5},{5,4},{6,7},{7,6},{8,9},{9,8},{10,11... | collective-permute-start | bytes 786440 | tf_op jit(solution)/shard_map/ppermute | solution.py:538
  49.4 15.9 %collective-permute-start.15 = (bf16[512,512]{1,0:T(8,128)(2,1)S(1)}, bf16[512,512]{1,0:T(8,128)(2,1)S(1)}, u32[]{:S(2)}, u32[]{:S(2)}) collective-permute-start(bf16[512,512]{1,0:T(8,128)(2,1)S(1)} %get-tuple-element.94.refs_5_.refs_0_), channel_id=1, source_target_pairs={{0,1},{1,0},{2,3},{3,2},{4,5},{5,4},{6,7},{7,6},{8,9},{9,8},{10,11... | collective-permute-start | bytes 1572872 | tf_op jit(solution)/shard_map/ppermute | solution.py:538
  52.9 8.0 %collective-permute-start.17 = (bf16[128,512]{1,0:T(8,128)(2,1)S(1)}, bf16[128,512]{1,0:T(8,128)(2,1)S(1)}, u32[]{:S(2)}, u32[]{:S(2)}) collective-permute-start(bf16[128,512]{1,0:T(8,128)(2,1)S(1)} %get-tuple-element.101), channel_id=1, source_target_pairs={{0,6},{1,7},{2,4},{3,5},{4,2},{5,3},{6,0},{7,1},{8,14},{9,15},{10,... | collective-permute-start | bytes 393224 | tf_op jit(solution)/shard_map/ppermute | solution.py:533
  55.5 9.8 %collective-permute-start.18 = (bf16[128,512]{1,0:T(8,128)(2,1)S(1)}, bf16[128,512]{1,0:T(8,128)(2,1)S(1)}, u32[]{:S(2)}, u32[]{:S(2)}) collective-permute-start(bf16[128,512]{1,0:T(8,128)(2,1)S(1)} %get-tuple-element.102), channel_id=1, source_target_pairs={{0,4},{1,5},{2,6},{3,7},{4,0},{5,1},{6,2},{7,3},{8,12},{9,13},{10,... | collective-permute-start | bytes 393224 | tf_op jit(solution)/shard_map/ppermute | solution.py:533
  56.0 15.8 %collective-permute-start.23 = (bf16[352,512]{1,0:T(8,128)(2,1)S(1)}, bf16[352,512]{1,0:T(8,128)(2,1)S(1)}, u32[]{:S(2)}, u32[]{:S(2)}) collective-permute-start(bf16[352,512]{1,0:T(8,128)(2,1)S(1)} %get-tuple-element.108), channel_id=1, source_target_pairs={{0,1},{1,0},{2,3},{3,2},{4,5},{5,4},{6,7},{7,6},{8,9},{9,8},{10,11... | collective-permute-start | bytes 1081352 | tf_op jit(solution)/shard_map/ppermute | solution.py:538
  58.4 11.4 %collective-permute-start.24 = (bf16[128,512]{1,0:T(8,128)(2,1)S(1)}, bf16[128,512]{1,0:T(8,128)(2,1)S(1)}, u32[]{:S(2)}, u32[]{:S(2)}) collective-permute-start(bf16[128,512]{1,0:T(8,128)(2,1)S(1)} %get-tuple-element.109), channel_id=1, source_target_pairs={{0,2},{1,3},{2,0},{3,1},{4,6},{5,7},{6,4},{7,5},{8,10},{9,11},{10,... | collective-permute-start | bytes 393224 | tf_op jit(solution)/shard_map/ppermute | solution.py:533
  65.9 8.6 %collective-permute-start.20 = (bf16[128,512]{1,0:T(8,128)(2,1)S(1)}, bf16[128,512]{1,0:T(8,128)(2,1)S(1)}, u32[]{:S(2)}, u32[]{:S(2)}) collective-permute-start(bf16[128,512]{1,0:T(8,128)(2,1)S(1)} %get-tuple-element.105), channel_id=1, source_target_pairs={{0,14},{1,15},{2,12},{3,13},{4,10},{5,11},{6,8},{7,9},{8,22},{9,23... | collective-permute-start | bytes 393224 | tf_op jit(solution)/shard_map/ppermute | solution.py:545
  66.3 15.8 %collective-permute-start.21 = (bf16[128,512]{1,0:T(8,128)(2,1)S(1)}, bf16[128,512]{1,0:T(8,128)(2,1)S(1)}, u32[]{:S(2)}, u32[]{:S(2)}) collective-permute-start(bf16[128,512]{1,0:T(8,128)(2,1)S(1)} %get-tuple-element.106), channel_id=1, source_target_pairs={{0,12},{1,13},{2,14},{3,15},{4,8},{5,9},{6,10},{7,11},{8,20},{9,21... | collective-permute-start | bytes 393224 | tf_op jit(solution)/shard_map/ppermute | solution.py:545
  67.7 14.4 %collective-permute-start.22 = (bf16[128,512]{1,0:T(8,128)(2,1)S(1)}, bf16[128,512]{1,0:T(8,128)(2,1)S(1)}, u32[]{:S(2)}, u32[]{:S(2)}) collective-permute-start(bf16[128,512]{1,0:T(8,128)(2,1)S(1)} %get-tuple-element.107), channel_id=1, source_target_pairs={{0,10},{1,11},{2,8},{3,9},{4,14},{5,15},{6,12},{7,13},{8,18},{9,19... | collective-permute-start | bytes 393224 | tf_op jit(solution)/shard_map/ppermute | solution.py:545
  69.8 13.5 %collective-permute-start.19 = (bf16[128,512]{1,0:T(8,128)(2,1)S(1)}, bf16[128,512]{1,0:T(8,128)(2,1)S(1)}, u32[]{:S(2)}, u32[]{:S(2)}) collective-permute-start(bf16[128,512]{1,0:T(8,128)(2,1)S(1)} %get-tuple-element.104.refs_7_), channel_id=1, source_target_pairs={{0,8},{1,9},{2,10},{3,11},{4,12},{5,13},{6,14},{7,15},{8,16},{9,17... | collective-permute-start | bytes 393224 | tf_op jit(solution)/shard_map/ppermute | solution.py:545
  71.8 12.3 %collective-permute-start.25 = (bf16[128,2048]{1,0:T(8,128)(2,1)S(1)}, bf16[128,2048]{1,0:T(8,128)(2,1)S(1)}, u32[]{:S(2)}, u32[]{:S(2)}) collective-permute-start(bf16[128,2048]{1,0:T(8,128)(2,1)S(1)} %input_grad.1.refs_4_), channel_id=1, source_target_pairs={{0,24},{8,0},{16,8},{24,16},{1,25},{9,1},{17,9},{25,17},{2,26},{10... | collective-permute-start | bytes 1572872 | tf_op jit(solution)/shard_map/ppermute | solution.py:659
  74.5 10.5 %collective-permute-start.26 = (bf16[352,128]{1,0:T(8,128)(2,1)S(1)}, bf16[352,128]{1,0:T(8,128)(2,1)S(1)}, u32[]{:S(2)}, u32[]{:S(2)}) collective-permute-start(bf16[352,128]{1,0:T(8,128)(2,1)S(1)} %get-tuple-element.114), channel_id=1, source_target_pairs={{0,6},{1,7},{2,4},{3,5},{4,2},{5,3},{6,0},{7,1},{8,14},{9,15},{10,... | collective-permute-start | bytes 270344 | tf_op jit(solution)/shard_map/ppermute | solution.py:533
  82.1 5.5 %collective-permute-start.27 = (bf16[352,128]{1,0:T(8,128)(2,1)S(1)}, bf16[352,128]{1,0:T(8,128)(2,1)S(1)}, u32[]{:S(2)}, u32[]{:S(2)}) collective-permute-start(bf16[352,128]{1,0:T(8,128)(2,1)S(1)} %get-tuple-element.115), channel_id=1, source_target_pairs={{0,4},{1,5},{2,6},{3,7},{4,0},{5,1},{6,2},{7,3},{8,12},{9,13},{10,... | collective-permute-start | bytes 270344 | tf_op jit(solution)/shard_map/ppermute | solution.py:533
  82.1 5.6 %collective-permute-start.28 = (bf16[352,128]{1,0:T(8,128)(2,1)S(1)}, bf16[352,128]{1,0:T(8,128)(2,1)S(1)}, u32[]{:S(2)}, u32[]{:S(2)}) collective-permute-start(bf16[352,128]{1,0:T(8,128)(2,1)S(1)} %get-tuple-element.116), channel_id=1, source_target_pairs={{0,2},{1,3},{2,0},{3,1},{4,6},{5,7},{6,4},{7,5},{8,10},{9,11},{10,... | collective-permute-start | bytes 270344 | tf_op jit(solution)/shard_map/ppermute | solution.py:533

commit v6 on v5

--- a/solution.py
+++ b/solution.py
@@ -12,7 +12,7 @@
 LANE = 128
 SUB = 16
 EPS = 1e-06
-COST = {"relay": 3, "norm_saved": 3.0, "take_grad": 6.0, "norm_act": 3, "join_weight": 3, "join_out": 5, "far_adj": 2}
+COST = {"relay": 3, "far_saved": 3, "far_grad": 6.0, "norm_act": 3, "join_weight": 3, "join_out": 5, "far_adj": 2}
 VMEM = 48 * 1024 * 1024
 
 
@@ -121,23 +121,28 @@
     return jnp.where(row == part * part_of + col, 1.0, 0.0).astype(BF)
 
 
+def share_of(ref, first, n, part_of, part):
+    if part_of % LANE == 0:
+        return ref[:, pl.ds(pl.multiple_of(first + part * part_of, LANE), part_of)]
+    return mm(ref[:, first : first + n], pick(n, part_of, part)).astype(BF)
+
+
 def split_features_body(nb, ngroups, x_ref, *outs):
     group, _ = position(ngroups)
     part_of = outs[0].shape[2]
     bd = x_ref.shape[1] // nb
     for e in range(ngroups):
-        take = pick(bd, part_of, group ^ e)
         for k in range(nb):
-            outs[e][k] = mm(x_ref[:, k * bd : (k + 1) * bd], take).astype(BF)
-
-
-def pack_shares_body(nb, ngroups, *refs):
+            outs[e][k] = share_of(x_ref, k * bd, bd, part_of, group ^ e)
+
+
+def pack_shares_body(nb, ngroups, which, *refs):
     group, place = position(ngroups)
     shares, outs = refs[:ngroups], refs[ngroups:]
     t = shares[0].shape[1]
-    for d in range(nb):
+    for d, out in zip(which, outs):
         for e in range(ngroups):
-            outs[d][rows((group ^ e) * t, t), :] = shares[e][place ^ far(d, nb)]
+            out[rows((group ^ e) * t, t), :] = shares[e][place ^ far(d, nb)]
 
 
 def relay_body(nb, ngroups, r4, ext, *refs):
@@ -235,12 +240,13 @@
         first_ref[at, :] = mm(bd_ref[group * nb + c], proj_ref[at, :]).astype(BF)
 
 
-def project_shares_body(ngroups, normin_ref, wk_ref, *outs):
-    group, _ = position(ngroups)
+def project_shares_body(ngroups, normin_ref, wk_ref, *refs):
+    group, _ = position(ngroups)
+    outs, proj_ref = refs[:ngroups], refs[ngroups]
     bd = wk_ref.shape[0]
-    proj = mm(normin_ref[...], wk_ref[...]).astype(BF)
+    proj_ref[...] = mm(normin_ref[...], wk_ref[...]).astype(BF)
     for e in range(ngroups):
-        outs[e][...] = mm(proj, pick(bd, bd // ngroups, group ^ e)).astype(BF)
+        outs[e][...] = share_of(proj_ref, 0, bd, bd // ngroups, group ^ e)
 
 
 def gather_positions(group, bl, parts, out_ref):
@@ -376,10 +382,15 @@
     adj_proj_ref, gain_part_ref, outs, adj_norm_ref = rest[0], rest[1], rest[2 : 2 + nb], rest[2 + nb]
     bd = wk_ref.shape[0]
     t = LANE
-    adj_proj = jnp.zeros(adj_proj_ref.shape, F32)
-    for e in range(ngroups):
-        adj_proj = adj_proj + mm(shares[e][...], pick(bd, bd // ngroups, group ^ e), 1, 1)
-    adj_proj_ref[...] = adj_proj.astype(BF)
+    part_of = bd // ngroups
+    if part_of % LANE == 0:
+        for e in range(ngroups):
+            adj_proj_ref[:, pl.ds(pl.multiple_of((group ^ e) * part_of, LANE), part_of)] = shares[e][...]
+    else:
+        adj_proj = jnp.zeros(adj_proj_ref.shape, F32)
+        for e in range(ngroups):
+            adj_proj = adj_proj + mm(shares[e][...], pick(bd, part_of, group ^ e), 1, 1)
+        adj_proj_ref[...] = adj_proj.astype(BF)
     adj_norm = mm(adj_proj_ref[...], wk_ref[...], 1, 1)
     adj_norm_ref[...] = adj_norm
     gain = gain_ref[:, pl.ds(pl.multiple_of(place * bd, LANE), bd)]
@@ -561,6 +572,9 @@
     def run(name, body, outs, scratch=(), direct=0):
         return call(body, outs, scratch, direct, name)
 
+    def arrived(name, *parts):
+        return run(name, arrived_body, [sds((8, LANE), F32)])(after=parts)
+
     pack = part(pack_tokens_body, nb, ngroups)
     norm = part(norm_body, nb, ngroups)
     join = part(join_body, nb, ngroups)
@@ -589,20 +603,27 @@
         *w_msgs, after=early
     )
     relays = gathered(relay)
-    grad_msgs = run("pack_grad", part(pack_shares_body, nb, ngroups), [sds((ngroups * t, part_of))] * nb)(
-        *grad_shares, after=[relay]
-    )
-    (sto_normin,) = run("norm_saved", norm, tokens)(*sto_msgs, gain, after=grad_msgs[:1])
+    def pack_grad(name, which, after):
+        body = part(pack_shares_body, nb, ngroups, which)
+        return run(name, body, [sds((ngroups * t, part_of))] * len(which))(*grad_shares, after=[after])
+
+    grad_msgs = pack_grad("pack_grad", range(nb - 1), relay)
+    (sto_arrived,) = arrived("far_saved", grad_msgs[0], *sto_msgs[1:3])
+    (sto_normin,) = run("norm_saved", norm, tokens)(*sto_msgs, gain, after=[sto_arrived])
     wk, mq, bd_left = run(
         "assemble",
         part(assemble_body, nb, ngroups, r, ext, bl),
         [sds((bd, bd)), sds((nq, n, n)), sds((nseq, LANE, LANE))],
         [pltpu.VMEM((nseq, ext, LANE), BF)],
     )(*relays, after=[sto_normin])
-    sto_shares = run("project_saved", part(project_shares_body, ngroups), shares)(sto_normin, wk)
-    cur_msgs = run("pack_act", part(pack, True), scaled_msgs)(act_in[0], after=sto_shares[:1])
-    grad_msgs = within(grad_msgs)
-    (grad,) = run("take_grad", part(take_grad_body, nb, ngroups), every)(*grad_msgs, after=cur_msgs[:1])
+    sto_shares = run(
+        "project_saved", part(project_shares_body, ngroups), shares, scratch(tokens)
+    )(sto_normin, wk)
+    grad_near = pack_grad("pack_grad_near", [nb - 1], sto_shares[0])
+    cur_msgs = run("pack_act", part(pack, True), scaled_msgs)(act_in[0], after=grad_near)
+    grad_msgs = within([*grad_msgs, *grad_near])
+    (grad_arrived,) = arrived("far_grad", cur_msgs[0], *grad_msgs[1:3])
+    (grad,) = run("take_grad", part(take_grad_body, nb, ngroups), every)(*grad_msgs, after=[grad_arrived])
     sto_shares, cur_msgs = exchanged(sto_shares), within(cur_msgs)
     sto_proj, sto_f, sto_mixed = run(
         "mix_saved", part(mix_shares_body, ngroups, bl), every + by_position + every, scratch(every)
@@ -619,7 +640,8 @@
         scratch([sds((ngroups, nb * ext, LANE)), sds((ngroups, nb * bl, LANE))]),
     )(sto_f, adj_f, adj_first, sto_proj, after=adj_wait)
     tiles_wait = tiles[:1]
-    (cur_normin,) = run("norm_act", norm, tokens)(*cur_msgs, gain, after=tiles_wait)
+    (cur_arrived,) = arrived("far_act", tiles_wait[0], *cur_msgs[1:3])
+    (cur_normin,) = run("norm_act", norm, tokens)(*cur_msgs, gain, after=[cur_arrived])
     cur_proj, cur_first = run("project_act", part(project_body, nb, ngroups), tokens * 2)(
         cur_normin, wk, bd_left
     )
@@ -639,7 +661,7 @@
         scratch([sds((bd, bd), F32)]),
     )(sto_normin, adj_proj, gain_part, *tiles[1:], after=adj_wait)
     recvs = [across(sends[e - 1], e) for e in range(1, ngroups)]
-    (adj_arrived,) = run("far_adj", arrived_body, [sds((8, LANE), F32)])(after=[own_gw, *adj_parts[1:3]])
+    (adj_arrived,) = arrived("far_adj", own_gw, *adj_parts[1:3])
     (cur_mixed,) = run(
         "mix_act", part(mix_body, ngroups, bl), tokens, scratch([sds((nq, n, bd))])
     )(*cur_firsts, mq, after=[adj_arrived])

time: 88.8 us -> 88.4 us (level)
  starting transfers between devices: 45.7 us -> 42.5 us
  waiting for transfers between devices: 29.8 us -> 32.6 us
  Pallas kernels: 11.2 us -> 10.3 us
    ppermute x6, starting transfers between devices: 13.6 us -> 8.38 us  [across(): return lax.ppermute(block, 'seq', [(s, s ^ e) for s in range(nseq)])]
    ppermute x18, waiting for transfers between devices: 23.3 us -> 26.1 us  [within(): lax.ppermute(parts[d], 'seq', [(s, s ^ far(d, nb) * ngroups) for s in ran...]
    ppermute x18, starting transfers between devices: 25.7 us -> 27.8 us  [within(): lax.ppermute(parts[d], 'seq', [(s, s ^ far(d, nb) * ngroups) for s in ran...]
    pallas_call x25 -> x29, Pallas kernels: 11.2 us -> 10.3 us  [run(): pl.pallas_call(without_waits, out_shape=list(outs), in_specs=[anywhere] *...]
  transfers between devices with their start and end apart: 29 -> 29, of which waited for: 10 -> 11; matrix products, arithmetic and copies ran while one was open for 0% -> 0% of each run, Pallas kernels for 11% -> 11%
where the time goes in v6:
time: 88.4 us; the launch traced here: 88.1 us
  starting transfers between devices  42.5 us (48%)
  waiting for transfers between devices  32.6 us (37%)
  Pallas kernels  10.3 us (12%)
  local copies, waits for them, and re-layouts  1.77 us (2%)
    ppermute x18, starting transfers between devices, within(): lax.ppermute(parts[d], 'seq', [(s, s ^ far(d, nb) * ngroups) for s in ran...  27.8 us
    ppermute x18, waiting for transfers between devices, within(): lax.ppermute(parts[d], 'seq', [(s, s ^ far(d, nb) * ngroups) for s in ran...  26.1 us
    pallas_call x29, Pallas kernels, run(): pl.pallas_call(without_waits, out_shape=list(outs), in_specs=[anywhere] *...  10.3 us
    ppermute x6, starting transfers between devices, across(): return lax.ppermute(block, 'seq', [(s, s ^ e) for s in range(nseq)])  8.38 us
    ppermute x4, waiting for transfers between devices, handed(): lax.ppermute(parts[d], ('pipe', 'seq'), [(p * nseq + s, (p + step) % npip...  6.44 us
    ppermute x4, starting transfers between devices, handed(): lax.ppermute(parts[d], ('pipe', 'seq'), [(p * nseq + s, (p + step) % npip...  5.17 us
    unnamed x13, local copies, waits for them, and re-layouts  1.77 us
  transfers between devices with their start and end apart: 29, of which 11 were waited for; matrix products, arithmetic and copies ran while one was open for 0% of the time, Pallas kernels for 11%

profile of v6, /device:TPU:0, one launch (start us, length us, event | category | flops | bytes accessed | tf_op | source)
XLA Modules:
  0.0 88.1 jit_solution(3493125887112930750)
XLA Ops:
  0.7 1.1 %copy.15 = bf16[1,64,4,512]{3,1,2,0:T(8,128)(2,1)S(1)} copy(bf16[1,64,4,512]{3,2,1,0:T(4,128)(2,1)} %param.11) | data formatting | bytes 524288 | tf_op args[4]
  1.8 5.1 %collective-permute-start.4 = (bf16[336,128]{1,0:T(8,128)(2,1)S(1)}, bf16[336,128]{1,0:T(8,128)(2,1)S(1)}, u32[]{:S(2)}, u32[]{:S(2)}) collective-permute-start(bf16[336,128]{1,0:T(8,128)(2,1)S(1)} %get-tuple-element.70), channel_id=1, source_target_pairs={{0,6},{1,7},{2,4},{3,5},{4,2},{5,3},{6,0},{7,1},{8,14},{9,15},{10,... | collective-permute-start | bytes 258056 | tf_op jit(solution)/shard_map/ppermute | solution.py:544
  7.0 0.6 collective-permute-start.6
  7.7 1.7 %collective-permute-start = (bf16[4,128,256]{2,1,0:T(8,128)(2,1)S(1)}, bf16[4,128,256]{2,1,0:T(8,128)(2,1)S(1)}, u32[]{:S(2)}, u32[]{:S(2)}) collective-permute-start(bf16[4,128,256]{2,1,0:T(8,128)(2,1)S(1)} %get-tuple-element.65), channel_id=1, source_target_pairs={{0,1},{1,0},{2,3},{3,2},{4,5},{5,4},{6,7},{7,6},{8,9},{9,8},{10,11... | collective-permute-start | bytes 786440 | tf_op jit(solution)/shard_map/ppermute | solution.py:549
  9.6 3.7 %collective-permute-start.1 = (bf16[528,128]{1,0:T(8,128)(2,1)S(1)}, bf16[528,128]{1,0:T(8,128)(2,1)S(1)}, u32[]{:S(2)}, u32[]{:S(2)}) collective-permute-start(bf16[528,128]{1,0:T(8,128)(2,1)S(1)} %get-tuple-element.67), channel_id=1, source_target_pairs={{0,6},{1,7},{2,4},{3,5},{4,2},{5,3},{6,0},{7,1},{8,14},{9,15},{10,... | collective-permute-start | bytes 405512 | tf_op jit(solution)/shard_map/ppermute | solution.py:544
  13.3 1.8 %collective-permute-start.2 = (bf16[528,128]{1,0:T(8,128)(2,1)S(1)}, bf16[528,128]{1,0:T(8,128)(2,1)S(1)}, u32[]{:S(2)}, u32[]{:S(2)}) collective-permute-start(bf16[528,128]{1,0:T(8,128)(2,1)S(1)} %get-tuple-element.68), channel_id=1, source_target_pairs={{0,4},{1,5},{2,6},{3,7},{4,0},{5,1},{6,2},{7,3},{8,12},{9,13},{10,... | collective-permute-start | bytes 405512 | tf_op jit(solution)/shard_map/ppermute | solution.py:544
  15.0 5.7 %collective-permute-done.5.refs_2_ = bf16[336,128]{1,0:T(8,128)(2,1)S(1)} collective-permute-done((bf16[336,128]{1,0:T(8,128)(2,1)S(1)}, bf16[336,128]{1,0:T(8,128)(2,1)S(1)}, u32[]{:S(2)}, u32[]{:S(2)}) %collective-permute-start.5) | collective-permute-done | bytes 86048 | tf_op jit(solution)/shard_map/ppermute | solution.py:544
  20.8 1.5 %collective-permute-start.7 = (bf16[1344,128]{1,0:T(8,128)(2,1)S(1)}, bf16[1344,128]{1,0:T(8,128)(2,1)S(1)}, u32[]{:S(2)}, u32[]{:S(2)}) collective-permute-start(bf16[1344,128]{1,0:T(8,128)(2,1)S(1)} %relay.1.refs_2_.refs_0_), channel_id=1, source_target_pairs={{0,1},{1,0},{2,3},{3,2},{4,5},{5,4},{6,7},{7,6},{8,9},{9,8},{10,11... | collective-permute-start | bytes 1032200 | tf_op jit(solution)/shard_map/ppermute | solution.py:549
  22.4 2.9 %collective-permute-start.12 = (bf16[256,256]{1,0:T(8,128)(2,1)S(1)}, bf16[256,256]{1,0:T(8,128)(2,1)S(1)}, u32[]{:S(2)}, u32[]{:S(2)}) collective-permute-start(bf16[256,256]{1,0:T(8,128)(2,1)S(1)} %get-tuple-element.83), channel_id=1, source_target_pairs={{0,6},{1,7},{2,4},{3,5},{4,2},{5,3},{6,0},{7,1},{8,14},{9,15},{10,... | collective-permute-start | bytes 393224 | tf_op jit(solution)/shard_map/ppermute | solution.py:544
  25.3 1.7 %collective-permute-start.13 = (bf16[256,256]{1,0:T(8,128)(2,1)S(1)}, bf16[256,256]{1,0:T(8,128)(2,1)S(1)}, u32[]{:S(2)}, u32[]{:S(2)}) collective-permute-start(bf16[256,256]{1,0:T(8,128)(2,1)S(1)} %get-tuple-element.84), channel_id=1, source_target_pairs={{0,4},{1,5},{2,6},{3,7},{4,0},{5,1},{6,2},{7,3},{8,12},{9,13},{10,... | collective-permute-start | bytes 393224 | tf_op jit(solution)/shard_map/ppermute | solution.py:544
  27.0 5.3 %collective-permute-done.2.refs_2_ = bf16[528,128]{1,0:T(8,128)(2,1)S(1)} collective-permute-done((bf16[528,128]{1,0:T(8,128)(2,1)S(1)}, bf16[528,128]{1,0:T(8,128)(2,1)S(1)}, u32[]{:S(2)}, u32[]{:S(2)}) %collective-permute-start.2) | collective-permute-done | bytes 135200 | tf_op jit(solution)/shard_map/ppermute | solution.py:544
  32.3 0.7 copy-done.3
  33.2 0.7 assemble.1
  33.9 0.5 project_saved.1
  34.5 1.5 %collective-permute-start.11 = (bf16[512,256]{1,0:T(8,128)(2,1)S(1)}, bf16[512,256]{1,0:T(8,128)(2,1)S(1)}, u32[]{:S(2)}, u32[]{:S(2)}) collective-permute-start(bf16[512,256]{1,0:T(8,128)(2,1)S(1)} %get-tuple-element.80), channel_id=1, source_target_pairs={{0,1},{1,0},{2,3},{3,2},{4,5},{5,4},{6,7},{7,6},{8,9},{9,8},{10,11... | collective-permute-start | bytes 786440 | tf_op jit(solution)/shard_map/ppermute | solution.py:549
  36.0 0.2 pack_act.1
  36.2 2.9 %collective-permute-start.8 = (bf16[528,128]{1,0:T(8,128)(2,1)S(1)}, bf16[528,128]{1,0:T(8,128)(2,1)S(1)}, u32[]{:S(2)}, u32[]{:S(2)}) collective-permute-start(bf16[528,128]{1,0:T(8,128)(2,1)S(1)} %get-tuple-element.77), channel_id=1, source_target_pairs={{0,6},{1,7},{2,4},{3,5},{4,2},{5,3},{6,0},{7,1},{8,14},{9,15},{10,... | collective-permute-start | bytes 405512 | tf_op jit(solution)/shard_map/ppermute | solution.py:544
  39.2 0.6 collective-permute-start.9
  39.7 1.1 %collective-permute-done.13.refs_2_ = bf16[256,256]{1,0:T(8,128)(2,1)S(1)} collective-permute-done((bf16[256,256]{1,0:T(8,128)(2,1)S(1)}, bf16[256,256]{1,0:T(8,128)(2,1)S(1)}, u32[]{:S(2)}, u32[]{:S(2)}) %collective-permute-start.13) | collective-permute-done | bytes 131104 | tf_op jit(solution)/shard_map/ppermute | solution.py:544
  41.0 0.6 mix_saved.1
  41.6 0.6 backward.1
  42.2 1.5 %collective-permute-start.16 = (bf16[512,256]{1,0:T(8,128)(2,1)S(1)}, bf16[512,256]{1,0:T(8,128)(2,1)S(1)}, u32[]{:S(2)}, u32[]{:S(2)}) collective-permute-start(bf16[512,256]{1,0:T(8,128)(2,1)S(1)} %get-tuple-element.93), channel_id=1, source_target_pairs={{0,1},{1,0},{2,3},{3,2},{4,5},{5,4},{6,7},{7,6},{8,9},{9,8},{10,11... | collective-permute-start | bytes 786440 | tf_op jit(solution)/shard_map/ppermute | solution.py:549
  43.7 0.9 %factor_grads.1 = (bf16[320,128]{1,0:T(8,128)(2,1)S(1)}, bf16[320,128]{1,0:T(8,128)(2,1)S(1)}) custom-call(bf16[4,256,256]{2,1,0:T(8,128)(2,1)S(1)} %get-tuple-element.85.refs_0_, bf16[4,256,256]{2,1,0:T(8,128)(2,1)S(1)} %get-tuple-element.88.refs_1_, bf16[1024,256]{1,0:T(8,128)(2,1)S(1)} %get-tuple-element.89.refs_2_, ...), custom_call_target="tpu_custom_call" | custom-call | tf_op jit(solution)/shard_map/factor_grads/pallas_call | solution.py:66
  44.7 4.0 %collective-permute-done.9.refs_2_.refs_4_ = bf16[528,128]{1,0:T(8,128)(2,1)S(1)} collective-permute-done((bf16[528,128]{1,0:T(8,128)(2,1)S(1)}, bf16[528,128]{1,0:T(8,128)(2,1)S(1)}, u32[]{:S(2)}, u32[]{:S(2)}) %collective-permute-start.9) | collective-permute-done | bytes 135200 | tf_op jit(solution)/shard_map/ppermute | solution.py:544
  49.0 0.6 project_act.1
  49.6 1.4 %collective-permute-start.15 = (bf16[512,512]{1,0:T(8,128)(2,1)S(1)}, bf16[512,512]{1,0:T(8,128)(2,1)S(1)}, u32[]{:S(2)}, u32[]{:S(2)}) collective-permute-start(bf16[512,512]{1,0:T(8,128)(2,1)S(1)} %get-tuple-element.92.refs_5_.refs_0_), channel_id=1, source_target_pairs={{0,1},{1,0},{2,3},{3,2},{4,5},{5,4},{6,7},{7,6},{8,9},{9,8},{10,11... | collective-permute-start | bytes 1572872 | tf_op jit(solution)/shard_map/ppermute | solution.py:549
  51.0 0.5 adj_norm.1
  51.5 2.8 %collective-permute-start.17 = (bf16[128,512]{1,0:T(8,128)(2,1)S(1)}, bf16[128,512]{1,0:T(8,128)(2,1)S(1)}, u32[]{:S(2)}, u32[]{:S(2)}) collective-permute-start(bf16[128,512]{1,0:T(8,128)(2,1)S(1)} %get-tuple-element.99), channel_id=1, source_target_pairs={{0,6},{1,7},{2,4},{3,5},{4,2},{5,3},{6,0},{7,1},{8,14},{9,15},{10,... | collective-permute-start | bytes 393224 | tf_op jit(solution)/shard_map/ppermute | solution.py:544
  54.3 0.5 weight_grad.1
  54.8 0.8 collective-permute-start.23
  55.6 1.7 %collective-permute-start.24 = (bf16[128,512]{1,0:T(8,128)(2,1)S(1)}, bf16[128,512]{1,0:T(8,128)(2,1)S(1)}, u32[]{:S(2)}, u32[]{:S(2)}) collective-permute-start(bf16[128,512]{1,0:T(8,128)(2,1)S(1)} %get-tuple-element.107), channel_id=1, source_target_pairs={{0,2},{1,3},{2,0},{3,1},{4,6},{5,7},{6,4},{7,5},{8,10},{9,11},{10,... | collective-permute-start | bytes 393224 | tf_op jit(solution)/shard_map/ppermute | solution.py:544
  57.3 2.5 %collective-permute-done.17.refs_1_.refs_4_ = bf16[128,512]{1,0:T(8,128)(2,1)S(1)} collective-permute-done((bf16[128,512]{1,0:T(8,128)(2,1)S(1)}, bf16[128,512]{1,0:T(8,128)(2,1)S(1)}, u32[]{:S(2)}, u32[]{:S(2)}) %collective-permute-start.17) | collective-permute-done | bytes 131104 | tf_op jit(solution)/shard_map/ppermute | solution.py:544
  59.8 5.0 %collective-permute-done.18.refs_2_.refs_5_ = bf16[128,512]{1,0:T(8,128)(2,1)S(1)} collective-permute-done((bf16[128,512]{1,0:T(8,128)(2,1)S(1)}, bf16[128,512]{1,0:T(8,128)(2,1)S(1)}, u32[]{:S(2)}, u32[]{:S(2)}) %collective-permute-start.18) | collective-permute-done | bytes 131104 | tf_op jit(solution)/shard_map/ppermute | solution.py:544
  64.8 0.4 mix_act.1.refs_0_
  65.4 0.5 collective-permute-start.20
  66.0 1.4 %collective-permute-start.21 = (bf16[128,512]{1,0:T(8,128)(2,1)S(1)}, bf16[128,512]{1,0:T(8,128)(2,1)S(1)}, u32[]{:S(2)}, u32[]{:S(2)}) collective-permute-start(bf16[128,512]{1,0:T(8,128)(2,1)S(1)} %get-tuple-element.104), channel_id=1, source_target_pairs={{0,12},{1,13},{2,14},{3,15},{4,8},{5,9},{6,10},{7,11},{8,20},{9,21... | collective-permute-start | bytes 393224 | tf_op jit(solution)/shard_map/ppermute | solution.py:556
  67.3 2.0 %collective-permute-start.22 = (bf16[128,512]{1,0:T(8,128)(2,1)S(1)}, bf16[128,512]{1,0:T(8,128)(2,1)S(1)}, u32[]{:S(2)}, u32[]{:S(2)}) collective-permute-start(bf16[128,512]{1,0:T(8,128)(2,1)S(1)} %get-tuple-element.105), channel_id=1, source_target_pairs={{0,10},{1,11},{2,8},{3,9},{4,14},{5,15},{6,12},{7,13},{8,18},{9,19... | collective-permute-start | bytes 393224 | tf_op jit(solution)/shard_map/ppermute | solution.py:556
  69.3 1.3 %collective-permute-start.19 = (bf16[128,512]{1,0:T(8,128)(2,1)S(1)}, bf16[128,512]{1,0:T(8,128)(2,1)S(1)}, u32[]{:S(2)}, u32[]{:S(2)}) collective-permute-start(bf16[128,512]{1,0:T(8,128)(2,1)S(1)} %get-tuple-element.102.refs_7_), channel_id=1, source_target_pairs={{0,8},{1,9},{2,10},{3,11},{4,12},{5,13},{6,14},{7,15},{8,16},{9,17... | collective-permute-start | bytes 393224 | tf_op jit(solution)/shard_map/ppermute | solution.py:556
  70.6 0.7 input_grad.1.refs_4_
  71.3 1.2 %collective-permute-start.25 = (bf16[128,2048]{1,0:T(8,128)(2,1)S(1)}, bf16[128,2048]{1,0:T(8,128)(2,1)S(1)}, u32[]{:S(2)}, u32[]{:S(2)}) collective-permute-start(bf16[128,2048]{1,0:T(8,128)(2,1)S(1)} %input_grad.1.refs_4_), channel_id=1, source_target_pairs={{0,24},{8,0},{16,8},{24,16},{1,25},{9,1},{17,9},{25,17},{2,26},{10... | collective-permute-start | bytes 1572872 | tf_op jit(solution)/shard_map/ppermute | solution.py:681
  72.7 1.4 %collective-permute-done.20.refs_1_ = bf16[128,512]{1,0:T(8,128)(2,1)S(1)} collective-permute-done((bf16[128,512]{1,0:T(8,128)(2,1)S(1)}, bf16[128,512]{1,0:T(8,128)(2,1)S(1)}, u32[]{:S(2)}, u32[]{:S(2)}) %collective-permute-start.20) | collective-permute-done | bytes 131104 | tf_op jit(solution)/shard_map/ppermute | solution.py:556
  74.0 2.6 %collective-permute-start.26 = (bf16[352,128]{1,0:T(8,128)(2,1)S(1)}, bf16[352,128]{1,0:T(8,128)(2,1)S(1)}, u32[]{:S(2)}, u32[]{:S(2)}) collective-permute-start(bf16[352,128]{1,0:T(8,128)(2,1)S(1)} %get-tuple-element.112), channel_id=1, source_target_pairs={{0,6},{1,7},{2,4},{3,5},{4,2},{5,3},{6,0},{7,1},{8,14},{9,15},{10,... | collective-permute-start | bytes 270344 | tf_op jit(solution)/shard_map/ppermute | solution.py:544
  76.6 5.1 %collective-permute-done.21.refs_2_ = bf16[128,512]{1,0:T(8,128)(2,1)S(1)} collective-permute-done((bf16[128,512]{1,0:T(8,128)(2,1)S(1)}, bf16[128,512]{1,0:T(8,128)(2,1)S(1)}, u32[]{:S(2)}, u32[]{:S(2)}) %collective-permute-start.21) | collective-permute-done | bytes 131104 | tf_op jit(solution)/shard_map/ppermute | solution.py:556
  81.7 1.5 %collective-permute-start.28 = (bf16[352,128]{1,0:T(8,128)(2,1)S(1)}, bf16[352,128]{1,0:T(8,128)(2,1)S(1)}, u32[]{:S(2)}, u32[]{:S(2)}) collective-permute-start(bf16[352,128]{1,0:T(8,128)(2,1)S(1)} %get-tuple-element.114), channel_id=1, source_target_pairs={{0,2},{1,3},{2,0},{3,1},{4,6},{5,7},{6,4},{7,5},{8,10},{9,11},{10,... | collective-permute-start | bytes 270344 | tf_op jit(solution)/shard_map/ppermute | solution.py:544
  83.2 0.8 join_out.1
  84.0 0.8 store.1
  84.9 2.3 %collective-permute-done.27.refs_2_ = bf16[352,128]{1,0:T(8,128)(2,1)S(1)} collective-permute-done((bf16[352,128]{1,0:T(8,128)(2,1)S(1)}, bf16[352,128]{1,0:T(8,128)(2,1)S(1)}, u32[]{:S(2)}, u32[]{:S(2)}) %collective-permute-start.27) | collective-permute-done | bytes 90144 | tf_op jit(solution)/shard_map/ppermute | solution.py:544
  87.2 1.0 %join_weight.1 = (f32[64,4,512]{2,1,0:T(4,128)}, f32[1,2048]{1,0:T(1,128)}, f32[2,64,64]{2,1,0:T(8,128)}, f32[8,16,16]{2,1,0:T(8,128)}) custom-call(bf16[352,128]{1,0:T(8,128)(2,1)S(1)} %get-tuple-element.108.refs_4_.refs_0_, bf16[352,128]{1,0:T(8,128)(2,1)S(1)} %collective-permute-done.26.refs_1_, bf16[352,128]{1,0:T(8,128)(2,1)S(1)} %collective-permute-done.27.refs_2_, ...), custom_call_target="tpu_custom_call" | custom-call | flops 3000000000 | tf_op jit(solution)/shard_map/join_weight/pallas_call | solution.py:66
  (52 shorter events, 1.7 us)
Async XLA Ops:
  0.6 1.1 %copy-start.5 = (bf16[1,8,16,16]{3,2,1,0:T(8,128)(2,1)S(1)}, bf16[1,8,16,16]{3,2,1,0:T(8,128)(2,1)}, u32[]{:S(2)}) copy-start(bf16[1,8,16,16]{3,2,1,0:T(8,128)(2,1)} %param.13) | copy-start | bytes 12292
  0.6 1.1 %copy-start.4 = (bf16[1,2,64,64]{3,2,1,0:T(8,128)(2,1)S(1)}, bf16[1,2,64,64]{3,2,1,0:T(8,128)(2,1)}, u32[]{:S(2)}) copy-start(bf16[1,2,64,64]{3,2,1,0:T(8,128)(2,1)} %param.12) | copy-start | bytes 49156
  0.7 7.0 %copy-start = (bf16[1,128,2048]{2,1,0:T(8,128)(2,1)S(1)}, bf16[1,128,2048]{2,1,0:T(8,128)(2,1)}, u32[]{:S(2)}) copy-start(bf16[1,128,2048]{2,1,0:T(8,128)(2,1)} %param.9) | copy-start | bytes 1572868
  1.7 7.7 %copy-start.1 = (bf16[1,128,2048]{2,1,0:T(8,128)(2,1)S(1)}, bf16[1,128,2048]{2,1,0:T(8,128)(2,1)}, u32[]{:S(2)}) copy-start(bf16[1,128,2048]{2,1,0:T(8,128)(2,1)} %param.8) | copy-start | bytes 1572868
  1.8 11.4 %collective-permute-start.4 = (bf16[336,128]{1,0:T(8,128)(2,1)S(1)}, bf16[336,128]{1,0:T(8,128)(2,1)S(1)}, u32[]{:S(2)}, u32[]{:S(2)}) collective-permute-start(bf16[336,128]{1,0:T(8,128)(2,1)S(1)} %get-tuple-element.70), channel_id=1, source_target_pairs={{0,6},{1,7},{2,4},{3,5},{4,2},{5,3},{6,0},{7,1},{8,14},{9,15},{10,... | collective-permute-start | bytes 258056 | tf_op jit(solution)/shard_map/ppermute | solution.py:544
  7.0 13.8 %collective-permute-start.5 = (bf16[336,128]{1,0:T(8,128)(2,1)S(1)}, bf16[336,128]{1,0:T(8,128)(2,1)S(1)}, u32[]{:S(2)}, u32[]{:S(2)}) collective-permute-start(bf16[336,128]{1,0:T(8,128)(2,1)S(1)} %get-tuple-element.71), channel_id=1, source_target_pairs={{0,4},{1,5},{2,6},{3,7},{4,0},{5,1},{6,2},{7,3},{8,12},{9,13},{10,... | collective-permute-start | bytes 258056 | tf_op jit(solution)/shard_map/ppermute | solution.py:544
  7.0 13.8 %collective-permute-start.6 = (bf16[336,128]{1,0:T(8,128)(2,1)S(1)}, bf16[336,128]{1,0:T(8,128)(2,1)S(1)}, u32[]{:S(2)}, u32[]{:S(2)}) collective-permute-start(bf16[336,128]{1,0:T(8,128)(2,1)S(1)} %get-tuple-element.72), channel_id=1, source_target_pairs={{0,2},{1,3},{2,0},{3,1},{4,6},{5,7},{6,4},{7,5},{8,10},{9,11},{10,... | collective-permute-start | bytes 258056 | tf_op jit(solution)/shard_map/ppermute | solution.py:544
  7.7 14.7 %collective-permute-start = (bf16[4,128,256]{2,1,0:T(8,128)(2,1)S(1)}, bf16[4,128,256]{2,1,0:T(8,128)(2,1)S(1)}, u32[]{:S(2)}, u32[]{:S(2)}) collective-permute-start(bf16[4,128,256]{2,1,0:T(8,128)(2,1)S(1)} %get-tuple-element.65), channel_id=1, source_target_pairs={{0,1},{1,0},{2,3},{3,2},{4,5},{5,4},{6,7},{7,6},{8,9},{9,8},{10,11... | collective-permute-start | bytes 786440 | tf_op jit(solution)/shard_map/ppermute | solution.py:549
  9.6 15.7 %collective-permute-start.1 = (bf16[528,128]{1,0:T(8,128)(2,1)S(1)}, bf16[528,128]{1,0:T(8,128)(2,1)S(1)}, u32[]{:S(2)}, u32[]{:S(2)}) collective-permute-start(bf16[528,128]{1,0:T(8,128)(2,1)S(1)} %get-tuple-element.67), channel_id=1, source_target_pairs={{0,6},{1,7},{2,4},{3,5},{4,2},{5,3},{6,0},{7,1},{8,14},{9,15},{10,... | collective-permute-start | bytes 405512 | tf_op jit(solution)/shard_map/ppermute | solution.py:544
  13.3 19.0 %collective-permute-start.2 = (bf16[528,128]{1,0:T(8,128)(2,1)S(1)}, bf16[528,128]{1,0:T(8,128)(2,1)S(1)}, u32[]{:S(2)}, u32[]{:S(2)}) collective-permute-start(bf16[528,128]{1,0:T(8,128)(2,1)S(1)} %get-tuple-element.68), channel_id=1, source_target_pairs={{0,4},{1,5},{2,6},{3,7},{4,0},{5,1},{6,2},{7,3},{8,12},{9,13},{10,... | collective-permute-start | bytes 405512 | tf_op jit(solution)/shard_map/ppermute | solution.py:544
  20.8 12.4 %collective-permute-start.7 = (bf16[1344,128]{1,0:T(8,128)(2,1)S(1)}, bf16[1344,128]{1,0:T(8,128)(2,1)S(1)}, u32[]{:S(2)}, u32[]{:S(2)}) collective-permute-start(bf16[1344,128]{1,0:T(8,128)(2,1)S(1)} %relay.1.refs_2_.refs_0_), channel_id=1, source_target_pairs={{0,1},{1,0},{2,3},{3,2},{4,5},{5,4},{6,7},{7,6},{8,9},{9,8},{10,11... | collective-permute-start | bytes 1032200 | tf_op jit(solution)/shard_map/ppermute | solution.py:549
  22.4 9.9 %collective-permute-start.3 = (bf16[528,128]{1,0:T(8,128)(2,1)S(1)}, bf16[528,128]{1,0:T(8,128)(2,1)S(1)}, u32[]{:S(2)}, u32[]{:S(2)}) collective-permute-start(bf16[528,128]{1,0:T(8,128)(2,1)S(1)} %get-tuple-element.69), channel_id=1, source_target_pairs={{0,2},{1,3},{2,0},{3,1},{4,6},{5,7},{6,4},{7,5},{8,10},{9,11},{10,... | collective-permute-start | bytes 405512 | tf_op jit(solution)/shard_map/ppermute | solution.py:544
  22.4 16.8 %collective-permute-start.12 = (bf16[256,256]{1,0:T(8,128)(2,1)S(1)}, bf16[256,256]{1,0:T(8,128)(2,1)S(1)}, u32[]{:S(2)}, u32[]{:S(2)}) collective-permute-start(bf16[256,256]{1,0:T(8,128)(2,1)S(1)} %get-tuple-element.83), channel_id=1, source_target_pairs={{0,6},{1,7},{2,4},{3,5},{4,2},{5,3},{6,0},{7,1},{8,14},{9,15},{10,... | collective-permute-start | bytes 393224 | tf_op jit(solution)/shard_map/ppermute | solution.py:544
  25.3 15.5 %collective-permute-start.13 = (bf16[256,256]{1,0:T(8,128)(2,1)S(1)}, bf16[256,256]{1,0:T(8,128)(2,1)S(1)}, u32[]{:S(2)}, u32[]{:S(2)}) collective-permute-start(bf16[256,256]{1,0:T(8,128)(2,1)S(1)} %get-tuple-element.84), channel_id=1, source_target_pairs={{0,4},{1,5},{2,6},{3,7},{4,0},{5,1},{6,2},{7,3},{8,12},{9,13},{10,... | collective-permute-start | bytes 393224 | tf_op jit(solution)/shard_map/ppermute | solution.py:544
  32.3 0.7 copy-start.3
  34.4 1.6 %copy-start.2 = (bf16[1,128,2048]{2,1,0:T(8,128)(2,1)S(1)}, bf16[1,128,2048]{2,1,0:T(8,128)(2,1)}, u32[]{:S(2)}) copy-start(bf16[1,128,2048]{2,1,0:T(8,128)(2,1)} %param.7) | copy-start | bytes 1572868
  34.5 6.3 %collective-permute-start.14 = (bf16[256,256]{1,0:T(8,128)(2,1)S(1)}, bf16[256,256]{1,0:T(8,128)(2,1)S(1)}, u32[]{:S(2)}, u32[]{:S(2)}) collective-permute-start(bf16[256,256]{1,0:T(8,128)(2,1)S(1)} %pack_grad_near.1.refs_1_), channel_id=1, source_target_pairs={{0,2},{1,3},{2,0},{3,1},{4,6},{5,7},{6,4},{7,5},{8,10},{9,11},{10,... | collective-permute-start | bytes 393224 | tf_op jit(solution)/shard_map/ppermute | solution.py:544
  34.5 6.4 %collective-permute-start.11 = (bf16[512,256]{1,0:T(8,128)(2,1)S(1)}, bf16[512,256]{1,0:T(8,128)(2,1)S(1)}, u32[]{:S(2)}, u32[]{:S(2)}) collective-permute-start(bf16[512,256]{1,0:T(8,128)(2,1)S(1)} %get-tuple-element.80), channel_id=1, source_target_pairs={{0,1},{1,0},{2,3},{3,2},{4,5},{5,4},{6,7},{7,6},{8,9},{9,8},{10,11... | collective-permute-start | bytes 786440 | tf_op jit(solution)/shard_map/ppermute | solution.py:549
  36.2 8.4 %collective-permute-start.8 = (bf16[528,128]{1,0:T(8,128)(2,1)S(1)}, bf16[528,128]{1,0:T(8,128)(2,1)S(1)}, u32[]{:S(2)}, u32[]{:S(2)}) collective-permute-start(bf16[528,128]{1,0:T(8,128)(2,1)S(1)} %get-tuple-element.77), channel_id=1, source_target_pairs={{0,6},{1,7},{2,4},{3,5},{4,2},{5,3},{6,0},{7,1},{8,14},{9,15},{10,... | collective-permute-start | bytes 405512 | tf_op jit(solution)/shard_map/ppermute | solution.py:544
  39.2 9.5 %collective-permute-start.9 = (bf16[528,128]{1,0:T(8,128)(2,1)S(1)}, bf16[528,128]{1,0:T(8,128)(2,1)S(1)}, u32[]{:S(2)}, u32[]{:S(2)}) collective-permute-start(bf16[528,128]{1,0:T(8,128)(2,1)S(1)} %get-tuple-element.78), channel_id=1, source_target_pairs={{0,4},{1,5},{2,6},{3,7},{4,0},{5,1},{6,2},{7,3},{8,12},{9,13},{10,... | collective-permute-start | bytes 405512 | tf_op jit(solution)/shard_map/ppermute | solution.py:544
  40.8 8.0 %collective-permute-start.10 = (bf16[528,128]{1,0:T(8,128)(2,1)S(1)}, bf16[528,128]{1,0:T(8,128)(2,1)S(1)}, u32[]{:S(2)}, u32[]{:S(2)}) collective-permute-start(bf16[528,128]{1,0:T(8,128)(2,1)S(1)} %get-tuple-element.79), channel_id=1, source_target_pairs={{0,2},{1,3},{2,0},{3,1},{4,6},{5,7},{6,4},{7,5},{8,10},{9,11},{10,... | collective-permute-start | bytes 405512 | tf_op jit(solution)/shard_map/ppermute | solution.py:544
  42.2 8.7 %collective-permute-start.16 = (bf16[512,256]{1,0:T(8,128)(2,1)S(1)}, bf16[512,256]{1,0:T(8,128)(2,1)S(1)}, u32[]{:S(2)}, u32[]{:S(2)}) collective-permute-start(bf16[512,256]{1,0:T(8,128)(2,1)S(1)} %get-tuple-element.93), channel_id=1, source_target_pairs={{0,1},{1,0},{2,3},{3,2},{4,5},{5,4},{6,7},{7,6},{8,9},{9,8},{10,11... | collective-permute-start | bytes 786440 | tf_op jit(solution)/shard_map/ppermute | solution.py:549
  49.6 15.2 %collective-permute-start.15 = (bf16[512,512]{1,0:T(8,128)(2,1)S(1)}, bf16[512,512]{1,0:T(8,128)(2,1)S(1)}, u32[]{:S(2)}, u32[]{:S(2)}) collective-permute-start(bf16[512,512]{1,0:T(8,128)(2,1)S(1)} %get-tuple-element.92.refs_5_.refs_0_), channel_id=1, source_target_pairs={{0,1},{1,0},{2,3},{3,2},{4,5},{5,4},{6,7},{7,6},{8,9},{9,8},{10,11... | collective-permute-start | bytes 1572872 | tf_op jit(solution)/shard_map/ppermute | solution.py:549
  51.5 8.3 %collective-permute-start.17 = (bf16[128,512]{1,0:T(8,128)(2,1)S(1)}, bf16[128,512]{1,0:T(8,128)(2,1)S(1)}, u32[]{:S(2)}, u32[]{:S(2)}) collective-permute-start(bf16[128,512]{1,0:T(8,128)(2,1)S(1)} %get-tuple-element.99), channel_id=1, source_target_pairs={{0,6},{1,7},{2,4},{3,5},{4,2},{5,3},{6,0},{7,1},{8,14},{9,15},{10,... | collective-permute-start | bytes 393224 | tf_op jit(solution)/shard_map/ppermute | solution.py:544
  54.3 10.6 %collective-permute-start.18 = (bf16[128,512]{1,0:T(8,128)(2,1)S(1)}, bf16[128,512]{1,0:T(8,128)(2,1)S(1)}, u32[]{:S(2)}, u32[]{:S(2)}) collective-permute-start(bf16[128,512]{1,0:T(8,128)(2,1)S(1)} %get-tuple-element.100), channel_id=1, source_target_pairs={{0,4},{1,5},{2,6},{3,7},{4,0},{5,1},{6,2},{7,3},{8,12},{9,13},{10,... | collective-permute-start | bytes 393224 | tf_op jit(solution)/shard_map/ppermute | solution.py:544
  54.8 16.5 %collective-permute-start.23 = (bf16[352,512]{1,0:T(8,128)(2,1)S(1)}, bf16[352,512]{1,0:T(8,128)(2,1)S(1)}, u32[]{:S(2)}, u32[]{:S(2)}) collective-permute-start(bf16[352,512]{1,0:T(8,128)(2,1)S(1)} %get-tuple-element.106), channel_id=1, source_target_pairs={{0,1},{1,0},{2,3},{3,2},{4,5},{5,4},{6,7},{7,6},{8,9},{9,8},{10,11... | collective-permute-start | bytes 1081352 | tf_op jit(solution)/shard_map/ppermute | solution.py:549
  55.6 13.7 %collective-permute-start.24 = (bf16[128,512]{1,0:T(8,128)(2,1)S(1)}, bf16[128,512]{1,0:T(8,128)(2,1)S(1)}, u32[]{:S(2)}, u32[]{:S(2)}) collective-permute-start(bf16[128,512]{1,0:T(8,128)(2,1)S(1)} %get-tuple-element.107), channel_id=1, source_target_pairs={{0,2},{1,3},{2,0},{3,1},{4,6},{5,7},{6,4},{7,5},{8,10},{9,11},{10,... | collective-permute-start | bytes 393224 | tf_op jit(solution)/shard_map/ppermute | solution.py:544
  65.4 8.6 %collective-permute-start.20 = (bf16[128,512]{1,0:T(8,128)(2,1)S(1)}, bf16[128,512]{1,0:T(8,128)(2,1)S(1)}, u32[]{:S(2)}, u32[]{:S(2)}) collective-permute-start(bf16[128,512]{1,0:T(8,128)(2,1)S(1)} %get-tuple-element.103), channel_id=1, source_target_pairs={{0,14},{1,15},{2,12},{3,13},{4,10},{5,11},{6,8},{7,9},{8,22},{9,23... | collective-permute-start | bytes 393224 | tf_op jit(solution)/shard_map/ppermute | solution.py:556
  66.0 15.7 %collective-permute-start.21 = (bf16[128,512]{1,0:T(8,128)(2,1)S(1)}, bf16[128,512]{1,0:T(8,128)(2,1)S(1)}, u32[]{:S(2)}, u32[]{:S(2)}) collective-permute-start(bf16[128,512]{1,0:T(8,128)(2,1)S(1)} %get-tuple-element.104), channel_id=1, source_target_pairs={{0,12},{1,13},{2,14},{3,15},{4,8},{5,9},{6,10},{7,11},{8,20},{9,21... | collective-permute-start | bytes 393224 | tf_op jit(solution)/shard_map/ppermute | solution.py:556
  67.3 14.3 %collective-permute-start.22 = (bf16[128,512]{1,0:T(8,128)(2,1)S(1)}, bf16[128,512]{1,0:T(8,128)(2,1)S(1)}, u32[]{:S(2)}, u32[]{:S(2)}) collective-permute-start(bf16[128,512]{1,0:T(8,128)(2,1)S(1)} %get-tuple-element.105), channel_id=1, source_target_pairs={{0,10},{1,11},{2,8},{3,9},{4,14},{5,15},{6,12},{7,13},{8,18},{9,19... | collective-permute-start | bytes 393224 | tf_op jit(solution)/shard_map/ppermute | solution.py:556
  69.3 13.9 %collective-permute-start.19 = (bf16[128,512]{1,0:T(8,128)(2,1)S(1)}, bf16[128,512]{1,0:T(8,128)(2,1)S(1)}, u32[]{:S(2)}, u32[]{:S(2)}) collective-permute-start(bf16[128,512]{1,0:T(8,128)(2,1)S(1)} %get-tuple-element.102.refs_7_), channel_id=1, source_target_pairs={{0,8},{1,9},{2,10},{3,11},{4,12},{5,13},{6,14},{7,15},{8,16},{9,17... | collective-permute-start | bytes 393224 | tf_op jit(solution)/shard_map/ppermute | solution.py:556
  71.3 12.7 %collective-permute-start.25 = (bf16[128,2048]{1,0:T(8,128)(2,1)S(1)}, bf16[128,2048]{1,0:T(8,128)(2,1)S(1)}, u32[]{:S(2)}, u32[]{:S(2)}) collective-permute-start(bf16[128,2048]{1,0:T(8,128)(2,1)S(1)} %input_grad.1.refs_4_), channel_id=1, source_target_pairs={{0,24},{8,0},{16,8},{24,16},{1,25},{9,1},{17,9},{25,17},{2,26},{10... | collective-permute-start | bytes 1572872 | tf_op jit(solution)/shard_map/ppermute | solution.py:681
  74.0 10.8 %collective-permute-start.26 = (bf16[352,128]{1,0:T(8,128)(2,1)S(1)}, bf16[352,128]{1,0:T(8,128)(2,1)S(1)}, u32[]{:S(2)}, u32[]{:S(2)}) collective-permute-start(bf16[352,128]{1,0:T(8,128)(2,1)S(1)} %get-tuple-element.112), channel_id=1, source_target_pairs={{0,6},{1,7},{2,4},{3,5},{4,2},{5,3},{6,0},{7,1},{8,14},{9,15},{10,... | collective-permute-start | bytes 270344 | tf_op jit(solution)/shard_map/ppermute | solution.py:544
  81.7 5.5 %collective-permute-start.27 = (bf16[352,128]{1,0:T(8,128)(2,1)S(1)}, bf16[352,128]{1,0:T(8,128)(2,1)S(1)}, u32[]{:S(2)}, u32[]{:S(2)}) collective-permute-start(bf16[352,128]{1,0:T(8,128)(2,1)S(1)} %get-tuple-element.113), channel_id=1, source_target_pairs={{0,4},{1,5},{2,6},{3,7},{4,0},{5,1},{6,2},{7,3},{8,12},{9,13},{10,... | collective-permute-start | bytes 270344 | tf_op jit(solution)/shard_map/ppermute | solution.py:544
  81.7 5.5 %collective-permute-start.28 = (bf16[352,128]{1,0:T(8,128)(2,1)S(1)}, bf16[352,128]{1,0:T(8,128)(2,1)S(1)}, u32[]{:S(2)}, u32[]{:S(2)}) collective-permute-start(bf16[352,128]{1,0:T(8,128)(2,1)S(1)} %get-tuple-element.114), channel_id=1, source_target_pairs={{0,2},{1,3},{2,0},{3,1},{4,6},{5,7},{6,4},{7,5},{8,10},{9,11},{10,... | collective-permute-start | bytes 270344 | tf_op jit(solution)/shard_map/ppermute | solution.py:544

commit v7 on v6

--- a/solution.py
+++ b/solution.py
@@ -97,7 +97,7 @@
         outs[d][chunks * r + bl :, :] = right
 
 
-def pack_tokens_body(nb, ngroups, with_scale, x_ref, *outs):
+def pack_tokens_body(nb, ngroups, with_scale, x_ref, *outs, which=None):
     _, block = position(ngroups)
     t, width = x_ref.shape
     bd = width // nb
@@ -107,12 +107,12 @@
         inv = lax.rsqrt(jnp.mean(x * x, axis=-1, keepdims=True) + EPS)
         parts = split3(to_row(inv))
         tile = jnp.concatenate(list(parts) + [jnp.zeros((SUB - 3, t), F32)], axis=0).astype(BF)
-    for d in range(nb):
+    for d, out in zip(which or range(nb), outs):
         for ch in range(chunks):
             lanes = pl.ds(pl.multiple_of((block ^ far(d, nb)) * bd + ch * LANE, LANE), LANE)
-            outs[d][ch * t : (ch + 1) * t, :] = x_ref[:, lanes]
+            out[ch * t : (ch + 1) * t, :] = x_ref[:, lanes]
         if with_scale:
-            outs[d][chunks * t :, :] = tile
+            out[chunks * t :, :] = tile
 
 
 def pick(n, part_of, part):
@@ -620,11 +620,11 @@
         "project_saved", part(project_shares_body, ngroups), shares, scratch(tokens)
     )(sto_normin, wk)
     grad_near = pack_grad("pack_grad_near", [nb - 1], sto_shares[0])
-    cur_msgs = run("pack_act", part(pack, True), scaled_msgs)(act_in[0], after=grad_near)
+    cur_msgs = run("pack_act", part(pack, True), scaled_msgs[1:])(act_in[0], after=grad_near)
     grad_msgs = within([*grad_msgs, *grad_near])
     (grad_arrived,) = arrived("far_grad", cur_msgs[0], *grad_msgs[1:3])
     (grad,) = run("take_grad", part(take_grad_body, nb, ngroups), every)(*grad_msgs, after=[grad_arrived])
-    sto_shares, cur_msgs = exchanged(sto_shares), within(cur_msgs)
+    sto_shares = exchanged(sto_shares)
     sto_proj, sto_f, sto_mixed = run(
         "mix_saved", part(mix_shares_body, ngroups, bl), every + by_position + every, scratch(every)
     )(*sto_shares, mq, bd_left, after=[grad])
@@ -632,6 +632,10 @@
         "backward", part(backward_body, nb, ngroups, bl), shares + by_position + every, scratch(every)
     )(grad, sto_proj, sto_mixed, mq, bd_left)
     adj_wait = adj_shares[:1]
+    cur_near = run("pack_act_near", part(pack, True, which=[nb - 1]), scaled_msgs[:1])(
+        act_in[0], after=adj_wait
+    )
+    cur_msgs = within([*cur_msgs, *cur_near])
     adj_shares = exchanged(adj_shares)
     tiles = run(
         "factor_grads",

time: 88.4 us -> 89.6 us (1.014)
  starting transfers between devices: 42.5 us -> 44.8 us
  waiting for transfers between devices: 32.6 us -> 31.4 us
    ppermute x18, starting transfers between devices: 27.8 us -> 30 us  [within(): lax.ppermute(parts[d], 'seq', [(s, s ^ far(d, nb) * ngroups) for s in ran...]
    ppermute x18, waiting for transfers between devices: 26.1 us -> 24.9 us  [within(): lax.ppermute(parts[d], 'seq', [(s, s ^ far(d, nb) * ngroups) for s in ran...]
    pallas_call x29 -> x30, Pallas kernels: 10.3 us -> 10.5 us  [run(): pl.pallas_call(without_waits, out_shape=list(outs), in_specs=[anywhere] *...]
  transfers between devices with their start and end apart: 29 -> 29, of which waited for: 11 -> 13; matrix products, arithmetic and copies ran while one was open for 0% -> 0% of each run, Pallas kernels for 11% -> 11%
where the time goes in v7:
time: 89.6 us; the launch traced here: 89.4 us
  starting transfers between devices  44.8 us (50%)
  waiting for transfers between devices  31.4 us (35%)
  Pallas kernels  10.5 us (12%)
  local copies, waits for them, and re-layouts  1.77 us (2%)
    ppermute x18, starting transfers between devices, within(): lax.ppermute(parts[d], 'seq', [(s, s ^ far(d, nb) * ngroups) for s in ran...  30 us
    ppermute x18, waiting for transfers between devices, within(): lax.ppermute(parts[d], 'seq', [(s, s ^ far(d, nb) * ngroups) for s in ran...  24.9 us
    pallas_call x30, Pallas kernels, run(): pl.pallas_call(without_waits, out_shape=list(outs), in_specs=[anywhere] *...  10.5 us
    ppermute x6, starting transfers between devices, across(): return lax.ppermute(block, 'seq', [(s, s ^ e) for s in range(nseq)])  8.45 us
    ppermute x4, waiting for transfers between devices, handed(): lax.ppermute(parts[d], ('pipe', 'seq'), [(p * nseq + s, (p + step) % npip...  6.23 us
    ppermute x4, starting transfers between devices, handed(): lax.ppermute(parts[d], ('pipe', 'seq'), [(p * nseq + s, (p + step) % npip...  5.17 us
  transfers between devices with their start and end apart: 29, of which 13 were waited for; matrix products, arithmetic and copies ran while one was open for 0% of the time, Pallas kernels for 11%

profile of v7, /device:TPU:0, one launch (start us, length us, event | category | flops | bytes accessed | tf_op | source)
XLA Modules:
  0.0 89.4 jit_solution(5753405222885444763)
XLA Ops:
  0.7 1.1 %copy.15 = bf16[1,64,4,512]{3,1,2,0:T(8,128)(2,1)S(1)} copy(bf16[1,64,4,512]{3,2,1,0:T(4,128)(2,1)} %param.11) | data formatting | bytes 524288 | tf_op args[4]
  1.8 5.1 %collective-permute-start.4 = (bf16[336,128]{1,0:T(8,128)(2,1)S(1)}, bf16[336,128]{1,0:T(8,128)(2,1)S(1)}, u32[]{:S(2)}, u32[]{:S(2)}) collective-permute-start(bf16[336,128]{1,0:T(8,128)(2,1)S(1)} %get-tuple-element.69), channel_id=1, source_target_pairs={{0,6},{1,7},{2,4},{3,5},{4,2},{5,3},{6,0},{7,1},{8,14},{9,15},{10,... | collective-permute-start | bytes 258056 | tf_op jit(solution)/shard_map/ppermute | solution.py:544
  7.0 0.6 collective-permute-start.6
  7.7 1.7 %collective-permute-start = (bf16[4,128,256]{2,1,0:T(8,128)(2,1)S(1)}, bf16[4,128,256]{2,1,0:T(8,128)(2,1)S(1)}, u32[]{:S(2)}, u32[]{:S(2)}) collective-permute-start(bf16[4,128,256]{2,1,0:T(8,128)(2,1)S(1)} %get-tuple-element.64), channel_id=1, source_target_pairs={{0,1},{1,0},{2,3},{3,2},{4,5},{5,4},{6,7},{7,6},{8,9},{9,8},{10,11... | collective-permute-start | bytes 786440 | tf_op jit(solution)/shard_map/ppermute | solution.py:549
  9.6 3.7 %collective-permute-start.1 = (bf16[528,128]{1,0:T(8,128)(2,1)S(1)}, bf16[528,128]{1,0:T(8,128)(2,1)S(1)}, u32[]{:S(2)}, u32[]{:S(2)}) collective-permute-start(bf16[528,128]{1,0:T(8,128)(2,1)S(1)} %get-tuple-element.66), channel_id=1, source_target_pairs={{0,6},{1,7},{2,4},{3,5},{4,2},{5,3},{6,0},{7,1},{8,14},{9,15},{10,... | collective-permute-start | bytes 405512 | tf_op jit(solution)/shard_map/ppermute | solution.py:544
  13.3 1.8 %collective-permute-start.2 = (bf16[528,128]{1,0:T(8,128)(2,1)S(1)}, bf16[528,128]{1,0:T(8,128)(2,1)S(1)}, u32[]{:S(2)}, u32[]{:S(2)}) collective-permute-start(bf16[528,128]{1,0:T(8,128)(2,1)S(1)} %get-tuple-element.67), channel_id=1, source_target_pairs={{0,4},{1,5},{2,6},{3,7},{4,0},{5,1},{6,2},{7,3},{8,12},{9,13},{10,... | collective-permute-start | bytes 405512 | tf_op jit(solution)/shard_map/ppermute | solution.py:544
  15.0 5.7 %collective-permute-done.5.refs_2_ = bf16[336,128]{1,0:T(8,128)(2,1)S(1)} collective-permute-done((bf16[336,128]{1,0:T(8,128)(2,1)S(1)}, bf16[336,128]{1,0:T(8,128)(2,1)S(1)}, u32[]{:S(2)}, u32[]{:S(2)}) %collective-permute-start.5) | collective-permute-done | bytes 86048 | tf_op jit(solution)/shard_map/ppermute | solution.py:544
  20.8 1.5 %collective-permute-start.7 = (bf16[1344,128]{1,0:T(8,128)(2,1)S(1)}, bf16[1344,128]{1,0:T(8,128)(2,1)S(1)}, u32[]{:S(2)}, u32[]{:S(2)}) collective-permute-start(bf16[1344,128]{1,0:T(8,128)(2,1)S(1)} %relay.1.refs_2_.refs_0_), channel_id=1, source_target_pairs={{0,1},{1,0},{2,3},{3,2},{4,5},{5,4},{6,7},{7,6},{8,9},{9,8},{10,11... | collective-permute-start | bytes 1032200 | tf_op jit(solution)/shard_map/ppermute | solution.py:549
  22.4 2.9 %collective-permute-start.10 = (bf16[256,256]{1,0:T(8,128)(2,1)S(1)}, bf16[256,256]{1,0:T(8,128)(2,1)S(1)}, u32[]{:S(2)}, u32[]{:S(2)}) collective-permute-start(bf16[256,256]{1,0:T(8,128)(2,1)S(1)} %get-tuple-element.78), channel_id=1, source_target_pairs={{0,6},{1,7},{2,4},{3,5},{4,2},{5,3},{6,0},{7,1},{8,14},{9,15},{10,... | collective-permute-start | bytes 393224 | tf_op jit(solution)/shard_map/ppermute | solution.py:544
  25.3 1.7 %collective-permute-start.11 = (bf16[256,256]{1,0:T(8,128)(2,1)S(1)}, bf16[256,256]{1,0:T(8,128)(2,1)S(1)}, u32[]{:S(2)}, u32[]{:S(2)}) collective-permute-start(bf16[256,256]{1,0:T(8,128)(2,1)S(1)} %get-tuple-element.79), channel_id=1, source_target_pairs={{0,4},{1,5},{2,6},{3,7},{4,0},{5,1},{6,2},{7,3},{8,12},{9,13},{10,... | collective-permute-start | bytes 393224 | tf_op jit(solution)/shard_map/ppermute | solution.py:544
  27.0 5.3 %collective-permute-done.2.refs_2_ = bf16[528,128]{1,0:T(8,128)(2,1)S(1)} collective-permute-done((bf16[528,128]{1,0:T(8,128)(2,1)S(1)}, bf16[528,128]{1,0:T(8,128)(2,1)S(1)}, u32[]{:S(2)}, u32[]{:S(2)}) %collective-permute-start.2) | collective-permute-done | bytes 135200 | tf_op jit(solution)/shard_map/ppermute | solution.py:544
  32.3 0.7 copy-done.3
  33.2 0.7 assemble.1
  33.9 0.5 project_saved.1
  34.5 1.5 %collective-permute-start.13 = (bf16[512,256]{1,0:T(8,128)(2,1)S(1)}, bf16[512,256]{1,0:T(8,128)(2,1)S(1)}, u32[]{:S(2)}, u32[]{:S(2)}) collective-permute-start(bf16[512,256]{1,0:T(8,128)(2,1)S(1)} %get-tuple-element.80), channel_id=1, source_target_pairs={{0,1},{1,0},{2,3},{3,2},{4,5},{5,4},{6,7},{7,6},{8,9},{9,8},{10,11... | collective-permute-start | bytes 786440 | tf_op jit(solution)/shard_map/ppermute | solution.py:549
  36.2 2.9 %collective-permute-start.8 = (bf16[528,128]{1,0:T(8,128)(2,1)S(1)}, bf16[528,128]{1,0:T(8,128)(2,1)S(1)}, u32[]{:S(2)}, u32[]{:S(2)}) collective-permute-start(bf16[528,128]{1,0:T(8,128)(2,1)S(1)} %get-tuple-element.76), channel_id=1, source_target_pairs={{0,6},{1,7},{2,4},{3,5},{4,2},{5,3},{6,0},{7,1},{8,14},{9,15},{10,... | collective-permute-start | bytes 405512 | tf_op jit(solution)/shard_map/ppermute | solution.py:544
  39.1 0.6 collective-permute-start.9
  39.7 1.1 %collective-permute-done.11.refs_2_ = bf16[256,256]{1,0:T(8,128)(2,1)S(1)} collective-permute-done((bf16[256,256]{1,0:T(8,128)(2,1)S(1)}, bf16[256,256]{1,0:T(8,128)(2,1)S(1)}, u32[]{:S(2)}, u32[]{:S(2)}) %collective-permute-start.11) | collective-permute-done | bytes 131104 | tf_op jit(solution)/shard_map/ppermute | solution.py:544
  41.0 0.6 mix_saved.1
  41.6 0.6 backward.1
  42.4 2.0 %collective-permute-start.14 = (bf16[528,128]{1,0:T(8,128)(2,1)S(1)}, bf16[528,128]{1,0:T(8,128)(2,1)S(1)}, u32[]{:S(2)}, u32[]{:S(2)}) collective-permute-start(bf16[528,128]{1,0:T(8,128)(2,1)S(1)} %pack_act_near.1), channel_id=1, source_target_pairs={{0,2},{1,3},{2,0},{3,1},{4,6},{5,7},{6,4},{7,5},{8,10},{9,11},{10,... | collective-permute-start | bytes 405512 | tf_op jit(solution)/shard_map/ppermute | solution.py:544
  44.4 1.4 %collective-permute-start.16 = (bf16[512,256]{1,0:T(8,128)(2,1)S(1)}, bf16[512,256]{1,0:T(8,128)(2,1)S(1)}, u32[]{:S(2)}, u32[]{:S(2)}) collective-permute-start(bf16[512,256]{1,0:T(8,128)(2,1)S(1)} %get-tuple-element.91), channel_id=1, source_target_pairs={{0,1},{1,0},{2,3},{3,2},{4,5},{5,4},{6,7},{7,6},{8,9},{9,8},{10,11... | collective-permute-start | bytes 786440 | tf_op jit(solution)/shard_map/ppermute | solution.py:549
  45.8 0.9 %factor_grads.1 = (bf16[320,128]{1,0:T(8,128)(2,1)S(1)}, bf16[320,128]{1,0:T(8,128)(2,1)S(1)}) custom-call(bf16[4,256,256]{2,1,0:T(8,128)(2,1)S(1)} %get-tuple-element.86.refs_0_, bf16[4,256,256]{2,1,0:T(8,128)(2,1)S(1)} %get-tuple-element.87.refs_1_, bf16[1024,256]{1,0:T(8,128)(2,1)S(1)} %get-tuple-element.88.refs_2_, ...), custom_call_target="tpu_custom_call" | custom-call | tf_op jit(solution)/shard_map/factor_grads/pallas_call | solution.py:66
  46.8 1.9 %collective-permute-done.9.refs_2_.refs_4_ = bf16[528,128]{1,0:T(8,128)(2,1)S(1)} collective-permute-done((bf16[528,128]{1,0:T(8,128)(2,1)S(1)}, bf16[528,128]{1,0:T(8,128)(2,1)S(1)}, u32[]{:S(2)}, u32[]{:S(2)}) %collective-permute-start.9) | collective-permute-done | bytes 135200 | tf_op jit(solution)/shard_map/ppermute | solution.py:544
  48.7 0.6 collective-permute-done.14.refs_3_.refs_5_
  49.5 0.6 project_act.1
  50.1 2.0 %collective-permute-start.15 = (bf16[512,512]{1,0:T(8,128)(2,1)S(1)}, bf16[512,512]{1,0:T(8,128)(2,1)S(1)}, u32[]{:S(2)}, u32[]{:S(2)}) collective-permute-start(bf16[512,512]{1,0:T(8,128)(2,1)S(1)} %get-tuple-element.90.refs_5_.refs_0_), channel_id=1, source_target_pairs={{0,1},{1,0},{2,3},{3,2},{4,5},{5,4},{6,7},{7,6},{8,9},{9,8},{10,11... | collective-permute-start | bytes 1572872 | tf_op jit(solution)/shard_map/ppermute | solution.py:549
  52.2 0.5 adj_norm.1
  52.7 2.8 %collective-permute-start.17 = (bf16[128,512]{1,0:T(8,128)(2,1)S(1)}, bf16[128,512]{1,0:T(8,128)(2,1)S(1)}, u32[]{:S(2)}, u32[]{:S(2)}) collective-permute-start(bf16[128,512]{1,0:T(8,128)(2,1)S(1)} %get-tuple-element.97), channel_id=1, source_target_pairs={{0,6},{1,7},{2,4},{3,5},{4,2},{5,3},{6,0},{7,1},{8,14},{9,15},{10,... | collective-permute-start | bytes 393224 | tf_op jit(solution)/shard_map/ppermute | solution.py:544
  55.4 0.5 weight_grad.1
  56.3 1.5 %collective-permute-start.24 = (bf16[128,512]{1,0:T(8,128)(2,1)S(1)}, bf16[128,512]{1,0:T(8,128)(2,1)S(1)}, u32[]{:S(2)}, u32[]{:S(2)}) collective-permute-start(bf16[128,512]{1,0:T(8,128)(2,1)S(1)} %get-tuple-element.105), channel_id=1, source_target_pairs={{0,2},{1,3},{2,0},{3,1},{4,6},{5,7},{6,4},{7,5},{8,10},{9,11},{10,... | collective-permute-start | bytes 393224 | tf_op jit(solution)/shard_map/ppermute | solution.py:544
  57.8 3.0 %collective-permute-done.17.refs_1_.refs_4_ = bf16[128,512]{1,0:T(8,128)(2,1)S(1)} collective-permute-done((bf16[128,512]{1,0:T(8,128)(2,1)S(1)}, bf16[128,512]{1,0:T(8,128)(2,1)S(1)}, u32[]{:S(2)}, u32[]{:S(2)}) %collective-permute-start.17) | collective-permute-done | bytes 131104 | tf_op jit(solution)/shard_map/ppermute | solution.py:544
  60.8 4.1 %collective-permute-done.18.refs_2_.refs_5_ = bf16[128,512]{1,0:T(8,128)(2,1)S(1)} collective-permute-done((bf16[128,512]{1,0:T(8,128)(2,1)S(1)}, bf16[128,512]{1,0:T(8,128)(2,1)S(1)}, u32[]{:S(2)}, u32[]{:S(2)}) %collective-permute-start.18) | collective-permute-done | bytes 131104 | tf_op jit(solution)/shard_map/ppermute | solution.py:544
  65.0 0.4 mix_act.1.refs_0_
  66.0 2.0 %collective-permute-start.21 = (bf16[128,512]{1,0:T(8,128)(2,1)S(1)}, bf16[128,512]{1,0:T(8,128)(2,1)S(1)}, u32[]{:S(2)}, u32[]{:S(2)}) collective-permute-start(bf16[128,512]{1,0:T(8,128)(2,1)S(1)} %get-tuple-element.102), channel_id=1, source_target_pairs={{0,12},{1,13},{2,14},{3,15},{4,8},{5,9},{6,10},{7,11},{8,20},{9,21... | collective-permute-start | bytes 393224 | tf_op jit(solution)/shard_map/ppermute | solution.py:556
  67.9 1.9 %collective-permute-start.22 = (bf16[128,512]{1,0:T(8,128)(2,1)S(1)}, bf16[128,512]{1,0:T(8,128)(2,1)S(1)}, u32[]{:S(2)}, u32[]{:S(2)}) collective-permute-start(bf16[128,512]{1,0:T(8,128)(2,1)S(1)} %get-tuple-element.103), channel_id=1, source_target_pairs={{0,10},{1,11},{2,8},{3,9},{4,14},{5,15},{6,12},{7,13},{8,18},{9,19... | collective-permute-start | bytes 393224 | tf_op jit(solution)/shard_map/ppermute | solution.py:556
  69.8 1.0 %collective-permute-start.19 = (bf16[128,512]{1,0:T(8,128)(2,1)S(1)}, bf16[128,512]{1,0:T(8,128)(2,1)S(1)}, u32[]{:S(2)}, u32[]{:S(2)}) collective-permute-start(bf16[128,512]{1,0:T(8,128)(2,1)S(1)} %get-tuple-element.100.refs_7_), channel_id=1, source_target_pairs={{0,8},{1,9},{2,10},{3,11},{4,12},{5,13},{6,14},{7,15},{8,16},{9,17... | collective-permute-start | bytes 393224 | tf_op jit(solution)/shard_map/ppermute | solution.py:556
  70.8 0.7 input_grad.1.refs_4_
  71.6 1.2 %collective-permute-start.25 = (bf16[128,2048]{1,0:T(8,128)(2,1)S(1)}, bf16[128,2048]{1,0:T(8,128)(2,1)S(1)}, u32[]{:S(2)}, u32[]{:S(2)}) collective-permute-start(bf16[128,2048]{1,0:T(8,128)(2,1)S(1)} %input_grad.1.refs_4_), channel_id=1, source_target_pairs={{0,24},{8,0},{16,8},{24,16},{1,25},{9,1},{17,9},{25,17},{2,26},{10... | collective-permute-start | bytes 1572872 | tf_op jit(solution)/shard_map/ppermute | solution.py:685
  72.9 1.4 %collective-permute-done.20.refs_1_ = bf16[128,512]{1,0:T(8,128)(2,1)S(1)} collective-permute-done((bf16[128,512]{1,0:T(8,128)(2,1)S(1)}, bf16[128,512]{1,0:T(8,128)(2,1)S(1)}, u32[]{:S(2)}, u32[]{:S(2)}) %collective-permute-start.20) | collective-permute-done | bytes 131104 | tf_op jit(solution)/shard_map/ppermute | solution.py:556
  74.3 2.8 %collective-permute-start.26 = (bf16[352,128]{1,0:T(8,128)(2,1)S(1)}, bf16[352,128]{1,0:T(8,128)(2,1)S(1)}, u32[]{:S(2)}, u32[]{:S(2)}) collective-permute-start(bf16[352,128]{1,0:T(8,128)(2,1)S(1)} %get-tuple-element.110), channel_id=1, source_target_pairs={{0,6},{1,7},{2,4},{3,5},{4,2},{5,3},{6,0},{7,1},{8,14},{9,15},{10,... | collective-permute-start | bytes 270344 | tf_op jit(solution)/shard_map/ppermute | solution.py:544
  77.1 4.9 %collective-permute-done.21.refs_2_ = bf16[128,512]{1,0:T(8,128)(2,1)S(1)} collective-permute-done((bf16[128,512]{1,0:T(8,128)(2,1)S(1)}, bf16[128,512]{1,0:T(8,128)(2,1)S(1)}, u32[]{:S(2)}, u32[]{:S(2)}) %collective-permute-start.21) | collective-permute-done | bytes 131104 | tf_op jit(solution)/shard_map/ppermute | solution.py:556
  82.0 1.6 %collective-permute-start.28 = (bf16[352,128]{1,0:T(8,128)(2,1)S(1)}, bf16[352,128]{1,0:T(8,128)(2,1)S(1)}, u32[]{:S(2)}, u32[]{:S(2)}) collective-permute-start(bf16[352,128]{1,0:T(8,128)(2,1)S(1)} %get-tuple-element.112), channel_id=1, source_target_pairs={{0,2},{1,3},{2,0},{3,1},{4,6},{5,7},{6,4},{7,5},{8,10},{9,11},{10,... | collective-permute-start | bytes 270344 | tf_op jit(solution)/shard_map/ppermute | solution.py:544
  83.5 0.8 join_out.1
  84.4 0.8 store.1
  85.2 2.5 %collective-permute-done.27.refs_2_ = bf16[352,128]{1,0:T(8,128)(2,1)S(1)} collective-permute-done((bf16[352,128]{1,0:T(8,128)(2,1)S(1)}, bf16[352,128]{1,0:T(8,128)(2,1)S(1)}, u32[]{:S(2)}, u32[]{:S(2)}) %collective-permute-start.27) | collective-permute-done | bytes 90144 | tf_op jit(solution)/shard_map/ppermute | solution.py:544
  87.8 0.7 collective-permute-done.28.refs_3_
  88.4 1.0 %join_weight.1 = (f32[64,4,512]{2,1,0:T(4,128)}, f32[1,2048]{1,0:T(1,128)}, f32[2,64,64]{2,1,0:T(8,128)}, f32[8,16,16]{2,1,0:T(8,128)}) custom-call(bf16[352,128]{1,0:T(8,128)(2,1)S(1)} %get-tuple-element.106.refs_4_.refs_0_, bf16[352,128]{1,0:T(8,128)(2,1)S(1)} %collective-permute-done.26.refs_1_, bf16[352,128]{1,0:T(8,128)(2,1)S(1)} %collective-permute-done.27.refs_2_, ...), custom_call_target="tpu_custom_call" | custom-call | flops 3000000000 | tf_op jit(solution)/shard_map/join_weight/pallas_call | solution.py:66
  (53 shorter events, 2.8 us)
Async XLA Ops:
  0.6 1.1 %copy-start.5 = (bf16[1,8,16,16]{3,2,1,0:T(8,128)(2,1)S(1)}, bf16[1,8,16,16]{3,2,1,0:T(8,128)(2,1)}, u32[]{:S(2)}) copy-start(bf16[1,8,16,16]{3,2,1,0:T(8,128)(2,1)} %param.13) | copy-start | bytes 12292
  0.6 1.1 %copy-start.4 = (bf16[1,2,64,64]{3,2,1,0:T(8,128)(2,1)S(1)}, bf16[1,2,64,64]{3,2,1,0:T(8,128)(2,1)}, u32[]{:S(2)}) copy-start(bf16[1,2,64,64]{3,2,1,0:T(8,128)(2,1)} %param.12) | copy-start | bytes 49156
  0.7 7.0 %copy-start.1 = (bf16[1,128,2048]{2,1,0:T(8,128)(2,1)S(1)}, bf16[1,128,2048]{2,1,0:T(8,128)(2,1)}, u32[]{:S(2)}) copy-start(bf16[1,128,2048]{2,1,0:T(8,128)(2,1)} %param.9) | copy-start | bytes 1572868
  1.7 7.7 %copy-start.2 = (bf16[1,128,2048]{2,1,0:T(8,128)(2,1)S(1)}, bf16[1,128,2048]{2,1,0:T(8,128)(2,1)}, u32[]{:S(2)}) copy-start(bf16[1,128,2048]{2,1,0:T(8,128)(2,1)} %param.8) | copy-start | bytes 1572868
  1.8 11.4 %collective-permute-start.4 = (bf16[336,128]{1,0:T(8,128)(2,1)S(1)}, bf16[336,128]{1,0:T(8,128)(2,1)S(1)}, u32[]{:S(2)}, u32[]{:S(2)}) collective-permute-start(bf16[336,128]{1,0:T(8,128)(2,1)S(1)} %get-tuple-element.69), channel_id=1, source_target_pairs={{0,6},{1,7},{2,4},{3,5},{4,2},{5,3},{6,0},{7,1},{8,14},{9,15},{10,... | collective-permute-start | bytes 258056 | tf_op jit(solution)/shard_map/ppermute | solution.py:544
  7.0 13.8 %collective-permute-start.5 = (bf16[336,128]{1,0:T(8,128)(2,1)S(1)}, bf16[336,128]{1,0:T(8,128)(2,1)S(1)}, u32[]{:S(2)}, u32[]{:S(2)}) collective-permute-start(bf16[336,128]{1,0:T(8,128)(2,1)S(1)} %get-tuple-element.70), channel_id=1, source_target_pairs={{0,4},{1,5},{2,6},{3,7},{4,0},{5,1},{6,2},{7,3},{8,12},{9,13},{10,... | collective-permute-start | bytes 258056 | tf_op jit(solution)/shard_map/ppermute | solution.py:544
  7.0 13.8 %collective-permute-start.6 = (bf16[336,128]{1,0:T(8,128)(2,1)S(1)}, bf16[336,128]{1,0:T(8,128)(2,1)S(1)}, u32[]{:S(2)}, u32[]{:S(2)}) collective-permute-start(bf16[336,128]{1,0:T(8,128)(2,1)S(1)} %get-tuple-element.71), channel_id=1, source_target_pairs={{0,2},{1,3},{2,0},{3,1},{4,6},{5,7},{6,4},{7,5},{8,10},{9,11},{10,... | collective-permute-start | bytes 258056 | tf_op jit(solution)/shard_map/ppermute | solution.py:544
  7.7 14.7 %collective-permute-start = (bf16[4,128,256]{2,1,0:T(8,128)(2,1)S(1)}, bf16[4,128,256]{2,1,0:T(8,128)(2,1)S(1)}, u32[]{:S(2)}, u32[]{:S(2)}) collective-permute-start(bf16[4,128,256]{2,1,0:T(8,128)(2,1)S(1)} %get-tuple-element.64), channel_id=1, source_target_pairs={{0,1},{1,0},{2,3},{3,2},{4,5},{5,4},{6,7},{7,6},{8,9},{9,8},{10,11... | collective-permute-start | bytes 786440 | tf_op jit(solution)/shard_map/ppermute | solution.py:549
  9.6 15.7 %collective-permute-start.1 = (bf16[528,128]{1,0:T(8,128)(2,1)S(1)}, bf16[528,128]{1,0:T(8,128)(2,1)S(1)}, u32[]{:S(2)}, u32[]{:S(2)}) collective-permute-start(bf16[528,128]{1,0:T(8,128)(2,1)S(1)} %get-tuple-element.66), channel_id=1, source_target_pairs={{0,6},{1,7},{2,4},{3,5},{4,2},{5,3},{6,0},{7,1},{8,14},{9,15},{10,... | collective-permute-start | bytes 405512 | tf_op jit(solution)/shard_map/ppermute | solution.py:544
  13.3 19.0 %collective-permute-start.2 = (bf16[528,128]{1,0:T(8,128)(2,1)S(1)}, bf16[528,128]{1,0:T(8,128)(2,1)S(1)}, u32[]{:S(2)}, u32[]{:S(2)}) collective-permute-start(bf16[528,128]{1,0:T(8,128)(2,1)S(1)} %get-tuple-element.67), channel_id=1, source_target_pairs={{0,4},{1,5},{2,6},{3,7},{4,0},{5,1},{6,2},{7,3},{8,12},{9,13},{10,... | collective-permute-start | bytes 405512 | tf_op jit(solution)/shard_map/ppermute | solution.py:544
  20.8 12.4 %collective-permute-start.7 = (bf16[1344,128]{1,0:T(8,128)(2,1)S(1)}, bf16[1344,128]{1,0:T(8,128)(2,1)S(1)}, u32[]{:S(2)}, u32[]{:S(2)}) collective-permute-start(bf16[1344,128]{1,0:T(8,128)(2,1)S(1)} %relay.1.refs_2_.refs_0_), channel_id=1, source_target_pairs={{0,1},{1,0},{2,3},{3,2},{4,5},{5,4},{6,7},{7,6},{8,9},{9,8},{10,11... | collective-permute-start | bytes 1032200 | tf_op jit(solution)/shard_map/ppermute | solution.py:549
  22.4 9.9 %collective-permute-start.3 = (bf16[528,128]{1,0:T(8,128)(2,1)S(1)}, bf16[528,128]{1,0:T(8,128)(2,1)S(1)}, u32[]{:S(2)}, u32[]{:S(2)}) collective-permute-start(bf16[528,128]{1,0:T(8,128)(2,1)S(1)} %get-tuple-element.68), channel_id=1, source_target_pairs={{0,2},{1,3},{2,0},{3,1},{4,6},{5,7},{6,4},{7,5},{8,10},{9,11},{10,... | collective-permute-start | bytes 405512 | tf_op jit(solution)/shard_map/ppermute | solution.py:544
  22.4 16.7 %collective-permute-start.10 = (bf16[256,256]{1,0:T(8,128)(2,1)S(1)}, bf16[256,256]{1,0:T(8,128)(2,1)S(1)}, u32[]{:S(2)}, u32[]{:S(2)}) collective-permute-start(bf16[256,256]{1,0:T(8,128)(2,1)S(1)} %get-tuple-element.78), channel_id=1, source_target_pairs={{0,6},{1,7},{2,4},{3,5},{4,2},{5,3},{6,0},{7,1},{8,14},{9,15},{10,... | collective-permute-start | bytes 393224 | tf_op jit(solution)/shard_map/ppermute | solution.py:544
  25.3 15.5 %collective-permute-start.11 = (bf16[256,256]{1,0:T(8,128)(2,1)S(1)}, bf16[256,256]{1,0:T(8,128)(2,1)S(1)}, u32[]{:S(2)}, u32[]{:S(2)}) collective-permute-start(bf16[256,256]{1,0:T(8,128)(2,1)S(1)} %get-tuple-element.79), channel_id=1, source_target_pairs={{0,4},{1,5},{2,6},{3,7},{4,0},{5,1},{6,2},{7,3},{8,12},{9,13},{10,... | collective-permute-start | bytes 393224 | tf_op jit(solution)/shard_map/ppermute | solution.py:544
  32.3 0.7 copy-start.3
  34.4 1.6 %copy-start = (bf16[1,128,2048]{2,1,0:T(8,128)(2,1)S(1)}, bf16[1,128,2048]{2,1,0:T(8,128)(2,1)}, u32[]{:S(2)}) copy-start(bf16[1,128,2048]{2,1,0:T(8,128)(2,1)} %param.7) | copy-start | bytes 1572868
  34.5 6.3 %collective-permute-start.12 = (bf16[256,256]{1,0:T(8,128)(2,1)S(1)}, bf16[256,256]{1,0:T(8,128)(2,1)S(1)}, u32[]{:S(2)}, u32[]{:S(2)}) collective-permute-start(bf16[256,256]{1,0:T(8,128)(2,1)S(1)} %pack_grad_near.1.refs_1_), channel_id=1, source_target_pairs={{0,2},{1,3},{2,0},{3,1},{4,6},{5,7},{6,4},{7,5},{8,10},{9,11},{10,... | collective-permute-start | bytes 393224 | tf_op jit(solution)/shard_map/ppermute | solution.py:544
  34.5 6.4 %collective-permute-start.13 = (bf16[512,256]{1,0:T(8,128)(2,1)S(1)}, bf16[512,256]{1,0:T(8,128)(2,1)S(1)}, u32[]{:S(2)}, u32[]{:S(2)}) collective-permute-start(bf16[512,256]{1,0:T(8,128)(2,1)S(1)} %get-tuple-element.80), channel_id=1, source_target_pairs={{0,1},{1,0},{2,3},{3,2},{4,5},{5,4},{6,7},{7,6},{8,9},{9,8},{10,11... | collective-permute-start | bytes 786440 | tf_op jit(solution)/shard_map/ppermute | solution.py:549
  36.2 10.6 %collective-permute-start.8 = (bf16[528,128]{1,0:T(8,128)(2,1)S(1)}, bf16[528,128]{1,0:T(8,128)(2,1)S(1)}, u32[]{:S(2)}, u32[]{:S(2)}) collective-permute-start(bf16[528,128]{1,0:T(8,128)(2,1)S(1)} %get-tuple-element.76), channel_id=1, source_target_pairs={{0,6},{1,7},{2,4},{3,5},{4,2},{5,3},{6,0},{7,1},{8,14},{9,15},{10,... | collective-permute-start | bytes 405512 | tf_op jit(solution)/shard_map/ppermute | solution.py:544
  39.1 9.6 %collective-permute-start.9 = (bf16[528,128]{1,0:T(8,128)(2,1)S(1)}, bf16[528,128]{1,0:T(8,128)(2,1)S(1)}, u32[]{:S(2)}, u32[]{:S(2)}) collective-permute-start(bf16[528,128]{1,0:T(8,128)(2,1)S(1)} %get-tuple-element.77), channel_id=1, source_target_pairs={{0,4},{1,5},{2,6},{3,7},{4,0},{5,1},{6,2},{7,3},{8,12},{9,13},{10,... | collective-permute-start | bytes 405512 | tf_op jit(solution)/shard_map/ppermute | solution.py:544
  42.4 6.9 %collective-permute-start.14 = (bf16[528,128]{1,0:T(8,128)(2,1)S(1)}, bf16[528,128]{1,0:T(8,128)(2,1)S(1)}, u32[]{:S(2)}, u32[]{:S(2)}) collective-permute-start(bf16[528,128]{1,0:T(8,128)(2,1)S(1)} %pack_act_near.1), channel_id=1, source_target_pairs={{0,2},{1,3},{2,0},{3,1},{4,6},{5,7},{6,4},{7,5},{8,10},{9,11},{10,... | collective-permute-start | bytes 405512 | tf_op jit(solution)/shard_map/ppermute | solution.py:544
  44.4 7.7 %collective-permute-start.16 = (bf16[512,256]{1,0:T(8,128)(2,1)S(1)}, bf16[512,256]{1,0:T(8,128)(2,1)S(1)}, u32[]{:S(2)}, u32[]{:S(2)}) collective-permute-start(bf16[512,256]{1,0:T(8,128)(2,1)S(1)} %get-tuple-element.91), channel_id=1, source_target_pairs={{0,1},{1,0},{2,3},{3,2},{4,5},{5,4},{6,7},{7,6},{8,9},{9,8},{10,11... | collective-permute-start | bytes 786440 | tf_op jit(solution)/shard_map/ppermute | solution.py:549
  50.1 14.9 %collective-permute-start.15 = (bf16[512,512]{1,0:T(8,128)(2,1)S(1)}, bf16[512,512]{1,0:T(8,128)(2,1)S(1)}, u32[]{:S(2)}, u32[]{:S(2)}) collective-permute-start(bf16[512,512]{1,0:T(8,128)(2,1)S(1)} %get-tuple-element.90.refs_5_.refs_0_), channel_id=1, source_target_pairs={{0,1},{1,0},{2,3},{3,2},{4,5},{5,4},{6,7},{7,6},{8,9},{9,8},{10,11... | collective-permute-start | bytes 1572872 | tf_op jit(solution)/shard_map/ppermute | solution.py:549
  52.7 8.1 %collective-permute-start.17 = (bf16[128,512]{1,0:T(8,128)(2,1)S(1)}, bf16[128,512]{1,0:T(8,128)(2,1)S(1)}, u32[]{:S(2)}, u32[]{:S(2)}) collective-permute-start(bf16[128,512]{1,0:T(8,128)(2,1)S(1)} %get-tuple-element.97), channel_id=1, source_target_pairs={{0,6},{1,7},{2,4},{3,5},{4,2},{5,3},{6,0},{7,1},{8,14},{9,15},{10,... | collective-permute-start | bytes 393224 | tf_op jit(solution)/shard_map/ppermute | solution.py:544
  55.4 9.4 %collective-permute-start.18 = (bf16[128,512]{1,0:T(8,128)(2,1)S(1)}, bf16[128,512]{1,0:T(8,128)(2,1)S(1)}, u32[]{:S(2)}, u32[]{:S(2)}) collective-permute-start(bf16[128,512]{1,0:T(8,128)(2,1)S(1)} %get-tuple-element.98), channel_id=1, source_target_pairs={{0,4},{1,5},{2,6},{3,7},{4,0},{5,1},{6,2},{7,3},{8,12},{9,13},{10,... | collective-permute-start | bytes 393224 | tf_op jit(solution)/shard_map/ppermute | solution.py:544
  56.0 15.6 %collective-permute-start.23 = (bf16[352,512]{1,0:T(8,128)(2,1)S(1)}, bf16[352,512]{1,0:T(8,128)(2,1)S(1)}, u32[]{:S(2)}, u32[]{:S(2)}) collective-permute-start(bf16[352,512]{1,0:T(8,128)(2,1)S(1)} %get-tuple-element.104), channel_id=1, source_target_pairs={{0,1},{1,0},{2,3},{3,2},{4,5},{5,4},{6,7},{7,6},{8,9},{9,8},{10,11... | collective-permute-start | bytes 1081352 | tf_op jit(solution)/shard_map/ppermute | solution.py:549
  56.3 13.5 %collective-permute-start.24 = (bf16[128,512]{1,0:T(8,128)(2,1)S(1)}, bf16[128,512]{1,0:T(8,128)(2,1)S(1)}, u32[]{:S(2)}, u32[]{:S(2)}) collective-permute-start(bf16[128,512]{1,0:T(8,128)(2,1)S(1)} %get-tuple-element.105), channel_id=1, source_target_pairs={{0,2},{1,3},{2,0},{3,1},{4,6},{5,7},{6,4},{7,5},{8,10},{9,11},{10,... | collective-permute-start | bytes 393224 | tf_op jit(solution)/shard_map/ppermute | solution.py:544
  65.7 8.6 %collective-permute-start.20 = (bf16[128,512]{1,0:T(8,128)(2,1)S(1)}, bf16[128,512]{1,0:T(8,128)(2,1)S(1)}, u32[]{:S(2)}, u32[]{:S(2)}) collective-permute-start(bf16[128,512]{1,0:T(8,128)(2,1)S(1)} %get-tuple-element.101), channel_id=1, source_target_pairs={{0,14},{1,15},{2,12},{3,13},{4,10},{5,11},{6,8},{7,9},{8,22},{9,23... | collective-permute-start | bytes 393224 | tf_op jit(solution)/shard_map/ppermute | solution.py:556
  66.0 16.0 %collective-permute-start.21 = (bf16[128,512]{1,0:T(8,128)(2,1)S(1)}, bf16[128,512]{1,0:T(8,128)(2,1)S(1)}, u32[]{:S(2)}, u32[]{:S(2)}) collective-permute-start(bf16[128,512]{1,0:T(8,128)(2,1)S(1)} %get-tuple-element.102), channel_id=1, source_target_pairs={{0,12},{1,13},{2,14},{3,15},{4,8},{5,9},{6,10},{7,11},{8,20},{9,21... | collective-permute-start | bytes 393224 | tf_op jit(solution)/shard_map/ppermute | solution.py:556
  67.9 14.0 %collective-permute-start.22 = (bf16[128,512]{1,0:T(8,128)(2,1)S(1)}, bf16[128,512]{1,0:T(8,128)(2,1)S(1)}, u32[]{:S(2)}, u32[]{:S(2)}) collective-permute-start(bf16[128,512]{1,0:T(8,128)(2,1)S(1)} %get-tuple-element.103), channel_id=1, source_target_pairs={{0,10},{1,11},{2,8},{3,9},{4,14},{5,15},{6,12},{7,13},{8,18},{9,19... | collective-permute-start | bytes 393224 | tf_op jit(solution)/shard_map/ppermute | solution.py:556
  69.8 13.7 %collective-permute-start.19 = (bf16[128,512]{1,0:T(8,128)(2,1)S(1)}, bf16[128,512]{1,0:T(8,128)(2,1)S(1)}, u32[]{:S(2)}, u32[]{:S(2)}) collective-permute-start(bf16[128,512]{1,0:T(8,128)(2,1)S(1)} %get-tuple-element.100.refs_7_), channel_id=1, source_target_pairs={{0,8},{1,9},{2,10},{3,11},{4,12},{5,13},{6,14},{7,15},{8,16},{9,17... | collective-permute-start | bytes 393224 | tf_op jit(solution)/shard_map/ppermute | solution.py:556
  71.6 12.8 %collective-permute-start.25 = (bf16[128,2048]{1,0:T(8,128)(2,1)S(1)}, bf16[128,2048]{1,0:T(8,128)(2,1)S(1)}, u32[]{:S(2)}, u32[]{:S(2)}) collective-permute-start(bf16[128,2048]{1,0:T(8,128)(2,1)S(1)} %input_grad.1.refs_4_), channel_id=1, source_target_pairs={{0,24},{8,0},{16,8},{24,16},{1,25},{9,1},{17,9},{25,17},{2,26},{10... | collective-permute-start | bytes 1572872 | tf_op jit(solution)/shard_map/ppermute | solution.py:685
  74.3 10.9 %collective-permute-start.26 = (bf16[352,128]{1,0:T(8,128)(2,1)S(1)}, bf16[352,128]{1,0:T(8,128)(2,1)S(1)}, u32[]{:S(2)}, u32[]{:S(2)}) collective-permute-start(bf16[352,128]{1,0:T(8,128)(2,1)S(1)} %get-tuple-element.110), channel_id=1, source_target_pairs={{0,6},{1,7},{2,4},{3,5},{4,2},{5,3},{6,0},{7,1},{8,14},{9,15},{10,... | collective-permute-start | bytes 270344 | tf_op jit(solution)/shard_map/ppermute | solution.py:544
  81.9 5.8 %collective-permute-start.27 = (bf16[352,128]{1,0:T(8,128)(2,1)S(1)}, bf16[352,128]{1,0:T(8,128)(2,1)S(1)}, u32[]{:S(2)}, u32[]{:S(2)}) collective-permute-start(bf16[352,128]{1,0:T(8,128)(2,1)S(1)} %get-tuple-element.111), channel_id=1, source_target_pairs={{0,4},{1,5},{2,6},{3,7},{4,0},{5,1},{6,2},{7,3},{8,12},{9,13},{10,... | collective-permute-start | bytes 270344 | tf_op jit(solution)/shard_map/ppermute | solution.py:544
  82.0 6.5 %collective-permute-start.28 = (bf16[352,128]{1,0:T(8,128)(2,1)S(1)}, bf16[352,128]{1,0:T(8,128)(2,1)S(1)}, u32[]{:S(2)}, u32[]{:S(2)}) collective-permute-start(bf16[352,128]{1,0:T(8,128)(2,1)S(1)} %get-tuple-element.112), channel_id=1, source_target_pairs={{0,2},{1,3},{2,0},{3,1},{4,6},{5,7},{6,4},{7,5},{8,10},{9,11},{10,... | collective-permute-start | bytes 270344 | tf_op jit(solution)/shard_map/ppermute | solution.py:544
